TPU v7x, 128 devices: a whole 4x4x4 slice. The times are simulated.
128 devices in a mesh: seq: 32 (over z_lo, y, x), chan: 4 (over z_hi, core).
Axes of the slice: x: 4, y: 4, z: 4 (z_hi: 2, z_lo: 2; z = z_hi * 2 + z_lo), core: 2. Of those that a mesh axis runs over, the one named last changes fastest.
Arguments:
- trunk: bfloat16 [4, 8192, 1536], P(None, 'seq', 'chan'), may hold values from -6 to 6
- merged: bfloat16 [4, 768, 16384], P(None, 'chan', 'seq'), may hold values from -40 to 40
- conv_w: bfloat16 [5, 1536, 768], P(None, 'chan'), may hold values from -0.0625 to 0.0625
- norm_gain: float32 [768], P('chan'), may hold values from 0.25 to 1.75
- head_w: bfloat16 [768, 1024], P('chan'), may hold values from -0.21875 to 0.21875
- head_bias: float32 [1024], replicated, may hold values from -4 to 4
- head_scale: float32 [7], replicated, may hold values from 0.5 to 2
- head_of_track: int32 [1024], replicated, may hold values from 0 to 6
- valid_len: int32 [4], replicated, may hold values from 4096 to 16384
- cot: bfloat16 [4, 1024, 16384], P(None, 'seq'), may hold values from -6 to 6
Outputs:
- d_trunk: bfloat16 [4, 8192, 1536], P(None, 'seq', 'chan')
- d_skip: bfloat16 [4, 768, 16384], P(None, 'chan', 'seq')
- d_conv_w: float32 [5, 768, 1536], P(None, 'seq', 'chan')
All inputs are finite; a program needn't handle non-finite values.
Results may differ from a plain program's by a relative error of at most 0.0059.
Values may be sent and summed in bfloat16 or wider, within the bound.
No kernel may reach another device: no remote copies, remote signals or barrier semaphores. Data moves between devices by JAX's collectives and lax.ppermute only.
A program may use at most 128 MiB of HBM per device.

v0:
```python
import math

import jax
import jax.numpy as jnp
from jax import lax
from jax.sharding import PartitionSpec as P

C_OUT = 768
KERNEL = 5


epsilon = 1e-06


def padded(x, sides, width):
    for axis, dim in sides:
        count, length = (lax.axis_size(axis), x.shape[dim])
        up = [(i, (i + 1) % count) for i in range(count - 1)]
        down = [(j, i) for i, j in up]
        last = lax.slice_in_dim(x, length - width, length, axis=dim)
        first = lax.slice_in_dim(x, 0, width, axis=dim)
        before = lax.ppermute(last, axis, up)
        after = lax.ppermute(first, axis, down)
        x = jnp.concatenate([before, x, after], axis=dim)
    return x


def local(
    trunk, merged, conv_w, norm_gain, head_w, head_bias, head_scale, head_of_track, valid_len, cot
):
    batch_count, chan_width, positions = merged.shape
    seq_count = lax.axis_size("seq")
    local_cot = lax.all_to_all(cot, "seq", split_axis=2, concat_axis=1, tiled=True)
    merged32 = merged.astype(jnp.float32)
    gain32 = norm_gain[:, None]
    normed = (merged32 * gain32).astype(jnp.bfloat16)
    squares = jnp.sum(merged32 * merged32, axis=1)
    partial_raw = jnp.einsum("bcp,ct->btp", normed, head_w, preferred_element_type=jnp.float32)
    raw_scores, total_sq = lax.psum((partial_raw, squares), "chan")
    inv_rms = lax.rsqrt(total_sq / C_OUT + epsilon)[:, None, :]
    logits = inv_rms * raw_scores + head_bias[:, None]
    offset = lax.axis_index("seq") * positions
    position_ids = offset + jnp.arange(positions, dtype=jnp.int32)
    live_mask = (position_ids[None, :] < valid_len[:, None]).astype(jnp.float32)[:, None, :]
    onehot = (
        head_of_track[:, None] == jnp.arange(head_scale.shape[0], dtype=jnp.int32)[None, :]
    ).astype(jnp.float32)
    track_scale = jnp.sum(onehot * head_scale[None, :], axis=1)[:, None]
    d_logits = live_mask * local_cot.astype(jnp.float32) * track_scale * jax.nn.sigmoid(logits)
    d_rms = jnp.sum(d_logits * raw_scores, axis=1, keepdims=True)
    scaled = (inv_rms * d_logits).astype(jnp.bfloat16)
    d_normed = jnp.einsum("btp,ct->bcp", scaled, head_w, preferred_element_type=jnp.float32)
    d_merged = d_normed * gain32 - inv_rms**3 * d_rms * merged32 / C_OUT
    d_skip = d_merged.astype(jnp.bfloat16)
    rimmed = padded(d_skip, (("seq", 2),), 2)
    full_grad = lax.all_gather(rimmed, "chan", axis=1, tiled=True)
    upsampled = jnp.repeat(trunk, 2, axis=1)
    in_width = trunk.shape[2]
    d_up = jnp.zeros((batch_count, positions, in_width), jnp.float32)
    grad_list = []
    for shift_tap in range(KERNEL):
        window = full_grad[:, :, 4 - shift_tap : 4 - shift_tap + positions]
        d_up = d_up + jnp.einsum(
            "bop,io->bpi", window, conv_w[shift_tap], preferred_element_type=jnp.float32
        )
        grad_list.append(
            jnp.einsum("bpi,bop->oi", upsampled, window, preferred_element_type=jnp.float32)
        )
    d_trunk = (
        d_up.reshape(batch_count, positions // 2, 2, in_width).sum(axis=2).astype(jnp.bfloat16)
    )
    grad_scale = 1.0 / math.sqrt(batch_count * positions * seq_count)
    weight_terms = jnp.stack(grad_list) * grad_scale
    d_conv_w = lax.psum_scatter(weight_terms, "seq", scatter_dimension=1, tiled=True)
    return (d_trunk, d_skip, d_conv_w)


def solution(mesh):
    placed = (
        P(None, "seq", "chan"),
        P(None, "chan", "seq"),
        P(None, "chan", None),
        P("chan"),
        P("chan", None),
        P(),
        P(),
        P(),
        P(),
        P(None, "seq", None),
    )
    return jax.shard_map(
        local,
        mesh=mesh,
        in_specs=placed,
        out_specs=(P(None, "seq", "chan"), P(None, "chan", "seq"), P(None, "seq", "chan")),
        check_vma=False,
    )
```

profile of v0, /device:TPU:0, one launch (start us, length us, event | category | flops | bytes accessed | tf_op | source)
XLA Modules:
  0.0 485.3 jit_solution(8368485349894044087)
XLA Ops:
  8.2 5.8 %convolution_bitcast_fusion = f32[4,1024,512]{1,2,0:T(8,128)} fusion(bf16[4,192,512]{2,1,0:T(8,128)(2,1)} %param.11, f32[192]{0:T(256)} %param.13, bf16[192,1024]{1,0:T(8,128)(2,1)S(1)} %copy-done), kind=kOutput, calls=%fused_computation.6 | convolution fusion | flops 806486016 | bytes 9569024 | tf_op jit(solution)/shard_map/bcp,ct->btp/dot_general | solution.py:38
  14.0 20.4 %copy.55 = bf16[4,32,16384]{1,0,2:T(4,128)(2,1)} copy(bf16[4,32,16384]{2,1,0:T(8,128)(2,1)} %param.19) | data formatting | bytes 8388608 | tf_op args[9]
  34.3 27.9 %reshape.69 = bf16[32,2,32768]{2,1,0:T(2,128)(2,1)} reshape(bf16[16384,4,32]{2,1,0:T(4,128)(2,1)} %bitcast.72) | data formatting | bytes 8388608
  62.3 9.0 %all-to-all-start = ((bf16[32,2,32768]{2,1,0:T(2,128)(2,1)}), bf16[32,2,32768]{2,1,0:T(2,128)(2,1)}, u32[]{:S(2)}, u32[]{:S(2)}) async-start(bf16[32,2,32768]{2,1,0:T(2,128)(2,1)} %reshape.69), calls=%async_computation | async-start | bytes 8388608 | tf_op jit(solution)/shard_map/all_to_all | solution.py:33
  71.5 53.5 %psum.14 = f32[4,512]{1,0:T(4,128)S(1)} all-reduce(f32[4,512]{1,0:T(4,128)S(1)} %fusion.22), channel_id=1, replica_groups=mesh['seq'=32,'chan'=4] {'chan'}, use_global_device_ids=true, to_apply=%region_1.0 | all-reduce | flops 2048 | bytes 16384 | tf_op jit(solution)/shard_map/psum | solution.py:39
  125.2 24.5 %reshape.70 = bf16[16384,4,32]{2,1,0:T(4,128)(2,1)} reshape(bf16[32,2,32768]{2,1,0:T(2,128)(2,1)} %all-to-all-done) | data formatting | bytes 8388608
  149.8 20.7 %copy.56 = bf16[4,32,16384]{2,1,0:T(8,128)(2,1)} copy(bf16[4,32,16384]{1,0,2:T(4,128)(2,1)} %bitcast.71) | data formatting | bytes 8388608 | tf_op jit(solution)/shard_map/all_to_all | solution.py:33
  170.5 3.9 copy.71
  174.4 1.9 bitcast_bitcast_fusion
  176.3 8.1 %copy.57 = f32[4,32,32,512]{3,2,1,0:T(8,128)} copy(f32[4,32,32,512]{3,1,2,0:T(8,128)S(1)} %bitcast_bitcast_fusion) | data formatting | bytes 16777216 | tf_op jit(solution)/shard_map/convert_element_type | solution.py:49
  184.4 8.8 %copy.58 = f32[4,1024,512]{1,2,0:T(8,128)} copy(f32[4,1024,512]{2,1,0:T(8,128)} %bitcast.74) | data formatting | bytes 16777216 | tf_op jit(solution)/shard_map/convert_element_type | solution.py:49
  193.2 29.0 %all-reduce.2.cloned.1.call-done = f32[4,1024,512]{1,2,0:T(8,128)} async-done(((f32[4,1024,512]{1,2,0:T(8,128)}), f32[4,1024,512]{1,2,0:T(8,128)}) %all-reduce.2.cloned.1.call-update) | async-done | bytes 8388624 | tf_op jit(solution)/shard_map/psum | solution.py:39
  222.1 7.7 %multiply_reduce_fusion = f32[4,512]{1,0:T(4,128)S(1)} fusion(f32[4,1024,512]{1,2,0:T(8,128)} %all-reduce.2.cloned.1.call-done, f32[1024]{0:T(1024)S(1)} %copy-done.11, f32[4,512]{1,0:T(4,128)S(1)} %add_rsqrt_fusion, f32[1024]{0:T(1024)S(1)} %select_reduce_fusion, f32[4,1024,512]{1,2,0:T(8,128)} %copy.58, f32[4,512]{1,0:T(4,128)S(1)} %compare_convert_fusion), kind=kLoop, calls=%fused_computation.1 | loop fusion | flops 20969472 | bytes 16809984 | tf_op jit(solution)/shard_map/reduce_sum | solution.py:50
  230.4 2.4 copy-done.3
  232.8 4.0 fusion.26
  236.9 3.5 collective-permute-start
  241.7 3.2 collective-permute-done
  244.9 4.1 collective-permute-done.1
  252.1 38.6 %all-gather.2.cloned.1.call-done = bf16[4,768,516]{2,1,0:T(8,128)(2,1)} async-done(((bf16[4,192,516]{2,1,0:T(8,128)(2,1)}), bf16[4,768,516]{2,1,0:T(8,128)(2,1)}) %all-gather.2.cloned.1.call-update) | async-done | bytes 3170320 | tf_op jit(solution)/shard_map/all_gather | solution.py:56
  290.7 4.1 fusion.30
  294.8 1.9 fusion.36
  296.7 1.9 fusion.42
  298.6 1.9 fusion.48
  302.3 2.9 broadcast_multiply_fusion
  307.0 5.0 %fusion.12 = f32[4,512,384]{2,1,0:T(8,128)S(1)} fusion(bf16[4,768,516]{2,1,0:T(8,128)(2,1)} %all-gather.2.cloned.1.call-done, bf16[5,384,768]{2,1,0:T(8,128)(2,1)S(1)} %copy-done.9), kind=kOutput, calls=%fused_computation.19 | convolution fusion | flops 1207959552 | bytes 6881280 | tf_op jit(solution)/shard_map/bop,io->bpi/dot_general | solution.py:63
  312.1 3.0 fusion.16
  315.1 2.8 fusion.20
  317.9 2.8 fusion.8
  320.7 3.4 add_add_fusion
  324.0 3.4 reshape.54
  327.4 6.6 %reduce_sum.39 = bf16[4,256,384]{2,1,0:T(8,128)(2,1)} reduce(f32[4,256,2,384]{3,2,1,0:T(2,128)} %reshape.54, f32[]{:T(128)} %constant.8.clone.1), dimensions={2}, to_apply=%region_5.0 | reduce | flops 393216 | bytes 3932164 | tf_op jit(solution)/shard_map/reduce_sum | solution.py:70
  334.0 144.5 %reduce-scatter.2.cloned.1.call-done = f32[5,24,384]{2,1,0:T(8,128)} async-done(((f32[5,768,384]{2,1,0:T(8,128)}), f32[5,24,384]{2,1,0:T(8,128)}) %reduce-scatter.2.cloned.1.call-update) | async-done | bytes 184336 | tf_op jit(solution)/shard_map/reduce_scatter | solution.py:74
  (48 shorter events, 10.0 us)
Async XLA Ops:
  7.2 1.0 copy-start
  7.2 215.0 %all-reduce.2.cloned.1.call-start = ((), (), s32[]{:S(2)}) async-start(), calls=%async_computation.2 | async-start | bytes 16777216 | tf_op jit(solution)/shard_map/psum | solution.py:39
  62.2 9.1 %copy-start.4 = (bf16[4,192,512]{2,1,0:T(8,128)(2,1)S(1)}, bf16[4,192,512]{2,1,0:T(8,128)(2,1)}, u32[]{:S(2)}) copy-start(bf16[4,192,512]{2,1,0:T(8,128)(2,1)} %param.11) | copy-start | bytes 2359300
  62.2 62.8 %copy-start.10 = (s32[1024]{0:T(1024)S(1)}, s32[1024]{0:T(1024)}, u32[]{:S(2)}) copy-start(s32[1024]{0:T(1024)} %param.17) | copy-start | bytes 12292
  62.2 62.8 %copy-start.13 = (f32[7]{0:T(128)S(1)}, f32[7]{0:T(128)}, u32[]{:S(2)}) copy-start(f32[7]{0:T(128)} %param.16) | copy-start | bytes 88
  62.2 62.9 %copy-start.14 = (s32[4]{0:T(128)S(1)}, s32[4]{0:T(128)}, u32[]{:S(2)}) copy-start(s32[4]{0:T(128)} %param.18) | copy-start | bytes 52
  62.3 63.0 %all-to-all-start = ((bf16[32,2,32768]{2,1,0:T(2,128)(2,1)}), bf16[32,2,32768]{2,1,0:T(2,128)(2,1)}, u32[]{:S(2)}, u32[]{:S(2)}) async-start(bf16[32,2,32768]{2,1,0:T(2,128)(2,1)} %reshape.69), calls=%async_computation | async-start | bytes 8388608 | tf_op jit(solution)/shard_map/all_to_all | solution.py:33
  71.3 219.4 %all-gather.2.cloned.1.call-start = ((), (), s32[]{:S(2)}) async-start(), calls=%async_computation.3 | async-start | bytes 4915200 | tf_op jit(solution)/shard_map/all_gather | solution.py:56
  184.4 37.8 %copy-start.11 = (f32[1024]{0:T(1024)S(1)}, f32[1024]{0:T(1024)}, u32[]{:S(2)}) copy-start(f32[1024]{0:T(1024)} %param.15) | copy-start | bytes 12292
  193.2 36.7 %copy-start.12 = (f32[192]{0:T(256)S(1)}, f32[192]{0:T(256)}, u32[]{:S(2)}) copy-start(f32[192]{0:T(256)} %param.13) | copy-start | bytes 2308
  222.1 8.2 %copy-start.2 = (f32[4,1024,512]{1,2,0:T(8,128)S(1)}, f32[4,1024,512]{1,2,0:T(8,128)}, u32[]{:S(2)}) copy-start(f32[4,1024,512]{1,2,0:T(8,128)} %copy.58) | copy-start | bytes 25165828
  222.1 10.6 %copy-start.3 = (f32[4,1024,512]{1,2,0:T(8,128)S(1)}, f32[4,1024,512]{1,2,0:T(8,128)}, u32[]{:S(2)}) copy-start(f32[4,1024,512]{1,2,0:T(8,128)} %all-reduce.2.cloned.1.call-done) | copy-start | bytes 25165828
  236.7 12.3 %copy-start.7 = (bf16[4,192,512]{2,1,0:T(8,128)(2,1)}, bf16[4,192,512]{2,1,0:T(8,128)(2,1)S(1)}, u32[]{:S(2)}) copy-start(bf16[4,192,512]{2,1,0:T(8,128)(2,1)S(1)} %fusion.26) | copy-start | bytes 2359300
  236.7 13.9 %copy-start.8 = (bf16[4,256,384]{2,1,0:T(8,128)(2,1)S(1)}, bf16[4,256,384]{2,1,0:T(8,128)(2,1)}, u32[]{:S(2)}) copy-start(bf16[4,256,384]{2,1,0:T(8,128)(2,1)} %param.10) | copy-start | bytes 2359300
  236.9 8.1 %collective-permute-start = (bf16[4,192,2]{2,1,0:T(8,128)(2,1)S(1)}, bf16[4,192,2]{2,1,0:T(8,128)(2,1)S(1)}, u32[]{:S(2)}, u32[]{:S(2)}) collective-permute-start(bf16[4,192,2]{2,1,0:T(8,128)(2,1)S(1)} %get-tuple-element.3), channel_id=1, source_target_pairs={{0,4},{4,8},{8,12},{12,16},{16,20},{20,24},{24,28},{28,32},{32,36}... | collective-permute-start | bytes 9224 | tf_op jit(solution)/shard_map/ppermute | solution.py:22
  240.4 8.7 %collective-permute-start.1 = (bf16[4,192,2]{2,1,0:T(8,128)(2,1)S(1)}, bf16[4,192,2]{2,1,0:T(8,128)(2,1)S(1)}, u32[]{:S(2)}, u32[]{:S(2)}) collective-permute-start(bf16[4,192,2]{2,1,0:T(8,128)(2,1)S(1)} %get-tuple-element.4), channel_id=1, source_target_pairs={{4,0},{8,4},{12,8},{16,12},{20,16},{24,20},{28,24},{32,28},{36,32}... | collective-permute-start | bytes 9224 | tf_op jit(solution)/shard_map/ppermute | solution.py:23
  250.6 227.9 %reduce-scatter.2.cloned.1.call-start = ((), (), s32[]{:S(2)}) async-start(), calls=%async_computation.4 | async-start | bytes 6082560 | tf_op jit(solution)/shard_map/reduce_scatter | solution.py:74
  290.7 4.1 copy-start.5
  305.2 1.8 copy-start.9
  307.0 5.0 %copy-start.6 = (bf16[4,768,516]{2,1,0:T(8,128)(2,1)S(1)}, bf16[4,768,516]{2,1,0:T(8,128)(2,1)}, u32[]{:S(2)}) copy-start(bf16[4,768,516]{2,1,0:T(8,128)(2,1)} %all-gather.2.cloned.1.call-done) | copy-start | bytes 9510916
  320.7 157.9 %copy-start.1 = (bf16[192,1024]{1,0:T(8,128)(2,1)S(1)}, bf16[192,1024]{1,0:T(8,128)(2,1)}, u32[]{:S(2)}) copy-start(bf16[192,1024]{1,0:T(8,128)(2,1)} %param.14) | copy-start | bytes 1179652
Sparse Core Ops, SparseCore 0:
  14.1 208.0 all-reduce.1
  250.7 39.9 all-gather.1
  305.3 173.1 reduce-scatter.1
where the time goes:
time: 491 us; the launch traced here: 485 us
  waiting for transfers between devices  220 us (45%)
  local copies, waits for them, and re-layouts  127 us (26%)
  blocking collectives  53.5 us (11%)
  matrix products  38.3 us (8%)
  other arithmetic  19.1 us (4%)
  between operations  14.3 us (3%)
  starting transfers between devices  14 us (3%)
    reduce_scatter x1, waiting for transfers between devices, local(): lax.psum_scatter(weight_terms, 'seq', scatter_dimension=1, tiled=True)  145 us
    unnamed x34, local copies, waits for them, and re-layouts  82.4 us
    psum x1, blocking collectives, local(): raw_scores, total_sq = lax.psum((partial_raw, squares), 'chan')  53.5 us
    all_gather x1, waiting for transfers between devices, local(): full_grad = lax.all_gather(rimmed, 'chan', axis=1, tiled=True)  38.6 us
    psum x1, waiting for transfers between devices, local(): raw_scores, total_sq = lax.psum((partial_raw, squares), 'chan')  29 us
    all_to_all x1, local copies, waits for them, and re-layouts, local(): lax.all_to_all(cot, 'seq', split_axis=2, concat_axis=1, tiled=True)  20.7 us
    convert_element_type x3, local copies, waits for them, and re-layouts, local(): local_cot.astype(jnp.float32)  18.7 us
    dot_general x5, matrix products, local(): jnp.einsum('bop,io->bpi', window, conv_w[shift_tap], preferred_element_ty...  17 us
  transfers between devices with their start and end apart: 6, of which 5 were waited for; matrix products, arithmetic and copies ran while one was open for 30% of the time, Pallas kernels for 0%

commit v1 on v0

v1 whole, which is shorter than its diff:
```python
import math

import jax
import jax.numpy as jnp
from jax import lax
from jax.experimental import pallas as pl
from jax.experimental.pallas import tpu as pltpu
from jax.sharding import PartitionSpec as P

BATCH = 4
C_OUT = 768
TRACKS = 1024
KERNEL = 5
SEQ = 32
CHAN = 4
LANES = 128
epsilon = 1e-06

BF = jnp.bfloat16
F32 = jnp.float32
VMEM_BYTES = 56 * 1024 * 1024


def params():
    return pltpu.CompilerParams(vmem_limit_bytes=VMEM_BYTES)


def dot(a, b, contract):
    return lax.dot_general(a, b, ((contract[:1], contract[1:]), ((), ())), preferred_element_type=F32)


ANY = pl.BlockSpec(memory_space=pl.ANY)
VM = pl.BlockSpec(memory_space=pltpu.VMEM)
SM = pl.BlockSpec(memory_space=pltpu.SMEM)


def prep_kernel(me_ref, cot_ref, merged_ref, head_ref, gain_ref, send_ref, p0, p1, p2, p3, hg_ref, sems):
    me = me_ref[0]
    copies = []
    for r, piece in enumerate((p0, p1, p2, p3)):
        start = pl.multiple_of((me ^ r) * LANES, LANES)
        copies.append(pltpu.make_async_copy(merged_ref.at[:, :, pl.ds(start, LANES)], piece, sems.at[r]))
    for d in range(SEQ):
        start = pl.multiple_of(d * CHAN * LANES + me * LANES, LANES)
        for b in range(BATCH):
            copies.append(
                pltpu.make_async_copy(
                    cot_ref.at[b, :, pl.ds(start, LANES)],
                    send_ref.at[d, pl.ds(b * 32, 32), :],
                    sems.at[4 + d * BATCH + b],
                )
            )
    for copy in copies:
        copy.start()
    hg_ref[...] = (head_ref[...].astype(F32) * gain_ref[...]).astype(BF)
    for copy in copies:
        copy.wait()


def prep(me, cot, merged, head_w, gain):
    piece = jax.ShapeDtypeStruct((BATCH, 192, LANES), BF)
    return pl.pallas_call(
        prep_kernel,
        out_shape=(jax.ShapeDtypeStruct((SEQ, BATCH * 32, LANES), BF), piece, piece, piece, piece,
                   jax.ShapeDtypeStruct(head_w.shape, BF)),
        in_specs=[SM, ANY, ANY, VM, VM],
        out_specs=(ANY, ANY, ANY, ANY, ANY, VM),
        scratch_shapes=[pltpu.SemaphoreType.DMA((4 + SEQ * BATCH,))],
        compiler_params=params(),
        name="prep",
    )(me, cot, merged, head_w, gain)


def rows_of(pieces):
    return jnp.concatenate(
        [jnp.concatenate([p[b] for b in range(BATCH)], axis=1) for p in pieces], axis=0
    )


def score_kernel(p0, p1, p2, p3, h0, h1, h2, h3, raw_ref, inv_ref):
    m = rows_of((p0, p1, p2, p3))
    m32 = m.astype(F32)
    total = jnp.sum(m32 * m32, axis=0, keepdims=True)
    inv_ref[...] = jnp.broadcast_to(lax.rsqrt(total / C_OUT + epsilon), inv_ref.shape)
    hg = jnp.concatenate([h0[...], h1[...], h2[...], h3[...]], axis=0)
    raw_ref[...] = dot(hg, m, (0, 0))


def scores(pieces, heads):
    return pl.pallas_call(
        score_kernel,
        out_shape=(jax.ShapeDtypeStruct((TRACKS, BATCH * LANES), F32),
                   jax.ShapeDtypeStruct((8, BATCH * LANES), F32)),
        in_specs=[VM] * 8,
        out_specs=(VM, VM),
        compiler_params=params(),
        name="scores",
    )(*pieces, *heads)


def head_kernel(ids_ref, valid_ref, raw_ref, inv_ref, cot_ref, cols_ref, p0, p1, p2, p3, h0, h1, h2, h3, out_ref):
    me = ids_ref[0]
    first = ids_ref[1]
    scale = cols_ref[:, 0:1]
    bias = cols_ref[:, 1:2]
    lane = lax.broadcasted_iota(jnp.int32, (1, LANES), 1)
    hg = jnp.concatenate([h0[...], h1[...], h2[...], h3[...]], axis=0)
    scaled, coefs = [], []
    for b in range(BATCH):
        cols = slice(b * LANES, (b + 1) * LANES)
        raw = raw_ref[:, cols]
        inv = inv_ref[0:1, cols]
        live = (first + lane < valid_ref[b]).astype(F32)
        gate = 0.5 * jnp.tanh(0.5 * (inv * raw + bias)) + 0.5
        cot = cot_ref[:, b * 32 : (b + 1) * 32, :].reshape(TRACKS, LANES).astype(F32)
        d_logits = (cot * scale) * gate
        d_rms = live * jnp.sum(d_logits * raw, axis=0, keepdims=True)
        scaled.append(((inv * live) * d_logits).astype(BF))
        coefs.append(inv * inv * inv * d_rms * (1.0 / C_OUT))
    d = dot(hg, jnp.concatenate(scaled, axis=1), (1, 0))
    for r, p in enumerate((p0, p1, p2, p3)):
        rows = pl.ds(pl.multiple_of((me ^ r) * 192, 64), 192)
        for b in range(BATCH):
            block = d[r * 192 : (r + 1) * 192, b * LANES : (b + 1) * LANES]
            out_ref[b, rows, :] = (block - coefs[b] * p[b].astype(F32)).astype(BF)


def head(ids, valid, raw, inv, cot, cols, pieces, heads):
    return pl.pallas_call(
        head_kernel,
        out_shape=jax.ShapeDtypeStruct((BATCH, C_OUT, LANES), BF),
        in_specs=[SM, SM] + [VM] * 12,
        out_specs=VM,
        compiler_params=params(),
        name="head",
    )(ids, valid, raw, inv, cot, cols, *pieces, *heads)


def gather_positions(me, pieces, full, sems):
    copies = []
    for r, piece in enumerate(pieces):
        start = pl.multiple_of((me ^ r) * LANES, LANES)
        copies.append(pltpu.make_async_copy(piece, full.at[:, :, pl.ds(start, LANES)], sems.at[r]))
    for copy in copies:
        copy.start()
    for copy in copies:
        copy.wait()


ROWS = 368


def weight_kernel(ids_ref, d0, d1, d2, d3, tr_ref, trx_ref, out_ref, edge_ref, full, sems):
    me = ids_ref[0]

    @pl.when(pl.program_id(0) == 0)
    def _():
        gather_positions(me, (d0, d1, d2, d3), full, sems)

    step = pl.program_id(0)
    rows = pl.ds(pl.multiple_of(step * 384, 384), 384)
    p = lax.broadcasted_iota(jnp.int32, (256, 256), 0)
    q = lax.broadcasted_iota(jnp.int32, (256, 256), 1)
    even = (q < 128) & (p // 2 == q)
    odd = (q >= 128) & ((p + 1) // 2 == q - 128)
    pick = (even | odd).astype(BF)
    p1 = lax.broadcasted_iota(jnp.int32, (LANES, LANES), 0)
    q1 = lax.broadcasted_iota(jnp.int32, (LANES, LANES), 1)
    evens, odds = [], []
    last = jnp.zeros((384, LANES), F32)
    for b in range(BATCH):
        for h in range(2):
            block = full[b, rows, h * 256 : (h + 1) * 256]
            e = dot(block, pick, (1, 0)).astype(BF)
            evens.append(e[:, :128])
            odds.append(e[:, 128:])
            sel = ((p1 == LANES - 1) & (q1 == b * 2 + h)).astype(BF)
            last = last + dot(block[:, 128:], sel, (1, 0))
    even_all = jnp.concatenate(evens, axis=1)
    odd_all = jnp.concatenate(odds, axis=1)
    g_even = dot(even_all, tr_ref[...], (1, 0))
    g_odd = dot(odd_all, tr_ref[:, :768], (1, 0)) + dot(last.astype(BF), trx_ref[...], (1, 0))
    pad = jnp.zeros((ROWS - 360, LANES), F32)
    taps = (g_even[:, :384], g_odd[:, :384], g_even[:, 384:768], g_odd[:, 384:], g_even[:, 768:])
    for s in range(16):
        blocks = []
        for l in range(3):
            for tap in taps:
                blocks.append(tap[s * 24 : (s + 1) * 24, l * LANES : (l + 1) * LANES])
        out_ref[s] = jnp.concatenate(blocks + [pad], axis=0).astype(BF)
    row = lax.broadcasted_iota(jnp.int32, (32, LANES), 0)
    col = lax.broadcasted_iota(jnp.int32, (32, LANES), 1)
    edge = jnp.zeros((32, 384), F32)
    for b in range(BATCH):
        head_sel = ((row < 16) & (row == b * 2 + col) & (col < 2)).astype(BF)
        tail_sel = ((row >= 16) & (row - 16 == b * 2 + col - 126) & (col >= 126)).astype(BF)
        edge = edge + dot(head_sel, full[b, rows, 0:LANES], (1, 1))
        edge = edge + dot(tail_sel, full[b, rows, 384:512], (1, 1))
    edge_ref[...] = edge.astype(BF)


def weight_grad(ids, pieces, tr, trx):
    return pl.pallas_call(
        weight_kernel,
        grid=(2,),
        out_shape=(jax.ShapeDtypeStruct((SEQ, ROWS, LANES), BF), jax.ShapeDtypeStruct((32, C_OUT), BF)),
        in_specs=[SM] + [ANY] * 4 + [
            pl.BlockSpec((1024, 1152), lambda i: (0, 0)),
            pl.BlockSpec((LANES, 768), lambda i: (0, 0)),
        ],
        out_specs=(pl.BlockSpec((16, ROWS, LANES), lambda i: (i, 0, 0)),
                   pl.BlockSpec((32, 384), lambda i: (0, i))),
        scratch_shapes=[pltpu.VMEM((BATCH, C_OUT, 512), BF), pltpu.SemaphoreType.DMA((4,))],
        compiler_params=params(),
        name="weight_grad",
    )(ids, *pieces, tr, trx)


def trunk_kernel(ids_ref, d0, d1, d2, d3, conv_ref, rim_ref, out_ref, skip_ref, full, sems, skip_sem):
    me = ids_ref[0]
    b = pl.program_id(0)
    skip = pltpu.make_async_copy(
        full.at[:, pl.ds(pl.multiple_of(me * 192, 64), 192), :], skip_ref, skip_sem
    )

    @pl.when(b == 0)
    def _():
        gather_positions(me, (d0, d1, d2, d3), full, sems)
        skip.start()

    j = lax.broadcasted_iota(jnp.int32, (256, 512), 0)
    p = lax.broadcasted_iota(jnp.int32, (256, 512), 1)
    jr = lax.broadcasted_iota(jnp.int32, (256, 32), 0)
    col = lax.broadcasted_iota(jnp.int32, (256, 32), 1)
    rim_pos = jnp.where(col < 16, col - 2 * b - 2, col - 16 - 2 * b + 512)
    rim_ok = ((col >= 2 * b) & (col < 2 * b + 2)) | ((col >= 16 + 2 * b) & (col < 18 + 2 * b))
    d = full[b]
    total = jnp.zeros((256, 384), F32)
    for k in range(KERNEL):
        lo = 2 * j - k + 2
        pick = ((p == lo) | (p == lo + 1)).astype(BF)
        lo_r = 2 * jr - k + 2
        pick_r = (rim_ok & ((rim_pos == lo_r) | (rim_pos == lo_r + 1))).astype(BF)
        window = dot(pick, d, (1, 1)) + dot(pick_r, rim_ref[...], (1, 0))
        total = total + dot(window.astype(BF), conv_ref[k], (1, 1))
    out_ref[0] = total.astype(BF)

    @pl.when(b == BATCH - 1)
    def _():
        skip.wait()


def trunk_grad(ids, pieces, conv_w, rim):
    return pl.pallas_call(
        trunk_kernel,
        grid=(BATCH,),
        out_shape=(jax.ShapeDtypeStruct((BATCH, 256, 384), BF), jax.ShapeDtypeStruct((BATCH, 192, 512), BF)),
        in_specs=[SM] + [ANY] * 4 + [
            pl.BlockSpec((KERNEL, 384, C_OUT), lambda i: (0, 0, 0)),
            pl.BlockSpec((32, C_OUT), lambda i: (0, 0)),
        ],
        out_specs=(pl.BlockSpec((1, 256, 384), lambda i: (i, 0, 0)), ANY),
        scratch_shapes=[pltpu.VMEM((BATCH, C_OUT, 512), BF), pltpu.SemaphoreType.DMA((4,)),
                        pltpu.SemaphoreType.DMA],
        compiler_params=params(),
        cost_estimate=pl.CostEstimate(flops=8 * 10**9, bytes_accessed=16 * 2**20, transcendentals=0),
        name="trunk_grad",
    )(ids, *pieces, conv_w, rim)


def sum_kernel(scale, in_ref, out_ref):
    total = in_ref[0].astype(F32)
    for s in range(1, SEQ):
        total = total + in_ref[s].astype(F32)
    total = total * scale
    for l in range(3):
        for k in range(KERNEL):
            start = l * 120 + k * 24
            out_ref[k, :, l * LANES : (l + 1) * LANES] = total[start : start + 24]


def sum_weights(terms, scale):
    return pl.pallas_call(
        lambda i, o: sum_kernel(scale, i, o),
        out_shape=jax.ShapeDtypeStruct((KERNEL, 24, 384), F32),
        in_specs=[VM],
        out_specs=VM,
        compiler_params=params(),
        name="sum_weights",
    )(terms)


def flip(x, r):
    return lax.ppermute(x, "chan", [(i, i ^ r) for i in range(CHAN)])


def shift(x, step):
    return lax.ppermute(x, "seq", [(i, i + step) for i in range(SEQ) if 0 <= i + step < SEQ])


def across(x):
    pairs = [(s * CHAN + c, (s ^ 16) * CHAN + (c ^ 2)) for s in range(SEQ) for c in range(CHAN)]
    return lax.ppermute(x, ("seq", "chan"), pairs)


def local(
    trunk, merged, conv_w, norm_gain, head_w, head_bias, head_scale, head_of_track, valid_len, cot
):
    me = lax.axis_index("chan").astype(jnp.int32)
    first = lax.axis_index("seq").astype(jnp.int32) * 512 + me * LANES
    ids = jnp.stack([me, first])
    send, p0, p1, p2, p3, hg = prep(ids, cot, merged, head_w, norm_gain[:, None])
    pieces = (p0, flip(p1, 1), flip(p2, 2), flip(p3, 3))
    hg_far = across(hg)
    heads = (hg, flip(hg, 1), hg_far, flip(hg_far, 1))
    got = lax.all_to_all(send, "seq", 0, 0, tiled=True)

    onehot = (
        head_of_track[:, None] == jnp.arange(head_scale.shape[0], dtype=jnp.int32)[None, :]
    ).astype(F32)
    track_scale = jnp.sum(onehot * head_scale[None, :], axis=1)
    cols = jnp.stack([track_scale, head_bias], axis=1)

    before = shift(trunk[:, 255:], 1)
    after = shift(trunk[:, :1], -1)
    tr_m = jnp.concatenate([before, trunk[:, :255]], axis=1)
    tr_p = jnp.concatenate([trunk[:, 1:], after], axis=1)
    tr = jnp.concatenate([tr_m, trunk, tr_p], axis=2).reshape(1024, 1152)
    trx = jnp.concatenate([trunk[:, 127::128], tr_p[:, 127::128]], axis=2).reshape(8, 768)
    trx = jnp.pad(trx, ((0, LANES - 8), (0, 0)))

    raw, inv = scores(pieces, heads)
    d_own = head(ids, valid_len, raw, inv, got, cols, pieces, heads)

    d_far = flip(d_own, 2)
    blocks = (d_own, flip(d_own, 1), d_far, flip(d_far, 1))
    terms, edges = weight_grad(ids, blocks, tr, trx)
    summed = lax.all_to_all(terms, "seq", 0, 0, tiled=True)
    rim = jnp.concatenate([shift(edges[16:], 1), shift(edges[:16], -1)], axis=0)
    d_trunk, d_skip = trunk_grad(ids, blocks, conv_w, rim)
    grad_scale = 1.0 / math.sqrt(BATCH * 512 * SEQ)
    d_conv_w = sum_weights(summed, grad_scale)
    return (d_trunk, d_skip, d_conv_w)


def solution(mesh):
    placed = (
        P(None, "seq", "chan"),
        P(None, "chan", "seq"),
        P(None, "chan", None),
        P("chan"),
        P("chan", None),
        P(),
        P(),
        P(),
        P(),
        P(None, "seq", None),
    )
    return jax.shard_map(
        local,
        mesh=mesh,
        in_specs=placed,
        out_specs=(P(None, "seq", "chan"), P(None, "chan", "seq"), P(None, "seq", "chan")),
        check_vma=False,
    )
```

time: 491 us -> 215 us (0.44)
  waiting for transfers between devices: 220 us -> 64.8 us
  local copies, waits for them, and re-layouts: 127 us -> 7.14 us
  Pallas kernels: 0 us -> 102 us
  blocking collectives: 53.5 us -> 0 us
  matrix products: 38.3 us -> 0 us
  starting transfers between devices: 14 us -> 34.2 us
  other arithmetic: 19.1 us -> 3.16 us
  between operations: 14.3 us -> 0.88 us
    reduce_scatter x1 -> x0, waiting for transfers between devices: 145 us -> none  [local(): lax.psum_scatter(weight_terms, 'seq', scatter_dimension=1, tiled=True)]
    pallas_call x0 -> x6, Pallas kernels: none -> 102 us  [the longest x1 59.7 us: prep(): pl.pallas_call(prep_kernel, out_shape=(jax.ShapeDtypeStruct((SEQ, BATCH *...]
    unnamed x34 -> x26, local copies, waits for them, and re-layouts: 82.4 us -> 3.53 us
    ppermute x2 -> x13, waiting for transfers between devices: 7.36 us -> 64.8 us  [the longest x4 31.9 us: shift(): lax.ppermute(x, 'seq', [(i, i + step) for i in range(SEQ) if 0 <= i + ste...]
    psum x1 -> x0, blocking collectives: 53.5 us -> none  [local(): raw_scores, total_sq = lax.psum((partial_raw, squares), 'chan')]
    all_gather x1 -> x0, waiting for transfers between devices: 38.6 us -> none  [local(): full_grad = lax.all_gather(rimmed, 'chan', axis=1, tiled=True)]
    dot_general x12 -> x0, matrix products: 38.3 us -> none  [the longest x5 17 us: local(): jnp.einsum('bop,io->bpi', window, conv_w[shift_tap], preferred_element_ty...]
    psum x1 -> x0, waiting for transfers between devices: 29 us -> none  [local(): raw_scores, total_sq = lax.psum((partial_raw, squares), 'chan')]
  transfers between devices with their start and end apart: 6 -> 15, of which waited for: 5 -> 6; matrix products, arithmetic and copies ran while one was open for 30% -> 2% of each run, Pallas kernels for 0% -> 11%
where the time goes in v1:
time: 215 us; the launch traced here: 212 us
  Pallas kernels  102 us (47%)
  waiting for transfers between devices  64.8 us (30%)
  starting transfers between devices  34.2 us (16%)
  local copies, waits for them, and re-layouts  7.14 us (3%)
  other arithmetic  3.16 us (1%)
    pallas_call x1, Pallas kernels, prep(): pl.pallas_call(prep_kernel, out_shape=(jax.ShapeDtypeStruct((SEQ, BATCH *...  59.7 us
    ppermute x4, waiting for transfers between devices, shift(): lax.ppermute(x, 'seq', [(i, i + step) for i in range(SEQ) if 0 <= i + ste...  31.9 us
    ppermute x8, waiting for transfers between devices, flip(): return lax.ppermute(x, 'chan', [(i, i ^ r) for i in range(CHAN)])  24.1 us
    pallas_call x1, Pallas kernels, trunk_grad(): pl.pallas_call(trunk_kernel, grid=(BATCH,), out_shape=(jax.ShapeDtypeStru...  19.4 us
    ppermute x4, starting transfers between devices, shift(): lax.ppermute(x, 'seq', [(i, i + step) for i in range(SEQ) if 0 <= i + ste...  11 us
    pallas_call x1, Pallas kernels, weight_grad(): pl.pallas_call(weight_kernel, grid=(2,), out_shape=(jax.ShapeDtypeStruct(...  10.9 us
    all_to_all x1, starting transfers between devices, local(): got = lax.all_to_all(send, 'seq', 0, 0, tiled=True)  8.77 us
    ppermute x1, waiting for transfers between devices, across(): return lax.ppermute(x, ('seq', 'chan'), pairs)  8.76 us
  transfers between devices with their start and end apart: 15, of which 6 were waited for; matrix products, arithmetic and copies ran while one was open for 2% of the time, Pallas kernels for 11%

profile of v1, /device:TPU:0, one launch (start us, length us, event | category | flops | bytes accessed | tf_op | source)
XLA Modules:
  0.0 212.4 jit_solution(4686703328477766787)
XLA Ops:
  0.6 1.4 copy.18.gain_ref
  2.1 0.6 pad_add_fusion.me_ref.ids_ref
  2.7 59.7 %prep.1 = (bf16[32,128,128]{2,1,0:T(8,128)(2,1)}, bf16[4,192,128]{2,1,0:T(8,128)(2,1)}, bf16[4,192,128]{2,1,0:T(8,128)(2,1)}, bf16[4,192,128]{2,1,0:T(8,128)(2,1...) custom-call(s32[2]{0:T(128)} %pad_add_fusion.me_ref.ids_ref, bf16[4,32,16384]{2,1,0:T(8,128)(2,1)} %cot_ref.1, ...), custom_call_target="tpu_custom_call" | custom-call | tf_op jit(solution)/shard_map/prep/pallas_call | solution.py:62
  62.4 8.8 %all-to-all-start = ((bf16[32,128,128]{2,1,0:T(8,128)(2,1)}), bf16[32,128,128]{2,1,0:T(8,128)(2,1)S(1)}, u32[]{:S(2)}, u32[]{:S(2)}) async-start(bf16[32,128,128]{2,1,0:T(8,128)(2,1)} %get-tuple-element.22), calls=%async_computation | async-start | bytes 2097152 | tf_op jit(solution)/shard_map/all_to_all | solution.py:316
  71.2 4.0 %collective-permute-start.4 = (bf16[192,1024]{1,0:T(8,128)(2,1)}, bf16[192,1024]{1,0:T(8,128)(2,1)S(1)}, u32[]{:S(2)}, u32[]{:S(2)}) collective-permute-start(bf16[192,1024]{1,0:T(8,128)(2,1)} %get-tuple-element.19.h0), channel_id=1, source_target_pairs={{0,66},{1,67},{2,64},{3,65},{4,70},{5,71},{6,68},{7,69},{8,74},{9,... | collective-permute-start | bytes 1179656 | tf_op jit(solution)/shard_map/ppermute | solution.py:303
  75.2 8.8 %collective-permute-done.4.h2 = bf16[192,1024]{1,0:T(8,128)(2,1)S(1)} collective-permute-done((bf16[192,1024]{1,0:T(8,128)(2,1)}, bf16[192,1024]{1,0:T(8,128)(2,1)S(1)}, u32[]{:S(2)}, u32[]{:S(2)}) %collective-permute-start.4) | collective-permute-done | bytes 393248 | tf_op jit(solution)/shard_map/ppermute | solution.py:303
  84.0 0.5 collective-permute-start
  84.5 1.7 collective-permute-start.1
  86.2 1.2 collective-permute-start.2
  87.5 1.0 copy.19.cols_ref
  88.5 5.7 %collective-permute-done.1.p2 = bf16[4,192,128]{2,1,0:T(8,128)(2,1)S(1)} collective-permute-done((bf16[4,192,128]{2,1,0:T(8,128)(2,1)}, bf16[4,192,128]{2,1,0:T(8,128)(2,1)S(1)}, u32[]{:S(2)}, u32[]{:S(2)}) %collective-permute-start.1) | collective-permute-done | bytes 196640 | tf_op jit(solution)/shard_map/ppermute | solution.py:294
  94.3 3.1 %collective-permute-done.2.p3 = bf16[4,192,128]{2,1,0:T(8,128)(2,1)S(1)} collective-permute-done((bf16[4,192,128]{2,1,0:T(8,128)(2,1)}, bf16[4,192,128]{2,1,0:T(8,128)(2,1)S(1)}, u32[]{:S(2)}, u32[]{:S(2)}) %collective-permute-start.2) | collective-permute-done | bytes 196640 | tf_op jit(solution)/shard_map/ppermute | solution.py:294
  97.5 0.6 copy-done.8
  98.4 4.0 %scores.1 = (f32[1024,512]{1,0:T(8,128)}, f32[8,512]{1,0:T(8,128)}) custom-call(bf16[4,192,128]{2,1,0:T(8,128)(2,1)} %get-tuple-element.15.p0, bf16[4,192,128]{2,1,0:T(8,128)(2,1)} %copy-done.6, bf16[4,192,128]{2,1,0:T(8,128)(2,1)} %copy-done.7, bf16[4,192,128]{2,1,0:T(8,128)(2,1)} %copy-done.8, bf16[192,1024]{1,0:T(8,128)(2,1)} %get-tuple-element.19.h0, ...), custom_call_target="tpu_custom_call" | custom-call | tf_op jit(solution)/shard_map/scores/pallas_call | solution.py:90
  102.4 1.0 copy-done.2
  103.4 5.3 %head.1.d0 = bf16[4,768,128]{2,1,0:T(8,128)(2,1)} custom-call(s32[2]{0:T(128)} %pad_add_fusion.me_ref.ids_ref, s32[4]{0:T(128)} %valid_ref.1, f32[1024,512]{1,0:T(8,128)} %get-tuple-element.20.raw_ref, f32[8,512]{1,0:T(8,128)} %get-tuple-element.21.inv_ref, bf16[32,128,128]{2,1,0:T(8,128)(2,1)} %copy-done.2, f32[1024,2]{1,0:T(8,128)} %copy.19.cols_ref, ...), custom_call_target="tpu_custom_call" | custom-call | tf_op jit(solution)/shard_map/head/pallas_call | solution.py:129
  108.7 0.6 collective-permute-start.7
  109.3 1.3 collective-permute-start.10
  110.6 4.5 %collective-permute-start.9 = (bf16[4,1,384]{2,1,0:T(2,128)(2,1)S(1)}, bf16[4,1,384]{2,1,0:T(2,128)(2,1)S(1)}, u32[]{:S(2)}, u32[]{:S(2)}) collective-permute-start(bf16[4,1,384]{2,1,0:T(2,128)(2,1)S(1)} %get-tuple-element.27), channel_id=1, source_target_pairs={{0,4},{4,8},{8,12},{12,16},{16,20},{20,24},{24,28},{28,32},{32,36}... | collective-permute-start | bytes 9224 | tf_op jit(solution)/shard_map/ppermute | solution.py:298
  115.2 15.2 %collective-permute-done.7.d2 = bf16[4,768,128]{2,1,0:T(8,128)(2,1)} collective-permute-done((bf16[4,768,128]{2,1,0:T(8,128)(2,1)}, bf16[4,768,128]{2,1,0:T(8,128)(2,1)}, u32[]{:S(2)}, u32[]{:S(2)}) %collective-permute-start.7) | collective-permute-done | bytes 786464 | tf_op jit(solution)/shard_map/ppermute | solution.py:294
  131.0 0.7 pad.4.trx_ref
  131.7 1.7 maximum_maximum_fusion
  133.4 10.9 %weight_grad.1 = (bf16[32,368,128]{2,1,0:T(8,128)(2,1)}, bf16[32,768]{1,0:T(8,128)(2,1)}) custom-call(s32[2]{0:T(128)} %pad_add_fusion.me_ref.ids_ref, bf16[4,768,128]{2,1,0:T(8,128)(2,1)} %head.1.d0, bf16[4,768,128]{2,1,0:T(8,128)(2,1)} %collective-permute-done.6.d1, bf16[4,768,128]{2,1,0:T(8,128)(2,1)} %collective-permute-done.7.d2, ...), custom_call_target="tpu_custom_call" | custom-call | tf_op jit(solution)/shard_map/weight_grad/pallas_call | solution.py:203
  144.3 6.4 %all-to-all-start.1 = ((bf16[32,368,128]{2,1,0:T(8,128)(2,1)}), bf16[32,368,128]{2,1,0:T(8,128)(2,1)S(1)}, u32[]{:S(2)}, u32[]{:S(2)}) async-start(bf16[32,368,128]{2,1,0:T(8,128)(2,1)} %get-tuple-element.26), calls=%async_computation.1 | async-start | bytes 6029312 | tf_op jit(solution)/shard_map/all_to_all | solution.py:338
  150.7 3.7 %collective-permute-start.11 = (bf16[16,768]{1,0:T(8,128)(2,1)S(1)}, bf16[16,768]{1,0:T(8,128)(2,1)S(1)}, u32[]{:S(2)}, u32[]{:S(2)}) collective-permute-start(bf16[16,768]{1,0:T(8,128)(2,1)S(1)} %get-tuple-element.31), channel_id=1, source_target_pairs={{0,4},{4,8},{8,12},{12,16},{16,20},{20,24},{24,28},{28,32},{32,36}... | collective-permute-start | bytes 73736 | tf_op jit(solution)/shard_map/ppermute | solution.py:298
  154.4 1.5 collective-permute-start.12
  155.9 29.9 %collective-permute-done.11 = bf16[16,768]{1,0:T(8,128)(2,1)S(1)} collective-permute-done((bf16[16,768]{1,0:T(8,128)(2,1)S(1)}, bf16[16,768]{1,0:T(8,128)(2,1)S(1)}, u32[]{:S(2)}, u32[]{:S(2)}) %collective-permute-start.11) | collective-permute-done | bytes 24608 | tf_op jit(solution)/shard_map/ppermute | solution.py:298
  185.8 2.0 collective-permute-done.12
  187.8 0.6 pad_maximum_fusion.1.rim_ref
  188.5 19.4 %trunk_grad.1 = (bf16[4,256,384]{2,1,0:T(8,128)(2,1)}, bf16[4,192,512]{2,1,0:T(8,128)(2,1)}) custom-call(s32[2]{0:T(128)} %pad_add_fusion.me_ref.ids_ref, bf16[4,768,128]{2,1,0:T(8,128)(2,1)} %head.1.d0, bf16[4,768,128]{2,1,0:T(8,128)(2,1)} %collective-permute-done.6.d1, bf16[4,768,128]{2,1,0:T(8,128)(2,1)} %collective-permute-done.7.d2, ...), custom_call_target="tpu_custom_call" | custom-call | flops 8000000000 | bytes 16777216 | tf_op jit(solution)/shard_map/trunk_grad/pallas_call | solution.py:254
  207.9 1.6 copy-done
  209.5 2.9 %sum_weights.1 = f32[5,24,384]{2,1,0:T(8,128)} custom-call(bf16[32,368,128]{2,1,0:T(8,128)(2,1)} %copy-done), custom_call_target="tpu_custom_call" | custom-call | tf_op jit(solution)/shard_map/sum_weights/pallas_call | solution.py:283
  (46 shorter events, 1.1 us)
Async XLA Ops:
  2.7 84.6 %copy-start.10 = (s32[1024]{0:T(1024)S(1)}, s32[1024]{0:T(1024)}, u32[]{:S(2)}) copy-start(s32[1024]{0:T(1024)} %param.17) | copy-start | bytes 12292
  2.7 84.6 %copy-start.12 = (f32[7]{0:T(128)S(1)}, f32[7]{0:T(128)}, u32[]{:S(2)}) copy-start(f32[7]{0:T(128)} %param.16) | copy-start | bytes 88
  2.7 84.7 %copy-start.11 = (f32[1024]{0:T(1024)S(1)}, f32[1024]{0:T(1024)}, u32[]{:S(2)}) copy-start(f32[1024]{0:T(1024)} %param.15) | copy-start | bytes 12292
  62.4 40.0 %all-to-all-start = ((bf16[32,128,128]{2,1,0:T(8,128)(2,1)}), bf16[32,128,128]{2,1,0:T(8,128)(2,1)S(1)}, u32[]{:S(2)}, u32[]{:S(2)}) async-start(bf16[32,128,128]{2,1,0:T(8,128)(2,1)} %get-tuple-element.22), calls=%async_computation | async-start | bytes 2097152 | tf_op jit(solution)/shard_map/all_to_all | solution.py:316
  71.2 12.8 %collective-permute-start.4 = (bf16[192,1024]{1,0:T(8,128)(2,1)}, bf16[192,1024]{1,0:T(8,128)(2,1)S(1)}, u32[]{:S(2)}, u32[]{:S(2)}) collective-permute-start(bf16[192,1024]{1,0:T(8,128)(2,1)} %get-tuple-element.19.h0), channel_id=1, source_target_pairs={{0,66},{1,67},{2,64},{3,65},{4,70},{5,71},{6,68},{7,69},{8,74},{9,... | collective-permute-start | bytes 1179656 | tf_op jit(solution)/shard_map/ppermute | solution.py:303
  75.2 22.2 %collective-permute-start.3 = (bf16[192,1024]{1,0:T(8,128)(2,1)}, bf16[192,1024]{1,0:T(8,128)(2,1)S(1)}, u32[]{:S(2)}, u32[]{:S(2)}) collective-permute-start(bf16[192,1024]{1,0:T(8,128)(2,1)} %get-tuple-element.19.h0), channel_id=1, source_target_pairs={{0,1},{1,0},{2,3},{3,2},{4,5},{5,4},{6,7},{7,6},{8,9},{9,8},{10,11... | collective-permute-start | bytes 1179656 | tf_op jit(solution)/shard_map/ppermute | solution.py:294
  84.0 13.4 %copy-start.3 = (bf16[192,1024]{1,0:T(8,128)(2,1)}, bf16[192,1024]{1,0:T(8,128)(2,1)S(1)}, u32[]{:S(2)}) copy-start(bf16[192,1024]{1,0:T(8,128)(2,1)S(1)} %collective-permute-done.4.h2) | copy-start | bytes 1179652
  84.0 13.4 %collective-permute-start.5 = (bf16[192,1024]{1,0:T(8,128)(2,1)S(1)}, bf16[192,1024]{1,0:T(8,128)(2,1)S(1)}, u32[]{:S(2)}, u32[]{:S(2)}) collective-permute-start(bf16[192,1024]{1,0:T(8,128)(2,1)S(1)} %collective-permute-done.4.h2), channel_id=1, source_target_pairs={{0,1},{1,0},{2,3},{3,2},{4,5},{5,4},{6,7},{7,6},{8,9},{9,8},{10,11... | collective-permute-start | bytes 1179656 | tf_op jit(solution)/shard_map/ppermute | solution.py:294
  84.0 4.5 %collective-permute-start = (bf16[4,192,128]{2,1,0:T(8,128)(2,1)}, bf16[4,192,128]{2,1,0:T(8,128)(2,1)S(1)}, u32[]{:S(2)}, u32[]{:S(2)}) collective-permute-start(bf16[4,192,128]{2,1,0:T(8,128)(2,1)} %get-tuple-element.16), channel_id=1, source_target_pairs={{0,1},{1,0},{2,3},{3,2},{4,5},{5,4},{6,7},{7,6},{8,9},{9,8},{10,11... | collective-permute-start | bytes 589832 | tf_op jit(solution)/shard_map/ppermute | solution.py:294
  84.5 9.8 %collective-permute-start.1 = (bf16[4,192,128]{2,1,0:T(8,128)(2,1)}, bf16[4,192,128]{2,1,0:T(8,128)(2,1)S(1)}, u32[]{:S(2)}, u32[]{:S(2)}) collective-permute-start(bf16[4,192,128]{2,1,0:T(8,128)(2,1)} %get-tuple-element.17), channel_id=1, source_target_pairs={{0,2},{1,3},{2,0},{3,1},{4,6},{5,7},{6,4},{7,5},{8,10},{9,11},{10,... | collective-permute-start | bytes 589832 | tf_op jit(solution)/shard_map/ppermute | solution.py:294
  86.2 11.2 %collective-permute-start.2 = (bf16[4,192,128]{2,1,0:T(8,128)(2,1)}, bf16[4,192,128]{2,1,0:T(8,128)(2,1)S(1)}, u32[]{:S(2)}, u32[]{:S(2)}) collective-permute-start(bf16[4,192,128]{2,1,0:T(8,128)(2,1)} %get-tuple-element.18), channel_id=1, source_target_pairs={{0,3},{1,2},{2,1},{3,0},{4,7},{5,6},{6,5},{7,4},{8,11},{9,10},{10,... | collective-permute-start | bytes 589832 | tf_op jit(solution)/shard_map/ppermute | solution.py:294
  88.5 8.9 %copy-start.6 = (bf16[4,192,128]{2,1,0:T(8,128)(2,1)}, bf16[4,192,128]{2,1,0:T(8,128)(2,1)S(1)}, u32[]{:S(2)}) copy-start(bf16[4,192,128]{2,1,0:T(8,128)(2,1)S(1)} %collective-permute-done.p1) | copy-start | bytes 589828
  94.3 3.2 %copy-start.7 = (bf16[4,192,128]{2,1,0:T(8,128)(2,1)}, bf16[4,192,128]{2,1,0:T(8,128)(2,1)S(1)}, u32[]{:S(2)}) copy-start(bf16[4,192,128]{2,1,0:T(8,128)(2,1)S(1)} %collective-permute-done.1.p2) | copy-start | bytes 589828
  97.4 0.7 copy-start.8
  97.4 0.9 copy-start.4
  97.4 1.0 copy-start.5
  102.4 1.0 copy-start.2
  103.4 5.8 %copy-start.1 = (bf16[4,256,384]{2,1,0:T(8,128)(2,1)S(1)}, bf16[4,256,384]{2,1,0:T(8,128)(2,1)}, u32[]{:S(2)}) copy-start(bf16[4,256,384]{2,1,0:T(8,128)(2,1)} %param.10) | copy-start | bytes 2359300
  108.7 21.8 %collective-permute-start.7 = (bf16[4,768,128]{2,1,0:T(8,128)(2,1)}, bf16[4,768,128]{2,1,0:T(8,128)(2,1)}, u32[]{:S(2)}, u32[]{:S(2)}) collective-permute-start(bf16[4,768,128]{2,1,0:T(8,128)(2,1)} %head.1.d0), channel_id=1, source_target_pairs={{0,2},{1,3},{2,0},{3,1},{4,6},{5,7},{6,4},{7,5},{8,10},{9,11},{10,... | collective-permute-start | bytes 2359304 | tf_op jit(solution)/shard_map/ppermute | solution.py:294
  109.3 21.5 %collective-permute-start.10 = (bf16[4,1,384]{2,1,0:T(2,128)(2,1)S(1)}, bf16[4,1,384]{2,1,0:T(2,128)(2,1)S(1)}, u32[]{:S(2)}, u32[]{:S(2)}) collective-permute-start(bf16[4,1,384]{2,1,0:T(2,128)(2,1)S(1)} %get-tuple-element.28), channel_id=1, source_target_pairs={{4,0},{8,4},{12,8},{16,12},{20,16},{24,20},{28,24},{32,28},{36,32}... | collective-permute-start | bytes 9224 | tf_op jit(solution)/shard_map/ppermute | solution.py:298
  110.6 21.2 %collective-permute-start.9 = (bf16[4,1,384]{2,1,0:T(2,128)(2,1)S(1)}, bf16[4,1,384]{2,1,0:T(2,128)(2,1)S(1)}, u32[]{:S(2)}, u32[]{:S(2)}) collective-permute-start(bf16[4,1,384]{2,1,0:T(2,128)(2,1)S(1)} %get-tuple-element.27), channel_id=1, source_target_pairs={{0,4},{4,8},{8,12},{12,16},{16,20},{20,24},{24,28},{28,32},{32,36}... | collective-permute-start | bytes 9224 | tf_op jit(solution)/shard_map/ppermute | solution.py:298
  115.1 18.3 %collective-permute-start.6 = (bf16[4,768,128]{2,1,0:T(8,128)(2,1)}, bf16[4,768,128]{2,1,0:T(8,128)(2,1)}, u32[]{:S(2)}, u32[]{:S(2)}) collective-permute-start(bf16[4,768,128]{2,1,0:T(8,128)(2,1)} %head.1.d0), channel_id=1, source_target_pairs={{0,1},{1,0},{2,3},{3,2},{4,5},{5,4},{6,7},{7,6},{8,9},{9,8},{10,11... | collective-permute-start | bytes 2359304 | tf_op jit(solution)/shard_map/ppermute | solution.py:294
  130.4 3.0 %collective-permute-start.8 = (bf16[4,768,128]{2,1,0:T(8,128)(2,1)}, bf16[4,768,128]{2,1,0:T(8,128)(2,1)}, u32[]{:S(2)}, u32[]{:S(2)}) collective-permute-start(bf16[4,768,128]{2,1,0:T(8,128)(2,1)} %collective-permute-done.7.d2), channel_id=1, source_target_pairs={{0,1},{1,0},{2,3},{3,2},{4,5},{5,4},{6,7},{7,6},{8,9},{9,8},{10,11... | collective-permute-start | bytes 2359304 | tf_op jit(solution)/shard_map/ppermute | solution.py:294
  144.3 6.4 %copy-start.9 = (bf16[32,768]{1,0:T(8,128)(2,1)S(1)}, bf16[32,768]{1,0:T(8,128)(2,1)}, u32[]{:S(2)}) copy-start(bf16[32,768]{1,0:T(8,128)(2,1)} %get-tuple-element.23) | copy-start | bytes 147460
  144.3 63.6 %all-to-all-start.1 = ((bf16[32,368,128]{2,1,0:T(8,128)(2,1)}), bf16[32,368,128]{2,1,0:T(8,128)(2,1)S(1)}, u32[]{:S(2)}, u32[]{:S(2)}) async-start(bf16[32,368,128]{2,1,0:T(8,128)(2,1)} %get-tuple-element.26), calls=%async_computation.1 | async-start | bytes 6029312 | tf_op jit(solution)/shard_map/all_to_all | solution.py:338
  150.7 35.1 %collective-permute-start.11 = (bf16[16,768]{1,0:T(8,128)(2,1)S(1)}, bf16[16,768]{1,0:T(8,128)(2,1)S(1)}, u32[]{:S(2)}, u32[]{:S(2)}) collective-permute-start(bf16[16,768]{1,0:T(8,128)(2,1)S(1)} %get-tuple-element.31), channel_id=1, source_target_pairs={{0,4},{4,8},{8,12},{12,16},{16,20},{20,24},{24,28},{28,32},{32,36}... | collective-permute-start | bytes 73736 | tf_op jit(solution)/shard_map/ppermute | solution.py:298
  154.4 33.4 %collective-permute-start.12 = (bf16[16,768]{1,0:T(8,128)(2,1)S(1)}, bf16[16,768]{1,0:T(8,128)(2,1)S(1)}, u32[]{:S(2)}, u32[]{:S(2)}) collective-permute-start(bf16[16,768]{1,0:T(8,128)(2,1)S(1)} %get-tuple-element.32), channel_id=1, source_target_pairs={{4,0},{8,4},{12,8},{16,12},{20,16},{24,20},{28,24},{32,28},{36,32}... | collective-permute-start | bytes 73736 | tf_op jit(solution)/shard_map/ppermute | solution.py:298
  207.9 1.6 copy-start

commit v2 on v1

--- a/solution.py
+++ b/solution.py
@@ -34,41 +34,51 @@
 SM = pl.BlockSpec(memory_space=pltpu.SMEM)
 
 
-def prep_kernel(me_ref, cot_ref, merged_ref, head_ref, gain_ref, send_ref, p0, p1, p2, p3, hg_ref, sems):
+def pieces_kernel(me_ref, merged_ref, head_ref, gain_ref, p0, p1, p2, p3, payload_ref):
     me = me_ref[0]
-    copies = []
     for r, piece in enumerate((p0, p1, p2, p3)):
         start = pl.multiple_of((me ^ r) * LANES, LANES)
-        copies.append(pltpu.make_async_copy(merged_ref.at[:, :, pl.ds(start, LANES)], piece, sems.at[r]))
+        piece[...] = merged_ref[:, :, pl.ds(start, LANES)]
+    payload_ref[0:192, :] = head_ref[...]
+    payload_ref[192:208, :] = gain_ref[...]
+
+
+def cut_pieces(me, merged, head_w, gains):
+    piece = jax.ShapeDtypeStruct((BATCH, 192, LANES), BF)
+    return pl.pallas_call(
+        pieces_kernel,
+        out_shape=(piece,) * CHAN + (jax.ShapeDtypeStruct((208, TRACKS), BF),),
+        in_specs=[SM, VM, VM, VM],
+        out_specs=(VM,) * (CHAN + 1),
+        compiler_params=params(),
+        name="cut_pieces",
+    )(me, merged, head_w, gains)
+
+
+def cot_kernel(me_ref, cot_ref, send_ref, sems):
+    copies = []
     for d in range(SEQ):
-        start = pl.multiple_of(d * CHAN * LANES + me * LANES, LANES)
-        for b in range(BATCH):
-            copies.append(
-                pltpu.make_async_copy(
-                    cot_ref.at[b, :, pl.ds(start, LANES)],
-                    send_ref.at[d, pl.ds(b * 32, 32), :],
-                    sems.at[4 + d * BATCH + b],
-                )
-            )
+        start = pl.multiple_of(d * CHAN * LANES + me_ref[0] * LANES, LANES)
+        copies.append(
+            pltpu.make_async_copy(cot_ref.at[:, :, pl.ds(start, LANES)], send_ref.at[d], sems.at[d])
+        )
     for copy in copies:
         copy.start()
-    hg_ref[...] = (head_ref[...].astype(F32) * gain_ref[...]).astype(BF)
     for copy in copies:
         copy.wait()
 
 
-def prep(me, cot, merged, head_w, gain):
-    piece = jax.ShapeDtypeStruct((BATCH, 192, LANES), BF)
-    return pl.pallas_call(
-        prep_kernel,
-        out_shape=(jax.ShapeDtypeStruct((SEQ, BATCH * 32, LANES), BF), piece, piece, piece, piece,
-                   jax.ShapeDtypeStruct(head_w.shape, BF)),
-        in_specs=[SM, ANY, ANY, VM, VM],
-        out_specs=(ANY, ANY, ANY, ANY, ANY, VM),
-        scratch_shapes=[pltpu.SemaphoreType.DMA((4 + SEQ * BATCH,))],
-        compiler_params=params(),
-        name="prep",
-    )(me, cot, merged, head_w, gain)
+def cut_cot(me, cot):
+    return pl.pallas_call(
+        cot_kernel,
+        out_shape=jax.ShapeDtypeStruct((SEQ, BATCH, 32, LANES), BF),
+        in_specs=[SM, ANY],
+        out_specs=VM,
+        scratch_shapes=[pltpu.SemaphoreType.DMA((SEQ,))],
+        compiler_params=params(),
+        cost_estimate=pl.CostEstimate(flops=0, bytes_accessed=5 * 2**20, transcendentals=0),
+        name="cut_cot",
+    )(me, cot)
 
 
 def rows_of(pieces):
@@ -77,13 +87,22 @@
     )
 
 
+def weights_of(heads):
+    return jnp.concatenate([h[0:192, :] for h in heads], axis=0)
+
+
+def gains_of(heads):
+    ones = jnp.ones((16, LANES), BF)
+    return jnp.concatenate([dot(h[192:208, 0:256], ones, (0, 0))[:192, 0:1] for h in heads], axis=0)
+
+
 def score_kernel(p0, p1, p2, p3, h0, h1, h2, h3, raw_ref, inv_ref):
-    m = rows_of((p0, p1, p2, p3))
-    m32 = m.astype(F32)
+    heads = (h0, h1, h2, h3)
+    m32 = rows_of((p0, p1, p2, p3)).astype(F32)
     total = jnp.sum(m32 * m32, axis=0, keepdims=True)
     inv_ref[...] = jnp.broadcast_to(lax.rsqrt(total / C_OUT + epsilon), inv_ref.shape)
-    hg = jnp.concatenate([h0[...], h1[...], h2[...], h3[...]], axis=0)
-    raw_ref[...] = dot(hg, m, (0, 0))
+    normed = (m32 * gains_of(heads)).astype(BF)
+    raw_ref[...] = dot(weights_of(heads), normed, (0, 0))
 
 
 def scores(pieces, heads):
@@ -98,13 +117,15 @@
     )(*pieces, *heads)
 
 
-def head_kernel(ids_ref, valid_ref, raw_ref, inv_ref, cot_ref, cols_ref, p0, p1, p2, p3, h0, h1, h2, h3, out_ref):
+def head_kernel(
+    ids_ref, valid_ref, raw_ref, inv_ref, cot_ref, cols_ref, p0, p1, p2, p3, h0, h1, h2, h3, out_ref, edge_ref
+):
     me = ids_ref[0]
     first = ids_ref[1]
     scale = cols_ref[:, 0:1]
     bias = cols_ref[:, 1:2]
     lane = lax.broadcasted_iota(jnp.int32, (1, LANES), 1)
-    hg = jnp.concatenate([h0[...], h1[...], h2[...], h3[...]], axis=0)
+    heads = (h0, h1, h2, h3)
     scaled, coefs = [], []
     for b in range(BATCH):
         cols = slice(b * LANES, (b + 1) * LANES)
@@ -117,20 +138,28 @@
         d_rms = live * jnp.sum(d_logits * raw, axis=0, keepdims=True)
         scaled.append(((inv * live) * d_logits).astype(BF))
         coefs.append(inv * inv * inv * d_rms * (1.0 / C_OUT))
-    d = dot(hg, jnp.concatenate(scaled, axis=1), (1, 0))
+    d = dot(weights_of(heads), jnp.concatenate(scaled, axis=1), (1, 0)) * gains_of(heads)
     for r, p in enumerate((p0, p1, p2, p3)):
         rows = pl.ds(pl.multiple_of((me ^ r) * 192, 64), 192)
         for b in range(BATCH):
             block = d[r * 192 : (r + 1) * 192, b * LANES : (b + 1) * LANES]
             out_ref[b, rows, :] = (block - coefs[b] * p[b].astype(F32)).astype(BF)
+    start = jnp.where(me == CHAN - 1, LANES - 2, 0)
+    row = lax.broadcasted_iota(jnp.int32, (16, LANES), 0)
+    col = lax.broadcasted_iota(jnp.int32, (16, LANES), 1) - start
+    edge = jnp.zeros((16, C_OUT), F32)
+    for b in range(BATCH):
+        sel = ((col >= 0) & (col < 2) & (row == b * 2 + col)).astype(BF)
+        edge = edge + dot(sel, out_ref[b], (1, 1))
+    edge_ref[...] = edge.astype(BF)
 
 
 def head(ids, valid, raw, inv, cot, cols, pieces, heads):
     return pl.pallas_call(
         head_kernel,
-        out_shape=jax.ShapeDtypeStruct((BATCH, C_OUT, LANES), BF),
+        out_shape=(jax.ShapeDtypeStruct((BATCH, C_OUT, LANES), BF), jax.ShapeDtypeStruct((16, C_OUT), BF)),
         in_specs=[SM, SM] + [VM] * 12,
-        out_specs=VM,
+        out_specs=(VM, VM),
         compiler_params=params(),
         name="head",
     )(ids, valid, raw, inv, cot, cols, *pieces, *heads)
@@ -150,7 +179,7 @@
 ROWS = 368
 
 
-def weight_kernel(ids_ref, d0, d1, d2, d3, tr_ref, trx_ref, out_ref, edge_ref, full, sems):
+def weight_kernel(ids_ref, d0, d1, d2, d3, tr_ref, trx_ref, out_ref, full, sems):
     me = ids_ref[0]
 
     @pl.when(pl.program_id(0) == 0)
@@ -188,35 +217,25 @@
             for tap in taps:
                 blocks.append(tap[s * 24 : (s + 1) * 24, l * LANES : (l + 1) * LANES])
         out_ref[s] = jnp.concatenate(blocks + [pad], axis=0).astype(BF)
-    row = lax.broadcasted_iota(jnp.int32, (32, LANES), 0)
-    col = lax.broadcasted_iota(jnp.int32, (32, LANES), 1)
-    edge = jnp.zeros((32, 384), F32)
-    for b in range(BATCH):
-        head_sel = ((row < 16) & (row == b * 2 + col) & (col < 2)).astype(BF)
-        tail_sel = ((row >= 16) & (row - 16 == b * 2 + col - 126) & (col >= 126)).astype(BF)
-        edge = edge + dot(head_sel, full[b, rows, 0:LANES], (1, 1))
-        edge = edge + dot(tail_sel, full[b, rows, 384:512], (1, 1))
-    edge_ref[...] = edge.astype(BF)
 
 
 def weight_grad(ids, pieces, tr, trx):
     return pl.pallas_call(
         weight_kernel,
         grid=(2,),
-        out_shape=(jax.ShapeDtypeStruct((SEQ, ROWS, LANES), BF), jax.ShapeDtypeStruct((32, C_OUT), BF)),
+        out_shape=jax.ShapeDtypeStruct((SEQ, ROWS, LANES), BF),
         in_specs=[SM] + [ANY] * 4 + [
             pl.BlockSpec((1024, 1152), lambda i: (0, 0)),
             pl.BlockSpec((LANES, 768), lambda i: (0, 0)),
         ],
-        out_specs=(pl.BlockSpec((16, ROWS, LANES), lambda i: (i, 0, 0)),
-                   pl.BlockSpec((32, 384), lambda i: (0, i))),
+        out_specs=pl.BlockSpec((16, ROWS, LANES), lambda i: (i, 0, 0)),
         scratch_shapes=[pltpu.VMEM((BATCH, C_OUT, 512), BF), pltpu.SemaphoreType.DMA((4,))],
         compiler_params=params(),
         name="weight_grad",
     )(ids, *pieces, tr, trx)
 
 
-def trunk_kernel(ids_ref, d0, d1, d2, d3, conv_ref, rim_ref, out_ref, skip_ref, full, sems, skip_sem):
+def trunk_kernel(ids_ref, d0, d1, d2, d3, conv_ref, r0, r1, r2, r3, out_ref, skip_ref, full, sems, skip_sem):
     me = ids_ref[0]
     b = pl.program_id(0)
     skip = pltpu.make_async_copy(
@@ -230,10 +249,12 @@
 
     j = lax.broadcasted_iota(jnp.int32, (256, 512), 0)
     p = lax.broadcasted_iota(jnp.int32, (256, 512), 1)
-    jr = lax.broadcasted_iota(jnp.int32, (256, 32), 0)
-    col = lax.broadcasted_iota(jnp.int32, (256, 32), 1)
-    rim_pos = jnp.where(col < 16, col - 2 * b - 2, col - 16 - 2 * b + 512)
-    rim_ok = ((col >= 2 * b) & (col < 2 * b + 2)) | ((col >= 16 + 2 * b) & (col < 18 + 2 * b))
+    jr = lax.broadcasted_iota(jnp.int32, (256, 64), 0)
+    col = lax.broadcasted_iota(jnp.int32, (256, 64), 1)
+    offset = col % 16 - 2 * b
+    rim_ok = (offset >= 0) & (offset < 2)
+    rim_pos = jnp.where(col // 16 == (me ^ 3), offset - 2, jnp.where(col // 16 == me, 512 + offset, -9))
+    rim = jnp.concatenate([r0[...], r1[...], r2[...], r3[...]], axis=0)
     d = full[b]
     total = jnp.zeros((256, 384), F32)
     for k in range(KERNEL):
@@ -241,7 +262,7 @@
         pick = ((p == lo) | (p == lo + 1)).astype(BF)
         lo_r = 2 * jr - k + 2
         pick_r = (rim_ok & ((rim_pos == lo_r) | (rim_pos == lo_r + 1))).astype(BF)
-        window = dot(pick, d, (1, 1)) + dot(pick_r, rim_ref[...], (1, 0))
+        window = dot(pick, d, (1, 1)) + dot(pick_r, rim, (1, 0))
         total = total + dot(window.astype(BF), conv_ref[k], (1, 1))
     out_ref[0] = total.astype(BF)
 
@@ -250,22 +271,21 @@
         skip.wait()
 
 
-def trunk_grad(ids, pieces, conv_w, rim):
+def trunk_grad(ids, pieces, conv_w, rims):
     return pl.pallas_call(
         trunk_kernel,
         grid=(BATCH,),
         out_shape=(jax.ShapeDtypeStruct((BATCH, 256, 384), BF), jax.ShapeDtypeStruct((BATCH, 192, 512), BF)),
         in_specs=[SM] + [ANY] * 4 + [
             pl.BlockSpec((KERNEL, 384, C_OUT), lambda i: (0, 0, 0)),
-            pl.BlockSpec((32, C_OUT), lambda i: (0, 0)),
-        ],
+        ] + [pl.BlockSpec((16, C_OUT), lambda i: (0, 0))] * CHAN,
         out_specs=(pl.BlockSpec((1, 256, 384), lambda i: (i, 0, 0)), ANY),
         scratch_shapes=[pltpu.VMEM((BATCH, C_OUT, 512), BF), pltpu.SemaphoreType.DMA((4,)),
                         pltpu.SemaphoreType.DMA],
         compiler_params=params(),
         cost_estimate=pl.CostEstimate(flops=8 * 10**9, bytes_accessed=16 * 2**20, transcendentals=0),
         name="trunk_grad",
-    )(ids, *pieces, conv_w, rim)
+    )(ids, *pieces, conv_w, *rims)
 
 
 def sum_kernel(scale, in_ref, out_ref):
@@ -298,6 +318,12 @@
     return lax.ppermute(x, "seq", [(i, i + step) for i in range(SEQ) if 0 <= i + step < SEQ])
 
 
+def rim_to(x, r):
+    up = [(s * CHAN + 3, (s + 1) * CHAN + (3 ^ r)) for s in range(SEQ - 1)]
+    down = [(s * CHAN, (s - 1) * CHAN + r) for s in range(1, SEQ)]
+    return lax.ppermute(x, ("seq", "chan"), up + down)
+
+
 def across(x):
     pairs = [(s * CHAN + c, (s ^ 16) * CHAN + (c ^ 2)) for s in range(SEQ) for c in range(CHAN)]
     return lax.ppermute(x, ("seq", "chan"), pairs)
@@ -309,11 +335,17 @@
     me = lax.axis_index("chan").astype(jnp.int32)
     first = lax.axis_index("seq").astype(jnp.int32) * 512 + me * LANES
     ids = jnp.stack([me, first])
-    send, p0, p1, p2, p3, hg = prep(ids, cot, merged, head_w, norm_gain[:, None])
-    pieces = (p0, flip(p1, 1), flip(p2, 2), flip(p3, 3))
-    hg_far = across(hg)
-    heads = (hg, flip(hg, 1), hg_far, flip(hg_far, 1))
-    got = lax.all_to_all(send, "seq", 0, 0, tiled=True)
+    hi = lax.reduce_precision(norm_gain, 8, 7)
+    mid = lax.reduce_precision(norm_gain - hi, 8, 7)
+    gains = jnp.pad(jnp.stack([hi, mid, norm_gain - hi - mid]).astype(BF), ((0, 13), (0, TRACKS - 192)))
+    p0, p1, p2, p3, own_head = cut_pieces(ids, merged, head_w, gains)
+    p1, p2, p3 = flip(p1, 1), flip(p2, 2), flip(p3, 3)
+    far_head = across(own_head)
+    send = cut_cot(ids, cot)
+    send, p2, p3, far_head = lax.optimization_barrier((send, p2, p3, far_head))
+    got = lax.all_to_all(send, "seq", 0, 0, tiled=True).reshape(SEQ, BATCH * 32, LANES)
+    pieces = (p0, p1, p2, p3)
+    heads = (own_head, flip(own_head, 1), far_head, flip(far_head, 1))
 
     onehot = (
         head_of_track[:, None] == jnp.arange(head_scale.shape[0], dtype=jnp.int32)[None, :]
@@ -329,15 +361,16 @@
     trx = jnp.concatenate([trunk[:, 127::128], tr_p[:, 127::128]], axis=2).reshape(8, 768)
     trx = jnp.pad(trx, ((0, LANES - 8), (0, 0)))
 
+    heads, tr, trx, cols = lax.optimization_barrier((heads, tr, trx, cols))
     raw, inv = scores(pieces, heads)
-    d_own = head(ids, valid_len, raw, inv, got, cols, pieces, heads)
-
-    d_far = flip(d_own, 2)
+    d_own, edge = head(ids, valid_len, raw, inv, got, cols, pieces, heads)
+
+    rims = [rim_to(edge, r) for r in range(CHAN)]
+    d_far, *rims = lax.optimization_barrier((flip(d_own, 2), *rims))
     blocks = (d_own, flip(d_own, 1), d_far, flip(d_far, 1))
-    terms, edges = weight_grad(ids, blocks, tr, trx)
+    terms = weight_grad(ids, blocks, tr, trx)
     summed = lax.all_to_all(terms, "seq", 0, 0, tiled=True)
-    rim = jnp.concatenate([shift(edges[16:], 1), shift(edges[:16], -1)], axis=0)
-    d_trunk, d_skip = trunk_grad(ids, blocks, conv_w, rim)
+    d_trunk, d_skip = trunk_grad(ids, blocks, conv_w, rims)
     grad_scale = 1.0 / math.sqrt(BATCH * 512 * SEQ)
     d_conv_w = sum_weights(summed, grad_scale)
     return (d_trunk, d_skip, d_conv_w)

time: 215 us -> 143 us (0.67)
  Pallas kernels: 102 us -> 49.5 us
  waiting for transfers between devices: 64.8 us -> 47 us
    pallas_call x3 -> x4, Pallas kernels: 75.8 us -> 22.7 us  [the longest x1 11.6 us: weight_grad(): pl.pallas_call(weight_kernel, grid=(2,), out_shape=jax.ShapeDtypeStruct((...]
    ppermute x4 -> x2, waiting for transfers between devices: 31.9 us -> 0.01 us  [shift(): lax.ppermute(x, 'seq', [(i, i + step) for i in range(SEQ) if 0 <= i + ste...]
    all_to_all x1, waiting for transfers between devices: 0.01 us -> 18.8 us  [local(): summed = lax.all_to_all(terms, 'seq', 0, 0, tiled=True)]
    ppermute x8, waiting for transfers between devices: 24.1 us -> 9.48 us  [flip(): return lax.ppermute(x, 'chan', [(i, i ^ r) for i in range(CHAN)])]
    all_to_all x1, waiting for transfers between devices: 0.01 us -> 7.71 us  [local(): lax.all_to_all(send, 'seq', 0, 0, tiled=True)]
    ppermute x4 -> x2, starting transfers between devices: 11 us -> 4.82 us  [shift(): lax.ppermute(x, 'seq', [(i, i + step) for i in range(SEQ) if 0 <= i + ste...]
    ppermute x0 -> x4, waiting for transfers between devices: none -> 5.82 us  [rim_to(): return lax.ppermute(x, ('seq', 'chan'), up + down)]
    ppermute x1, waiting for transfers between devices: 8.76 us -> 5.23 us  [across(): return lax.ppermute(x, ('seq', 'chan'), pairs)]
  transfers between devices with their start and end apart: 15 -> 17, of which waited for: 6 -> 7; matrix products, arithmetic and copies ran while one was open for 2% -> 3% of each run, Pallas kernels for 11% -> 19%
where the time goes in v2:
time: 143 us; the launch traced here: 140 us
  Pallas kernels  49.5 us (35%)
  waiting for transfers between devices  47 us (33%)
  starting transfers between devices  32.3 us (23%)
  local copies, waits for them, and re-layouts  6.58 us (5%)
  other arithmetic  3.86 us (3%)
    pallas_call x1, Pallas kernels, trunk_grad(): pl.pallas_call(trunk_kernel, grid=(BATCH,), out_shape=(jax.ShapeDtypeStru...  19.6 us
    all_to_all x1, waiting for transfers between devices, local(): summed = lax.all_to_all(terms, 'seq', 0, 0, tiled=True)  18.8 us
    pallas_call x1, Pallas kernels, weight_grad(): pl.pallas_call(weight_kernel, grid=(2,), out_shape=jax.ShapeDtypeStruct((...  11.6 us
    ppermute x8, waiting for transfers between devices, flip(): return lax.ppermute(x, 'chan', [(i, i ^ r) for i in range(CHAN)])  9.48 us
    all_to_all x1, waiting for transfers between devices, local(): lax.all_to_all(send, 'seq', 0, 0, tiled=True)  7.71 us
    ppermute x8, starting transfers between devices, flip(): return lax.ppermute(x, 'chan', [(i, i ^ r) for i in range(CHAN)])  7.38 us
    all_to_all x1, starting transfers between devices, local(): lax.all_to_all(send, 'seq', 0, 0, tiled=True)  7.32 us
    ppermute x4, waiting for transfers between devices, rim_to(): return lax.ppermute(x, ('seq', 'chan'), up + down)  5.82 us
  transfers between devices with their start and end apart: 17, of which 7 were waited for; matrix products, arithmetic and copies ran while one was open for 3% of the time, Pallas kernels for 19%

profile of v2, /device:TPU:0, one launch (start us, length us, event | category | flops | bytes accessed | tf_op | source)
XLA Modules:
  0.0 140.2 jit_solution(10432931553825312007)
XLA Ops:
  0.6 0.7 reduce-precision_convert_fusion.1
  2.6 2.4 %cut_pieces.1 = (bf16[4,192,128]{2,1,0:T(8,128)(2,1)}, bf16[4,192,128]{2,1,0:T(8,128)(2,1)}, bf16[4,192,128]{2,1,0:T(8,128)(2,1)}, bf16[4,192,128]{2,1,0:T(8,128)(2,1)}, bf16[208,1024]{1,0:T(8,128)(2,1)}) custom-call(s32[2]{0:T(128)} %pad_add_fusion.me_ref.ids_ref, bf16[4,192,512]{2,1,0:T(8,128)(2,1)} %merged_ref.1, bf16[192,1024]{1,0:T(8,128)(2,1)} %head_ref.1, ...), custom_call_target="tpu_custom_call" | custom-call | tf_op jit(solution)/shard_map/cut_pieces/pallas_call | solution.py:48
  5.1 4.1 %collective-permute-start.3 = (bf16[208,1024]{1,0:T(8,128)(2,1)}, bf16[208,1024]{1,0:T(8,128)(2,1)}, u32[]{:S(2)}, u32[]{:S(2)}) collective-permute-start(bf16[208,1024]{1,0:T(8,128)(2,1)} %get-tuple-element.38.h0), channel_id=1, source_target_pairs={{0,66},{1,67},{2,64},{3,65},{4,70},{5,71},{6,68},{7,69},{8,74},{9,... | collective-permute-start | bytes 1277960 | tf_op jit(solution)/shard_map/ppermute | solution.py:329
  9.2 3.4 %collective-permute-start.2 = (bf16[4,192,128]{2,1,0:T(8,128)(2,1)}, bf16[4,192,128]{2,1,0:T(8,128)(2,1)}, u32[]{:S(2)}, u32[]{:S(2)}) collective-permute-start(bf16[4,192,128]{2,1,0:T(8,128)(2,1)} %get-tuple-element.33), channel_id=1, source_target_pairs={{0,3},{1,2},{2,1},{3,0},{4,7},{5,6},{6,5},{7,4},{8,11},{9,10},{10,... | collective-permute-start | bytes 589832 | tf_op jit(solution)/shard_map/ppermute | solution.py:314
  12.5 0.8 fusion.10
  13.3 3.5 %collective-permute-start.6 = (bf16[4,1,384]{2,1,0:T(2,128)(2,1)S(1)}, bf16[4,1,384]{2,1,0:T(2,128)(2,1)S(1)}, u32[]{:S(2)}, u32[]{:S(2)}) collective-permute-start(bf16[4,1,384]{2,1,0:T(2,128)(2,1)S(1)} %get-tuple-element.57), channel_id=1, source_target_pairs={{0,4},{4,8},{8,12},{12,16},{16,20},{20,24},{24,28},{28,32},{32,36}... | collective-permute-start | bytes 9224 | tf_op jit(solution)/shard_map/ppermute | solution.py:318
  16.9 3.2 %cut_cot.1 = bf16[32,4,32,128]{3,2,1,0:T(8,128)(2,1)} custom-call(s32[2]{0:T(128)} %pad_add_fusion.me_ref.ids_ref, bf16[4,32,16384]{2,1,0:T(8,128)(2,1)} %cot_ref.1), custom_call_target="tpu_custom_call" | custom-call | bytes 5242880 | tf_op jit(solution)/shard_map/cut_cot/pallas_call | solution.py:72
  20.1 1.3 collective-permute-start.7
  21.4 0.9 collective-permute-done.2.p3
  22.5 5.2 %collective-permute-done.3.h2 = bf16[208,1024]{1,0:T(8,128)(2,1)} collective-permute-done((bf16[208,1024]{1,0:T(8,128)(2,1)}, bf16[208,1024]{1,0:T(8,128)(2,1)}, u32[]{:S(2)}, u32[]{:S(2)}) %collective-permute-start.3) | collective-permute-done | bytes 426016 | tf_op jit(solution)/shard_map/ppermute | solution.py:329
  27.7 7.3 %all-to-all-start = ((bf16[32,4,32,128]{3,2,1,0:T(8,128)(2,1)}), bf16[32,4,32,128]{3,2,1,0:T(8,128)(2,1)S(1)}, u32[]{:S(2)}, u32[]{:S(2)}) async-start(bf16[32,4,32,128]{3,2,1,0:T(8,128)(2,1)} %cut_cot.1), calls=%async_computation | async-start | bytes 2097152 | tf_op jit(solution)/shard_map/all_to_all | solution.py:346
  35.7 1.7 %maximum_maximum_fusion = bf16[4,256,1152]{2,1,0:T(8,128)(2,1)} fusion(bf16[4,1,384]{2,1,0:T(2,128)(2,1)S(1)} %collective-permute-done.7, bf16[4,255,384]{2,1,0:T(8,128)(2,1)S(1)} %get-tuple-element.60, bf16[4,256,384]{2,1,0:T(8,128)(2,1)S(1)} %copy-done.1, bf16[4,255,384]{2,1,0:T(8,128)(2,1)S(1)} %get-tuple-element.59, ...), kind=kLoop, calls=%fused_computation | loop fusion | flops 11796480 | bytes 4718592 | tf_op jit(solution)/shard_map/concatenate | solution.py:360
  37.6 0.7 pad.9.trx_ref
  38.3 1.0 copy.16.cols_ref
  39.3 4.3 %scores.1 = (f32[1024,512]{1,0:T(8,128)}, f32[8,512]{1,0:T(8,128)}) custom-call(bf16[4,192,128]{2,1,0:T(8,128)(2,1)} %get-tuple-element.30.p0, bf16[4,192,128]{2,1,0:T(8,128)(2,1)} %collective-permute-done.p1, bf16[4,192,128]{2,1,0:T(8,128)(2,1)} %collective-permute-done.1.p2, bf16[4,192,128]{2,1,0:T(8,128)(2,1)} %collective-permute-done.2.p3, ...), custom_call_target="tpu_custom_call" | custom-call | tf_op jit(solution)/shard_map/scores/pallas_call | solution.py:109
  43.7 7.7 %all-to-all-done = bf16[32,4,32,128]{3,2,1,0:T(8,128)(2,1)S(1)} async-done(((bf16[32,4,32,128]{3,2,1,0:T(8,128)(2,1)}), bf16[32,4,32,128]{3,2,1,0:T(8,128)(2,1)S(1)}, u32[]{:S(2)}, u32[]{:S(2)}) %all-to-all-start) | async-done | bytes 1048608 | tf_op jit(solution)/shard_map/all_to_all | solution.py:346
  51.4 1.0 copy-done.2
  52.4 5.5 %head.1 = (bf16[4,768,128]{2,1,0:T(8,128)(2,1)}, bf16[16,768]{1,0:T(8,128)(2,1)}) custom-call(s32[2]{0:T(128)} %pad_add_fusion.me_ref.ids_ref, s32[4]{0:T(128)} %valid_ref.1, f32[1024,512]{1,0:T(8,128)} %get-tuple-element.42.raw_ref, f32[8,512]{1,0:T(8,128)} %get-tuple-element.43.inv_ref, bf16[32,128,128]{2,1,0:T(8,128)(2,1)} %bitcast.7, ...), custom_call_target="tpu_custom_call" | custom-call | tf_op jit(solution)/shard_map/head/pallas_call | solution.py:158
  57.9 3.6 %collective-permute-start.9 = (bf16[4,768,128]{2,1,0:T(8,128)(2,1)}, bf16[4,768,128]{2,1,0:T(8,128)(2,1)S(1)}, u32[]{:S(2)}, u32[]{:S(2)}) collective-permute-start(bf16[4,768,128]{2,1,0:T(8,128)(2,1)} %get-tuple-element.46.d0), channel_id=1, source_target_pairs={{0,2},{1,3},{2,0},{3,1},{4,6},{5,7},{6,4},{7,5},{8,10},{9,11},{10,... | collective-permute-start | bytes 2359304 | tf_op jit(solution)/shard_map/ppermute | solution.py:314
  62.1 0.7 collective-permute-start.12
  62.8 0.7 collective-permute-start.11
  63.5 1.3 collective-permute-start.10
  64.9 5.8 %collective-permute-done.10.r0 = bf16[16,768]{1,0:T(8,128)(2,1)S(1)} collective-permute-done((bf16[16,768]{1,0:T(8,128)(2,1)}, bf16[16,768]{1,0:T(8,128)(2,1)S(1)}, u32[]{:S(2)}, u32[]{:S(2)}) %collective-permute-start.10) | collective-permute-done | bytes 24608 | tf_op jit(solution)/shard_map/ppermute | solution.py:324
  70.7 6.3 %collective-permute-done.9.d2 = bf16[4,768,128]{2,1,0:T(8,128)(2,1)S(1)} collective-permute-done((bf16[4,768,128]{2,1,0:T(8,128)(2,1)}, bf16[4,768,128]{2,1,0:T(8,128)(2,1)S(1)}, u32[]{:S(2)}, u32[]{:S(2)}) %collective-permute-start.9) | collective-permute-done | bytes 786464 | tf_op jit(solution)/shard_map/ppermute | solution.py:314
  77.1 2.3 %collective-permute-done.14.d3 = bf16[4,768,128]{2,1,0:T(8,128)(2,1)S(1)} collective-permute-done((bf16[4,768,128]{2,1,0:T(8,128)(2,1)S(1)}, bf16[4,768,128]{2,1,0:T(8,128)(2,1)S(1)}, u32[]{:S(2)}, u32[]{:S(2)}) %collective-permute-start.14) | collective-permute-done | bytes 786464 | tf_op jit(solution)/shard_map/ppermute | solution.py:314
  79.4 0.9 copy-done.5
  80.3 11.6 %weight_grad.1 = bf16[32,368,128]{2,1,0:T(8,128)(2,1)} custom-call(s32[2]{0:T(128)} %pad_add_fusion.me_ref.ids_ref, bf16[4,768,128]{2,1,0:T(8,128)(2,1)} %get-tuple-element.46.d0, bf16[4,768,128]{2,1,0:T(8,128)(2,1)} %copy-done.4, bf16[4,768,128]{2,1,0:T(8,128)(2,1)} %copy-done.3, bf16[4,768,128]{2,1,0:T(8,128)(2,1)} %copy-done.5, ...), custom_call_target="tpu_custom_call" | custom-call | tf_op jit(solution)/shard_map/weight_grad/pallas_call | solution.py:223
  91.9 5.4 %all-to-all-start.1 = ((bf16[32,368,128]{2,1,0:T(8,128)(2,1)}), bf16[32,368,128]{2,1,0:T(8,128)(2,1)S(1)}, u32[]{:S(2)}, u32[]{:S(2)}) async-start(bf16[32,368,128]{2,1,0:T(8,128)(2,1)} %weight_grad.1), calls=%async_computation.1 | async-start | bytes 6029312 | tf_op jit(solution)/shard_map/all_to_all | solution.py:372
  97.4 19.6 %trunk_grad.1 = (bf16[4,256,384]{2,1,0:T(8,128)(2,1)}, bf16[4,192,512]{2,1,0:T(8,128)(2,1)}) custom-call(s32[2]{0:T(128)} %pad_add_fusion.me_ref.ids_ref, bf16[4,768,128]{2,1,0:T(8,128)(2,1)} %get-tuple-element.46.d0, bf16[4,768,128]{2,1,0:T(8,128)(2,1)} %copy-done.4, bf16[4,768,128]{2,1,0:T(8,128)(2,1)} %copy-done.3, bf16[4,768,128]{2,1,0:T(8,128)(2,1)} %copy-done.5, ...), custom_call_target="tpu_custom_call" | custom-call | flops 8000000000 | bytes 16777216 | tf_op jit(solution)/shard_map/trunk_grad/pallas_call | solution.py:275
  117.0 18.8 %all-to-all-done.1.i = bf16[32,368,128]{2,1,0:T(8,128)(2,1)S(1)} async-done(((bf16[32,368,128]{2,1,0:T(8,128)(2,1)}), bf16[32,368,128]{2,1,0:T(8,128)(2,1)S(1)}, u32[]{:S(2)}, u32[]{:S(2)}) %all-to-all-start.1) | async-done | bytes 3014688 | tf_op jit(solution)/shard_map/all_to_all | solution.py:372
  135.7 1.6 %copy-done = bf16[32,368,128]{2,1,0:T(8,128)(2,1)} copy-done((bf16[32,368,128]{2,1,0:T(8,128)(2,1)}, bf16[32,368,128]{2,1,0:T(8,128)(2,1)S(1)}, u32[]{:S(2)}) %copy-start) | copy-done | bytes 3014680
  137.3 2.9 %sum_weights.1 = f32[5,24,384]{2,1,0:T(8,128)} custom-call(bf16[32,368,128]{2,1,0:T(8,128)(2,1)} %copy-done), custom_call_target="tpu_custom_call" | custom-call | tf_op jit(solution)/shard_map/sum_weights/pallas_call | solution.py:303
  (53 shorter events, 3.1 us)
Async XLA Ops:
  5.1 22.7 %collective-permute-start.3 = (bf16[208,1024]{1,0:T(8,128)(2,1)}, bf16[208,1024]{1,0:T(8,128)(2,1)}, u32[]{:S(2)}, u32[]{:S(2)}) collective-permute-start(bf16[208,1024]{1,0:T(8,128)(2,1)} %get-tuple-element.38.h0), channel_id=1, source_target_pairs={{0,66},{1,67},{2,64},{3,65},{4,70},{5,71},{6,68},{7,69},{8,74},{9,... | collective-permute-start | bytes 1277960 | tf_op jit(solution)/shard_map/ppermute | solution.py:329
  9.2 29.1 %collective-permute-start.4 = (bf16[208,1024]{1,0:T(8,128)(2,1)}, bf16[208,1024]{1,0:T(8,128)(2,1)}, u32[]{:S(2)}, u32[]{:S(2)}) collective-permute-start(bf16[208,1024]{1,0:T(8,128)(2,1)} %get-tuple-element.38.h0), channel_id=1, source_target_pairs={{0,1},{1,0},{2,3},{3,2},{4,5},{5,4},{6,7},{7,6},{8,9},{9,8},{10,11... | collective-permute-start | bytes 1277960 | tf_op jit(solution)/shard_map/ppermute | solution.py:314
  9.2 10.9 %collective-permute-start.1 = (bf16[4,192,128]{2,1,0:T(8,128)(2,1)}, bf16[4,192,128]{2,1,0:T(8,128)(2,1)}, u32[]{:S(2)}, u32[]{:S(2)}) collective-permute-start(bf16[4,192,128]{2,1,0:T(8,128)(2,1)} %get-tuple-element.32), channel_id=1, source_target_pairs={{0,2},{1,3},{2,0},{3,1},{4,6},{5,7},{6,4},{7,5},{8,10},{9,11},{10,... | collective-permute-start | bytes 589832 | tf_op jit(solution)/shard_map/ppermute | solution.py:314
  9.2 13.1 %collective-permute-start.2 = (bf16[4,192,128]{2,1,0:T(8,128)(2,1)}, bf16[4,192,128]{2,1,0:T(8,128)(2,1)}, u32[]{:S(2)}, u32[]{:S(2)}) collective-permute-start(bf16[4,192,128]{2,1,0:T(8,128)(2,1)} %get-tuple-element.33), channel_id=1, source_target_pairs={{0,3},{1,2},{2,1},{3,0},{4,7},{5,6},{6,5},{7,4},{8,11},{9,10},{10,... | collective-permute-start | bytes 589832 | tf_op jit(solution)/shard_map/ppermute | solution.py:314
  13.3 21.8 %copy-start.1 = (bf16[4,256,384]{2,1,0:T(8,128)(2,1)S(1)}, bf16[4,256,384]{2,1,0:T(8,128)(2,1)}, u32[]{:S(2)}) copy-start(bf16[4,256,384]{2,1,0:T(8,128)(2,1)} %param.10) | copy-start | bytes 2359300
  13.3 22.3 %collective-permute-start.6 = (bf16[4,1,384]{2,1,0:T(2,128)(2,1)S(1)}, bf16[4,1,384]{2,1,0:T(2,128)(2,1)S(1)}, u32[]{:S(2)}, u32[]{:S(2)}) collective-permute-start(bf16[4,1,384]{2,1,0:T(2,128)(2,1)S(1)} %get-tuple-element.57), channel_id=1, source_target_pairs={{0,4},{4,8},{8,12},{12,16},{16,20},{20,24},{24,28},{28,32},{32,36}... | collective-permute-start | bytes 9224 | tf_op jit(solution)/shard_map/ppermute | solution.py:318
  20.1 15.3 %copy-start.6 = (s32[1024]{0:T(1024)S(1)}, s32[1024]{0:T(1024)}, u32[]{:S(2)}) copy-start(s32[1024]{0:T(1024)} %param.17) | copy-start | bytes 12292
  20.1 15.3 %copy-start.8 = (f32[7]{0:T(128)S(1)}, f32[7]{0:T(128)}, u32[]{:S(2)}) copy-start(f32[7]{0:T(128)} %param.16) | copy-start | bytes 88
  20.1 15.4 %copy-start.7 = (f32[1024]{0:T(1024)S(1)}, f32[1024]{0:T(1024)}, u32[]{:S(2)}) copy-start(f32[1024]{0:T(1024)} %param.15) | copy-start | bytes 12292
  20.1 15.6 %collective-permute-start.7 = (bf16[4,1,384]{2,1,0:T(2,128)(2,1)S(1)}, bf16[4,1,384]{2,1,0:T(2,128)(2,1)S(1)}, u32[]{:S(2)}, u32[]{:S(2)}) collective-permute-start(bf16[4,1,384]{2,1,0:T(2,128)(2,1)S(1)} %get-tuple-element.58), channel_id=1, source_target_pairs={{4,0},{8,4},{12,8},{16,12},{20,16},{24,20},{28,24},{32,28},{36,32}... | collective-permute-start | bytes 9224 | tf_op jit(solution)/shard_map/ppermute | solution.py:318
  22.3 17.1 %collective-permute-start = (bf16[4,192,128]{2,1,0:T(8,128)(2,1)}, bf16[4,192,128]{2,1,0:T(8,128)(2,1)}, u32[]{:S(2)}, u32[]{:S(2)}) collective-permute-start(bf16[4,192,128]{2,1,0:T(8,128)(2,1)} %get-tuple-element.31), channel_id=1, source_target_pairs={{0,1},{1,0},{2,3},{3,2},{4,5},{5,4},{6,7},{7,6},{8,9},{9,8},{10,11... | collective-permute-start | bytes 589832 | tf_op jit(solution)/shard_map/ppermute | solution.py:314
  27.7 23.6 %all-to-all-start = ((bf16[32,4,32,128]{3,2,1,0:T(8,128)(2,1)}), bf16[32,4,32,128]{3,2,1,0:T(8,128)(2,1)S(1)}, u32[]{:S(2)}, u32[]{:S(2)}) async-start(bf16[32,4,32,128]{3,2,1,0:T(8,128)(2,1)} %cut_cot.1), calls=%async_computation | async-start | bytes 2097152 | tf_op jit(solution)/shard_map/all_to_all | solution.py:346
  35.6 2.7 %collective-permute-start.5 = (bf16[208,1024]{1,0:T(8,128)(2,1)}, bf16[208,1024]{1,0:T(8,128)(2,1)}, u32[]{:S(2)}, u32[]{:S(2)}) collective-permute-start(bf16[208,1024]{1,0:T(8,128)(2,1)} %collective-permute-done.3.h2), channel_id=1, source_target_pairs={{0,1},{1,0},{2,3},{3,2},{4,5},{5,4},{6,7},{7,6},{8,9},{9,8},{10,11... | collective-permute-start | bytes 1277960 | tf_op jit(solution)/shard_map/ppermute | solution.py:314
  51.4 1.0 copy-start.2
  57.9 19.2 %collective-permute-start.9 = (bf16[4,768,128]{2,1,0:T(8,128)(2,1)}, bf16[4,768,128]{2,1,0:T(8,128)(2,1)S(1)}, u32[]{:S(2)}, u32[]{:S(2)}) collective-permute-start(bf16[4,768,128]{2,1,0:T(8,128)(2,1)} %get-tuple-element.46.d0), channel_id=1, source_target_pairs={{0,2},{1,3},{2,0},{3,1},{4,6},{5,7},{6,4},{7,5},{8,10},{9,11},{10,... | collective-permute-start | bytes 2359304 | tf_op jit(solution)/shard_map/ppermute | solution.py:314
  61.5 3.3 %collective-permute-start.13 = (bf16[16,768]{1,0:T(8,128)(2,1)}, bf16[16,768]{1,0:T(8,128)(2,1)S(1)}, u32[]{:S(2)}, u32[]{:S(2)}) collective-permute-start(bf16[16,768]{1,0:T(8,128)(2,1)} %get-tuple-element.47), channel_id=1, source_target_pairs={{3,4},{7,8},{11,12},{15,16},{19,20},{23,24},{27,28},{31,32},{35,36... | collective-permute-start | bytes 73736 | tf_op jit(solution)/shard_map/ppermute | solution.py:324
  62.1 2.8 %collective-permute-start.12 = (bf16[16,768]{1,0:T(8,128)(2,1)}, bf16[16,768]{1,0:T(8,128)(2,1)S(1)}, u32[]{:S(2)}, u32[]{:S(2)}) collective-permute-start(bf16[16,768]{1,0:T(8,128)(2,1)} %get-tuple-element.47), channel_id=1, source_target_pairs={{3,5},{7,9},{11,13},{15,17},{19,21},{23,25},{27,29},{31,33},{35,37... | collective-permute-start | bytes 73736 | tf_op jit(solution)/shard_map/ppermute | solution.py:324
  62.8 2.1 %collective-permute-start.11 = (bf16[16,768]{1,0:T(8,128)(2,1)}, bf16[16,768]{1,0:T(8,128)(2,1)S(1)}, u32[]{:S(2)}, u32[]{:S(2)}) collective-permute-start(bf16[16,768]{1,0:T(8,128)(2,1)} %get-tuple-element.47), channel_id=1, source_target_pairs={{3,6},{7,10},{11,14},{15,18},{19,22},{23,26},{27,30},{31,34},{35,3... | collective-permute-start | bytes 73736 | tf_op jit(solution)/shard_map/ppermute | solution.py:324
  63.5 7.3 %collective-permute-start.10 = (bf16[16,768]{1,0:T(8,128)(2,1)}, bf16[16,768]{1,0:T(8,128)(2,1)S(1)}, u32[]{:S(2)}, u32[]{:S(2)}) collective-permute-start(bf16[16,768]{1,0:T(8,128)(2,1)} %get-tuple-element.47), channel_id=1, source_target_pairs={{3,7},{7,11},{11,15},{15,19},{19,23},{23,27},{27,31},{31,35},{35,3... | collective-permute-start | bytes 73736 | tf_op jit(solution)/shard_map/ppermute | solution.py:324
  64.8 32.6 %copy-start.9 = (bf16[16,768]{1,0:T(8,128)(2,1)}, bf16[16,768]{1,0:T(8,128)(2,1)S(1)}, u32[]{:S(2)}) copy-start(bf16[16,768]{1,0:T(8,128)(2,1)S(1)} %collective-permute-done.13.r3) | copy-start | bytes 73732
  64.8 12.3 %collective-permute-start.8 = (bf16[4,768,128]{2,1,0:T(8,128)(2,1)}, bf16[4,768,128]{2,1,0:T(8,128)(2,1)S(1)}, u32[]{:S(2)}, u32[]{:S(2)}) collective-permute-start(bf16[4,768,128]{2,1,0:T(8,128)(2,1)} %get-tuple-element.46.d0), channel_id=1, source_target_pairs={{0,1},{1,0},{2,3},{3,2},{4,5},{5,4},{6,7},{7,6},{8,9},{9,8},{10,11... | collective-permute-start | bytes 2359304 | tf_op jit(solution)/shard_map/ppermute | solution.py:314
  64.9 32.5 %copy-start.10 = (bf16[16,768]{1,0:T(8,128)(2,1)}, bf16[16,768]{1,0:T(8,128)(2,1)S(1)}, u32[]{:S(2)}) copy-start(bf16[16,768]{1,0:T(8,128)(2,1)S(1)} %collective-permute-done.12.r2) | copy-start | bytes 73732
  64.9 32.4 %copy-start.11 = (bf16[16,768]{1,0:T(8,128)(2,1)}, bf16[16,768]{1,0:T(8,128)(2,1)S(1)}, u32[]{:S(2)}) copy-start(bf16[16,768]{1,0:T(8,128)(2,1)S(1)} %collective-permute-done.11.r1) | copy-start | bytes 73732
  70.7 26.6 %copy-start.12 = (bf16[16,768]{1,0:T(8,128)(2,1)}, bf16[16,768]{1,0:T(8,128)(2,1)S(1)}, u32[]{:S(2)}) copy-start(bf16[16,768]{1,0:T(8,128)(2,1)S(1)} %collective-permute-done.10.r0) | copy-start | bytes 73732
  77.1 2.3 %copy-start.3 = (bf16[4,768,128]{2,1,0:T(8,128)(2,1)}, bf16[4,768,128]{2,1,0:T(8,128)(2,1)S(1)}, u32[]{:S(2)}) copy-start(bf16[4,768,128]{2,1,0:T(8,128)(2,1)S(1)} %collective-permute-done.9.d2) | copy-start | bytes 2359300
  77.1 2.3 %collective-permute-start.14 = (bf16[4,768,128]{2,1,0:T(8,128)(2,1)S(1)}, bf16[4,768,128]{2,1,0:T(8,128)(2,1)S(1)}, u32[]{:S(2)}, u32[]{:S(2)}) collective-permute-start(bf16[4,768,128]{2,1,0:T(8,128)(2,1)S(1)} %collective-permute-done.9.d2), channel_id=1, source_target_pairs={{0,1},{1,0},{2,3},{3,2},{4,5},{5,4},{6,7},{7,6},{8,9},{9,8},{10,11... | collective-permute-start | bytes 2359304 | tf_op jit(solution)/shard_map/ppermute | solution.py:314
  77.1 2.3 %copy-start.4 = (bf16[4,768,128]{2,1,0:T(8,128)(2,1)}, bf16[4,768,128]{2,1,0:T(8,128)(2,1)S(1)}, u32[]{:S(2)}) copy-start(bf16[4,768,128]{2,1,0:T(8,128)(2,1)S(1)} %collective-permute-done.8.d1) | copy-start | bytes 2359300
  79.4 0.9 copy-start.5
  91.9 43.8 %all-to-all-start.1 = ((bf16[32,368,128]{2,1,0:T(8,128)(2,1)}), bf16[32,368,128]{2,1,0:T(8,128)(2,1)S(1)}, u32[]{:S(2)}, u32[]{:S(2)}) async-start(bf16[32,368,128]{2,1,0:T(8,128)(2,1)} %weight_grad.1), calls=%async_computation.1 | async-start | bytes 6029312 | tf_op jit(solution)/shard_map/all_to_all | solution.py:372
  135.7 1.6 %copy-start = (bf16[32,368,128]{2,1,0:T(8,128)(2,1)}, bf16[32,368,128]{2,1,0:T(8,128)(2,1)S(1)}, u32[]{:S(2)}) copy-start(bf16[32,368,128]{2,1,0:T(8,128)(2,1)S(1)} %all-to-all-done.1.i) | copy-start | bytes 9043972

commit v3 on v2

v3 whole, which is shorter than its diff:
```python
import math

import jax
import jax.numpy as jnp
from jax import lax
from jax.experimental import pallas as pl
from jax.experimental.pallas import tpu as pltpu
from jax.sharding import PartitionSpec as P

BATCH = 4
C_OUT = 768
TRACKS = 1024
KERNEL = 5
SEQ = 32
CHAN = 4
LANES = 128
epsilon = 1e-06

BF = jnp.bfloat16
F32 = jnp.float32
VMEM_BYTES = 56 * 1024 * 1024


def params():
    return pltpu.CompilerParams(vmem_limit_bytes=VMEM_BYTES)


def dot(a, b, contract):
    return lax.dot_general(a, b, ((contract[:1], contract[1:]), ((), ())), preferred_element_type=F32)


ANY = pl.BlockSpec(memory_space=pl.ANY)
VM = pl.BlockSpec(memory_space=pltpu.VMEM)
SM = pl.BlockSpec(memory_space=pltpu.SMEM)


PIECE = BATCH * 192 + 16


def pieces_kernel(me_ref, merged_ref, gain_ref, *outs):
    me = me_ref[0]
    tail = jnp.concatenate([gain_ref[:, LANES:], jnp.zeros((1, 2 * LANES - 192), F32)], axis=1)
    rest = jnp.concatenate([gain_ref[:, :LANES], tail], axis=0)
    rows = []
    for _ in range(3):
        part = rest.astype(BF).astype(F32)
        rows.append(part)
        rest = rest - part
    gains = jnp.concatenate(rows + [jnp.zeros((10, LANES), F32)], axis=0).astype(BF)
    for r, piece in enumerate(outs):
        start = pl.multiple_of((me ^ r) * LANES, LANES)
        for b in range(BATCH):
            piece[b * 192 : (b + 1) * 192, :] = merged_ref[b, :, pl.ds(start, LANES)]
        piece[BATCH * 192 :, :] = gains


def cut_pieces(me, merged, gain):
    return pl.pallas_call(
        pieces_kernel,
        out_shape=(jax.ShapeDtypeStruct((PIECE, LANES), BF),) * CHAN,
        in_specs=[SM, VM, VM],
        out_specs=(VM,) * CHAN,
        compiler_params=params(),
        name="cut_pieces",
    )(me, merged, gain)


def cot_kernel(me_ref, cot_ref, send_ref, sems):
    copies = []
    for d in range(SEQ):
        start = pl.multiple_of(d * CHAN * LANES + me_ref[0] * LANES, LANES)
        copies.append(
            pltpu.make_async_copy(cot_ref.at[:, :, pl.ds(start, LANES)], send_ref.at[d], sems.at[d])
        )
    for copy in copies:
        copy.start()
    for copy in copies:
        copy.wait()


def cut_cot(me, cot):
    return pl.pallas_call(
        cot_kernel,
        out_shape=jax.ShapeDtypeStruct((SEQ, BATCH, 32, LANES), BF),
        in_specs=[SM, ANY],
        out_specs=VM,
        scratch_shapes=[pltpu.SemaphoreType.DMA((SEQ,))],
        compiler_params=params(),
        cost_estimate=pl.CostEstimate(flops=0, bytes_accessed=5 * 2**20, transcendentals=0),
        name="cut_cot",
    )(me, cot)


def batch_of(piece, b):
    return piece[b * 192 : (b + 1) * 192, :]


def rows_of(pieces):
    return jnp.concatenate(
        [jnp.concatenate([batch_of(p, b) for b in range(BATCH)], axis=1) for p in pieces], axis=0
    )


def weights_of(heads):
    return jnp.concatenate([h[...] for h in heads], axis=0)


def gains_of(pieces):
    row = lax.broadcasted_iota(jnp.int32, (16, LANES), 0)
    blocks = []
    for p in pieces:
        parts = p[BATCH * 192 :, :]
        for side in range(2):
            pick = ((row < 6) & (row % 2 == side)).astype(BF)
            blocks.append(dot(parts, pick, (0, 0))[: LANES - side * 64, 0:1])
    return jnp.concatenate(blocks, axis=0)


def score_kernel(p0, p1, p2, p3, h0, h1, h2, h3, raw_ref, inv_ref):
    heads = (h0, h1, h2, h3)
    m32 = rows_of((p0, p1, p2, p3)).astype(F32)
    total = jnp.sum(m32 * m32, axis=0, keepdims=True)
    inv_ref[...] = jnp.broadcast_to(lax.rsqrt(total / C_OUT + epsilon), inv_ref.shape)
    normed = (m32 * gains_of((p0, p1, p2, p3))).astype(BF)
    raw_ref[...] = dot(weights_of(heads), normed, (0, 0))


def scores(pieces, heads):
    return pl.pallas_call(
        score_kernel,
        out_shape=(jax.ShapeDtypeStruct((TRACKS, BATCH * LANES), F32),
                   jax.ShapeDtypeStruct((8, BATCH * LANES), F32)),
        in_specs=[VM] * 8,
        out_specs=(VM, VM),
        compiler_params=params(),
        cost_estimate=pl.CostEstimate(flops=2 * 10**9, bytes_accessed=8 * 2**20, transcendentals=0),
        name="scores",
    )(*pieces, *heads)


def head_kernel(
    ids_ref, valid_ref, raw_ref, inv_ref, cot_ref, cols_ref, p0, p1, p2, p3, h0, h1, h2, h3,
    mine_ref, other_ref, edge_ref, full
):
    me = ids_ref[0]
    first = ids_ref[1]
    half = ids_ref[2]
    scale = cols_ref[:, 0:1]
    bias = cols_ref[:, 1:2]
    lane = lax.broadcasted_iota(jnp.int32, (1, LANES), 1)
    heads = (h0, h1, h2, h3)
    scaled, coefs = [], []
    for b in range(BATCH):
        cols = slice(b * LANES, (b + 1) * LANES)
        raw = raw_ref[:, cols]
        inv = inv_ref[0:1, cols]
        live = (first + lane < valid_ref[b]).astype(F32)
        gate = 0.5 * jnp.tanh(0.5 * (inv * raw + bias)) + 0.5
        cot = cot_ref[:, b * 32 : (b + 1) * 32, :].reshape(TRACKS, LANES).astype(F32)
        d_logits = (cot * scale) * gate
        d_rms = live * jnp.sum(d_logits * raw, axis=0, keepdims=True)
        scaled.append(((inv * live) * d_logits).astype(BF))
        coefs.append(inv * inv * inv * d_rms * (1.0 / C_OUT))
    d = dot(weights_of(heads), jnp.concatenate(scaled, axis=1), (1, 0)) * gains_of((p0, p1, p2, p3))
    for r, p in enumerate((p0, p1, p2, p3)):
        for b in range(BATCH):
            block = d[r * 192 : (r + 1) * 192, b * LANES : (b + 1) * LANES]
            full[b, me ^ r] = block - coefs[b] * batch_of(p, b).astype(F32)
    for b in range(BATCH):
        for g in range(CHAN):
            mine_ref[b, g] = full[b, g, pl.ds(pl.multiple_of(96 * half, 32), 96), :].astype(BF)
            other_ref[b, g] = full[b, g, pl.ds(pl.multiple_of(96 * (1 - half), 32), 96), :].astype(BF)
    start = jnp.where(me == CHAN - 1, LANES - 2, 0)
    row = lax.broadcasted_iota(jnp.int32, (16, LANES), 0)
    col = lax.broadcasted_iota(jnp.int32, (16, LANES), 1) - start
    edge = jnp.zeros((16, C_OUT), F32)
    for b in range(BATCH):
        sel = ((col >= 0) & (col < 2) & (row == b * 2 + col)).astype(BF)
        edge = edge + dot(sel, full[b].reshape(C_OUT, LANES).astype(BF), (1, 1))
    edge_ref[...] = edge.astype(BF)


def head(ids, valid, raw, inv, cot, cols, pieces, heads):
    return pl.pallas_call(
        head_kernel,
        out_shape=(jax.ShapeDtypeStruct((BATCH, CHAN, 96, LANES), BF),) * 2
        + (jax.ShapeDtypeStruct((16, C_OUT), BF),),
        in_specs=[SM, SM] + [VM] * 12,
        out_specs=(VM,) * 3,
        scratch_shapes=[pltpu.VMEM((BATCH, CHAN, 192, LANES), F32)],
        compiler_params=params(),
        name="head",
    )(ids, valid, raw, inv, cot, cols, *pieces, *heads)


PAIR = 2


def rows_kernel(own_ref, far_ref, tr_ref, trx_ref):
    row = lax.broadcasted_iota(jnp.int32, (256, 384), 0)
    ends = [jnp.zeros((LANES, 384), F32) for _ in range(KERNEL)]
    at = lax.broadcasted_iota(jnp.int32, (LANES, 384), 0)
    for q, ref in enumerate((own_ref, far_ref)):
        for b in range(BATCH):
            t = ref[b].astype(F32)
            rows = slice(b * 256, (b + 1) * 256)
            tr_ref[q, rows, 0:384] = jnp.where(row == 0, 0.0, pltpu.roll(t, 1, 0)).astype(BF)
            tr_ref[q, rows, 384:768] = ref[b]
            tr_ref[q, rows, 768:1152] = jnp.where(row == 255, 0.0, pltpu.roll(t, 255, 0)).astype(BF)
            base = (q * BATCH + b) * 5
            for place, tap, j in ((0, 1, 127), (0, 3, 128), (1, 1, 255), (2, 0, 255), (3, 3, 0), (4, 4, 0)):
                ends[tap] = jnp.where(at == base + place, t[j : j + 1], ends[tap])
    for k in range(KERNEL):
        trx_ref[:, k * 384 : (k + 1) * 384] = ends[k].astype(BF)


def trunk_rows(own, far):
    return pl.pallas_call(
        rows_kernel,
        out_shape=(jax.ShapeDtypeStruct((PAIR, 1024, 1152), BF),
                   jax.ShapeDtypeStruct((LANES, KERNEL * 384), BF)),
        in_specs=[VM, VM],
        out_specs=(VM, VM),
        compiler_params=params(),
        cost_estimate=pl.CostEstimate(flops=10**7, bytes_accessed=8 * 2**20, transcendentals=0),
        name="trunk_rows",
    )(own, far)


ROWS = 368


def weight_kernel(ids_ref, *refs):
    pieces, (tr_ref, trx_ref, rim0, rim1, out_ref, full, tr, ends, sems, tr_sems) = refs[:8], refs[8:]
    me = ids_ref[0]
    half = ids_ref[2]
    copies = []
    for q in range(PAIR):
        for r in range(CHAN):
            lanes = pl.ds(pl.multiple_of((me ^ r) * LANES, LANES), LANES)
            copies.append(
                pltpu.make_async_copy(pieces[q * CHAN + r], full.at[q, :, :, :, lanes], sems.at[q, r])
            )
    loads = [pltpu.make_async_copy(tr_ref.at[q], tr.at[q], tr_sems.at[q]) for q in range(PAIR)]
    for copy in copies + loads:
        copy.start()
    p = lax.broadcasted_iota(jnp.int32, (256, 256), 0)
    q_ = lax.broadcasted_iota(jnp.int32, (256, 256), 1)
    even = (q_ < 128) & (p // 2 == q_)
    odd = (q_ >= 128) & ((p + 1) // 2 == q_ - 128)
    pick = (even | odd).astype(BF)
    row = lax.broadcasted_iota(jnp.int32, (64, LANES), 0)
    col = lax.broadcasted_iota(jnp.int32, (64, LANES), 1)
    batch, tap = (row % 16) // 2, row % 2
    before, after = row // 16 == (me ^ 3), row // 16 == me
    edge = jnp.zeros((C_OUT, LANES), F32)
    for q, rim in enumerate((rim0, rim1)):
        place = col - (q * BATCH + batch) * 5
        picks = (
            (before & (place == 4)) | (before & (place == 3) & (tap == 1))
            | (after & (place == 2)) | (after & (place == 1) & (tap == 0))
        )
        picks = (picks & (row % 16 < 8)).astype(BF)
        edge = edge + dot(rim[...], picks, (0, 0))
    ends[...] = edge
    last = jnp.concatenate(
        [ends[pl.ds(pl.multiple_of(192 * g + 96 * half, 32), 96), :] for g in range(CHAN)], axis=0
    )
    p1 = lax.broadcasted_iota(jnp.int32, (LANES, LANES), 0)
    q1 = lax.broadcasted_iota(jnp.int32, (LANES, LANES), 1)
    g_even = jnp.zeros((384, 1152), F32)
    g_odd = jnp.zeros((384, 768), F32)
    for q in range(PAIR):
        for copy in copies[q * CHAN : (q + 1) * CHAN]:
            copy.wait()
        evens, odds = [], []
        for b in range(BATCH):
            for h in range(2):
                block = full[q, b, :, :, h * 256 : (h + 1) * 256].reshape(384, 256)
                e = dot(block, pick, (1, 0)).astype(BF)
                evens.append(e[:, :128])
                odds.append(e[:, 128:])
                sel = ((p1 == LANES - 1) & (q1 == (q * BATCH + b) * 5 + h)).astype(BF)
                last = last + dot(block[:, 128:], sel, (1, 0))
        loads[q].wait()
        g_even = g_even + dot(jnp.concatenate(evens, axis=1), tr[q], (1, 0))
        g_odd = g_odd + dot(jnp.concatenate(odds, axis=1), tr[q, :, :768], (1, 0))
    last = last.astype(BF)
    side = [dot(last, trx_ref[:, k * 384 : (k + 1) * 384], (1, 0)) for k in range(KERNEL)]
    pad = jnp.zeros((ROWS - 360, LANES), F32)
    taps = (g_even[:, :384], g_odd[:, :384], g_even[:, 384:768], g_odd[:, 384:], g_even[:, 768:])
    taps = [tap + term for tap, term in zip(taps, side)]
    for s in range(16):
        blocks = []
        for l in range(3):
            for tap in taps:
                blocks.append(tap[s * 24 : (s + 1) * 24, l * LANES : (l + 1) * LANES])
        out_ref[s] = jnp.concatenate(blocks + [pad], axis=0).astype(BF)


def weight_grad(ids, pieces, tr, trx, rims, rims_far):
    return pl.pallas_call(
        weight_kernel,
        out_shape=jax.ShapeDtypeStruct((16, ROWS, LANES), BF),
        in_specs=[SM] + [ANY] * 9 + [VM] * 3,
        out_specs=VM,
        scratch_shapes=[
            pltpu.VMEM((PAIR, BATCH, CHAN, 96, 512), BF),
            pltpu.VMEM((PAIR, 1024, 1152), BF),
            pltpu.VMEM((C_OUT, LANES), F32),
            pltpu.SemaphoreType.DMA((PAIR, CHAN)),
            pltpu.SemaphoreType.DMA((PAIR,)),
        ],
        compiler_params=params(),
        cost_estimate=pl.CostEstimate(flops=4 * 10**9, bytes_accessed=10 * 2**20, transcendentals=0),
        name="weight_grad",
    )(ids, *pieces, tr, trx, rims, rims_far)


def trunk_kernel(ids_ref, *refs):
    mine, other = refs[:4], refs[4:8]
    conv_ref, rim_ref, out_ref, skip_ref, full, sums, sems, skip_sem = refs[8:]
    me = ids_ref[0]
    half = ids_ref[2]
    skip = pltpu.make_async_copy(full.at[:, me], skip_ref, skip_sem)
    copies = []
    for r in range(CHAN):
        lanes = pl.ds(pl.multiple_of((me ^ r) * LANES, LANES), LANES)
        copies.append(pltpu.make_async_copy(mine[r], full.at[:, :, half, :, lanes], sems.at[0, r]))
        copies.append(pltpu.make_async_copy(other[r], full.at[:, :, 1 - half, :, lanes], sems.at[1, r]))
    for copy in copies:
        copy.start()
    row = lax.broadcasted_iota(jnp.int32, (2 * EXT, 512), 0)
    p = lax.broadcasted_iota(jnp.int32, (2 * EXT, 512), 1)
    lo = jnp.where(row < EXT, 2 * (row - 8), 2 * (row - EXT - 8) - 1)
    pick = ((p == lo) | (p == lo + 1)).astype(BF)
    col = lax.broadcasted_iota(jnp.int32, (2 * EXT, 64), 1)
    lo = lo[:, :64]
    rim = rim_ref[...]
    for copy in copies:
        copy.wait()
    skip.start()
    for b in range(BATCH):
        offset = col % 16 - 2 * b
        rim_ok = (offset >= 0) & (offset < 2)
        rim_pos = jnp.where(col // 16 == (me ^ 3), offset - 2, jnp.where(col // 16 == me, 512 + offset, -99))
        pick_r = (rim_ok & ((rim_pos == lo) | (rim_pos == lo + 1))).astype(BF)
        e = (dot(pick, full[b].reshape(C_OUT, 512), (1, 1)) + dot(pick_r, rim, (1, 0))).astype(BF)
        sums[pl.ds(b * EXT, EXT), :C_OUT] = e[:EXT]
        sums[pl.ds(b * EXT, EXT), C_OUT:] = e[EXT:]
    even, odd = sums[:, :C_OUT], sums[:, C_OUT:]
    up = dot(even, conv_ref[0], (1, 1)) + dot(odd, conv_ref[1], (1, 1))
    here = dot(even, conv_ref[2], (1, 1)) + dot(odd, conv_ref[3], (1, 1))
    down = dot(even, conv_ref[4], (1, 1))
    for b in range(BATCH):
        o = b * EXT + 8
        total = up[o + 1 : o + 257] + here[o : o + 256] + down[o - 1 : o + 255]
        out_ref[b] = total.astype(BF)
    skip.wait()


EXT = 272


def trunk_grad(ids, mine, other, conv_w, rims):
    return pl.pallas_call(
        trunk_kernel,
        out_shape=(jax.ShapeDtypeStruct((BATCH, 256, 384), BF), jax.ShapeDtypeStruct((BATCH, 2, 96, 512), BF)),
        in_specs=[SM] + [ANY] * 8 + [VM] * 2,
        out_specs=(VM, ANY),
        scratch_shapes=[pltpu.VMEM((BATCH, CHAN, 2, 96, 512), BF), pltpu.VMEM((BATCH * EXT, 2 * C_OUT), BF),
                        pltpu.SemaphoreType.DMA((2, CHAN)), pltpu.SemaphoreType.DMA],
        compiler_params=params(),
        cost_estimate=pl.CostEstimate(flops=8 * 10**9, bytes_accessed=16 * 2**20, transcendentals=0),
        name="trunk_grad",
    )(ids, *mine, *other, conv_w, rims)


def sum_kernel(scale, in_ref, out_ref):
    total = in_ref[0].astype(F32)
    for s in range(1, in_ref.shape[0]):
        total = total + in_ref[s].astype(F32)
    total = total * scale
    for l in range(3):
        for k in range(KERNEL):
            start = l * 120 + k * 24
            out_ref[k, :, l * LANES : (l + 1) * LANES] = total[start : start + 24]


def sum_weights(terms, scale):
    return pl.pallas_call(
        lambda i, o: sum_kernel(scale, i, o),
        out_shape=jax.ShapeDtypeStruct((KERNEL, 24, 384), F32),
        in_specs=[VM],
        out_specs=VM,
        compiler_params=params(),
        name="sum_weights",
    )(terms)


def flip(x, r):
    return lax.ppermute(x, "chan", [(i, i ^ r) for i in range(CHAN)])


def shift(x, step):
    return lax.ppermute(x, "seq", [(i, i + step) for i in range(SEQ) if 0 <= i + step < SEQ])


def partner(x):
    return lax.ppermute(x, "seq", [(i, i ^ 4) for i in range(SEQ)])


def partner_far(x):
    pairs = [(s * CHAN + c, (s ^ 4) * CHAN + (c ^ 2)) for s in range(SEQ) for c in range(CHAN)]
    return lax.ppermute(x, ("seq", "chan"), pairs)


def rim_to(x, r):
    up = [(s * CHAN + 3, (s + 1) * CHAN + (3 ^ r)) for s in range(SEQ - 1)]
    down = [(s * CHAN, (s - 1) * CHAN + r) for s in range(1, SEQ)]
    return lax.ppermute(x, ("seq", "chan"), up + down)


def across(x):
    pairs = [(s * CHAN + c, (s ^ 16) * CHAN + (c ^ 2)) for s in range(SEQ) for c in range(CHAN)]
    return lax.ppermute(x, ("seq", "chan"), pairs)


def local(
    trunk, merged, conv_w, norm_gain, head_w, head_bias, head_scale, head_of_track, valid_len, cot
):
    me = lax.axis_index("chan").astype(jnp.int32)
    place = lax.axis_index("seq").astype(jnp.int32)
    half = (place // 4) % 2
    ids = jnp.stack([me, place * 512 + me * LANES, half])
    far_head = across(head_w)
    trunk_far = partner(trunk)
    p0, p1, p2, p3 = cut_pieces(ids, merged, norm_gain[None])
    p1, p2, p3 = flip(p1, 1), flip(p2, 2), flip(p3, 3)
    send = cut_cot(ids, cot)
    send, p1, p2, p3, far_head, trunk_far = lax.optimization_barrier((send, p1, p2, p3, far_head, trunk_far))
    got = lax.all_to_all(send, "seq", 0, 0, tiled=True).reshape(SEQ, BATCH * 32, LANES)
    heads = (head_w, flip(head_w, 1), far_head, flip(far_head, 1))
    pieces = (p0, p1, p2, p3)

    onehot = (
        head_of_track[:, None] == jnp.arange(head_scale.shape[0], dtype=jnp.int32)[None, :]
    ).astype(F32)
    track_scale = jnp.sum(onehot * head_scale[None, :], axis=1)
    cols = jnp.stack([track_scale, head_bias], axis=1)

    tr, trx = trunk_rows(trunk, trunk_far)
    heads, tr, trx, cols = lax.optimization_barrier((heads, tr, trx, cols))
    raw, inv = scores(pieces, heads)
    mine, other, edge = head(ids, valid_len, raw, inv, got, cols, pieces, heads)

    rims = [rim_to(edge, r) for r in range(CHAN)]
    mine_far, other_x, other_far_x = flip(mine, 2), partner(other), partner_far(other)
    mine_far, other_x, other_far_x, *rims = lax.optimization_barrier((mine_far, other_x, other_far_x, *rims))
    rims = jnp.concatenate(rims)
    mine_all = (mine, flip(mine, 1), mine_far, flip(mine_far, 1))
    blocks = mine_all + (other_x, flip(other_x, 1), other_far_x, flip(other_far_x, 1))
    terms = weight_grad(ids, blocks, tr, trx, rims, partner(rims))
    other_late, _ = lax.optimization_barrier((other, mine_far))
    other_far = flip(other_late, 2)
    other_all = (other, flip(other, 1), other_far, flip(other_far, 1))
    groups = [[s for s in range(SEQ) if (s // 4) % 2 == u] for u in range(2)]
    summed = lax.all_to_all(terms, "seq", 0, 0, tiled=True, axis_index_groups=groups)
    d_trunk, d_skip = trunk_grad(ids, mine_all, other_all, conv_w, rims)
    grad_scale = 1.0 / math.sqrt(BATCH * 512 * SEQ)
    d_conv_w = sum_weights(summed, grad_scale)
    return (d_trunk, d_skip.reshape(BATCH, 192, 512), d_conv_w)


def solution(mesh):
    placed = (
        P(None, "seq", "chan"),
        P(None, "chan", "seq"),
        P(None, "chan", None),
        P("chan"),
        P("chan", None),
        P(),
        P(),
        P(),
        P(),
        P(None, "seq", None),
    )
    return jax.shard_map(
        local,
        mesh=mesh,
        in_specs=placed,
        out_specs=(P(None, "seq", "chan"), P(None, "chan", "seq"), P(None, "seq", "chan")),
        check_vma=False,
    )
```

time: 143 us -> 128 us (0.90); the launches traced: 140 us -> 127 us
  waiting for transfers between devices: 47 us -> 29 us
  starting transfers between devices: 32.3 us -> 46.1 us
  Pallas kernels: 49.5 us -> 44.2 us
  other arithmetic: 3.86 us -> 0.69 us
    ppermute x8 -> x13, starting transfers between devices: 7.38 us -> 18.1 us  [flip(): return lax.ppermute(x, 'chan', [(i, i ^ r) for i in range(CHAN)])]
    all_to_all x1, waiting for transfers between devices: 18.8 us -> 8.24 us  [local(): lax.all_to_all(terms, 'seq', 0, 0, tiled=True, axis_index_groups=groups)]
    pallas_call x4 -> x5, Pallas kernels: 39 us -> 34.4 us  [the longest x1 12.2 us: trunk_grad(): pl.pallas_call(trunk_kernel, out_shape=(jax.ShapeDtypeStruct((BATCH, 256,...]
    ppermute x4, waiting for transfers between devices: 5.82 us -> 1.83 us  [rim_to(): return lax.ppermute(x, ('seq', 'chan'), up + down)]
    ppermute x1, waiting for transfers between devices: 5.23 us -> 1.74 us  [across(): return lax.ppermute(x, ('seq', 'chan'), pairs)]
    ppermute x2 -> x4, waiting for transfers between devices: 0.01 us -> 3.47 us  [the longest x3 3.46 us: partner(): return lax.ppermute(x, 'seq', [(i, i ^ 4) for i in range(SEQ)])]
    all_to_all x1, waiting for transfers between devices: 7.71 us -> 5.52 us  [local(): lax.all_to_all(send, 'seq', 0, 0, tiled=True)]
    concatenate x3 -> x0, other arithmetic: 1.8 us -> none  [the longest x1 1.7 us: local(): tr = jnp.concatenate([tr_m, trunk, tr_p], axis=2).reshape(1024, 1152)]
  transfers between devices with their start and end apart: 17 -> 24, of which waited for: 7 -> 10; matrix products, arithmetic and copies ran while one was open for 3% -> 1% of each run, Pallas kernels for 19% -> 29%
where the time goes in v3:
time: 128 us; the launch traced here: 127 us
  starting transfers between devices  46.1 us (36%)
  Pallas kernels  44.2 us (35%)
  waiting for transfers between devices  29 us (23%)
  local copies, waits for them, and re-layouts  5.9 us (5%)
    ppermute x13, starting transfers between devices, flip(): return lax.ppermute(x, 'chan', [(i, i ^ r) for i in range(CHAN)])  18.1 us
    pallas_call x1, Pallas kernels, trunk_grad(): pl.pallas_call(trunk_kernel, out_shape=(jax.ShapeDtypeStruct((BATCH, 256,...  12.2 us
    pallas_call x1, Pallas kernels, weight_grad(): pl.pallas_call(weight_kernel, out_shape=jax.ShapeDtypeStruct((16, ROWS, L...  9.88 us
    all_to_all x1, waiting for transfers between devices, local(): lax.all_to_all(terms, 'seq', 0, 0, tiled=True, axis_index_groups=groups)  8.24 us
    ppermute x13, waiting for transfers between devices, flip(): return lax.ppermute(x, 'chan', [(i, i ^ r) for i in range(CHAN)])  8.24 us
    all_to_all x1, starting transfers between devices, local(): lax.all_to_all(terms, 'seq', 0, 0, tiled=True, axis_index_groups=groups)  7.15 us
    all_to_all x1, starting transfers between devices, local(): lax.all_to_all(send, 'seq', 0, 0, tiled=True)  7.04 us
    ppermute x3, starting transfers between devices, partner(): return lax.ppermute(x, 'seq', [(i, i ^ 4) for i in range(SEQ)])  6.39 us
  transfers between devices with their start and end apart: 24, of which 10 were waited for; matrix products, arithmetic and copies ran while one was open for 1% of the time, Pallas kernels for 29%

profile of v3, /device:TPU:0, one launch (start us, length us, event | category | flops | bytes accessed | tf_op | source)
XLA Modules:
  0.0 127.0 jit_solution(9806988608546933279)
XLA Ops:
  0.6 1.7 %collective-permute-start.4 = (bf16[4,256,384]{2,1,0:T(8,128)(2,1)}, bf16[4,256,384]{2,1,0:T(8,128)(2,1)S(1)}, u32[]{:S(2)}, u32[]{:S(2)}) collective-permute-start(bf16[4,256,384]{2,1,0:T(8,128)(2,1)} %own_ref.1), channel_id=1, source_target_pairs={{0,16},{4,20},{8,24},{12,28},{16,0},{20,4},{24,8},{28,12},{32,48},... | collective-permute-start | bytes 2359304 | tf_op jit(solution)/shard_map/ppermute | solution.py:410
  2.4 4.0 %collective-permute-start.3 = (bf16[192,1024]{1,0:T(8,128)(2,1)}, bf16[192,1024]{1,0:T(8,128)(2,1)S(1)}, u32[]{:S(2)}, u32[]{:S(2)}) collective-permute-start(bf16[192,1024]{1,0:T(8,128)(2,1)} %h0.1), channel_id=1, source_target_pairs={{0,66},{1,67},{2,64},{3,65},{4,70},{5,71},{6,68},{7,69},{8,74},{9,... | collective-permute-start | bytes 1179656 | tf_op jit(solution)/shard_map/ppermute | solution.py:426
  7.0 2.2 %cut_pieces.1 = (bf16[784,128]{1,0:T(8,128)(2,1)}, bf16[784,128]{1,0:T(8,128)(2,1)}, bf16[784,128]{1,0:T(8,128)(2,1)}, bf16[784,128]{1,0:T(8,128)(2,1)}) custom-call(s32[3]{0:T(128)} %pad_add_fusion.me_ref.ids_ref, bf16[4,192,512]{2,1,0:T(8,128)(2,1)} %merged_ref.1, f32[1,192]{1,0:T(1,128)} %bitcast.11), custom_call_target="tpu_custom_call" | custom-call | tf_op jit(solution)/shard_map/cut_pieces/pallas_call | solution.py:58
  9.2 3.4 %collective-permute-start.2 = (bf16[784,128]{1,0:T(8,128)(2,1)}, bf16[784,128]{1,0:T(8,128)(2,1)S(1)}, u32[]{:S(2)}, u32[]{:S(2)}) collective-permute-start(bf16[784,128]{1,0:T(8,128)(2,1)} %get-tuple-element.40), channel_id=1, source_target_pairs={{0,3},{1,2},{2,1},{3,0},{4,7},{5,6},{6,5},{7,4},{8,11},{9,10},{10,... | collective-permute-start | bytes 602120 | tf_op jit(solution)/shard_map/ppermute | solution.py:402
  12.6 3.2 %cut_cot.1 = bf16[32,4,32,128]{3,2,1,0:T(8,128)(2,1)} custom-call(s32[3]{0:T(128)} %pad_add_fusion.me_ref.ids_ref, bf16[4,32,16384]{2,1,0:T(8,128)(2,1)} %cot_ref.1), custom_call_target="tpu_custom_call" | custom-call | bytes 5242880 | tf_op jit(solution)/shard_map/cut_cot/pallas_call | solution.py:82
  15.9 2.9 %collective-permute-done.1.p2 = bf16[784,128]{1,0:T(8,128)(2,1)S(1)} collective-permute-done((bf16[784,128]{1,0:T(8,128)(2,1)}, bf16[784,128]{1,0:T(8,128)(2,1)S(1)}, u32[]{:S(2)}, u32[]{:S(2)}) %collective-permute-start.1) | collective-permute-done | bytes 200736 | tf_op jit(solution)/shard_map/ppermute | solution.py:402
  18.8 3.5 %collective-permute-done.2.p3 = bf16[784,128]{1,0:T(8,128)(2,1)S(1)} collective-permute-done((bf16[784,128]{1,0:T(8,128)(2,1)}, bf16[784,128]{1,0:T(8,128)(2,1)S(1)}, u32[]{:S(2)}, u32[]{:S(2)}) %collective-permute-start.2) | collective-permute-done | bytes 200736 | tf_op jit(solution)/shard_map/ppermute | solution.py:402
  22.3 1.7 %collective-permute-done.3.h2 = bf16[192,1024]{1,0:T(8,128)(2,1)S(1)} collective-permute-done((bf16[192,1024]{1,0:T(8,128)(2,1)}, bf16[192,1024]{1,0:T(8,128)(2,1)S(1)}, u32[]{:S(2)}, u32[]{:S(2)}) %collective-permute-start.3) | collective-permute-done | bytes 393248 | tf_op jit(solution)/shard_map/ppermute | solution.py:426
  24.1 7.0 %all-to-all-start = ((bf16[32,4,32,128]{3,2,1,0:T(8,128)(2,1)}), bf16[32,4,32,128]{3,2,1,0:T(8,128)(2,1)S(1)}, u32[]{:S(2)}, u32[]{:S(2)}) async-start(bf16[32,4,32,128]{3,2,1,0:T(8,128)(2,1)} %cut_cot.1), calls=%async_computation | async-start | bytes 2097152 | tf_op jit(solution)/shard_map/all_to_all | solution.py:442
  31.9 4.5 %trunk_rows.1 = (bf16[2,1024,1152]{2,1,0:T(8,128)(2,1)}, bf16[128,1920]{1,0:T(8,128)(2,1)}) custom-call(bf16[4,256,384]{2,1,0:T(8,128)(2,1)} %own_ref.1, bf16[4,256,384]{2,1,0:T(8,128)(2,1)} %copy-done.2), custom_call_target="tpu_custom_call" | custom-call | flops 10000000 | bytes 8388608 | tf_op jit(solution)/shard_map/trunk_rows/pallas_call | solution.py:218
  36.4 1.0 copy.16.cols_ref
  37.4 4.3 %scores.1 = (f32[1024,512]{1,0:T(8,128)}, f32[8,512]{1,0:T(8,128)}) custom-call(bf16[784,128]{1,0:T(8,128)(2,1)} %get-tuple-element.37.p0, bf16[784,128]{1,0:T(8,128)(2,1)} %copy-done.7, bf16[784,128]{1,0:T(8,128)(2,1)} %copy-done.8, bf16[784,128]{1,0:T(8,128)(2,1)} %copy-done.9, bf16[192,1024]{1,0:T(8,128)(2,1)} %h0.1, bf16[192,1024]{1,0:T(8,128)(2,1)} %copy-done.5, ...), custom_call_target="tpu_custom_call" | custom-call | flops 2000000000 | bytes 8388608 | tf_op jit(solution)/shard_map/scores/pallas_call | solution.py:129
  41.8 5.5 %all-to-all-done = bf16[32,4,32,128]{3,2,1,0:T(8,128)(2,1)S(1)} async-done(((bf16[32,4,32,128]{3,2,1,0:T(8,128)(2,1)}), bf16[32,4,32,128]{3,2,1,0:T(8,128)(2,1)S(1)}, u32[]{:S(2)}, u32[]{:S(2)}) %all-to-all-start) | async-done | bytes 1048608 | tf_op jit(solution)/shard_map/all_to_all | solution.py:442
  47.3 1.1 copy-done.1
  48.3 5.7 %head.1 = (bf16[4,4,96,128]{3,2,1,0:T(8,128)(2,1)}, bf16[4,4,96,128]{3,2,1,0:T(8,128)(2,1)}, bf16[16,768]{1,0:T(8,128)(2,1)}) custom-call(s32[3]{0:T(128)} %pad_add_fusion.me_ref.ids_ref, s32[4]{0:T(128)} %valid_ref.1, f32[1024,512]{1,0:T(8,128)} %get-tuple-element.52.raw_ref, f32[8,512]{1,0:T(8,128)} %get-tuple-element.53.inv_ref, ...), custom_call_target="tpu_custom_call" | custom-call | tf_op jit(solution)/shard_map/head/pallas_call | solution.py:184
  54.1 3.4 %collective-permute-start.8 = (bf16[4,4,96,128]{3,2,1,0:T(8,128)(2,1)}, bf16[4,4,96,128]{3,2,1,0:T(8,128)(2,1)S(1)}, u32[]{:S(2)}, u32[]{:S(2)}) collective-permute-start(bf16[4,4,96,128]{3,2,1,0:T(8,128)(2,1)} %get-tuple-element.56.refs_0_), channel_id=1, source_target_pairs={{0,2},{1,3},{2,0},{3,1},{4,6},{5,7},{6,4},{7,5},{8,10},{9,11},{10,... | collective-permute-start | bytes 1179656 | tf_op jit(solution)/shard_map/ppermute | solution.py:402
  57.6 1.5 %collective-permute-start.9 = (bf16[4,4,96,128]{3,2,1,0:T(8,128)(2,1)}, bf16[4,4,96,128]{3,2,1,0:T(8,128)(2,1)S(1)}, u32[]{:S(2)}, u32[]{:S(2)}) collective-permute-start(bf16[4,4,96,128]{3,2,1,0:T(8,128)(2,1)} %get-tuple-element.60.refs_4_), channel_id=1, source_target_pairs={{0,16},{4,20},{8,24},{12,28},{16,0},{20,4},{24,8},{28,12},{32,48},... | collective-permute-start | bytes 1179656 | tf_op jit(solution)/shard_map/ppermute | solution.py:410
  61.1 1.3 %collective-permute-start.11 = (bf16[16,768]{1,0:T(8,128)(2,1)}, bf16[16,768]{1,0:T(8,128)(2,1)S(1)}, u32[]{:S(2)}, u32[]{:S(2)}) collective-permute-start(bf16[16,768]{1,0:T(8,128)(2,1)} %get-tuple-element.58), channel_id=1, source_target_pairs={{3,7},{7,11},{11,15},{15,19},{19,23},{23,27},{27,31},{31,35},{35,3... | collective-permute-start | bytes 73736 | tf_op jit(solution)/shard_map/ppermute | solution.py:421
  62.4 8.7 %collective-permute-start.7 = (bf16[4,4,96,128]{3,2,1,0:T(8,128)(2,1)}, bf16[4,4,96,128]{3,2,1,0:T(8,128)(2,1)S(1)}, u32[]{:S(2)}, u32[]{:S(2)}) collective-permute-start(bf16[4,4,96,128]{3,2,1,0:T(8,128)(2,1)} %get-tuple-element.56.refs_0_), channel_id=1, source_target_pairs={{0,1},{1,0},{2,3},{3,2},{4,5},{5,4},{6,7},{7,6},{8,9},{9,8},{10,11... | collective-permute-start | bytes 1179656 | tf_op jit(solution)/shard_map/ppermute | solution.py:402
  71.0 1.8 %collective-permute-done.11 = bf16[16,768]{1,0:T(8,128)(2,1)S(1)} collective-permute-done((bf16[16,768]{1,0:T(8,128)(2,1)}, bf16[16,768]{1,0:T(8,128)(2,1)S(1)}, u32[]{:S(2)}, u32[]{:S(2)}) %collective-permute-start.11) | collective-permute-done | bytes 24608 | tf_op jit(solution)/shard_map/ppermute | solution.py:421
  72.9 1.0 collective-permute-done.9.refs_4_
  74.5 3.2 %collective-permute-start.21 = (bf16[64,768]{1,0:T(8,128)(2,1)S(1)}, bf16[64,768]{1,0:T(8,128)(2,1)S(1)}, u32[]{:S(2)}, u32[]{:S(2)}) collective-permute-start(bf16[64,768]{1,0:T(8,128)(2,1)S(1)} %constant_dynamic-update-slice_fusion.refs_9_.refs_10_), channel_id=1, source_target_pairs={{0,16},{4,20},{8,24},{12,28},{16,0},{20,4},{24,8},{28,12},{32,48},... | collective-permute-start | bytes 294920 | tf_op jit(solution)/shard_map/ppermute | solution.py:410
  77.7 0.9 collective-permute-start.17
  78.6 2.5 %collective-permute-done.21.refs_11_ = bf16[64,768]{1,0:T(8,128)(2,1)S(1)} collective-permute-done((bf16[64,768]{1,0:T(8,128)(2,1)S(1)}, bf16[64,768]{1,0:T(8,128)(2,1)S(1)}, u32[]{:S(2)}, u32[]{:S(2)}) %collective-permute-start.21) | collective-permute-done | bytes 98336 | tf_op jit(solution)/shard_map/ppermute | solution.py:410
  82.7 9.9 %weight_grad.1 = bf16[16,368,128]{2,1,0:T(8,128)(2,1)} custom-call(s32[3]{0:T(128)} %pad_add_fusion.me_ref.ids_ref, bf16[4,4,96,128]{3,2,1,0:T(8,128)(2,1)} %get-tuple-element.56.refs_0_, bf16[4,4,96,128]{3,2,1,0:T(8,128)(2,1)} %copy-done.17, bf16[4,4,96,128]{3,2,1,0:T(8,128)(2,1)} %copy-done.15, bf16[4,4,96,128]{3,2,1,0:T(8,128)(2,1)} %copy-done.19, ...), custom_call_target="tpu_custom_call" | custom-call | flops 4000000000 | bytes 10485760 | tf_op jit(solution)/shard_map/weight_grad/pallas_call | solution.py:302
  92.6 7.1 %all-to-all-start.1 = ((bf16[16,368,128]{2,1,0:T(8,128)(2,1)}), bf16[16,368,128]{2,1,0:T(8,128)(2,1)S(1)}, u32[]{:S(2)}, u32[]{:S(2)}) async-start(bf16[16,368,128]{2,1,0:T(8,128)(2,1)} %weight_grad.1), calls=%async_computation.1 | async-start | bytes 3014656 | tf_op jit(solution)/shard_map/all_to_all | solution.py:468
  100.4 1.2 collective-permute-done.16.refs_5_
  102.4 0.8 copy-done.24
  103.2 12.2 %trunk_grad.1 = (bf16[4,256,384]{2,1,0:T(8,128)(2,1)}, bf16[4,2,96,512]{3,2,1,0:T(8,128)(2,1)}) custom-call(s32[3]{0:T(128)} %pad_add_fusion.me_ref.ids_ref, bf16[4,4,96,128]{3,2,1,0:T(8,128)(2,1)} %get-tuple-element.56.refs_0_, bf16[4,4,96,128]{3,2,1,0:T(8,128)(2,1)} %copy-done.17, bf16[4,4,96,128]{3,2,1,0:T(8,128)(2,1)} %copy-done.15, ...), custom_call_target="tpu_custom_call" | custom-call | flops 8000000000 | bytes 16777216 | tf_op jit(solution)/shard_map/trunk_grad/pallas_call | solution.py:366
  115.3 8.2 %all-to-all-done.1.i = bf16[16,368,128]{2,1,0:T(8,128)(2,1)S(1)} async-done(((bf16[16,368,128]{2,1,0:T(8,128)(2,1)}), bf16[16,368,128]{2,1,0:T(8,128)(2,1)S(1)}, u32[]{:S(2)}, u32[]{:S(2)}) %all-to-all-start.1) | async-done | bytes 1507360 | tf_op jit(solution)/shard_map/all_to_all | solution.py:468
  123.6 1.2 copy-done
  124.7 2.3 %sum_weights.1 = f32[5,24,384]{2,1,0:T(8,128)} custom-call(bf16[16,368,128]{2,1,0:T(8,128)(2,1)} %copy-done), custom_call_target="tpu_custom_call" | custom-call | tf_op jit(solution)/shard_map/sum_weights/pallas_call | solution.py:391
  (84 shorter events, 7.1 us)
Async XLA Ops:
  0.6 23.4 %collective-permute-start.4 = (bf16[4,256,384]{2,1,0:T(8,128)(2,1)}, bf16[4,256,384]{2,1,0:T(8,128)(2,1)S(1)}, u32[]{:S(2)}, u32[]{:S(2)}) collective-permute-start(bf16[4,256,384]{2,1,0:T(8,128)(2,1)} %own_ref.1), channel_id=1, source_target_pairs={{0,16},{4,20},{8,24},{12,28},{16,0},{20,4},{24,8},{28,12},{32,48},... | collective-permute-start | bytes 2359304 | tf_op jit(solution)/shard_map/ppermute | solution.py:410
  2.4 21.7 %collective-permute-start.3 = (bf16[192,1024]{1,0:T(8,128)(2,1)}, bf16[192,1024]{1,0:T(8,128)(2,1)S(1)}, u32[]{:S(2)}, u32[]{:S(2)}) collective-permute-start(bf16[192,1024]{1,0:T(8,128)(2,1)} %h0.1), channel_id=1, source_target_pairs={{0,66},{1,67},{2,64},{3,65},{4,70},{5,71},{6,68},{7,69},{8,74},{9,... | collective-permute-start | bytes 1179656 | tf_op jit(solution)/shard_map/ppermute | solution.py:426
  9.2 6.7 %collective-permute-start = (bf16[784,128]{1,0:T(8,128)(2,1)}, bf16[784,128]{1,0:T(8,128)(2,1)S(1)}, u32[]{:S(2)}, u32[]{:S(2)}) collective-permute-start(bf16[784,128]{1,0:T(8,128)(2,1)} %get-tuple-element.38), channel_id=1, source_target_pairs={{0,1},{1,0},{2,3},{3,2},{4,5},{5,4},{6,7},{7,6},{8,9},{9,8},{10,11... | collective-permute-start | bytes 602120 | tf_op jit(solution)/shard_map/ppermute | solution.py:402
  9.2 9.6 %collective-permute-start.1 = (bf16[784,128]{1,0:T(8,128)(2,1)}, bf16[784,128]{1,0:T(8,128)(2,1)S(1)}, u32[]{:S(2)}, u32[]{:S(2)}) collective-permute-start(bf16[784,128]{1,0:T(8,128)(2,1)} %get-tuple-element.39), channel_id=1, source_target_pairs={{0,2},{1,3},{2,0},{3,1},{4,6},{5,7},{6,4},{7,5},{8,10},{9,11},{10,... | collective-permute-start | bytes 602120 | tf_op jit(solution)/shard_map/ppermute | solution.py:402
  9.2 22.0 %copy-start.3 = (bf16[192,1024]{1,0:T(8,128)(2,1)S(1)}, bf16[192,1024]{1,0:T(8,128)(2,1)}, u32[]{:S(2)}) copy-start(bf16[192,1024]{1,0:T(8,128)(2,1)} %h0.1) | copy-start | bytes 1179652
  9.2 22.5 %copy-start.11 = (s32[1024]{0:T(1024)S(1)}, s32[1024]{0:T(1024)}, u32[]{:S(2)}) copy-start(s32[1024]{0:T(1024)} %param.17) | copy-start | bytes 12292
  9.2 22.5 %copy-start.13 = (f32[7]{0:T(128)S(1)}, f32[7]{0:T(128)}, u32[]{:S(2)}) copy-start(f32[7]{0:T(128)} %param.16) | copy-start | bytes 88
  9.2 22.6 %copy-start.12 = (f32[1024]{0:T(1024)S(1)}, f32[1024]{0:T(1024)}, u32[]{:S(2)}) copy-start(f32[1024]{0:T(1024)} %param.15) | copy-start | bytes 12292
  9.2 13.1 %collective-permute-start.2 = (bf16[784,128]{1,0:T(8,128)(2,1)}, bf16[784,128]{1,0:T(8,128)(2,1)S(1)}, u32[]{:S(2)}, u32[]{:S(2)}) collective-permute-start(bf16[784,128]{1,0:T(8,128)(2,1)} %get-tuple-element.40), channel_id=1, source_target_pairs={{0,3},{1,2},{2,1},{3,0},{4,7},{5,6},{6,5},{7,4},{8,11},{9,10},{10,... | collective-permute-start | bytes 602120 | tf_op jit(solution)/shard_map/ppermute | solution.py:402
  15.8 8.2 %copy-start.7 = (bf16[784,128]{1,0:T(8,128)(2,1)}, bf16[784,128]{1,0:T(8,128)(2,1)S(1)}, u32[]{:S(2)}) copy-start(bf16[784,128]{1,0:T(8,128)(2,1)S(1)} %collective-permute-done.p1) | copy-start | bytes 602116
  24.1 13.3 %copy-start.4 = (bf16[192,1024]{1,0:T(8,128)(2,1)}, bf16[192,1024]{1,0:T(8,128)(2,1)S(1)}, u32[]{:S(2)}) copy-start(bf16[192,1024]{1,0:T(8,128)(2,1)S(1)} %collective-permute-done.3.h2) | copy-start | bytes 1179652
  24.1 23.2 %all-to-all-start = ((bf16[32,4,32,128]{3,2,1,0:T(8,128)(2,1)}), bf16[32,4,32,128]{3,2,1,0:T(8,128)(2,1)S(1)}, u32[]{:S(2)}, u32[]{:S(2)}) async-start(bf16[32,4,32,128]{3,2,1,0:T(8,128)(2,1)} %cut_cot.1), calls=%async_computation | async-start | bytes 2097152 | tf_op jit(solution)/shard_map/all_to_all | solution.py:442
  31.1 5.2 %collective-permute-start.5 = (bf16[192,1024]{1,0:T(8,128)(2,1)S(1)}, bf16[192,1024]{1,0:T(8,128)(2,1)S(1)}, u32[]{:S(2)}, u32[]{:S(2)}) collective-permute-start(bf16[192,1024]{1,0:T(8,128)(2,1)S(1)} %copy-done.3), channel_id=1, source_target_pairs={{0,1},{1,0},{2,3},{3,2},{4,5},{5,4},{6,7},{7,6},{8,9},{9,8},{10,11... | collective-permute-start | bytes 1179656 | tf_op jit(solution)/shard_map/ppermute | solution.py:402
  31.2 5.1 %collective-permute-start.6 = (bf16[192,1024]{1,0:T(8,128)(2,1)S(1)}, bf16[192,1024]{1,0:T(8,128)(2,1)S(1)}, u32[]{:S(2)}, u32[]{:S(2)}) collective-permute-start(bf16[192,1024]{1,0:T(8,128)(2,1)S(1)} %collective-permute-done.3.h2), channel_id=1, source_target_pairs={{0,1},{1,0},{2,3},{3,2},{4,5},{5,4},{6,7},{7,6},{8,9},{9,8},{10,11... | collective-permute-start | bytes 1179656 | tf_op jit(solution)/shard_map/ppermute | solution.py:402
  54.1 18.8 %collective-permute-start.8 = (bf16[4,4,96,128]{3,2,1,0:T(8,128)(2,1)}, bf16[4,4,96,128]{3,2,1,0:T(8,128)(2,1)S(1)}, u32[]{:S(2)}, u32[]{:S(2)}) collective-permute-start(bf16[4,4,96,128]{3,2,1,0:T(8,128)(2,1)} %get-tuple-element.56.refs_0_), channel_id=1, source_target_pairs={{0,2},{1,3},{2,0},{3,1},{4,6},{5,7},{6,4},{7,5},{8,10},{9,11},{10,... | collective-permute-start | bytes 1179656 | tf_op jit(solution)/shard_map/ppermute | solution.py:402
  57.5 15.4 %collective-permute-start.10 = (bf16[4,4,96,128]{3,2,1,0:T(8,128)(2,1)}, bf16[4,4,96,128]{3,2,1,0:T(8,128)(2,1)S(1)}, u32[]{:S(2)}, u32[]{:S(2)}) collective-permute-start(bf16[4,4,96,128]{3,2,1,0:T(8,128)(2,1)} %get-tuple-element.60.refs_4_), channel_id=1, source_target_pairs={{0,18},{1,19},{2,16},{3,17},{4,22},{5,23},{6,20},{7,21},{8,26},{9,... | collective-permute-start | bytes 1179656 | tf_op jit(solution)/shard_map/ppermute | solution.py:415
  57.6 16.3 %collective-permute-start.9 = (bf16[4,4,96,128]{3,2,1,0:T(8,128)(2,1)}, bf16[4,4,96,128]{3,2,1,0:T(8,128)(2,1)S(1)}, u32[]{:S(2)}, u32[]{:S(2)}) collective-permute-start(bf16[4,4,96,128]{3,2,1,0:T(8,128)(2,1)} %get-tuple-element.60.refs_4_), channel_id=1, source_target_pairs={{0,16},{4,20},{8,24},{12,28},{16,0},{20,4},{24,8},{28,12},{32,48},... | collective-permute-start | bytes 1179656 | tf_op jit(solution)/shard_map/ppermute | solution.py:410
  59.1 1.3 %collective-permute-start.14 = (bf16[16,768]{1,0:T(8,128)(2,1)}, bf16[16,768]{1,0:T(8,128)(2,1)S(1)}, u32[]{:S(2)}, u32[]{:S(2)}) collective-permute-start(bf16[16,768]{1,0:T(8,128)(2,1)} %get-tuple-element.58), channel_id=1, source_target_pairs={{3,4},{7,8},{11,12},{15,16},{19,20},{23,24},{27,28},{31,32},{35,36... | collective-permute-start | bytes 73736 | tf_op jit(solution)/shard_map/ppermute | solution.py:421
  59.7 1.4 %collective-permute-start.13 = (bf16[16,768]{1,0:T(8,128)(2,1)}, bf16[16,768]{1,0:T(8,128)(2,1)S(1)}, u32[]{:S(2)}, u32[]{:S(2)}) collective-permute-start(bf16[16,768]{1,0:T(8,128)(2,1)} %get-tuple-element.58), channel_id=1, source_target_pairs={{3,5},{7,9},{11,13},{15,17},{19,21},{23,25},{27,29},{31,33},{35,37... | collective-permute-start | bytes 73736 | tf_op jit(solution)/shard_map/ppermute | solution.py:421
  60.4 2.0 %collective-permute-start.12 = (bf16[16,768]{1,0:T(8,128)(2,1)}, bf16[16,768]{1,0:T(8,128)(2,1)S(1)}, u32[]{:S(2)}, u32[]{:S(2)}) collective-permute-start(bf16[16,768]{1,0:T(8,128)(2,1)} %get-tuple-element.58), channel_id=1, source_target_pairs={{3,6},{7,10},{11,14},{15,18},{19,22},{23,26},{27,30},{31,34},{35,3... | collective-permute-start | bytes 73736 | tf_op jit(solution)/shard_map/ppermute | solution.py:421
  61.1 11.8 %collective-permute-start.11 = (bf16[16,768]{1,0:T(8,128)(2,1)}, bf16[16,768]{1,0:T(8,128)(2,1)S(1)}, u32[]{:S(2)}, u32[]{:S(2)}) collective-permute-start(bf16[16,768]{1,0:T(8,128)(2,1)} %get-tuple-element.58), channel_id=1, source_target_pairs={{3,7},{7,11},{11,15},{15,19},{19,23},{23,27},{27,31},{31,35},{35,3... | collective-permute-start | bytes 73736 | tf_op jit(solution)/shard_map/ppermute | solution.py:421
  62.4 15.3 %collective-permute-start.7 = (bf16[4,4,96,128]{3,2,1,0:T(8,128)(2,1)}, bf16[4,4,96,128]{3,2,1,0:T(8,128)(2,1)S(1)}, u32[]{:S(2)}, u32[]{:S(2)}) collective-permute-start(bf16[4,4,96,128]{3,2,1,0:T(8,128)(2,1)} %get-tuple-element.56.refs_0_), channel_id=1, source_target_pairs={{0,1},{1,0},{2,3},{3,2},{4,5},{5,4},{6,7},{7,6},{8,9},{9,8},{10,11... | collective-permute-start | bytes 1179656 | tf_op jit(solution)/shard_map/ppermute | solution.py:402
  72.9 8.2 %copy-start.15 = (bf16[4,4,96,128]{3,2,1,0:T(8,128)(2,1)}, bf16[4,4,96,128]{3,2,1,0:T(8,128)(2,1)S(1)}, u32[]{:S(2)}) copy-start(bf16[4,4,96,128]{3,2,1,0:T(8,128)(2,1)S(1)} %collective-permute-done.8.refs_2_) | copy-start | bytes 1179652
  72.9 8.3 %copy-start.16 = (bf16[4,4,96,128]{3,2,1,0:T(8,128)(2,1)}, bf16[4,4,96,128]{3,2,1,0:T(8,128)(2,1)S(1)}, u32[]{:S(2)}) copy-start(bf16[4,4,96,128]{3,2,1,0:T(8,128)(2,1)S(1)} %collective-permute-done.10.refs_6_) | copy-start | bytes 1179652
  73.9 7.2 %collective-permute-start.19 = (bf16[4,4,96,128]{3,2,1,0:T(8,128)(2,1)S(1)}, bf16[4,4,96,128]{3,2,1,0:T(8,128)(2,1)S(1)}, u32[]{:S(2)}, u32[]{:S(2)}) collective-permute-start(bf16[4,4,96,128]{3,2,1,0:T(8,128)(2,1)S(1)} %collective-permute-done.9.refs_4_), channel_id=1, source_target_pairs={{0,1},{1,0},{2,3},{3,2},{4,5},{5,4},{6,7},{7,6},{8,9},{9,8},{10,11... | collective-permute-start | bytes 1179656 | tf_op jit(solution)/shard_map/ppermute | solution.py:402
  73.9 7.2 %collective-permute-start.20 = (bf16[4,4,96,128]{3,2,1,0:T(8,128)(2,1)S(1)}, bf16[4,4,96,128]{3,2,1,0:T(8,128)(2,1)S(1)}, u32[]{:S(2)}, u32[]{:S(2)}) collective-permute-start(bf16[4,4,96,128]{3,2,1,0:T(8,128)(2,1)S(1)} %collective-permute-done.10.refs_6_), channel_id=1, source_target_pairs={{0,1},{1,0},{2,3},{3,2},{4,5},{5,4},{6,7},{7,6},{8,9},{9,8},{10,11... | collective-permute-start | bytes 1179656 | tf_op jit(solution)/shard_map/ppermute | solution.py:402
  74.4 6.7 %collective-permute-start.15 = (bf16[4,4,96,128]{3,2,1,0:T(8,128)(2,1)S(1)}, bf16[4,4,96,128]{3,2,1,0:T(8,128)(2,1)S(1)}, u32[]{:S(2)}, u32[]{:S(2)}) collective-permute-start(bf16[4,4,96,128]{3,2,1,0:T(8,128)(2,1)S(1)} %collective-permute-done.8.refs_2_), channel_id=1, source_target_pairs={{0,1},{1,0},{2,3},{3,2},{4,5},{5,4},{6,7},{7,6},{8,9},{9,8},{10,11... | collective-permute-start | bytes 1179656 | tf_op jit(solution)/shard_map/ppermute | solution.py:402
  74.5 6.6 %collective-permute-start.21 = (bf16[64,768]{1,0:T(8,128)(2,1)S(1)}, bf16[64,768]{1,0:T(8,128)(2,1)S(1)}, u32[]{:S(2)}, u32[]{:S(2)}) collective-permute-start(bf16[64,768]{1,0:T(8,128)(2,1)S(1)} %constant_dynamic-update-slice_fusion.refs_9_.refs_10_), channel_id=1, source_target_pairs={{0,16},{4,20},{8,24},{12,28},{16,0},{20,4},{24,8},{28,12},{32,48},... | collective-permute-start | bytes 294920 | tf_op jit(solution)/shard_map/ppermute | solution.py:410
  77.7 22.2 %collective-permute-start.17 = (bf16[4,4,96,128]{3,2,1,0:T(8,128)(2,1)}, bf16[4,4,96,128]{3,2,1,0:T(8,128)(2,1)S(1)}, u32[]{:S(2)}, u32[]{:S(2)}) collective-permute-start(bf16[4,4,96,128]{3,2,1,0:T(8,128)(2,1)} %get-tuple-element.60.refs_4_), channel_id=1, source_target_pairs={{0,2},{1,3},{2,0},{3,1},{4,6},{5,7},{6,4},{7,5},{8,10},{9,11},{10,... | collective-permute-start | bytes 1179656 | tf_op jit(solution)/shard_map/ppermute | solution.py:402
  92.6 30.9 %all-to-all-start.1 = ((bf16[16,368,128]{2,1,0:T(8,128)(2,1)}), bf16[16,368,128]{2,1,0:T(8,128)(2,1)S(1)}, u32[]{:S(2)}, u32[]{:S(2)}) async-start(bf16[16,368,128]{2,1,0:T(8,128)(2,1)} %weight_grad.1), calls=%async_computation.1 | async-start | bytes 3014656 | tf_op jit(solution)/shard_map/all_to_all | solution.py:468
  99.8 1.8 %collective-permute-start.16 = (bf16[4,4,96,128]{3,2,1,0:T(8,128)(2,1)S(1)}, bf16[4,4,96,128]{3,2,1,0:T(8,128)(2,1)S(1)}, u32[]{:S(2)}, u32[]{:S(2)}) collective-permute-start(bf16[4,4,96,128]{3,2,1,0:T(8,128)(2,1)S(1)} %copy-done.14), channel_id=1, source_target_pairs={{0,1},{1,0},{2,3},{3,2},{4,5},{5,4},{6,7},{7,6},{8,9},{9,8},{10,11... | collective-permute-start | bytes 1179656 | tf_op jit(solution)/shard_map/ppermute | solution.py:402
  99.9 2.3 %collective-permute-start.18 = (bf16[4,4,96,128]{3,2,1,0:T(8,128)(2,1)S(1)}, bf16[4,4,96,128]{3,2,1,0:T(8,128)(2,1)S(1)}, u32[]{:S(2)}, u32[]{:S(2)}) collective-permute-start(bf16[4,4,96,128]{3,2,1,0:T(8,128)(2,1)S(1)} %collective-permute-done.17.refs_6_), channel_id=1, source_target_pairs={{0,1},{1,0},{2,3},{3,2},{4,5},{5,4},{6,7},{7,6},{8,9},{9,8},{10,11... | collective-permute-start | bytes 1179656 | tf_op jit(solution)/shard_map/ppermute | solution.py:402
  (18 other events, 50.5 us)

commit v4 on v3

v4 whole, which is shorter than its diff:
```python
import math

import jax
import jax.numpy as jnp
from jax import lax
from jax.experimental import pallas as pl
from jax.experimental.pallas import tpu as pltpu
from jax.sharding import PartitionSpec as P

BATCH = 4
C_OUT = 768
TRACKS = 1024
KERNEL = 5
SEQ = 32
CHAN = 4
LANES = 128
epsilon = 1e-06

BF = jnp.bfloat16
F32 = jnp.float32
MIB = 1024 * 1024


def params(limit=62 * MIB):
    return pltpu.CompilerParams(vmem_limit_bytes=limit)


def dot(a, b, contract):
    return lax.dot_general(a, b, ((contract[:1], contract[1:]), ((), ())), preferred_element_type=F32)


ANY = pl.BlockSpec(memory_space=pl.ANY)
VM = pl.BlockSpec(memory_space=pltpu.VMEM)
HBM = pl.BlockSpec(memory_space=pltpu.HBM)
SM = pl.BlockSpec(memory_space=pltpu.SMEM)


PIECE = BATCH * 192 + 16


def pieces_kernel(ids_ref, merged_ref, gain_ref, p0, p1, p2, p3, line, sems, line_sem):
    me = ids_ref[0]
    load = pltpu.make_async_copy(gain_ref, line, line_sem)
    load.start()
    copies = []
    for r, piece in enumerate((p0, p1, p2, p3)):
        lanes = pl.ds(pl.multiple_of((me ^ r) * LANES, LANES), LANES)
        for b in range(BATCH):
            rows = pl.ds(b * 192, 192)
            copies.append(pltpu.make_async_copy(merged_ref.at[b, :, lanes], piece.at[rows, :], sems.at[r, b]))
    for copy in copies:
        copy.start()
    load.wait()
    tail = jnp.concatenate([line[:, LANES:], jnp.zeros((1, 2 * LANES - 192), F32)], axis=1)
    rest = jnp.concatenate([line[:, :LANES], tail], axis=0)
    rows = []
    for _ in range(3):
        part = rest.astype(BF).astype(F32)
        rows.append(part)
        rest = rest - part
    gains = jnp.concatenate(rows + [jnp.zeros((10, LANES), F32)], axis=0).astype(BF)
    for piece in (p0, p1, p2, p3):
        piece[BATCH * 192 :, :] = gains
    for copy in copies:
        copy.wait()


def cut_pieces(ids, merged, gain):
    return pl.pallas_call(
        pieces_kernel,
        out_shape=(jax.ShapeDtypeStruct((PIECE, LANES), BF),) * CHAN,
        in_specs=[SM, HBM, HBM],
        out_specs=(VM,) * CHAN,
        scratch_shapes=[pltpu.VMEM((1, 192), F32), pltpu.SemaphoreType.DMA((CHAN, BATCH)), pltpu.SemaphoreType.DMA],
        compiler_params=params(),
        name="cut_pieces",
    )(ids, merged, gain)


COT_ROWS = 9 * 16


def cot_kernel(ids_ref, cot_ref, trunk_ref, send_ref, edges, sems, edge_sems):
    me, place = ids_ref[0], ids_ref[3]
    copies = []
    for d in range(SEQ):
        start = pl.multiple_of(d * CHAN * LANES + me * LANES, LANES)
        copies.append(
            pltpu.make_async_copy(cot_ref.at[:, :, pl.ds(start, LANES)], send_ref.at[d, pl.ds(0, 8)], sems.at[d])
        )
    loads = [
        pltpu.make_async_copy(trunk_ref.at[:, pl.ds(row, 16), :], edges.at[i], edge_sems.at[i])
        for i, row in enumerate((0, 240))
    ]
    for copy in loads + copies:
        copy.start()
    for load in loads:
        load.wait()
    rows = []
    for i, row in enumerate((0, 15)):
        parts = []
        for b in range(BATCH):
            line = edges[i, b].astype(F32)[row : row + 1]
            parts += [line[:, l * LANES : (l + 1) * LANES] for l in range(3)]
        rows.append(jnp.concatenate(parts + [jnp.zeros((4, LANES), F32)], axis=0))
    for d in range(SEQ):
        up = ((place + 1 == d) | (place + 1 == (d ^ 4))).astype(F32)
        down = ((place - 1 == d) | (place - 1 == (d ^ 4))).astype(F32)
        send_ref[d, 8] = (rows[1] * up + rows[0] * down).astype(BF)
    for copy in copies:
        copy.wait()


def cut_cot(ids, cot, trunk):
    return pl.pallas_call(
        cot_kernel,
        out_shape=jax.ShapeDtypeStruct((SEQ, 9, 16, LANES), BF),
        in_specs=[SM, HBM, HBM],
        out_specs=VM,
        scratch_shapes=[pltpu.VMEM((2, BATCH, 16, 384), BF), pltpu.SemaphoreType.DMA((SEQ,)),
                        pltpu.SemaphoreType.DMA((2,))],
        compiler_params=params(),
        cost_estimate=pl.CostEstimate(flops=0, bytes_accessed=5 * 2**20, transcendentals=0),
        name="cut_cot",
    )(ids, cot.reshape(BATCH * 2, 16, -1), trunk)


def score_kernel(*refs):
    pieces, heads, (bias_ref, of_track_ref, scale_ref) = refs[:4], refs[4:8], refs[8:11]
    raw_ref, inv_ref, weights_ref, merged_ref, gain_ref, cols_ref, parts, sems, head_sems, part_sems = refs[11:]
    copies = []
    for r in range(CHAN):
        rows = pl.ds(r * 192, 192)
        for b in range(BATCH):
            copies.append(
                pltpu.make_async_copy(
                    pieces[r].at[pl.ds(b * 192, 192), :],
                    merged_ref.at[rows, pl.ds(b * LANES, LANES)],
                    sems.at[r, b],
                )
            )
        copies.append(
            pltpu.make_async_copy(pieces[r].at[pl.ds(BATCH * 192, 16), :], parts.at[r], part_sems.at[r])
        )
    loads = [
        pltpu.make_async_copy(heads[r], weights_ref.at[pl.ds(r * 192, 192), :], head_sems.at[r])
        for r in range(CHAN)
    ]
    for copy in copies + loads:
        copy.start()
    track_scale = jnp.zeros((1, TRACKS), F32)
    for h in range(scale_ref.shape[0]):
        track_scale = jnp.where(of_track_ref[...] == h, scale_ref[h], track_scale)
    lines = []
    for rest in (bias_ref[...], track_scale):
        for _ in range(3):
            part = rest.astype(BF).astype(F32)
            lines.append(part)
            rest = rest - part
    lines = jnp.concatenate(lines + [jnp.zeros((10, TRACKS), F32)], axis=0).astype(BF)
    row = lax.broadcasted_iota(jnp.int32, (16, LANES), 0)
    lane = lax.broadcasted_iota(jnp.int32, (16, LANES), 1)
    cols_ref[...] = dot(lines, ((row < 6) & (row // 3 == lane)).astype(BF), (0, 0))
    for copy in copies:
        copy.wait()
    for r in range(CHAN):
        for side in range(2):
            pick = ((row < 6) & (row % 2 == side)).astype(BF)
            size = LANES - side * 64
            start = r * 192 + side * LANES
            gain_ref[start : start + size, :] = dot(parts[r], pick, (0, 0))[:size]
    m32 = merged_ref[...].astype(F32)
    total = jnp.sum(m32 * m32, axis=0, keepdims=True)
    inv_ref[...] = jnp.broadcast_to(lax.rsqrt(total / C_OUT + epsilon), inv_ref.shape)
    normed = (m32 * gain_ref[:, 0:1]).astype(BF)
    for load in loads:
        load.wait()
    raw_ref[...] = dot(weights_ref[...], normed, (0, 0))


def scores(pieces, heads, bias, of_track, scale):
    return pl.pallas_call(
        score_kernel,
        out_shape=(jax.ShapeDtypeStruct((TRACKS, BATCH * LANES), F32),
                   jax.ShapeDtypeStruct((8, BATCH * LANES), F32),
                   jax.ShapeDtypeStruct((C_OUT, TRACKS), BF),
                   jax.ShapeDtypeStruct((C_OUT, BATCH * LANES), BF),
                   jax.ShapeDtypeStruct((C_OUT, LANES), F32),
                   jax.ShapeDtypeStruct((TRACKS, LANES), F32)),
        in_specs=[HBM] * 8 + [VM, VM, SM],
        out_specs=(VM,) * 6,
        scratch_shapes=[pltpu.VMEM((CHAN, 16, LANES), BF), pltpu.SemaphoreType.DMA((CHAN, BATCH)),
                        pltpu.SemaphoreType.DMA((CHAN,)), pltpu.SemaphoreType.DMA((CHAN,))],
        compiler_params=params(),
        cost_estimate=pl.CostEstimate(flops=45 * 10**8, bytes_accessed=8 * 2**20, transcendentals=0),
        name="scores",
    )(*pieces, *heads, bias, of_track, scale)


def head_kernel(
    ids_ref, valid_ref, raw_hbm, inv_ref, weights_hbm, merged_hbm, gain_ref, cols_ref, cot_ref,
    mine_ref, other_ref, edge_ref, full, raw_ref, weights_ref, merged_ref, sems
):
    loads = []
    for b in range(BATCH):
        loads.append(
            pltpu.make_async_copy(raw_hbm.at[:, pl.ds(b * LANES, LANES)], raw_ref.at[b], sems.at[0, b])
        )
    load_weights = pltpu.make_async_copy(weights_hbm, weights_ref, sems.at[1, 0])
    load_merged = pltpu.make_async_copy(merged_hbm, merged_ref, sems.at[1, 1])
    for copy in loads:
        copy.start()
    load_weights.start()
    load_merged.start()
    me = ids_ref[0]
    first = ids_ref[1]
    half = ids_ref[2]
    scale = cols_ref[:, 1:2]
    bias = cols_ref[:, 0:1]
    lane = lax.broadcasted_iota(jnp.int32, (1, LANES), 1)
    scaled, coefs = [], []
    for b in range(BATCH):
        cols = slice(b * LANES, (b + 1) * LANES)
        loads[b].wait()
        raw = raw_ref[b]
        inv = inv_ref[0:1, cols]
        live = (first + lane < valid_ref[b]).astype(F32)
        gate = 0.5 * jnp.tanh(0.5 * (inv * raw + bias)) + 0.5
        cot = cot_ref[:, b * 32 : (b + 1) * 32, :].reshape(TRACKS, LANES).astype(F32)
        d_logits = (cot * scale) * gate
        d_rms = live * jnp.sum(d_logits * raw, axis=0, keepdims=True)
        scaled.append(((inv * live) * d_logits).astype(BF))
        coefs.append(inv * inv * inv * d_rms * (1.0 / C_OUT))
    load_weights.wait()
    load_merged.wait()
    d = dot(weights_ref[...], jnp.concatenate(scaled, axis=1), (1, 0)) * gain_ref[:, 0:1]
    for r in range(CHAN):
        rows = slice(r * 192, (r + 1) * 192)
        for b in range(BATCH):
            cols = slice(b * LANES, (b + 1) * LANES)
            full[b, me ^ r] = d[rows, cols] - coefs[b] * merged_ref[rows, cols].astype(F32)
    for b in range(BATCH):
        for g in range(CHAN):
            mine_ref[b, g] = full[b, g, pl.ds(pl.multiple_of(96 * half, 32), 96), :].astype(BF)
            other_ref[b, g] = full[b, g, pl.ds(pl.multiple_of(96 * (1 - half), 32), 96), :].astype(BF)
    start = jnp.where(me == CHAN - 1, LANES - 2, 0)
    row = lax.broadcasted_iota(jnp.int32, (16, LANES), 0)
    col = lax.broadcasted_iota(jnp.int32, (16, LANES), 1) - start
    edge = jnp.zeros((16, C_OUT), F32)
    for b in range(BATCH):
        sel = ((col >= 0) & (col < 2) & (row == b * 2 + col)).astype(BF)
        edge = edge + dot(sel, full[b].reshape(C_OUT, LANES).astype(BF), (1, 1))
    for l in range(6):
        edge_ref[l * 16 : (l + 1) * 16, :] = edge[:, l * LANES : (l + 1) * LANES].astype(BF)


def head(ids, valid, scored, cot):
    return pl.pallas_call(
        head_kernel,
        out_shape=(jax.ShapeDtypeStruct((BATCH, CHAN, 96, LANES), BF),) * 2
        + (jax.ShapeDtypeStruct((96, LANES), BF),),
        in_specs=[SM, SM, HBM, VM, HBM, HBM, VM, VM, VM],
        out_specs=(VM,) * 3,
        scratch_shapes=[
            pltpu.VMEM((BATCH, CHAN, 192, LANES), F32),
            pltpu.VMEM((BATCH, TRACKS, LANES), F32),
            pltpu.VMEM((C_OUT, TRACKS), BF),
            pltpu.VMEM((C_OUT, BATCH * LANES), BF),
            pltpu.SemaphoreType.DMA((2, BATCH)),
        ],
        compiler_params=params(61 * MIB),
        name="head",
    )(ids, valid, *scored, cot)


PAIR = 2


def rows_kernel(ids_ref, own_ref, far_ref, got_ref, tr_ref, trx_ref, edges, trunks, sems, trunk_sems):
    place = ids_ref[3]
    copies = [
        pltpu.make_async_copy(ref, trunks.at[q], trunk_sems.at[q]) for q, ref in enumerate((own_ref, far_ref))
    ]
    for q in range(PAIR):
        for i, step in enumerate((-1, 1)):
            source = jnp.clip((place ^ (4 * q)) + step, 0, SEQ - 1)
            copies.append(
                pltpu.make_async_copy(got_ref.at[source, pl.ds(128, 16)], edges.at[q, i], sems.at[q, i])
            )
    for copy in copies:
        copy.start()
    for copy in copies:
        copy.wait()
    row = lax.broadcasted_iota(jnp.int32, (256, 384), 0)
    ends = [jnp.zeros((LANES, 384), F32) for _ in range(KERNEL)]
    at = lax.broadcasted_iota(jnp.int32, (LANES, 384), 0)
    for q in range(PAIR):
        before = edges[q, 0].astype(F32) * ((place ^ (4 * q)) > 0).astype(F32)
        after = edges[q, 1].astype(F32) * ((place ^ (4 * q)) < SEQ - 1).astype(F32)
        for b in range(BATCH):
            t = trunks[q, b].astype(F32)
            rows = slice(b * 256, (b + 1) * 256)
            tr_ref[q, rows, 0:384] = jnp.where(row == 0, 0.0, pltpu.roll(t, 1, 0)).astype(BF)
            tr_ref[q, rows, 384:768] = trunks[q, b]
            tr_ref[q, rows, 768:1152] = jnp.where(row == 255, 0.0, pltpu.roll(t, 255, 0)).astype(BF)
            base = (q * BATCH + b) * 5
            first, last = (
                jnp.concatenate([x[b * 3 + l : b * 3 + l + 1] for l in range(3)], axis=1)
                for x in (before, after)
            )
            for column, tap, x in (
                (0, 1, t[127:128]), (0, 3, t[128:129]), (1, 1, t[255:256]), (1, 3, last),
                (2, 4, last), (3, 0, first), (4, 1, first),
            ):
                ends[tap] = jnp.where(at == base + column, x, ends[tap])
    for k in range(KERNEL):
        trx_ref[:, k * 384 : (k + 1) * 384] = ends[k].astype(BF)


def trunk_rows(ids, own, far, got):
    return pl.pallas_call(
        rows_kernel,
        out_shape=(jax.ShapeDtypeStruct((PAIR, 1024, 1152), BF),
                   jax.ShapeDtypeStruct((LANES, KERNEL * 384), BF)),
        in_specs=[SM, HBM, HBM, ANY],
        out_specs=(VM, VM),
        scratch_shapes=[pltpu.VMEM((PAIR, 2, 16, LANES), BF), pltpu.VMEM((PAIR, BATCH, 256, 384), BF),
                        pltpu.SemaphoreType.DMA((PAIR, 2)), pltpu.SemaphoreType.DMA((PAIR,))],
        compiler_params=params(30 * MIB),
        cost_estimate=pl.CostEstimate(flops=10**7, bytes_accessed=8 * 2**20, transcendentals=0),
        name="trunk_rows",
    )(ids, own, far, got)


ROWS = 368


def weight_kernel(ids_ref, *refs):
    pieces, (tr_ref, trx_ref, out_hbm, own_ref, full, out_ref, sems, own_sem, out_sems) = refs[:8], refs[8:]
    me = ids_ref[0]
    copies = []
    for q in range(PAIR):
        for r in range(CHAN):
            lanes = pl.ds(pl.multiple_of((me ^ r) * LANES, LANES), LANES)
            copies.append(
                pltpu.make_async_copy(pieces[q * CHAN + r], full.at[q, :, :, :, lanes], sems.at[q, r])
            )
    for copy in copies:
        copy.start()
    keep = pltpu.make_async_copy(full.at[0], own_ref, own_sem)
    p = lax.broadcasted_iota(jnp.int32, (256, 256), 0)
    q_ = lax.broadcasted_iota(jnp.int32, (256, 256), 1)
    even = (q_ < 128) & (p // 2 == q_)
    odd = (q_ >= 128) & ((p + 1) // 2 == q_ - 128)
    pick = (even | odd).astype(BF)
    last = jnp.zeros((384, LANES), F32)
    p1 = lax.broadcasted_iota(jnp.int32, (LANES, LANES), 0)
    q1 = lax.broadcasted_iota(jnp.int32, (LANES, LANES), 1)
    g_even = jnp.zeros((384, 1152), F32)
    g_odd = jnp.zeros((384, 768), F32)
    for q in range(PAIR):
        for copy in copies[q * CHAN : (q + 1) * CHAN]:
            copy.wait()
        if q == 0:
            keep.start()
        evens, odds = [], []
        for b in range(BATCH):
            for h in range(2):
                block = full[q, b, :, :, h * 256 : (h + 1) * 256].reshape(384, 256)
                e = dot(block, pick, (1, 0)).astype(BF)
                evens.append(e[:, :128])
                odds.append(e[:, 128:])
                place = q1 - (q * BATCH + b) * 5
                if h == 0:
                    sel = (((p1 < 2) & (place == 3)) | ((p1 == 0) & (place == 4))).astype(BF)
                    last = last + dot(block[:, :128], sel, (1, 0))
                    sel = (p1 == 127) & (place == 0)
                else:
                    sel = ((p1 == 127) & (place == 1)) | ((p1 >= 126) & (place == 2))
                last = last + dot(block[:, 128:], sel.astype(BF), (1, 0))
        g_even = g_even + dot(jnp.concatenate(evens, axis=1), tr_ref[q], (1, 0))
        g_odd = g_odd + dot(jnp.concatenate(odds, axis=1), tr_ref[q, :, :768], (1, 0))
    last = last.astype(BF)
    side = [dot(last, trx_ref[:, k * 384 : (k + 1) * 384], (1, 0)) for k in range(KERNEL)]
    pad = jnp.zeros((ROWS - 360, LANES), F32)
    taps = (g_even[:, :384], g_odd[:, :384], g_even[:, 384:768], g_odd[:, 384:], g_even[:, 768:])
    taps = [tap + term for tap, term in zip(taps, side)]
    stores = []
    for s in range(16):
        blocks = []
        for l in range(3):
            for tap in taps:
                blocks.append(tap[s * 24 : (s + 1) * 24, l * LANES : (l + 1) * LANES])
        out_ref[s] = jnp.concatenate(blocks + [pad], axis=0).astype(BF)
        if s % 4 == 3:
            part = pl.ds(s - 3, 4)
            stores.append(pltpu.make_async_copy(out_ref.at[part], out_hbm.at[part], out_sems.at[s // 4]))
            stores[-1].start()
    for store in stores:
        store.wait()
    keep.wait()


def weight_grad(ids, pieces, tr, trx):
    return pl.pallas_call(
        weight_kernel,
        out_shape=(jax.ShapeDtypeStruct((16, ROWS, LANES), BF),
                   jax.ShapeDtypeStruct((BATCH, CHAN, 96, 512), BF)),
        in_specs=[SM] + [ANY] * 8 + [VM] * 2,
        out_specs=(HBM, HBM),
        scratch_shapes=[pltpu.VMEM((PAIR, BATCH, CHAN, 96, 512), BF), pltpu.VMEM((16, ROWS, LANES), BF),
                        pltpu.SemaphoreType.DMA((PAIR, CHAN)), pltpu.SemaphoreType.DMA,
                        pltpu.SemaphoreType.DMA((4,))],
        compiler_params=params(30 * MIB),
        cost_estimate=pl.CostEstimate(flops=4 * 10**9, bytes_accessed=10 * 2**20, transcendentals=0),
        name="weight_grad",
    )(ids, *pieces, tr, trx)


def trunk_kernel(ids_ref, *refs):
    mine, other = refs[0], refs[1:5]
    conv_hbm, out_ref, skip_ref, full, sums, rims, conv_ref, sems, other_sems, skip_sem, conv_sem = refs[5:]
    me = ids_ref[0]
    half = ids_ref[2]
    skip = pltpu.make_async_copy(full.at[:, me], skip_ref, skip_sem)
    copies = [pltpu.make_async_copy(mine, full.at[:, :, half], sems.at[0, 0])]
    for r in range(CHAN):
        lanes = pl.ds(pl.multiple_of((me ^ r) * LANES, LANES), LANES)
        copies.append(pltpu.make_async_copy(other[r].at[BATCH * CHAN], rims.at[r], sems.at[1, r]))
        for b in range(BATCH):
            copies.append(
                pltpu.make_async_copy(
                    other[r].at[pl.ds(b * CHAN, CHAN)], full.at[b, :, 1 - half, :, lanes], other_sems.at[r, b]
                )
            )
    load = pltpu.make_async_copy(conv_hbm, conv_ref, conv_sem)
    for copy in copies + [load]:
        copy.start()
    row = lax.broadcasted_iota(jnp.int32, (2 * EXT, 512), 0)
    p = lax.broadcasted_iota(jnp.int32, (2 * EXT, 512), 1)
    lo = jnp.where(row < EXT, 2 * (row - 8), 2 * (row - EXT - 8) - 1)
    pick = ((p == lo) | (p == lo + 1)).astype(BF)
    col = lax.broadcasted_iota(jnp.int32, (2 * EXT, 32), 1)
    lo = lo[:, :32]
    for copy in copies:
        copy.wait()
    skip.start()
    rim = jnp.concatenate(
        [jnp.concatenate([rims[x, l * 16 : (l + 1) * 16, :] for l in range(6)], axis=1) for x in (me, me ^ 3)],
        axis=0,
    )
    for b in range(BATCH):
        offset = col % 16 - 2 * b
        rim_ok = (offset >= 0) & (offset < 2)
        rim_pos = jnp.where(col < 16, offset - 2, 512 + offset)
        pick_r = (rim_ok & ((rim_pos == lo) | (rim_pos == lo + 1))).astype(BF)
        e = (dot(pick, full[b].reshape(C_OUT, 512), (1, 1)) + dot(pick_r, rim, (1, 0))).astype(BF)
        sums[pl.ds(b * EXT, EXT), :C_OUT] = e[:EXT]
        sums[pl.ds(b * EXT, EXT), C_OUT:] = e[EXT:]
    load.wait()
    even, odd = sums[:, :C_OUT], sums[:, C_OUT:]
    up = dot(even, conv_ref[0], (1, 1)) + dot(odd, conv_ref[1], (1, 1))
    here = dot(even, conv_ref[2], (1, 1)) + dot(odd, conv_ref[3], (1, 1))
    down = dot(even, conv_ref[4], (1, 1))
    for b in range(BATCH):
        o = b * EXT + 8
        total = up[o + 1 : o + 257] + here[o : o + 256] + down[o - 1 : o + 255]
        out_ref[b] = total.astype(BF)
    skip.wait()


EXT = 272


def trunk_grad(ids, mine, other, conv_w):
    return pl.pallas_call(
        trunk_kernel,
        out_shape=(jax.ShapeDtypeStruct((BATCH, 256, 384), BF), jax.ShapeDtypeStruct((BATCH, 2, 96, 512), BF)),
        in_specs=[SM] + [HBM] * 6,
        out_specs=(VM, HBM),
        scratch_shapes=[pltpu.VMEM((BATCH, CHAN, 2, 96, 512), BF), pltpu.VMEM((BATCH * EXT, 2 * C_OUT), BF),
                        pltpu.VMEM((CHAN, 96, LANES), BF), pltpu.VMEM((KERNEL, 384, C_OUT), BF),
                        pltpu.SemaphoreType.DMA((2, CHAN)), pltpu.SemaphoreType.DMA((CHAN, BATCH)),
                        pltpu.SemaphoreType.DMA, pltpu.SemaphoreType.DMA],
        compiler_params=params(),
        cost_estimate=pl.CostEstimate(flops=8 * 10**9, bytes_accessed=16 * 2**20, transcendentals=0),
        name="trunk_grad",
    )(ids, mine, *other, conv_w)


def sum_kernel(scale, in_hbm, out_ref, terms, sems):
    copies = [
        pltpu.make_async_copy(in_hbm.at[pl.ds(i * 4, 4)], terms.at[pl.ds(i * 4, 4)], sems.at[i]) for i in range(4)
    ]
    for copy in copies:
        copy.start()
    total = jnp.zeros((ROWS, LANES), F32)
    for i in range(4):
        copies[i].wait()
        for s in range(i * 4, i * 4 + 4):
            total = total + terms[s].astype(F32)
    total = total * scale
    for l in range(3):
        for k in range(KERNEL):
            start = l * 120 + k * 24
            out_ref[k, :, l * LANES : (l + 1) * LANES] = total[start : start + 24]


def sum_weights(terms, scale):
    return pl.pallas_call(
        lambda *refs: sum_kernel(scale, *refs),
        out_shape=jax.ShapeDtypeStruct((KERNEL, 24, 384), F32),
        in_specs=[HBM],
        out_specs=VM,
        scratch_shapes=[pltpu.VMEM((16, ROWS, LANES), BF), pltpu.SemaphoreType.DMA((4,))],
        compiler_params=params(30 * MIB),
        name="sum_weights",
    )(terms)


def flip(x, r):
    return lax.ppermute(x, "chan", [(i, i ^ r) for i in range(CHAN)])


def partner(x):
    return lax.ppermute(x, "seq", [(i, i ^ 4) for i in range(SEQ)])


def partner_far(x):
    pairs = [(s * CHAN + c, (s ^ 4) * CHAN + (c ^ 2)) for s in range(SEQ) for c in range(CHAN)]
    return lax.ppermute(x, ("seq", "chan"), pairs)


def rim(x):
    up = [(s * CHAN + 3, (s + 1) * CHAN) for s in range(SEQ - 1)]
    down = [(s * CHAN, (s - 1) * CHAN + 3) for s in range(1, SEQ)]
    return lax.ppermute(x, ("seq", "chan"), up + down)


def across(x):
    pairs = [(s * CHAN + c, (s ^ 16) * CHAN + (c ^ 2)) for s in range(SEQ) for c in range(CHAN)]
    return lax.ppermute(x, ("seq", "chan"), pairs)


def local(
    trunk, merged, conv_w, norm_gain, head_w, head_bias, head_scale, head_of_track, valid_len, cot
):
    me = lax.axis_index("chan").astype(jnp.int32)
    place = lax.axis_index("seq").astype(jnp.int32)
    half = (place // 4) % 2
    ids = jnp.stack([me, place * 512 + me * LANES, half, place])
    trunk_far = partner(trunk)
    p0, p1, p2, p3 = cut_pieces(ids, merged, norm_gain[None])
    p1, p2, p3, cot = lax.optimization_barrier((p1, p2, p3, cot))
    send = cut_cot(ids, cot, trunk)
    p1, p2, p3 = flip(p1, 1), flip(p2, 2), flip(p3, 3)
    send, trunk, head_w = lax.optimization_barrier((send, trunk, head_w))
    far_head = across(head_w)
    near_head = flip(head_w, 1)
    send, p1, p2, p3, trunk_far = lax.optimization_barrier((send, p1, p2, p3, trunk_far))
    got = lax.all_to_all(send, "seq", 0, 0, tiled=True).reshape(SEQ, COT_ROWS, LANES)
    pieces = (p0, p1, p2, p3)
    heads = (head_w, near_head, far_head, flip(far_head, 1))

    scored = scores(pieces, heads, head_bias[None], head_of_track[None], head_scale)
    mine, other, edge = head(ids, valid_len, scored, got)
    trunk, _ = lax.optimization_barrier((trunk, mine))
    tr, trx = trunk_rows(ids, trunk, trunk_far, got)

    mine_far, other_x, other_far_x = flip(mine, 2), partner(other), partner_far(other)
    other = jnp.concatenate([other.reshape(BATCH * CHAN, 96, LANES), rim(edge)[None]])
    mine_far, other_x, other_far_x, other, tr, trx = lax.optimization_barrier(
        (mine_far, other_x, other_far_x, other, tr, trx)
    )
    mine_all = (mine, flip(mine, 1), mine_far, flip(mine_far, 1))
    blocks = mine_all + (other_x, flip(other_x, 1), other_far_x, flip(other_far_x, 1))
    terms, mine_rows = weight_grad(ids, blocks, tr, trx)
    other_late, _ = lax.optimization_barrier((other, mine_far))
    other_far = flip(other_late, 2)
    other_all = (other, flip(other, 1), other_far, flip(other_far, 1))
    groups = [[s for s in range(SEQ) if (s // 4) % 2 == u] for u in range(2)]
    summed = lax.all_to_all(terms, "seq", 0, 0, tiled=True, axis_index_groups=groups)
    d_trunk, d_skip = trunk_grad(ids, mine_rows, other_all, conv_w)
    grad_scale = 1.0 / math.sqrt(BATCH * 512 * SEQ)
    d_conv_w = sum_weights(summed, grad_scale)
    return (d_trunk, d_skip.reshape(BATCH, 192, 512), d_conv_w)


def solution(mesh):
    placed = (
        P(None, "seq", "chan"),
        P(None, "chan", "seq"),
        P(None, "chan", None),
        P("chan"),
        P("chan", None),
        P(),
        P(),
        P(),
        P(),
        P(None, "seq", None),
    )
    return jax.shard_map(
        local,
        mesh=mesh,
        in_specs=placed,
        out_specs=(P(None, "seq", "chan"), P(None, "chan", "seq"), P(None, "seq", "chan")),
        check_vma=False,
    )
```

time: 128 us -> 120 us (0.938)
  starting transfers between devices: 46.1 us -> 32.6 us
  waiting for transfers between devices: 29 us -> 36.2 us
  Pallas kernels: 44.2 us -> 41 us
    ppermute x13, starting transfers between devices: 18.1 us -> 9.04 us  [flip(): return lax.ppermute(x, 'chan', [(i, i ^ r) for i in range(CHAN)])]
    ppermute x1, waiting for transfers between devices: 0.01 us -> 5.89 us  [partner_far(): return lax.ppermute(x, ('seq', 'chan'), pairs)]
    ppermute x1, starting transfers between devices: 0.14 us -> 3.66 us  [partner_far(): return lax.ppermute(x, ('seq', 'chan'), pairs)]
    all_to_all x1, waiting for transfers between devices: 5.52 us -> 8.9 us  [local(): lax.all_to_all(send, 'seq', 0, 0, tiled=True).reshape(SEQ, COT_ROWS, LANES)]
    ppermute x3 -> x2, starting transfers between devices: 6.39 us -> 3.2 us  [partner(): return lax.ppermute(x, 'seq', [(i, i ^ 4) for i in range(SEQ)])]
    all_to_all x1, starting transfers between devices: 7.15 us -> 4.09 us  [local(): lax.all_to_all(terms, 'seq', 0, 0, tiled=True, axis_index_groups=groups)]
    pallas_call x1, Pallas kernels: 4.48 us -> 1.62 us  [trunk_rows(): pl.pallas_call(rows_kernel, out_shape=(jax.ShapeDtypeStruct((PAIR, 1024,...]
    ppermute x3 -> x2, waiting for transfers between devices: 3.46 us -> 6.2 us  [partner(): return lax.ppermute(x, 'seq', [(i, i ^ 4) for i in range(SEQ)])]
  transfers between devices with their start and end apart: 24 -> 20, of which waited for: 10 -> 10; matrix products, arithmetic and copies ran while one was open for 1% -> 1% of each run, Pallas kernels for 29% -> 28%
where the time goes in v4:
time: 120 us; the launch traced here: 118 us
  Pallas kernels  41 us (34%)
  waiting for transfers between devices  36.2 us (30%)
  starting transfers between devices  32.6 us (27%)
  local copies, waits for them, and re-layouts  6.29 us (5%)
    pallas_call x1, Pallas kernels, trunk_grad(): pl.pallas_call(trunk_kernel, out_shape=(jax.ShapeDtypeStruct((BATCH, 256,...  12.1 us
    ppermute x13, starting transfers between devices, flip(): return lax.ppermute(x, 'chan', [(i, i ^ r) for i in range(CHAN)])  9.04 us
    all_to_all x1, waiting for transfers between devices, local(): lax.all_to_all(terms, 'seq', 0, 0, tiled=True, axis_index_groups=groups)  8.99 us
    all_to_all x1, waiting for transfers between devices, local(): lax.all_to_all(send, 'seq', 0, 0, tiled=True).reshape(SEQ, COT_ROWS, LANES)  8.9 us
    all_to_all x1, starting transfers between devices, local(): lax.all_to_all(send, 'seq', 0, 0, tiled=True).reshape(SEQ, COT_ROWS, LANES)  8.53 us
    pallas_call x1, Pallas kernels, weight_grad(): pl.pallas_call(weight_kernel, out_shape=(jax.ShapeDtypeStruct((16, ROWS,...  7.92 us
    unnamed x34, local copies, waits for them, and re-layouts  6.29 us
    pallas_call x1, Pallas kernels, head(): pl.pallas_call(head_kernel, out_shape=(jax.ShapeDtypeStruct((BATCH, CHAN,...  6.2 us
  transfers between devices with their start and end apart: 20, of which 10 were waited for; matrix products, arithmetic and copies ran while one was open for 1% of the time, Pallas kernels for 28%

profile of v4, /device:TPU:0, one launch (start us, length us, event | category | flops | bytes accessed | tf_op | source)
XLA Modules:
  0.0 117.8 jit_solution(16098567710904903738)
XLA Ops:
  0.6 1.7 %collective-permute-start.3 = (bf16[4,256,384]{2,1,0:T(8,128)(2,1)}, bf16[4,256,384]{2,1,0:T(8,128)(2,1)S(1)}, u32[]{:S(2)}, u32[]{:S(2)}) collective-permute-start(bf16[4,256,384]{2,1,0:T(8,128)(2,1)} %own_ref), channel_id=1, source_target_pairs={{0,16},{4,20},{8,24},{12,28},{16,0},{20,4},{24,8},{28,12},{32,48},... | collective-permute-start | bytes 2359304 | tf_op jit(solution)/shard_map/ppermute | solution.py:526
  2.4 0.6 pad_add_fusion.ids_ref
  3.0 2.8 %cut_pieces.1 = (bf16[784,128]{1,0:T(8,128)(2,1)}, bf16[784,128]{1,0:T(8,128)(2,1)}, bf16[784,128]{1,0:T(8,128)(2,1)}, bf16[784,128]{1,0:T(8,128)(2,1)}) custom-call(s32[4]{0:T(128)} %pad_add_fusion.ids_ref, bf16[4,192,512]{2,1,0:T(8,128)(2,1)} %merged_ref.1, f32[1,192]{1,0:T(1,128)} %bitcast.17), custom_call_target="tpu_custom_call" | custom-call | tf_op jit(solution)/shard_map/cut_pieces/pallas_call | solution.py:69
  5.9 4.0 %collective-permute-start.1 = (bf16[784,128]{1,0:T(8,128)(2,1)}, bf16[784,128]{1,0:T(8,128)(2,1)S(1)}, u32[]{:S(2)}, u32[]{:S(2)}) collective-permute-start(bf16[784,128]{1,0:T(8,128)(2,1)} %get-tuple-element.49), channel_id=1, source_target_pairs={{0,2},{1,3},{2,0},{3,1},{4,6},{5,7},{6,4},{7,5},{8,10},{9,11},{10,... | collective-permute-start | bytes 602120 | tf_op jit(solution)/shard_map/ppermute | solution.py:522
  9.9 3.4 %cut_cot.1 = bf16[32,9,16,128]{3,2,1,0:T(8,128)(2,1)} custom-call(s32[4]{0:T(128)} %pad_add_fusion.ids_ref, bf16[8,16,16384]{2,1,0:T(8,128)(2,1)} %bitcast.14, bf16[4,256,384]{2,1,0:T(8,128)(2,1)} %own_ref), custom_call_target="tpu_custom_call" | custom-call | bytes 5242880 | tf_op jit(solution)/shard_map/cut_cot/pallas_call | solution.py:115
  13.3 3.5 %collective-permute-start.5 = (bf16[192,1024]{1,0:T(8,128)(2,1)}, bf16[192,1024]{1,0:T(8,128)(2,1)S(1)}, u32[]{:S(2)}, u32[]{:S(2)}) collective-permute-start(bf16[192,1024]{1,0:T(8,128)(2,1)} %refs_4_), channel_id=1, source_target_pairs={{0,66},{1,67},{2,64},{3,65},{4,70},{5,71},{6,68},{7,69},{8,74},{9,... | collective-permute-start | bytes 1179656 | tf_op jit(solution)/shard_map/ppermute | solution.py:542
  16.8 3.0 %collective-permute-done.2.refs_3_ = bf16[784,128]{1,0:T(8,128)(2,1)S(1)} collective-permute-done((bf16[784,128]{1,0:T(8,128)(2,1)}, bf16[784,128]{1,0:T(8,128)(2,1)S(1)}, u32[]{:S(2)}, u32[]{:S(2)}) %collective-permute-start.2) | collective-permute-done | bytes 200736 | tf_op jit(solution)/shard_map/ppermute | solution.py:522
  20.4 8.5 %all-to-all-start = ((bf16[32,9,16,128]{3,2,1,0:T(8,128)(2,1)}), bf16[32,9,16,128]{3,2,1,0:T(8,128)(2,1)S(1)}, u32[]{:S(2)}, u32[]{:S(2)}) async-start(bf16[32,9,16,128]{3,2,1,0:T(8,128)(2,1)} %cut_cot.1), calls=%async_computation | async-start | bytes 2359296 | tf_op jit(solution)/shard_map/all_to_all | solution.py:561
  29.1 0.7 copy-done.11
  30.3 0.7 collective-permute-done.4.refs_5_
  31.0 0.7 collective-permute-done.6.refs_7_
  31.7 0.7 copy-done.13
  32.5 5.4 %scores.1 = (f32[1024,512]{1,0:T(8,128)}, f32[8,512]{1,0:T(8,128)}, bf16[768,1024]{1,0:T(8,128)(2,1)}, bf16[768,512]{1,0:T(8,128)(2,1)}, f32[768,128]{1,0:T(8,128)}, /*index=5*/f32[1024,128]{1,0:T(8,128)}) custom-call(bf16[784,128]{1,0:T(8,128)(2,1)} %get-tuple-element.42.refs_0_, bf16[784,128]{1,0:T(8,128)(2,1)} %copy-done.14, bf16[784,128]{1,0:T(8,128)(2,1)} %copy-done.15, ...), custom_call_target="tpu_custom_call" | custom-call | flops 4499999744 | bytes 8388608 | tf_op jit(solution)/shard_map/scores/pallas_call | solution.py:182
  37.9 8.9 %all-to-all-done = bf16[32,9,16,128]{3,2,1,0:T(8,128)(2,1)S(1)} async-done(((bf16[32,9,16,128]{3,2,1,0:T(8,128)(2,1)}), bf16[32,9,16,128]{3,2,1,0:T(8,128)(2,1)S(1)}, u32[]{:S(2)}, u32[]{:S(2)}) %all-to-all-start) | async-done | bytes 1179680 | tf_op jit(solution)/shard_map/all_to_all | solution.py:561
  46.8 1.0 copy-done
  47.8 6.2 %head.1 = (bf16[4,4,96,128]{3,2,1,0:T(8,128)(2,1)}, bf16[4,4,96,128]{3,2,1,0:T(8,128)(2,1)}, bf16[96,128]{1,0:T(8,128)(2,1)}) custom-call(s32[4]{0:T(128)} %pad_add_fusion.ids_ref, s32[4]{0:T(128)} %valid_ref.1, f32[1024,512]{1,0:T(8,128)} %get-tuple-element.55.raw_hbm, f32[8,512]{1,0:T(8,128)} %get-tuple-element.56.inv_ref, ...), custom_call_target="tpu_custom_call" | custom-call | tf_op jit(solution)/shard_map/head/pallas_call | solution.py:258
  54.0 3.7 %collective-permute-start.10 = (bf16[4,4,96,128]{3,2,1,0:T(8,128)(2,1)}, bf16[4,4,96,128]{3,2,1,0:T(8,128)(2,1)S(1)}, u32[]{:S(2)}, u32[]{:S(2)}) collective-permute-start(bf16[4,4,96,128]{3,2,1,0:T(8,128)(2,1)} %get-tuple-element.63), channel_id=1, source_target_pairs={{0,18},{1,19},{2,16},{3,17},{4,22},{5,23},{6,20},{7,21},{8,26},{9,... | collective-permute-start | bytes 1179656 | tf_op jit(solution)/shard_map/ppermute | solution.py:531
  57.6 1.5 %collective-permute-start.9 = (bf16[4,4,96,128]{3,2,1,0:T(8,128)(2,1)}, bf16[4,4,96,128]{3,2,1,0:T(8,128)(2,1)S(1)}, u32[]{:S(2)}, u32[]{:S(2)}) collective-permute-start(bf16[4,4,96,128]{3,2,1,0:T(8,128)(2,1)} %get-tuple-element.63), channel_id=1, source_target_pairs={{0,16},{4,20},{8,24},{12,28},{16,0},{20,4},{24,8},{28,12},{32,48},... | collective-permute-start | bytes 1179656 | tf_op jit(solution)/shard_map/ppermute | solution.py:526
  59.1 0.7 collective-permute-start.11
  59.9 1.3 %copy-done.1 = bf16[32,9,16,128]{3,2,1,0:T(8,128)(2,1)S(1)} copy-done((bf16[32,9,16,128]{3,2,1,0:T(8,128)(2,1)S(1)}, bf16[32,9,16,128]{3,2,1,0:T(8,128)(2,1)}, u32[]{:S(2)}) %copy-start.1) | copy-done | bytes 1179672
  61.2 1.6 %trunk_rows.1 = (bf16[2,1024,1152]{2,1,0:T(8,128)(2,1)S(1)}, bf16[128,1920]{1,0:T(8,128)(2,1)S(1)}) custom-call(s32[4]{0:T(128)S(1)} %copy-done.3, bf16[4,256,384]{2,1,0:T(8,128)(2,1)S(1)} %copy-done.2, bf16[4,256,384]{2,1,0:T(8,128)(2,1)S(1)} %collective-permute-done.3.far_ref, bf16[32,144,128]{2,1,0:T(8,128)(2,1)S(1)} %bitcast.13), custom_call_target="tpu_custom_call" | custom-call | flops 10000000 | bytes 8388608 | tf_op jit(solution)/shard_map/trunk_rows/pallas_call | solution.py:321
  62.9 5.9 %collective-permute-done.10.refs_6_ = bf16[4,4,96,128]{3,2,1,0:T(8,128)(2,1)S(1)} collective-permute-done((bf16[4,4,96,128]{3,2,1,0:T(8,128)(2,1)}, bf16[4,4,96,128]{3,2,1,0:T(8,128)(2,1)S(1)}, u32[]{:S(2)}, u32[]{:S(2)}) %collective-permute-start.10) | collective-permute-done | bytes 393248 | tf_op jit(solution)/shard_map/ppermute | solution.py:531
  68.8 5.9 %collective-permute-done.9.refs_4_ = bf16[4,4,96,128]{3,2,1,0:T(8,128)(2,1)S(1)} collective-permute-done((bf16[4,4,96,128]{3,2,1,0:T(8,128)(2,1)}, bf16[4,4,96,128]{3,2,1,0:T(8,128)(2,1)S(1)}, u32[]{:S(2)}, u32[]{:S(2)}) %collective-permute-start.9) | collective-permute-done | bytes 393248 | tf_op jit(solution)/shard_map/ppermute | solution.py:526
  75.1 3.2 %collective-permute-start.16 = (bf16[17,96,128]{2,1,0:T(8,128)(2,1)S(1)}, bf16[17,96,128]{2,1,0:T(8,128)(2,1)S(1)}, u32[]{:S(2)}, u32[]{:S(2)}) collective-permute-start(bf16[17,96,128]{2,1,0:T(8,128)(2,1)S(1)} %pad_maximum_fusion.refs_1_), channel_id=1, source_target_pairs={{0,2},{1,3},{2,0},{3,1},{4,6},{5,7},{6,4},{7,5},{8,10},{9,11},{10,... | collective-permute-start | bytes 1253384 | tf_op jit(solution)/shard_map/ppermute | solution.py:522
  78.4 7.9 %weight_grad.1 = (bf16[16,368,128]{2,1,0:T(8,128)(2,1)}, bf16[4,4,96,512]{3,2,1,0:T(8,128)(2,1)S(1)}) custom-call(s32[4]{0:T(128)S(1)} %copy-done.3, bf16[4,4,96,128]{3,2,1,0:T(8,128)(2,1)S(1)} %copy-done.4, bf16[4,4,96,128]{3,2,1,0:T(8,128)(2,1)S(1)} %collective-permute-done.7.refs_1_, bf16[4,4,96,128]{3,2,1,0:T(8,128)(2,1)S(1)} %collective-permute-done.8.refs_2_, ...), custom_call_target="tpu_custom_call" | custom-call | flops 4000000000 | bytes 10485760 | tf_op jit(solution)/shard_map/weight_grad/pallas_call | solution.py:405
  86.3 1.2 copy-done.5
  87.5 4.1 %all-to-all-start.1 = ((bf16[16,368,128]{2,1,0:T(8,128)(2,1)}), bf16[16,368,128]{2,1,0:T(8,128)(2,1)S(1)}, u32[]{:S(2)}, u32[]{:S(2)}) async-start(bf16[16,368,128]{2,1,0:T(8,128)(2,1)} %get-tuple-element.80), calls=%async_computation.1 | async-start | bytes 3014656 | tf_op jit(solution)/shard_map/all_to_all | solution.py:582
  92.2 1.2 %collective-permute-done.15.refs_2_ = bf16[17,96,128]{2,1,0:T(8,128)(2,1)S(1)} collective-permute-done((bf16[17,96,128]{2,1,0:T(8,128)(2,1)S(1)}, bf16[17,96,128]{2,1,0:T(8,128)(2,1)S(1)}, u32[]{:S(2)}, u32[]{:S(2)}) %collective-permute-start.15) | collective-permute-done | bytes 417824 | tf_op jit(solution)/shard_map/ppermute | solution.py:522
  94.2 0.8 copy-done.10
  94.9 12.1 %trunk_grad.1 = (bf16[4,256,384]{2,1,0:T(8,128)(2,1)}, bf16[4,2,96,512]{3,2,1,0:T(8,128)(2,1)}) custom-call(s32[4]{0:T(128)} %pad_add_fusion.ids_ref, bf16[4,4,96,512]{3,2,1,0:T(8,128)(2,1)} %copy-done.5, bf16[17,96,128]{2,1,0:T(8,128)(2,1)} %copy-done.6, bf16[17,96,128]{2,1,0:T(8,128)(2,1)} %copy-done.9, bf16[17,96,128]{2,1,0:T(8,128)(2,1)} %copy-done.8, ...), custom_call_target="tpu_custom_call" | custom-call | flops 8000000000 | bytes 16777216 | tf_op jit(solution)/shard_map/trunk_grad/pallas_call | solution.py:476
  107.0 9.0 %all-to-all-done.1.refs_0_ = bf16[16,368,128]{2,1,0:T(8,128)(2,1)S(1)} async-done(((bf16[16,368,128]{2,1,0:T(8,128)(2,1)}), bf16[16,368,128]{2,1,0:T(8,128)(2,1)S(1)}, u32[]{:S(2)}, u32[]{:S(2)}) %all-to-all-start.1) | async-done | bytes 1507360 | tf_op jit(solution)/shard_map/all_to_all | solution.py:582
  116.0 1.6 %sum_weights.1 = f32[5,24,384]{2,1,0:T(8,128)} custom-call(bf16[16,368,128]{2,1,0:T(8,128)(2,1)S(1)} %all-to-all-done.1.refs_0_), custom_call_target="tpu_custom_call" | custom-call | tf_op jit(solution)/shard_map/sum_weights/pallas_call | solution.py:510
  (52 shorter events, 3.5 us)
Async XLA Ops:
  0.6 19.5 %collective-permute-start.3 = (bf16[4,256,384]{2,1,0:T(8,128)(2,1)}, bf16[4,256,384]{2,1,0:T(8,128)(2,1)S(1)}, u32[]{:S(2)}, u32[]{:S(2)}) collective-permute-start(bf16[4,256,384]{2,1,0:T(8,128)(2,1)} %own_ref), channel_id=1, source_target_pairs={{0,16},{4,20},{8,24},{12,28},{16,0},{20,4},{24,8},{28,12},{32,48},... | collective-permute-start | bytes 2359304 | tf_op jit(solution)/shard_map/ppermute | solution.py:526
  5.8 11.0 %collective-permute-start = (bf16[784,128]{1,0:T(8,128)(2,1)}, bf16[784,128]{1,0:T(8,128)(2,1)S(1)}, u32[]{:S(2)}, u32[]{:S(2)}) collective-permute-start(bf16[784,128]{1,0:T(8,128)(2,1)} %get-tuple-element.48), channel_id=1, source_target_pairs={{0,1},{1,0},{2,3},{3,2},{4,5},{5,4},{6,7},{7,6},{8,9},{9,8},{10,11... | collective-permute-start | bytes 602120 | tf_op jit(solution)/shard_map/ppermute | solution.py:522
  5.9 10.9 %collective-permute-start.1 = (bf16[784,128]{1,0:T(8,128)(2,1)}, bf16[784,128]{1,0:T(8,128)(2,1)S(1)}, u32[]{:S(2)}, u32[]{:S(2)}) collective-permute-start(bf16[784,128]{1,0:T(8,128)(2,1)} %get-tuple-element.49), channel_id=1, source_target_pairs={{0,2},{1,3},{2,0},{3,1},{4,6},{5,7},{6,4},{7,5},{8,10},{9,11},{10,... | collective-permute-start | bytes 602120 | tf_op jit(solution)/shard_map/ppermute | solution.py:522
  9.9 9.9 %collective-permute-start.2 = (bf16[784,128]{1,0:T(8,128)(2,1)}, bf16[784,128]{1,0:T(8,128)(2,1)S(1)}, u32[]{:S(2)}, u32[]{:S(2)}) collective-permute-start(bf16[784,128]{1,0:T(8,128)(2,1)} %get-tuple-element.50), channel_id=1, source_target_pairs={{0,3},{1,2},{2,1},{3,0},{4,7},{5,6},{6,5},{7,4},{8,11},{9,10},{10,... | collective-permute-start | bytes 602120 | tf_op jit(solution)/shard_map/ppermute | solution.py:522
  13.3 15.8 %collective-permute-start.5 = (bf16[192,1024]{1,0:T(8,128)(2,1)}, bf16[192,1024]{1,0:T(8,128)(2,1)S(1)}, u32[]{:S(2)}, u32[]{:S(2)}) collective-permute-start(bf16[192,1024]{1,0:T(8,128)(2,1)} %refs_4_), channel_id=1, source_target_pairs={{0,66},{1,67},{2,64},{3,65},{4,70},{5,71},{6,68},{7,69},{8,74},{9,... | collective-permute-start | bytes 1179656 | tf_op jit(solution)/shard_map/ppermute | solution.py:542
  16.8 3.3 %copy-start.14 = (bf16[784,128]{1,0:T(8,128)(2,1)}, bf16[784,128]{1,0:T(8,128)(2,1)S(1)}, u32[]{:S(2)}) copy-start(bf16[784,128]{1,0:T(8,128)(2,1)S(1)} %collective-permute-done.refs_1_) | copy-start | bytes 602116
  16.8 3.3 %copy-start.15 = (bf16[784,128]{1,0:T(8,128)(2,1)}, bf16[784,128]{1,0:T(8,128)(2,1)S(1)}, u32[]{:S(2)}) copy-start(bf16[784,128]{1,0:T(8,128)(2,1)S(1)} %collective-permute-done.1.refs_2_) | copy-start | bytes 602116
  20.4 26.3 %all-to-all-start = ((bf16[32,9,16,128]{3,2,1,0:T(8,128)(2,1)}), bf16[32,9,16,128]{3,2,1,0:T(8,128)(2,1)S(1)}, u32[]{:S(2)}, u32[]{:S(2)}) async-start(bf16[32,9,16,128]{3,2,1,0:T(8,128)(2,1)} %cut_cot.1), calls=%async_computation | async-start | bytes 2359296 | tf_op jit(solution)/shard_map/all_to_all | solution.py:561
  29.0 2.0 %collective-permute-start.4 = (bf16[192,1024]{1,0:T(8,128)(2,1)}, bf16[192,1024]{1,0:T(8,128)(2,1)S(1)}, u32[]{:S(2)}, u32[]{:S(2)}) collective-permute-start(bf16[192,1024]{1,0:T(8,128)(2,1)} %refs_4_), channel_id=1, source_target_pairs={{0,1},{1,0},{2,3},{3,2},{4,5},{5,4},{6,7},{7,6},{8,9},{9,8},{10,11... | collective-permute-start | bytes 1179656 | tf_op jit(solution)/shard_map/ppermute | solution.py:522
  29.9 1.8 %collective-permute-start.6 = (bf16[192,1024]{1,0:T(8,128)(2,1)S(1)}, bf16[192,1024]{1,0:T(8,128)(2,1)S(1)}, u32[]{:S(2)}, u32[]{:S(2)}) collective-permute-start(bf16[192,1024]{1,0:T(8,128)(2,1)S(1)} %collective-permute-done.5.refs_6_), channel_id=1, source_target_pairs={{0,1},{1,0},{2,3},{3,2},{4,5},{5,4},{6,7},{7,6},{8,9},{9,8},{10,11... | collective-permute-start | bytes 1179656 | tf_op jit(solution)/shard_map/ppermute | solution.py:522
  46.8 1.0 copy-start
  47.8 12.1 %copy-start.2 = (bf16[4,256,384]{2,1,0:T(8,128)(2,1)S(1)}, bf16[4,256,384]{2,1,0:T(8,128)(2,1)}, u32[]{:S(2)}) copy-start(bf16[4,256,384]{2,1,0:T(8,128)(2,1)} %own_ref) | copy-start | bytes 2359300
  47.8 12.1 %copy-start.3 = (s32[4]{0:T(128)S(1)}, s32[4]{0:T(128)}, u32[]{:S(2)}) copy-start(s32[4]{0:T(128)} %pad_add_fusion.ids_ref) | copy-start | bytes 52
  54.0 14.8 %collective-permute-start.10 = (bf16[4,4,96,128]{3,2,1,0:T(8,128)(2,1)}, bf16[4,4,96,128]{3,2,1,0:T(8,128)(2,1)S(1)}, u32[]{:S(2)}, u32[]{:S(2)}) collective-permute-start(bf16[4,4,96,128]{3,2,1,0:T(8,128)(2,1)} %get-tuple-element.63), channel_id=1, source_target_pairs={{0,18},{1,19},{2,16},{3,17},{4,22},{5,23},{6,20},{7,21},{8,26},{9,... | collective-permute-start | bytes 1179656 | tf_op jit(solution)/shard_map/ppermute | solution.py:531
  57.6 17.0 %collective-permute-start.9 = (bf16[4,4,96,128]{3,2,1,0:T(8,128)(2,1)}, bf16[4,4,96,128]{3,2,1,0:T(8,128)(2,1)S(1)}, u32[]{:S(2)}, u32[]{:S(2)}) collective-permute-start(bf16[4,4,96,128]{3,2,1,0:T(8,128)(2,1)} %get-tuple-element.63), channel_id=1, source_target_pairs={{0,16},{4,20},{8,24},{12,28},{16,0},{20,4},{24,8},{28,12},{32,48},... | collective-permute-start | bytes 1179656 | tf_op jit(solution)/shard_map/ppermute | solution.py:526
  59.1 15.5 %collective-permute-start.8 = (bf16[4,4,96,128]{3,2,1,0:T(8,128)(2,1)}, bf16[4,4,96,128]{3,2,1,0:T(8,128)(2,1)S(1)}, u32[]{:S(2)}, u32[]{:S(2)}) collective-permute-start(bf16[4,4,96,128]{3,2,1,0:T(8,128)(2,1)} %get-tuple-element.62.refs_0_), channel_id=1, source_target_pairs={{0,2},{1,3},{2,0},{3,1},{4,6},{5,7},{6,4},{7,5},{8,10},{9,11},{10,... | collective-permute-start | bytes 1179656 | tf_op jit(solution)/shard_map/ppermute | solution.py:522
  59.1 3.7 %collective-permute-start.11 = (bf16[96,128]{1,0:T(8,128)(2,1)}, bf16[96,128]{1,0:T(8,128)(2,1)S(1)}, u32[]{:S(2)}, u32[]{:S(2)}) collective-permute-start(bf16[96,128]{1,0:T(8,128)(2,1)} %get-tuple-element.64), channel_id=1, source_target_pairs={{3,4},{7,8},{11,12},{15,16},{19,20},{23,24},{27,28},{31,32},{35,36... | collective-permute-start | bytes 73736 | tf_op jit(solution)/shard_map/ppermute | solution.py:537
  59.8 18.6 %collective-permute-start.7 = (bf16[4,4,96,128]{3,2,1,0:T(8,128)(2,1)}, bf16[4,4,96,128]{3,2,1,0:T(8,128)(2,1)S(1)}, u32[]{:S(2)}, u32[]{:S(2)}) collective-permute-start(bf16[4,4,96,128]{3,2,1,0:T(8,128)(2,1)} %get-tuple-element.62.refs_0_), channel_id=1, source_target_pairs={{0,1},{1,0},{2,3},{3,2},{4,5},{5,4},{6,7},{7,6},{8,9},{9,8},{10,11... | collective-permute-start | bytes 1179656 | tf_op jit(solution)/shard_map/ppermute | solution.py:522
  59.9 1.3 %copy-start.1 = (bf16[32,9,16,128]{3,2,1,0:T(8,128)(2,1)S(1)}, bf16[32,9,16,128]{3,2,1,0:T(8,128)(2,1)}, u32[]{:S(2)}) copy-start(bf16[32,9,16,128]{3,2,1,0:T(8,128)(2,1)} %copy-done) | copy-start | bytes 3538948
  61.2 1.6 %copy-start.7 = (bf16[4,4,96,128]{3,2,1,0:T(8,128)(2,1)S(1)}, bf16[4,4,96,128]{3,2,1,0:T(8,128)(2,1)}, u32[]{:S(2)}) copy-start(bf16[4,4,96,128]{3,2,1,0:T(8,128)(2,1)} %get-tuple-element.63) | copy-start | bytes 1179652
  61.2 17.2 %copy-start.4 = (bf16[4,4,96,128]{3,2,1,0:T(8,128)(2,1)S(1)}, bf16[4,4,96,128]{3,2,1,0:T(8,128)(2,1)}, u32[]{:S(2)}) copy-start(bf16[4,4,96,128]{3,2,1,0:T(8,128)(2,1)} %get-tuple-element.62.refs_0_) | copy-start | bytes 1179652
  62.9 28.7 %copy-start.6 = (bf16[17,96,128]{2,1,0:T(8,128)(2,1)}, bf16[17,96,128]{2,1,0:T(8,128)(2,1)S(1)}, u32[]{:S(2)}) copy-start(bf16[17,96,128]{2,1,0:T(8,128)(2,1)S(1)} %pad_maximum_fusion.refs_1_) | copy-start | bytes 1253380
  74.6 3.7 %collective-permute-start.13 = (bf16[4,4,96,128]{3,2,1,0:T(8,128)(2,1)S(1)}, bf16[4,4,96,128]{3,2,1,0:T(8,128)(2,1)S(1)}, u32[]{:S(2)}, u32[]{:S(2)}) collective-permute-start(bf16[4,4,96,128]{3,2,1,0:T(8,128)(2,1)S(1)} %collective-permute-done.9.refs_4_), channel_id=1, source_target_pairs={{0,1},{1,0},{2,3},{3,2},{4,5},{5,4},{6,7},{7,6},{8,9},{9,8},{10,11... | collective-permute-start | bytes 1179656 | tf_op jit(solution)/shard_map/ppermute | solution.py:522
  74.6 3.7 %collective-permute-start.14 = (bf16[4,4,96,128]{3,2,1,0:T(8,128)(2,1)S(1)}, bf16[4,4,96,128]{3,2,1,0:T(8,128)(2,1)S(1)}, u32[]{:S(2)}, u32[]{:S(2)}) collective-permute-start(bf16[4,4,96,128]{3,2,1,0:T(8,128)(2,1)S(1)} %collective-permute-done.10.refs_6_), channel_id=1, source_target_pairs={{0,1},{1,0},{2,3},{3,2},{4,5},{5,4},{6,7},{7,6},{8,9},{9,8},{10,11... | collective-permute-start | bytes 1179656 | tf_op jit(solution)/shard_map/ppermute | solution.py:522
  75.1 3.2 %collective-permute-start.12 = (bf16[4,4,96,128]{3,2,1,0:T(8,128)(2,1)S(1)}, bf16[4,4,96,128]{3,2,1,0:T(8,128)(2,1)S(1)}, u32[]{:S(2)}, u32[]{:S(2)}) collective-permute-start(bf16[4,4,96,128]{3,2,1,0:T(8,128)(2,1)S(1)} %collective-permute-done.8.refs_2_), channel_id=1, source_target_pairs={{0,1},{1,0},{2,3},{3,2},{4,5},{5,4},{6,7},{7,6},{8,9},{9,8},{10,11... | collective-permute-start | bytes 1179656 | tf_op jit(solution)/shard_map/ppermute | solution.py:522
  75.1 16.5 %collective-permute-start.16 = (bf16[17,96,128]{2,1,0:T(8,128)(2,1)S(1)}, bf16[17,96,128]{2,1,0:T(8,128)(2,1)S(1)}, u32[]{:S(2)}, u32[]{:S(2)}) collective-permute-start(bf16[17,96,128]{2,1,0:T(8,128)(2,1)S(1)} %pad_maximum_fusion.refs_1_), channel_id=1, source_target_pairs={{0,2},{1,3},{2,0},{3,1},{4,6},{5,7},{6,4},{7,5},{8,10},{9,11},{10,... | collective-permute-start | bytes 1253384 | tf_op jit(solution)/shard_map/ppermute | solution.py:522
  86.3 1.2 copy-start.5
  87.5 28.6 %all-to-all-start.1 = ((bf16[16,368,128]{2,1,0:T(8,128)(2,1)}), bf16[16,368,128]{2,1,0:T(8,128)(2,1)S(1)}, u32[]{:S(2)}, u32[]{:S(2)}) async-start(bf16[16,368,128]{2,1,0:T(8,128)(2,1)} %get-tuple-element.80), calls=%async_computation.1 | async-start | bytes 3014656 | tf_op jit(solution)/shard_map/all_to_all | solution.py:582
  91.6 1.8 %collective-permute-start.15 = (bf16[17,96,128]{2,1,0:T(8,128)(2,1)S(1)}, bf16[17,96,128]{2,1,0:T(8,128)(2,1)S(1)}, u32[]{:S(2)}, u32[]{:S(2)}) collective-permute-start(bf16[17,96,128]{2,1,0:T(8,128)(2,1)S(1)} %pad_maximum_fusion.refs_1_), channel_id=1, source_target_pairs={{0,1},{1,0},{2,3},{3,2},{4,5},{5,4},{6,7},{7,6},{8,9},{9,8},{10,11... | collective-permute-start | bytes 1253384 | tf_op jit(solution)/shard_map/ppermute | solution.py:522
  91.7 1.7 %copy-start.8 = (bf16[17,96,128]{2,1,0:T(8,128)(2,1)}, bf16[17,96,128]{2,1,0:T(8,128)(2,1)S(1)}, u32[]{:S(2)}) copy-start(bf16[17,96,128]{2,1,0:T(8,128)(2,1)S(1)} %collective-permute-done.16.refs_3_) | copy-start | bytes 1253380
  91.7 2.3 %collective-permute-start.17 = (bf16[17,96,128]{2,1,0:T(8,128)(2,1)S(1)}, bf16[17,96,128]{2,1,0:T(8,128)(2,1)S(1)}, u32[]{:S(2)}, u32[]{:S(2)}) collective-permute-start(bf16[17,96,128]{2,1,0:T(8,128)(2,1)S(1)} %collective-permute-done.16.refs_3_), channel_id=1, source_target_pairs={{0,1},{1,0},{2,3},{3,2},{4,5},{5,4},{6,7},{7,6},{8,9},{9,8},{10,11... | collective-permute-start | bytes 1253384 | tf_op jit(solution)/shard_map/ppermute | solution.py:522
  94.2 0.8 copy-start.10
  (5 other events, 3.7 us)

commit v5 on v4

--- a/solution.py
+++ b/solution.py
@@ -104,8 +104,8 @@
             parts += [line[:, l * LANES : (l + 1) * LANES] for l in range(3)]
         rows.append(jnp.concatenate(parts + [jnp.zeros((4, LANES), F32)], axis=0))
     for d in range(SEQ):
-        up = ((place + 1 == d) | (place + 1 == (d ^ 4))).astype(F32)
-        down = ((place - 1 == d) | (place - 1 == (d ^ 4))).astype(F32)
+        up = ((place + 1 == d) | (place + 1 == (d ^ 8))).astype(F32)
+        down = ((place - 1 == d) | (place - 1 == (d ^ 8))).astype(F32)
         send_ref[d, 8] = (rows[1] * up + rows[0] * down).astype(BF)
     for copy in copies:
         copy.wait()
@@ -125,9 +125,15 @@
     )(ids, cot.reshape(BATCH * 2, 16, -1), trunk)
 
 
+WIDE, NARROW = 9, 12
+
+
 def score_kernel(*refs):
     pieces, heads, (bias_ref, of_track_ref, scale_ref) = refs[:4], refs[4:8], refs[8:11]
-    raw_ref, inv_ref, weights_ref, merged_ref, gain_ref, cols_ref, parts, sems, head_sems, part_sems = refs[11:]
+    wide_hbm, narrow_hbm, raw_ref, small_ref, weights_ref, merged_ref = refs[11:17]
+    parts, sems, head_sems, part_sems, out_sems = refs[17:]
+    cols_ref = small_ref.at[:, 0:LANES]
+    gain_ref = small_ref.at[0:C_OUT, LANES : 2 * LANES]
     copies = []
     for r in range(CHAN):
         rows = pl.ds(r * 192, 192)
@@ -171,59 +177,85 @@
             gain_ref[start : start + size, :] = dot(parts[r], pick, (0, 0))[:size]
     m32 = merged_ref[...].astype(F32)
     total = jnp.sum(m32 * m32, axis=0, keepdims=True)
-    inv_ref[...] = jnp.broadcast_to(lax.rsqrt(total / C_OUT + epsilon), inv_ref.shape)
+    inv = lax.rsqrt(total / C_OUT + epsilon)
+    for b in range(BATCH):
+        small_ref[8 * b : 8 * b + 8, 2 * LANES : 3 * LANES] = jnp.broadcast_to(
+            inv[:, b * LANES : (b + 1) * LANES], (8, LANES)
+        )
     normed = (m32 * gain_ref[:, 0:1]).astype(BF)
     for load in loads:
         load.wait()
+    stores = [
+        pltpu.make_async_copy(small_ref, wide_hbm.at[1, :, pl.ds(0, 3 * LANES)], out_sems.at[0]),
+        pltpu.make_async_copy(weights_ref, narrow_hbm.at[0], out_sems.at[1]),
+        pltpu.make_async_copy(merged_ref, narrow_hbm.at[1, :, pl.ds(0, BATCH * LANES)], out_sems.at[2]),
+    ]
+    for store in stores:
+        store.start()
     raw_ref[...] = dot(weights_ref[...], normed, (0, 0))
+    stores.append(pltpu.make_async_copy(raw_ref, wide_hbm.at[0], out_sems.at[3]))
+    stores[-1].start()
+    for store in stores:
+        store.wait()
 
 
 def scores(pieces, heads, bias, of_track, scale):
     return pl.pallas_call(
         score_kernel,
-        out_shape=(jax.ShapeDtypeStruct((TRACKS, BATCH * LANES), F32),
-                   jax.ShapeDtypeStruct((8, BATCH * LANES), F32),
-                   jax.ShapeDtypeStruct((C_OUT, TRACKS), BF),
-                   jax.ShapeDtypeStruct((C_OUT, BATCH * LANES), BF),
-                   jax.ShapeDtypeStruct((C_OUT, LANES), F32),
-                   jax.ShapeDtypeStruct((TRACKS, LANES), F32)),
+        out_shape=(jax.ShapeDtypeStruct((WIDE, TRACKS, BATCH * LANES), F32),
+                   jax.ShapeDtypeStruct((NARROW, C_OUT, TRACKS), BF)),
         in_specs=[HBM] * 8 + [VM, VM, SM],
-        out_specs=(VM,) * 6,
-        scratch_shapes=[pltpu.VMEM((CHAN, 16, LANES), BF), pltpu.SemaphoreType.DMA((CHAN, BATCH)),
-                        pltpu.SemaphoreType.DMA((CHAN,)), pltpu.SemaphoreType.DMA((CHAN,))],
+        out_specs=(HBM, HBM),
+        scratch_shapes=[
+            pltpu.VMEM((TRACKS, BATCH * LANES), F32),
+            pltpu.VMEM((TRACKS, 3 * LANES), F32),
+            pltpu.VMEM((C_OUT, TRACKS), BF),
+            pltpu.VMEM((C_OUT, BATCH * LANES), BF),
+            pltpu.VMEM((CHAN, 16, LANES), BF),
+            pltpu.SemaphoreType.DMA((CHAN, BATCH)),
+            pltpu.SemaphoreType.DMA((CHAN,)),
+            pltpu.SemaphoreType.DMA((CHAN,)),
+            pltpu.SemaphoreType.DMA((4,)),
+        ],
         compiler_params=params(),
         cost_estimate=pl.CostEstimate(flops=45 * 10**8, bytes_accessed=8 * 2**20, transcendentals=0),
         name="scores",
     )(*pieces, *heads, bias, of_track, scale)
 
 
+HALF = BATCH * 384
+
+
 def head_kernel(
-    ids_ref, valid_ref, raw_hbm, inv_ref, weights_hbm, merged_hbm, gain_ref, cols_ref, cot_ref,
-    mine_ref, other_ref, edge_ref, full, raw_ref, weights_ref, merged_ref, sems
+    ids_ref, valid_ref, wide_hbm, narrow_hbm, cot_ref,
+    mine_ref, other_ref, edge_ref, full, raw_ref, small_ref, weights_ref, merged_ref, sems
 ):
+    load_small = pltpu.make_async_copy(wide_hbm.at[1, :, pl.ds(0, 3 * LANES)], small_ref, sems.at[1, 2])
+    load_small.start()
     loads = []
     for b in range(BATCH):
         loads.append(
-            pltpu.make_async_copy(raw_hbm.at[:, pl.ds(b * LANES, LANES)], raw_ref.at[b], sems.at[0, b])
+            pltpu.make_async_copy(wide_hbm.at[0, :, pl.ds(b * LANES, LANES)], raw_ref.at[b], sems.at[0, b])
         )
-    load_weights = pltpu.make_async_copy(weights_hbm, weights_ref, sems.at[1, 0])
-    load_merged = pltpu.make_async_copy(merged_hbm, merged_ref, sems.at[1, 1])
+    load_weights = pltpu.make_async_copy(narrow_hbm.at[0], weights_ref, sems.at[1, 0])
+    load_merged = pltpu.make_async_copy(narrow_hbm.at[1, :, pl.ds(0, BATCH * LANES)], merged_ref, sems.at[1, 1])
     for copy in loads:
         copy.start()
     load_weights.start()
     load_merged.start()
+    load_small.wait()
     me = ids_ref[0]
     first = ids_ref[1]
     half = ids_ref[2]
-    scale = cols_ref[:, 1:2]
-    bias = cols_ref[:, 0:1]
+    scale = small_ref[:, 1:2]
+    bias = small_ref[:, 0:1]
     lane = lax.broadcasted_iota(jnp.int32, (1, LANES), 1)
     scaled, coefs = [], []
     for b in range(BATCH):
         cols = slice(b * LANES, (b + 1) * LANES)
         loads[b].wait()
         raw = raw_ref[b]
-        inv = inv_ref[0:1, cols]
+        inv = small_ref[8 * b : 8 * b + 1, 2 * LANES : 3 * LANES]
         live = (first + lane < valid_ref[b]).astype(F32)
         gate = 0.5 * jnp.tanh(0.5 * (inv * raw + bias)) + 0.5
         cot = cot_ref[:, b * 32 : (b + 1) * 32, :].reshape(TRACKS, LANES).astype(F32)
@@ -233,16 +265,17 @@
         coefs.append(inv * inv * inv * d_rms * (1.0 / C_OUT))
     load_weights.wait()
     load_merged.wait()
-    d = dot(weights_ref[...], jnp.concatenate(scaled, axis=1), (1, 0)) * gain_ref[:, 0:1]
+    d = dot(weights_ref[...], jnp.concatenate(scaled, axis=1), (1, 0)) * small_ref[0:C_OUT, LANES : LANES + 1]
     for r in range(CHAN):
         rows = slice(r * 192, (r + 1) * 192)
         for b in range(BATCH):
             cols = slice(b * LANES, (b + 1) * LANES)
             full[b, me ^ r] = d[rows, cols] - coefs[b] * merged_ref[rows, cols].astype(F32)
     for b in range(BATCH):
-        for g in range(CHAN):
-            mine_ref[b, g] = full[b, g, pl.ds(pl.multiple_of(96 * half, 32), 96), :].astype(BF)
-            other_ref[b, g] = full[b, g, pl.ds(pl.multiple_of(96 * (1 - half), 32), 96), :].astype(BF)
+        for g in range(2):
+            rows = slice((b * 2 + g) * 192, (b * 2 + g + 1) * 192)
+            mine_ref[rows, :] = full[b, 2 * g + half].astype(BF)
+            other_ref[rows, :] = full[b, 2 * g + 1 - half].astype(BF)
     start = jnp.where(me == CHAN - 1, LANES - 2, 0)
     row = lax.broadcasted_iota(jnp.int32, (16, LANES), 0)
     col = lax.broadcasted_iota(jnp.int32, (16, LANES), 1) - start
@@ -257,18 +290,18 @@
 def head(ids, valid, scored, cot):
     return pl.pallas_call(
         head_kernel,
-        out_shape=(jax.ShapeDtypeStruct((BATCH, CHAN, 96, LANES), BF),) * 2
-        + (jax.ShapeDtypeStruct((96, LANES), BF),),
-        in_specs=[SM, SM, HBM, VM, HBM, HBM, VM, VM, VM],
+        out_shape=(jax.ShapeDtypeStruct((HALF, LANES), BF),) * 2 + (jax.ShapeDtypeStruct((96, LANES), BF),),
+        in_specs=[SM, SM, HBM, HBM, VM],
         out_specs=(VM,) * 3,
         scratch_shapes=[
             pltpu.VMEM((BATCH, CHAN, 192, LANES), F32),
             pltpu.VMEM((BATCH, TRACKS, LANES), F32),
+            pltpu.VMEM((TRACKS, 3 * LANES), F32),
             pltpu.VMEM((C_OUT, TRACKS), BF),
             pltpu.VMEM((C_OUT, BATCH * LANES), BF),
             pltpu.SemaphoreType.DMA((2, BATCH)),
         ],
-        compiler_params=params(61 * MIB),
+        compiler_params=params(48 * MIB),
         name="head",
     )(ids, valid, *scored, cot)
 
@@ -283,7 +316,7 @@
     ]
     for q in range(PAIR):
         for i, step in enumerate((-1, 1)):
-            source = jnp.clip((place ^ (4 * q)) + step, 0, SEQ - 1)
+            source = jnp.clip((place ^ (8 * q)) + step, 0, SEQ - 1)
             copies.append(
                 pltpu.make_async_copy(got_ref.at[source, pl.ds(128, 16)], edges.at[q, i], sems.at[q, i])
             )
@@ -295,8 +328,8 @@
     ends = [jnp.zeros((LANES, 384), F32) for _ in range(KERNEL)]
     at = lax.broadcasted_iota(jnp.int32, (LANES, 384), 0)
     for q in range(PAIR):
-        before = edges[q, 0].astype(F32) * ((place ^ (4 * q)) > 0).astype(F32)
-        after = edges[q, 1].astype(F32) * ((place ^ (4 * q)) < SEQ - 1).astype(F32)
+        before = edges[q, 0].astype(F32) * ((place ^ (8 * q)) > 0).astype(F32)
+        after = edges[q, 1].astype(F32) * ((place ^ (8 * q)) < SEQ - 1).astype(F32)
         for b in range(BATCH):
             t = trunks[q, b].astype(F32)
             rows = slice(b * 256, (b + 1) * 256)
@@ -333,6 +366,7 @@
 
 
 ROWS = 368
+KEPT = 18
 
 
 def weight_kernel(ids_ref, *refs):
@@ -342,12 +376,10 @@
     for q in range(PAIR):
         for r in range(CHAN):
             lanes = pl.ds(pl.multiple_of((me ^ r) * LANES, LANES), LANES)
-            copies.append(
-                pltpu.make_async_copy(pieces[q * CHAN + r], full.at[q, :, :, :, lanes], sems.at[q, r])
-            )
-    for copy in copies:
-        copy.start()
-    keep = pltpu.make_async_copy(full.at[0], own_ref, own_sem)
+            copies.append(pltpu.make_async_copy(pieces[q * CHAN + r], full.at[q, :, lanes], sems.at[q, r]))
+    for copy in copies:
+        copy.start()
+    keep = pltpu.make_async_copy(full.at[0], own_ref.at[0], own_sem)
     p = lax.broadcasted_iota(jnp.int32, (256, 256), 0)
     q_ = lax.broadcasted_iota(jnp.int32, (256, 256), 1)
     even = (q_ < 128) & (p // 2 == q_)
@@ -366,7 +398,7 @@
         evens, odds = [], []
         for b in range(BATCH):
             for h in range(2):
-                block = full[q, b, :, :, h * 256 : (h + 1) * 256].reshape(384, 256)
+                block = full[q, b * 384 : (b + 1) * 384, h * 256 : (h + 1) * 256]
                 e = dot(block, pick, (1, 0)).astype(BF)
                 evens.append(e[:, :128])
                 odds.append(e[:, 128:])
@@ -405,13 +437,13 @@
     return pl.pallas_call(
         weight_kernel,
         out_shape=(jax.ShapeDtypeStruct((16, ROWS, LANES), BF),
-                   jax.ShapeDtypeStruct((BATCH, CHAN, 96, 512), BF)),
+                   jax.ShapeDtypeStruct((KEPT, HALF, 512), BF)),
         in_specs=[SM] + [ANY] * 8 + [VM] * 2,
         out_specs=(HBM, HBM),
-        scratch_shapes=[pltpu.VMEM((PAIR, BATCH, CHAN, 96, 512), BF), pltpu.VMEM((16, ROWS, LANES), BF),
+        scratch_shapes=[pltpu.VMEM((PAIR, HALF, 512), BF), pltpu.VMEM((16, ROWS, LANES), BF),
                         pltpu.SemaphoreType.DMA((PAIR, CHAN)), pltpu.SemaphoreType.DMA,
                         pltpu.SemaphoreType.DMA((4,))],
-        compiler_params=params(30 * MIB),
+        compiler_params=params(40 * MIB),
         cost_estimate=pl.CostEstimate(flops=4 * 10**9, bytes_accessed=10 * 2**20, transcendentals=0),
         name="weight_grad",
     )(ids, *pieces, tr, trx)
@@ -419,20 +451,24 @@
 
 def trunk_kernel(ids_ref, *refs):
     mine, other = refs[0], refs[1:5]
-    conv_hbm, out_ref, skip_ref, full, sums, rims, conv_ref, sems, other_sems, skip_sem, conv_sem = refs[5:]
+    conv_hbm, out_ref, skip_ref, full, sums, rims, conv_ref, sems, mine_sems, other_sems, skip_sem, conv_sem = refs[5:]
     me = ids_ref[0]
     half = ids_ref[2]
-    skip = pltpu.make_async_copy(full.at[:, me], skip_ref, skip_sem)
-    copies = [pltpu.make_async_copy(mine, full.at[:, :, half], sems.at[0, 0])]
+    skip = pltpu.make_async_copy(full.at[:, me // 2, me % 2], skip_ref, skip_sem)
+    copies = []
+    for b in range(BATCH):
+        for g in range(2):
+            rows = pl.ds((b * 2 + g) * 192, 192)
+            copies.append(pltpu.make_async_copy(mine.at[0, rows, :], full.at[b, g, half], mine_sems.at[b, g]))
+            for r in range(CHAN):
+                lanes = pl.ds(pl.multiple_of((me ^ r) * LANES, LANES), LANES)
+                copies.append(
+                    pltpu.make_async_copy(
+                        other[r].at[rows, :], full.at[b, g, 1 - half, :, lanes], other_sems.at[r, b, g]
+                    )
+                )
     for r in range(CHAN):
-        lanes = pl.ds(pl.multiple_of((me ^ r) * LANES, LANES), LANES)
-        copies.append(pltpu.make_async_copy(other[r].at[BATCH * CHAN], rims.at[r], sems.at[1, r]))
-        for b in range(BATCH):
-            copies.append(
-                pltpu.make_async_copy(
-                    other[r].at[pl.ds(b * CHAN, CHAN)], full.at[b, :, 1 - half, :, lanes], other_sems.at[r, b]
-                )
-            )
+        copies.append(pltpu.make_async_copy(other[r].at[pl.ds(HALF, 96), :], rims.at[r], sems.at[r]))
     load = pltpu.make_async_copy(conv_hbm, conv_ref, conv_sem)
     for copy in copies + [load]:
         copy.start()
@@ -475,13 +511,14 @@
 def trunk_grad(ids, mine, other, conv_w):
     return pl.pallas_call(
         trunk_kernel,
-        out_shape=(jax.ShapeDtypeStruct((BATCH, 256, 384), BF), jax.ShapeDtypeStruct((BATCH, 2, 96, 512), BF)),
+        out_shape=(jax.ShapeDtypeStruct((BATCH, 256, 384), BF), jax.ShapeDtypeStruct((BATCH, 192, 512), BF)),
         in_specs=[SM] + [HBM] * 6,
         out_specs=(VM, HBM),
-        scratch_shapes=[pltpu.VMEM((BATCH, CHAN, 2, 96, 512), BF), pltpu.VMEM((BATCH * EXT, 2 * C_OUT), BF),
+        scratch_shapes=[pltpu.VMEM((BATCH, 2, 2, 192, 512), BF), pltpu.VMEM((BATCH * EXT, 2 * C_OUT), BF),
                         pltpu.VMEM((CHAN, 96, LANES), BF), pltpu.VMEM((KERNEL, 384, C_OUT), BF),
-                        pltpu.SemaphoreType.DMA((2, CHAN)), pltpu.SemaphoreType.DMA((CHAN, BATCH)),
-                        pltpu.SemaphoreType.DMA, pltpu.SemaphoreType.DMA],
+                        pltpu.SemaphoreType.DMA((CHAN,)), pltpu.SemaphoreType.DMA((BATCH, 2)),
+                        pltpu.SemaphoreType.DMA((CHAN, BATCH, 2)), pltpu.SemaphoreType.DMA,
+                        pltpu.SemaphoreType.DMA],
         compiler_params=params(),
         cost_estimate=pl.CostEstimate(flops=8 * 10**9, bytes_accessed=16 * 2**20, transcendentals=0),
         name="trunk_grad",
@@ -523,11 +560,11 @@
 
 
 def partner(x):
-    return lax.ppermute(x, "seq", [(i, i ^ 4) for i in range(SEQ)])
+    return lax.ppermute(x, "seq", [(i, i ^ 8) for i in range(SEQ)])
 
 
 def partner_far(x):
-    pairs = [(s * CHAN + c, (s ^ 4) * CHAN + (c ^ 2)) for s in range(SEQ) for c in range(CHAN)]
+    pairs = [(s * CHAN + c, (s ^ 8) * CHAN + (c ^ 2)) for s in range(SEQ) for c in range(CHAN)]
     return lax.ppermute(x, ("seq", "chan"), pairs)
 
 
@@ -547,7 +584,7 @@
 ):
     me = lax.axis_index("chan").astype(jnp.int32)
     place = lax.axis_index("seq").astype(jnp.int32)
-    half = (place // 4) % 2
+    half = (place // 8) % 2
     ids = jnp.stack([me, place * 512 + me * LANES, half, place])
     trunk_far = partner(trunk)
     p0, p1, p2, p3 = cut_pieces(ids, merged, norm_gain[None])
@@ -568,7 +605,7 @@
     tr, trx = trunk_rows(ids, trunk, trunk_far, got)
 
     mine_far, other_x, other_far_x = flip(mine, 2), partner(other), partner_far(other)
-    other = jnp.concatenate([other.reshape(BATCH * CHAN, 96, LANES), rim(edge)[None]])
+    other = jnp.concatenate([other, rim(edge)])
     mine_far, other_x, other_far_x, other, tr, trx = lax.optimization_barrier(
         (mine_far, other_x, other_far_x, other, tr, trx)
     )
@@ -578,12 +615,12 @@
     other_late, _ = lax.optimization_barrier((other, mine_far))
     other_far = flip(other_late, 2)
     other_all = (other, flip(other, 1), other_far, flip(other_far, 1))
-    groups = [[s for s in range(SEQ) if (s // 4) % 2 == u] for u in range(2)]
+    groups = [[s for s in range(SEQ) if (s // 8) % 2 == u] for u in range(2)]
     summed = lax.all_to_all(terms, "seq", 0, 0, tiled=True, axis_index_groups=groups)
     d_trunk, d_skip = trunk_grad(ids, mine_rows, other_all, conv_w)
     grad_scale = 1.0 / math.sqrt(BATCH * 512 * SEQ)
     d_conv_w = sum_weights(summed, grad_scale)
-    return (d_trunk, d_skip.reshape(BATCH, 192, 512), d_conv_w)
+    return (d_trunk, d_skip, d_conv_w)
 
 
 def solution(mesh):

time: 120 us -> 117 us (0.975); the launches traced: 118 us -> 117 us
  local copies, waits for them, and re-layouts: 6.29 us -> 2.01 us
  starting transfers between devices: 32.6 us -> 36 us
    unnamed x34 -> x26, local copies, waits for them, and re-layouts: 6.29 us -> 2.01 us
    ppermute x2, starting transfers between devices: 3.2 us -> 5.37 us  [partner(): return lax.ppermute(x, 'seq', [(i, i ^ 8) for i in range(SEQ)])]
  transfers between devices with their start and end apart: 20 -> 20, of which waited for: 10 -> 10; matrix products, arithmetic and copies ran while one was open for 1% -> 1% of each run, Pallas kernels for 28% -> 29%
where the time goes in v5:
time: 117 us
  Pallas kernels  40.3 us (34%)
  waiting for transfers between devices  36.7 us (31%)
  starting transfers between devices  36 us (31%)
  local copies, waits for them, and re-layouts  2.01 us (2%)
    pallas_call x1, Pallas kernels, trunk_grad(): pl.pallas_call(trunk_kernel, out_shape=(jax.ShapeDtypeStruct((BATCH, 256,...  12.3 us
    ppermute x13, starting transfers between devices, flip(): return lax.ppermute(x, 'chan', [(i, i ^ r) for i in range(CHAN)])  9.03 us
    all_to_all x1, waiting for transfers between devices, local(): lax.all_to_all(terms, 'seq', 0, 0, tiled=True, axis_index_groups=groups)  8.84 us
    all_to_all x1, waiting for transfers between devices, local(): lax.all_to_all(send, 'seq', 0, 0, tiled=True).reshape(SEQ, COT_ROWS, LANES)  8.68 us
    all_to_all x1, starting transfers between devices, local(): lax.all_to_all(send, 'seq', 0, 0, tiled=True).reshape(SEQ, COT_ROWS, LANES)  8.4 us
    pallas_call x1, Pallas kernels, weight_grad(): pl.pallas_call(weight_kernel, out_shape=(jax.ShapeDtypeStruct((16, ROWS,...  7.94 us
    ppermute x1, waiting for transfers between devices, partner_far(): return lax.ppermute(x, ('seq', 'chan'), pairs)  6.95 us
    ppermute x13, waiting for transfers between devices, flip(): return lax.ppermute(x, 'chan', [(i, i ^ r) for i in range(CHAN)])  6.6 us
  transfers between devices with their start and end apart: 20, of which 10 were waited for; matrix products, arithmetic and copies ran while one was open for 1% of the time, Pallas kernels for 29%

profile of v5, /device:TPU:0, one launch (start us, length us, event | category | flops | bytes accessed | tf_op | source)
XLA Modules:
  0.0 116.7 jit_solution(2667396604540651415)
XLA Ops:
  0.6 3.4 %collective-permute-start.3 = (bf16[4,256,384]{2,1,0:T(8,128)(2,1)}, bf16[4,256,384]{2,1,0:T(8,128)(2,1)S(1)}, u32[]{:S(2)}, u32[]{:S(2)}) collective-permute-start(bf16[4,256,384]{2,1,0:T(8,128)(2,1)} %own_ref), channel_id=1, source_target_pairs={{0,32},{4,36},{8,40},{12,44},{16,48},{20,52},{24,56},{28,60},{32,0... | collective-permute-start | bytes 2359304 | tf_op jit(solution)/shard_map/ppermute | solution.py:563
  4.0 0.6 pad_add_fusion.ids_ref
  4.6 2.8 %cut_pieces.1 = (bf16[784,128]{1,0:T(8,128)(2,1)}, bf16[784,128]{1,0:T(8,128)(2,1)}, bf16[784,128]{1,0:T(8,128)(2,1)}, bf16[784,128]{1,0:T(8,128)(2,1)}) custom-call(s32[4]{0:T(128)} %pad_add_fusion.ids_ref, bf16[4,192,512]{2,1,0:T(8,128)(2,1)} %merged_ref.1, f32[1,192]{1,0:T(1,128)} %bitcast.12), custom_call_target="tpu_custom_call" | custom-call | tf_op jit(solution)/shard_map/cut_pieces/pallas_call | solution.py:69
  7.5 4.0 %collective-permute-start.1 = (bf16[784,128]{1,0:T(8,128)(2,1)}, bf16[784,128]{1,0:T(8,128)(2,1)S(1)}, u32[]{:S(2)}, u32[]{:S(2)}) collective-permute-start(bf16[784,128]{1,0:T(8,128)(2,1)} %get-tuple-element.45), channel_id=1, source_target_pairs={{0,2},{1,3},{2,0},{3,1},{4,6},{5,7},{6,4},{7,5},{8,10},{9,11},{10,... | collective-permute-start | bytes 602120 | tf_op jit(solution)/shard_map/ppermute | solution.py:559
  11.6 3.3 %cut_cot.1 = bf16[32,9,16,128]{3,2,1,0:T(8,128)(2,1)} custom-call(s32[4]{0:T(128)} %pad_add_fusion.ids_ref, bf16[8,16,16384]{2,1,0:T(8,128)(2,1)} %bitcast.11, bf16[4,256,384]{2,1,0:T(8,128)(2,1)} %own_ref), custom_call_target="tpu_custom_call" | custom-call | bytes 5242880 | tf_op jit(solution)/shard_map/cut_cot/pallas_call | solution.py:115
  14.9 3.5 %collective-permute-start.5 = (bf16[192,1024]{1,0:T(8,128)(2,1)}, bf16[192,1024]{1,0:T(8,128)(2,1)S(1)}, u32[]{:S(2)}, u32[]{:S(2)}) collective-permute-start(bf16[192,1024]{1,0:T(8,128)(2,1)} %refs_4_), channel_id=1, source_target_pairs={{0,66},{1,67},{2,64},{3,65},{4,70},{5,71},{6,68},{7,69},{8,74},{9,... | collective-permute-start | bytes 1179656 | tf_op jit(solution)/shard_map/ppermute | solution.py:579
  18.4 3.0 %collective-permute-done.2.refs_3_ = bf16[784,128]{1,0:T(8,128)(2,1)S(1)} collective-permute-done((bf16[784,128]{1,0:T(8,128)(2,1)}, bf16[784,128]{1,0:T(8,128)(2,1)S(1)}, u32[]{:S(2)}, u32[]{:S(2)}) %collective-permute-start.2) | collective-permute-done | bytes 200736 | tf_op jit(solution)/shard_map/ppermute | solution.py:559
  22.1 8.4 %all-to-all-start = ((bf16[32,9,16,128]{3,2,1,0:T(8,128)(2,1)}), bf16[32,9,16,128]{3,2,1,0:T(8,128)(2,1)S(1)}, u32[]{:S(2)}, u32[]{:S(2)}) async-start(bf16[32,9,16,128]{3,2,1,0:T(8,128)(2,1)} %cut_cot.1), calls=%async_computation | async-start | bytes 2359296 | tf_op jit(solution)/shard_map/all_to_all | solution.py:598
  30.6 0.5 collective-permute-start.6
  31.1 1.4 %collective-permute-done.4.refs_5_ = bf16[192,1024]{1,0:T(8,128)(2,1)S(1)} collective-permute-done((bf16[192,1024]{1,0:T(8,128)(2,1)}, bf16[192,1024]{1,0:T(8,128)(2,1)S(1)}, u32[]{:S(2)}, u32[]{:S(2)}) %collective-permute-start.4) | collective-permute-done | bytes 393248 | tf_op jit(solution)/shard_map/ppermute | solution.py:559
  32.5 0.3 collective-permute-done.6.refs_7_
  32.9 0.4 copy-done.8
  33.6 5.6 %scores.1 = (f32[9,1024,512]{2,1,0:T(8,128)}, bf16[12,768,1024]{2,1,0:T(8,128)(2,1)}) custom-call(bf16[784,128]{1,0:T(8,128)(2,1)} %get-tuple-element.38.refs_0_, bf16[784,128]{1,0:T(8,128)(2,1)} %copy-done.10, bf16[784,128]{1,0:T(8,128)(2,1)} %copy-done.11, bf16[784,128]{1,0:T(8,128)(2,1)} %copy-done.12, bf16[192,1024]{1,0:T(8,128)(2,1)} %refs_4_, ...), custom_call_target="tpu_custom_call" | custom-call | flops 4499999744 | bytes 8388608 | tf_op jit(solution)/shard_map/scores/pallas_call | solution.py:203
  39.2 8.7 %all-to-all-done = bf16[32,9,16,128]{3,2,1,0:T(8,128)(2,1)S(1)} async-done(((bf16[32,9,16,128]{3,2,1,0:T(8,128)(2,1)}), bf16[32,9,16,128]{3,2,1,0:T(8,128)(2,1)S(1)}, u32[]{:S(2)}, u32[]{:S(2)}) %all-to-all-start) | async-done | bytes 1179680 | tf_op jit(solution)/shard_map/all_to_all | solution.py:598
  47.9 5.0 %head.1 = (bf16[1536,128]{1,0:T(8,128)(2,1)S(1)}, bf16[1536,128]{1,0:T(8,128)(2,1)S(1)}, bf16[96,128]{1,0:T(8,128)(2,1)S(1)}) custom-call(s32[4]{0:T(128)S(1)} %copy-done.1, s32[4]{0:T(128)S(1)} %copy-done.2, f32[9,1024,512]{2,1,0:T(8,128)} %get-tuple-element.51.wide_hbm, bf16[12,768,1024]{2,1,0:T(8,128)(2,1)} %get-tuple-element.52.narrow_hbm, ...), custom_call_target="tpu_custom_call" | custom-call | tf_op jit(solution)/shard_map/head/pallas_call | solution.py:291
  52.9 4.6 %collective-permute-start.10 = (bf16[1536,128]{1,0:T(8,128)(2,1)S(1)}, bf16[1536,128]{1,0:T(8,128)(2,1)S(1)}, u32[]{:S(2)}, u32[]{:S(2)}) collective-permute-start(bf16[1536,128]{1,0:T(8,128)(2,1)S(1)} %get-tuple-element.55), channel_id=1, source_target_pairs={{0,34},{1,35},{2,32},{3,33},{4,38},{5,39},{6,36},{7,37},{8,42},{9,... | collective-permute-start | bytes 1179656 | tf_op jit(solution)/shard_map/ppermute | solution.py:568
  57.5 2.0 %collective-permute-start.9 = (bf16[1536,128]{1,0:T(8,128)(2,1)S(1)}, bf16[1536,128]{1,0:T(8,128)(2,1)S(1)}, u32[]{:S(2)}, u32[]{:S(2)}) collective-permute-start(bf16[1536,128]{1,0:T(8,128)(2,1)S(1)} %get-tuple-element.55), channel_id=1, source_target_pairs={{0,32},{4,36},{8,40},{12,44},{16,48},{20,52},{24,56},{28,60},{32,0... | collective-permute-start | bytes 1179656 | tf_op jit(solution)/shard_map/ppermute | solution.py:563
  59.6 0.7 collective-permute-start.11
  60.3 1.6 %trunk_rows.1 = (bf16[2,1024,1152]{2,1,0:T(8,128)(2,1)S(1)}, bf16[128,1920]{1,0:T(8,128)(2,1)S(1)}) custom-call(s32[4]{0:T(128)S(1)} %copy-done.1, bf16[4,256,384]{2,1,0:T(8,128)(2,1)S(1)} %copy-done, bf16[4,256,384]{2,1,0:T(8,128)(2,1)S(1)} %collective-permute-done.3.far_ref, bf16[32,144,128]{2,1,0:T(8,128)(2,1)S(1)} %bitcast.10), custom_call_target="tpu_custom_call" | custom-call | flops 10000000 | bytes 8388608 | tf_op jit(solution)/shard_map/trunk_rows/pallas_call | solution.py:354
  62.0 6.9 %collective-permute-done.10.refs_6_ = bf16[1536,128]{1,0:T(8,128)(2,1)S(1)} collective-permute-done((bf16[1536,128]{1,0:T(8,128)(2,1)S(1)}, bf16[1536,128]{1,0:T(8,128)(2,1)S(1)}, u32[]{:S(2)}, u32[]{:S(2)}) %collective-permute-start.10) | collective-permute-done | bytes 393248 | tf_op jit(solution)/shard_map/ppermute | solution.py:568
  69.0 5.3 %collective-permute-done.9.refs_4_ = bf16[1536,128]{1,0:T(8,128)(2,1)S(1)} collective-permute-done((bf16[1536,128]{1,0:T(8,128)(2,1)S(1)}, bf16[1536,128]{1,0:T(8,128)(2,1)S(1)}, u32[]{:S(2)}, u32[]{:S(2)}) %collective-permute-start.9) | collective-permute-done | bytes 393248 | tf_op jit(solution)/shard_map/ppermute | solution.py:563
  74.3 0.5 collective-permute-start.14
  74.8 3.2 %collective-permute-start.16 = (bf16[1632,128]{1,0:T(8,128)(2,1)S(1)}, bf16[1632,128]{1,0:T(8,128)(2,1)S(1)}, u32[]{:S(2)}, u32[]{:S(2)}) collective-permute-start(bf16[1632,128]{1,0:T(8,128)(2,1)S(1)} %pad_maximum_fusion.refs_1_), channel_id=1, source_target_pairs={{0,2},{1,3},{2,0},{3,1},{4,6},{5,7},{6,4},{7,5},{8,10},{9,11},{10,... | collective-permute-start | bytes 1253384 | tf_op jit(solution)/shard_map/ppermute | solution.py:559
  78.0 7.9 %weight_grad.1 = (bf16[16,368,128]{2,1,0:T(8,128)(2,1)}, bf16[18,1536,512]{2,1,0:T(8,128)(2,1)}) custom-call(s32[4]{0:T(128)S(1)} %copy-done.1, bf16[1536,128]{1,0:T(8,128)(2,1)S(1)} %get-tuple-element.54.refs_0_, bf16[1536,128]{1,0:T(8,128)(2,1)S(1)} %collective-permute-done.7.refs_1_, bf16[1536,128]{1,0:T(8,128)(2,1)S(1)} %collective-permute-done.8.refs_2_, ...), custom_call_target="tpu_custom_call" | custom-call | flops 4000000000 | bytes 10485760 | tf_op jit(solution)/shard_map/weight_grad/pallas_call | solution.py:437
  85.9 4.4 %all-to-all-start.1 = ((bf16[16,368,128]{2,1,0:T(8,128)(2,1)}), bf16[16,368,128]{2,1,0:T(8,128)(2,1)S(1)}, u32[]{:S(2)}, u32[]{:S(2)}) async-start(bf16[16,368,128]{2,1,0:T(8,128)(2,1)} %get-tuple-element.72), calls=%async_computation.1 | async-start | bytes 3014656 | tf_op jit(solution)/shard_map/all_to_all | solution.py:619
  90.5 0.5 collective-permute-start.17
  91.0 1.2 %collective-permute-done.15.refs_2_ = bf16[1632,128]{1,0:T(8,128)(2,1)S(1)} collective-permute-done((bf16[1632,128]{1,0:T(8,128)(2,1)S(1)}, bf16[1632,128]{1,0:T(8,128)(2,1)S(1)}, u32[]{:S(2)}, u32[]{:S(2)}) %collective-permute-start.15) | collective-permute-done | bytes 417824 | tf_op jit(solution)/shard_map/ppermute | solution.py:559
  92.2 0.6 collective-permute-done.17.refs_4_
  93.0 0.7 copy-done.6
  93.7 12.3 %trunk_grad.1 = (bf16[4,256,384]{2,1,0:T(8,128)(2,1)}, bf16[4,192,512]{2,1,0:T(8,128)(2,1)}) custom-call(s32[4]{0:T(128)} %pad_add_fusion.ids_ref, bf16[18,1536,512]{2,1,0:T(8,128)(2,1)} %get-tuple-element.67.refs_0_, bf16[1632,128]{1,0:T(8,128)(2,1)} %copy-done.3, bf16[1632,128]{1,0:T(8,128)(2,1)} %copy-done.5, bf16[1632,128]{1,0:T(8,128)(2,1)} %copy-done.4, ...), custom_call_target="tpu_custom_call" | custom-call | flops 8000000000 | bytes 16777216 | tf_op jit(solution)/shard_map/trunk_grad/pallas_call | solution.py:512
  106.1 8.8 %all-to-all-done.1.refs_0_ = bf16[16,368,128]{2,1,0:T(8,128)(2,1)S(1)} async-done(((bf16[16,368,128]{2,1,0:T(8,128)(2,1)}), bf16[16,368,128]{2,1,0:T(8,128)(2,1)S(1)}, u32[]{:S(2)}, u32[]{:S(2)}) %all-to-all-start.1) | async-done | bytes 1507360 | tf_op jit(solution)/shard_map/all_to_all | solution.py:619
  114.9 1.6 %sum_weights.1 = f32[5,24,384]{2,1,0:T(8,128)} custom-call(bf16[16,368,128]{2,1,0:T(8,128)(2,1)S(1)} %all-to-all-done.1.refs_0_), custom_call_target="tpu_custom_call" | custom-call | tf_op jit(solution)/shard_map/sum_weights/pallas_call | solution.py:547
  (44 shorter events, 1.7 us)
Async XLA Ops:
  0.6 21.1 %collective-permute-start.3 = (bf16[4,256,384]{2,1,0:T(8,128)(2,1)}, bf16[4,256,384]{2,1,0:T(8,128)(2,1)S(1)}, u32[]{:S(2)}, u32[]{:S(2)}) collective-permute-start(bf16[4,256,384]{2,1,0:T(8,128)(2,1)} %own_ref), channel_id=1, source_target_pairs={{0,32},{4,36},{8,40},{12,44},{16,48},{20,52},{24,56},{28,60},{32,0... | collective-permute-start | bytes 2359304 | tf_op jit(solution)/shard_map/ppermute | solution.py:563
  7.4 11.0 %collective-permute-start = (bf16[784,128]{1,0:T(8,128)(2,1)}, bf16[784,128]{1,0:T(8,128)(2,1)S(1)}, u32[]{:S(2)}, u32[]{:S(2)}) collective-permute-start(bf16[784,128]{1,0:T(8,128)(2,1)} %get-tuple-element.44), channel_id=1, source_target_pairs={{0,1},{1,0},{2,3},{3,2},{4,5},{5,4},{6,7},{7,6},{8,9},{9,8},{10,11... | collective-permute-start | bytes 602120 | tf_op jit(solution)/shard_map/ppermute | solution.py:559
  7.5 10.9 %collective-permute-start.1 = (bf16[784,128]{1,0:T(8,128)(2,1)}, bf16[784,128]{1,0:T(8,128)(2,1)S(1)}, u32[]{:S(2)}, u32[]{:S(2)}) collective-permute-start(bf16[784,128]{1,0:T(8,128)(2,1)} %get-tuple-element.45), channel_id=1, source_target_pairs={{0,2},{1,3},{2,0},{3,1},{4,6},{5,7},{6,4},{7,5},{8,10},{9,11},{10,... | collective-permute-start | bytes 602120 | tf_op jit(solution)/shard_map/ppermute | solution.py:559
  11.5 9.9 %collective-permute-start.2 = (bf16[784,128]{1,0:T(8,128)(2,1)}, bf16[784,128]{1,0:T(8,128)(2,1)S(1)}, u32[]{:S(2)}, u32[]{:S(2)}) collective-permute-start(bf16[784,128]{1,0:T(8,128)(2,1)} %get-tuple-element.46), channel_id=1, source_target_pairs={{0,3},{1,2},{2,1},{3,0},{4,7},{5,6},{6,5},{7,4},{8,11},{9,10},{10,... | collective-permute-start | bytes 602120 | tf_op jit(solution)/shard_map/ppermute | solution.py:559
  14.9 15.7 %collective-permute-start.5 = (bf16[192,1024]{1,0:T(8,128)(2,1)}, bf16[192,1024]{1,0:T(8,128)(2,1)S(1)}, u32[]{:S(2)}, u32[]{:S(2)}) collective-permute-start(bf16[192,1024]{1,0:T(8,128)(2,1)} %refs_4_), channel_id=1, source_target_pairs={{0,66},{1,67},{2,64},{3,65},{4,70},{5,71},{6,68},{7,69},{8,74},{9,... | collective-permute-start | bytes 1179656 | tf_op jit(solution)/shard_map/ppermute | solution.py:579
  18.4 3.3 %copy-start.10 = (bf16[784,128]{1,0:T(8,128)(2,1)}, bf16[784,128]{1,0:T(8,128)(2,1)S(1)}, u32[]{:S(2)}) copy-start(bf16[784,128]{1,0:T(8,128)(2,1)S(1)} %collective-permute-done.refs_1_) | copy-start | bytes 602116
  18.4 3.3 %copy-start.11 = (bf16[784,128]{1,0:T(8,128)(2,1)}, bf16[784,128]{1,0:T(8,128)(2,1)S(1)}, u32[]{:S(2)}) copy-start(bf16[784,128]{1,0:T(8,128)(2,1)S(1)} %collective-permute-done.1.refs_2_) | copy-start | bytes 602116
  22.1 25.8 %all-to-all-start = ((bf16[32,9,16,128]{3,2,1,0:T(8,128)(2,1)}), bf16[32,9,16,128]{3,2,1,0:T(8,128)(2,1)S(1)}, u32[]{:S(2)}, u32[]{:S(2)}) async-start(bf16[32,9,16,128]{3,2,1,0:T(8,128)(2,1)} %cut_cot.1), calls=%async_computation | async-start | bytes 2359296 | tf_op jit(solution)/shard_map/all_to_all | solution.py:598
  30.5 2.0 %collective-permute-start.4 = (bf16[192,1024]{1,0:T(8,128)(2,1)}, bf16[192,1024]{1,0:T(8,128)(2,1)S(1)}, u32[]{:S(2)}, u32[]{:S(2)}) collective-permute-start(bf16[192,1024]{1,0:T(8,128)(2,1)} %refs_4_), channel_id=1, source_target_pairs={{0,1},{1,0},{2,3},{3,2},{4,5},{5,4},{6,7},{7,6},{8,9},{9,8},{10,11... | collective-permute-start | bytes 1179656 | tf_op jit(solution)/shard_map/ppermute | solution.py:559
  30.6 2.3 %copy-start.7 = (bf16[192,1024]{1,0:T(8,128)(2,1)}, bf16[192,1024]{1,0:T(8,128)(2,1)S(1)}, u32[]{:S(2)}) copy-start(bf16[192,1024]{1,0:T(8,128)(2,1)S(1)} %collective-permute-done.5.refs_6_) | copy-start | bytes 1179652
  30.6 2.2 %collective-permute-start.6 = (bf16[192,1024]{1,0:T(8,128)(2,1)S(1)}, bf16[192,1024]{1,0:T(8,128)(2,1)S(1)}, u32[]{:S(2)}, u32[]{:S(2)}) collective-permute-start(bf16[192,1024]{1,0:T(8,128)(2,1)S(1)} %collective-permute-done.5.refs_6_), channel_id=1, source_target_pairs={{0,1},{1,0},{2,3},{3,2},{4,5},{5,4},{6,7},{7,6},{8,9},{9,8},{10,11... | collective-permute-start | bytes 1179656 | tf_op jit(solution)/shard_map/ppermute | solution.py:559
  32.5 0.7 copy-start.8
  32.9 0.7 copy-start.9
  33.6 14.3 %copy-start.1 = (s32[4]{0:T(128)S(1)}, s32[4]{0:T(128)}, u32[]{:S(2)}) copy-start(s32[4]{0:T(128)} %pad_add_fusion.ids_ref) | copy-start | bytes 52
  33.6 14.3 %copy-start.2 = (s32[4]{0:T(128)S(1)}, s32[4]{0:T(128)}, u32[]{:S(2)}) copy-start(s32[4]{0:T(128)} %valid_ref.1) | copy-start | bytes 52
  47.9 12.4 %copy-start = (bf16[4,256,384]{2,1,0:T(8,128)(2,1)S(1)}, bf16[4,256,384]{2,1,0:T(8,128)(2,1)}, u32[]{:S(2)}) copy-start(bf16[4,256,384]{2,1,0:T(8,128)(2,1)} %own_ref) | copy-start | bytes 2359300
  52.9 16.0 %collective-permute-start.10 = (bf16[1536,128]{1,0:T(8,128)(2,1)S(1)}, bf16[1536,128]{1,0:T(8,128)(2,1)S(1)}, u32[]{:S(2)}, u32[]{:S(2)}) collective-permute-start(bf16[1536,128]{1,0:T(8,128)(2,1)S(1)} %get-tuple-element.55), channel_id=1, source_target_pairs={{0,34},{1,35},{2,32},{3,33},{4,38},{5,39},{6,36},{7,37},{8,42},{9,... | collective-permute-start | bytes 1179656 | tf_op jit(solution)/shard_map/ppermute | solution.py:568
  57.5 16.7 %collective-permute-start.9 = (bf16[1536,128]{1,0:T(8,128)(2,1)S(1)}, bf16[1536,128]{1,0:T(8,128)(2,1)S(1)}, u32[]{:S(2)}, u32[]{:S(2)}) collective-permute-start(bf16[1536,128]{1,0:T(8,128)(2,1)S(1)} %get-tuple-element.55), channel_id=1, source_target_pairs={{0,32},{4,36},{8,40},{12,44},{16,48},{20,52},{24,56},{28,60},{32,0... | collective-permute-start | bytes 1179656 | tf_op jit(solution)/shard_map/ppermute | solution.py:563
  59.6 14.7 %collective-permute-start.8 = (bf16[1536,128]{1,0:T(8,128)(2,1)S(1)}, bf16[1536,128]{1,0:T(8,128)(2,1)S(1)}, u32[]{:S(2)}, u32[]{:S(2)}) collective-permute-start(bf16[1536,128]{1,0:T(8,128)(2,1)S(1)} %get-tuple-element.54.refs_0_), channel_id=1, source_target_pairs={{0,2},{1,3},{2,0},{3,1},{4,6},{5,7},{6,4},{7,5},{8,10},{9,11},{10,... | collective-permute-start | bytes 1179656 | tf_op jit(solution)/shard_map/ppermute | solution.py:559
  59.6 2.4 %collective-permute-start.11 = (bf16[96,128]{1,0:T(8,128)(2,1)S(1)}, bf16[96,128]{1,0:T(8,128)(2,1)S(1)}, u32[]{:S(2)}, u32[]{:S(2)}) collective-permute-start(bf16[96,128]{1,0:T(8,128)(2,1)S(1)} %get-tuple-element.56), channel_id=1, source_target_pairs={{3,4},{7,8},{11,12},{15,16},{19,20},{23,24},{27,28},{31,32},{35,36... | collective-permute-start | bytes 73736 | tf_op jit(solution)/shard_map/ppermute | solution.py:574
  60.2 17.7 %collective-permute-start.7 = (bf16[1536,128]{1,0:T(8,128)(2,1)S(1)}, bf16[1536,128]{1,0:T(8,128)(2,1)S(1)}, u32[]{:S(2)}, u32[]{:S(2)}) collective-permute-start(bf16[1536,128]{1,0:T(8,128)(2,1)S(1)} %get-tuple-element.54.refs_0_), channel_id=1, source_target_pairs={{0,1},{1,0},{2,3},{3,2},{4,5},{5,4},{6,7},{7,6},{8,9},{9,8},{10,11... | collective-permute-start | bytes 1179656 | tf_op jit(solution)/shard_map/ppermute | solution.py:559
  62.0 28.4 %copy-start.3 = (bf16[1632,128]{1,0:T(8,128)(2,1)}, bf16[1632,128]{1,0:T(8,128)(2,1)S(1)}, u32[]{:S(2)}) copy-start(bf16[1632,128]{1,0:T(8,128)(2,1)S(1)} %pad_maximum_fusion.refs_1_) | copy-start | bytes 1253380
  74.3 3.7 %collective-permute-start.13 = (bf16[1536,128]{1,0:T(8,128)(2,1)S(1)}, bf16[1536,128]{1,0:T(8,128)(2,1)S(1)}, u32[]{:S(2)}, u32[]{:S(2)}) collective-permute-start(bf16[1536,128]{1,0:T(8,128)(2,1)S(1)} %collective-permute-done.9.refs_4_), channel_id=1, source_target_pairs={{0,1},{1,0},{2,3},{3,2},{4,5},{5,4},{6,7},{7,6},{8,9},{9,8},{10,11... | collective-permute-start | bytes 1179656 | tf_op jit(solution)/shard_map/ppermute | solution.py:559
  74.3 3.7 %collective-permute-start.14 = (bf16[1536,128]{1,0:T(8,128)(2,1)S(1)}, bf16[1536,128]{1,0:T(8,128)(2,1)S(1)}, u32[]{:S(2)}, u32[]{:S(2)}) collective-permute-start(bf16[1536,128]{1,0:T(8,128)(2,1)S(1)} %collective-permute-done.10.refs_6_), channel_id=1, source_target_pairs={{0,1},{1,0},{2,3},{3,2},{4,5},{5,4},{6,7},{7,6},{8,9},{9,8},{10,11... | collective-permute-start | bytes 1179656 | tf_op jit(solution)/shard_map/ppermute | solution.py:559
  74.8 3.2 %collective-permute-start.12 = (bf16[1536,128]{1,0:T(8,128)(2,1)S(1)}, bf16[1536,128]{1,0:T(8,128)(2,1)S(1)}, u32[]{:S(2)}, u32[]{:S(2)}) collective-permute-start(bf16[1536,128]{1,0:T(8,128)(2,1)S(1)} %collective-permute-done.8.refs_2_), channel_id=1, source_target_pairs={{0,1},{1,0},{2,3},{3,2},{4,5},{5,4},{6,7},{7,6},{8,9},{9,8},{10,11... | collective-permute-start | bytes 1179656 | tf_op jit(solution)/shard_map/ppermute | solution.py:559
  74.8 15.7 %collective-permute-start.16 = (bf16[1632,128]{1,0:T(8,128)(2,1)S(1)}, bf16[1632,128]{1,0:T(8,128)(2,1)S(1)}, u32[]{:S(2)}, u32[]{:S(2)}) collective-permute-start(bf16[1632,128]{1,0:T(8,128)(2,1)S(1)} %pad_maximum_fusion.refs_1_), channel_id=1, source_target_pairs={{0,2},{1,3},{2,0},{3,1},{4,6},{5,7},{6,4},{7,5},{8,10},{9,11},{10,... | collective-permute-start | bytes 1253384 | tf_op jit(solution)/shard_map/ppermute | solution.py:559
  85.9 28.9 %all-to-all-start.1 = ((bf16[16,368,128]{2,1,0:T(8,128)(2,1)}), bf16[16,368,128]{2,1,0:T(8,128)(2,1)S(1)}, u32[]{:S(2)}, u32[]{:S(2)}) async-start(bf16[16,368,128]{2,1,0:T(8,128)(2,1)} %get-tuple-element.72), calls=%async_computation.1 | async-start | bytes 3014656 | tf_op jit(solution)/shard_map/all_to_all | solution.py:619
  90.4 1.8 %collective-permute-start.15 = (bf16[1632,128]{1,0:T(8,128)(2,1)S(1)}, bf16[1632,128]{1,0:T(8,128)(2,1)S(1)}, u32[]{:S(2)}, u32[]{:S(2)}) collective-permute-start(bf16[1632,128]{1,0:T(8,128)(2,1)S(1)} %pad_maximum_fusion.refs_1_), channel_id=1, source_target_pairs={{0,1},{1,0},{2,3},{3,2},{4,5},{5,4},{6,7},{7,6},{8,9},{9,8},{10,11... | collective-permute-start | bytes 1253384 | tf_op jit(solution)/shard_map/ppermute | solution.py:559
  90.5 1.7 %copy-start.4 = (bf16[1632,128]{1,0:T(8,128)(2,1)}, bf16[1632,128]{1,0:T(8,128)(2,1)S(1)}, u32[]{:S(2)}) copy-start(bf16[1632,128]{1,0:T(8,128)(2,1)S(1)} %collective-permute-done.16.refs_3_) | copy-start | bytes 1253380
  90.5 2.3 %collective-permute-start.17 = (bf16[1632,128]{1,0:T(8,128)(2,1)S(1)}, bf16[1632,128]{1,0:T(8,128)(2,1)S(1)}, u32[]{:S(2)}, u32[]{:S(2)}) collective-permute-start(bf16[1632,128]{1,0:T(8,128)(2,1)S(1)} %collective-permute-done.16.refs_3_), channel_id=1, source_target_pairs={{0,1},{1,0},{2,3},{3,2},{4,5},{5,4},{6,7},{7,6},{8,9},{9,8},{10,11... | collective-permute-start | bytes 1253384 | tf_op jit(solution)/shard_map/ppermute | solution.py:559
  92.2 0.8 copy-start.5
  93.0 0.7 copy-start.6
  (1 other events, 0.7 us)

commit v6 on v5

--- a/solution.py
+++ b/solution.py
@@ -1,3 +1,4 @@
+import functools
 import math
 
 import jax
@@ -218,7 +219,7 @@
             pltpu.SemaphoreType.DMA((4,)),
         ],
         compiler_params=params(),
-        cost_estimate=pl.CostEstimate(flops=45 * 10**8, bytes_accessed=8 * 2**20, transcendentals=0),
+        cost_estimate=pl.CostEstimate(flops=6500000000, bytes_accessed=8 * 2**20, transcendentals=0),
         name="scores",
     )(*pieces, *heads, bias, of_track, scale)
 
@@ -525,17 +526,10 @@
     )(ids, mine, *other, conv_w)
 
 
-def sum_kernel(scale, in_hbm, out_ref, terms, sems):
-    copies = [
-        pltpu.make_async_copy(in_hbm.at[pl.ds(i * 4, 4)], terms.at[pl.ds(i * 4, 4)], sems.at[i]) for i in range(4)
-    ]
-    for copy in copies:
-        copy.start()
-    total = jnp.zeros((ROWS, LANES), F32)
-    for i in range(4):
-        copies[i].wait()
-        for s in range(i * 4, i * 4 + 4):
-            total = total + terms[s].astype(F32)
+def sum_kernel(scale, in_ref, out_ref):
+    total = in_ref[0].astype(F32)
+    for s in range(1, in_ref.shape[0]):
+        total = total + in_ref[s].astype(F32)
     total = total * scale
     for l in range(3):
         for k in range(KERNEL):
@@ -545,11 +539,10 @@
 
 def sum_weights(terms, scale):
     return pl.pallas_call(
-        lambda *refs: sum_kernel(scale, *refs),
+        functools.partial(sum_kernel, scale),
         out_shape=jax.ShapeDtypeStruct((KERNEL, 24, 384), F32),
-        in_specs=[HBM],
+        in_specs=[VM],
         out_specs=VM,
-        scratch_shapes=[pltpu.VMEM((16, ROWS, LANES), BF), pltpu.SemaphoreType.DMA((4,))],
         compiler_params=params(30 * MIB),
         name="sum_weights",
     )(terms)
@@ -594,7 +587,8 @@
     send, trunk, head_w = lax.optimization_barrier((send, trunk, head_w))
     far_head = across(head_w)
     near_head = flip(head_w, 1)
-    send, p1, p2, p3, trunk_far = lax.optimization_barrier((send, p1, p2, p3, trunk_far))
+    send, p1, p2 = lax.optimization_barrier((send, p1, p2))
+    p3, trunk_far, far_head = lax.optimization_barrier((p3, trunk_far, far_head))
     got = lax.all_to_all(send, "seq", 0, 0, tiled=True).reshape(SEQ, COT_ROWS, LANES)
     pieces = (p0, p1, p2, p3)
     heads = (head_w, near_head, far_head, flip(far_head, 1))

time: 117 us -> 115 us (0.983)
  starting transfers between devices: 36 us -> 30.7 us
  waiting for transfers between devices: 36.7 us -> 40.4 us
    ppermute x13, waiting for transfers between devices: 6.6 us -> 12.7 us  [flip(): return lax.ppermute(x, 'chan', [(i, i ^ r) for i in range(CHAN)])]
    all_to_all x1, starting transfers between devices: 8.4 us -> 5.18 us  [local(): lax.all_to_all(send, 'seq', 0, 0, tiled=True).reshape(SEQ, COT_ROWS, LANES)]
    ppermute x2, waiting for transfers between devices: 5.63 us -> 2.76 us  [partner(): return lax.ppermute(x, 'seq', [(i, i ^ 8) for i in range(SEQ)])]
    ppermute x1, starting transfers between devices: 4.62 us -> 2.03 us  [partner_far(): return lax.ppermute(x, ('seq', 'chan'), pairs)]
    ppermute x1, waiting for transfers between devices: 0.01 us -> 2.17 us  [across(): return lax.ppermute(x, ('seq', 'chan'), pairs)]
    all_to_all x1, waiting for transfers between devices: 8.68 us -> 7.12 us  [local(): lax.all_to_all(send, 'seq', 0, 0, tiled=True).reshape(SEQ, COT_ROWS, LANES)]
    unnamed x26 -> x30, local copies, waits for them, and re-layouts: 2.01 us -> 2.37 us
  transfers between devices with their start and end apart: 20 -> 20, of which waited for: 10 -> 12; matrix products, arithmetic and copies ran while one was open for 1% -> 1% of each run, Pallas kernels for 29% -> 29%
where the time goes in v6:
time: 115 us
  waiting for transfers between devices  40.4 us (35%)
  Pallas kernels  39.6 us (34%)
  starting transfers between devices  30.7 us (27%)
  local copies, waits for them, and re-layouts  2.37 us (2%)
    ppermute x13, waiting for transfers between devices, flip(): return lax.ppermute(x, 'chan', [(i, i ^ r) for i in range(CHAN)])  12.7 us
    pallas_call x1, Pallas kernels, trunk_grad(): pl.pallas_call(trunk_kernel, out_shape=(jax.ShapeDtypeStruct((BATCH, 256,...  12.3 us
    all_to_all x1, waiting for transfers between devices, local(): lax.all_to_all(terms, 'seq', 0, 0, tiled=True, axis_index_groups=groups)  8.59 us
    ppermute x13, starting transfers between devices, flip(): return lax.ppermute(x, 'chan', [(i, i ^ r) for i in range(CHAN)])  8.47 us
    pallas_call x1, Pallas kernels, weight_grad(): pl.pallas_call(weight_kernel, out_shape=(jax.ShapeDtypeStruct((16, ROWS,...  7.9 us
    all_to_all x1, waiting for transfers between devices, local(): lax.all_to_all(send, 'seq', 0, 0, tiled=True).reshape(SEQ, COT_ROWS, LANES)  7.12 us
    ppermute x1, waiting for transfers between devices, partner_far(): return lax.ppermute(x, ('seq', 'chan'), pairs)  7.07 us
    pallas_call x1, Pallas kernels, scores(): pl.pallas_call(score_kernel, out_shape=(jax.ShapeDtypeStruct((WIDE, TRACK...  5.59 us
  transfers between devices with their start and end apart: 20, of which 12 were waited for; matrix products, arithmetic and copies ran while one was open for 1% of the time, Pallas kernels for 29%

profile of v6, /device:TPU:0, one launch (start us, length us, event | category | flops | bytes accessed | tf_op | source)
XLA Modules:
  0.0 114.6 jit_solution(1872015064100720651)
XLA Ops:
  0.6 3.4 %collective-permute-start.3 = (bf16[4,256,384]{2,1,0:T(8,128)(2,1)}, bf16[4,256,384]{2,1,0:T(8,128)(2,1)S(1)}, u32[]{:S(2)}, u32[]{:S(2)}) collective-permute-start(bf16[4,256,384]{2,1,0:T(8,128)(2,1)} %own_ref), channel_id=1, source_target_pairs={{0,32},{4,36},{8,40},{12,44},{16,48},{20,52},{24,56},{28,60},{32,0... | collective-permute-start | bytes 2359304 | tf_op jit(solution)/shard_map/ppermute | solution.py:556
  4.5 2.8 %cut_pieces.1 = (bf16[784,128]{1,0:T(8,128)(2,1)}, bf16[784,128]{1,0:T(8,128)(2,1)}, bf16[784,128]{1,0:T(8,128)(2,1)}, bf16[784,128]{1,0:T(8,128)(2,1)}) custom-call(s32[4]{0:T(128)} %pad_add_fusion.ids_ref, bf16[4,192,512]{2,1,0:T(8,128)(2,1)} %merged_ref.1, f32[1,192]{1,0:T(1,128)} %bitcast.12), custom_call_target="tpu_custom_call" | custom-call | tf_op jit(solution)/shard_map/cut_pieces/pallas_call | solution.py:70
  7.4 3.5 %cut_cot.1 = bf16[32,9,16,128]{3,2,1,0:T(8,128)(2,1)} custom-call(s32[4]{0:T(128)} %pad_add_fusion.ids_ref, bf16[8,16,16384]{2,1,0:T(8,128)(2,1)} %bitcast.11, bf16[4,256,384]{2,1,0:T(8,128)(2,1)} %own_ref), custom_call_target="tpu_custom_call" | custom-call | bytes 5242880 | tf_op jit(solution)/shard_map/cut_cot/pallas_call | solution.py:116
  10.9 4.1 %collective-permute-start.4 = (bf16[192,1024]{1,0:T(8,128)(2,1)}, bf16[192,1024]{1,0:T(8,128)(2,1)S(1)}, u32[]{:S(2)}, u32[]{:S(2)}) collective-permute-start(bf16[192,1024]{1,0:T(8,128)(2,1)} %refs_4_), channel_id=1, source_target_pairs={{0,66},{1,67},{2,64},{3,65},{4,70},{5,71},{6,68},{7,69},{8,74},{9,... | collective-permute-start | bytes 1179656 | tf_op jit(solution)/shard_map/ppermute | solution.py:572
  15.1 3.3 %collective-permute-start.2 = (bf16[784,128]{1,0:T(8,128)(2,1)}, bf16[784,128]{1,0:T(8,128)(2,1)S(1)}, u32[]{:S(2)}, u32[]{:S(2)}) collective-permute-start(bf16[784,128]{1,0:T(8,128)(2,1)} %get-tuple-element.49), channel_id=1, source_target_pairs={{0,3},{1,2},{2,1},{3,0},{4,7},{5,6},{6,5},{7,4},{8,11},{9,10},{10,... | collective-permute-start | bytes 602120 | tf_op jit(solution)/shard_map/ppermute | solution.py:552
  18.4 6.1 %collective-permute-done.1.refs_2_ = bf16[784,128]{1,0:T(8,128)(2,1)S(1)} collective-permute-done((bf16[784,128]{1,0:T(8,128)(2,1)S(1)}, bf16[784,128]{1,0:T(8,128)(2,1)S(1)}, u32[]{:S(2)}, u32[]{:S(2)}) %collective-permute-start.1) | collective-permute-done | bytes 200736 | tf_op jit(solution)/shard_map/ppermute | solution.py:552
  24.5 0.7 copy-done.11
  25.2 5.2 %all-to-all-start = ((bf16[32,9,16,128]{3,2,1,0:T(8,128)(2,1)}), bf16[32,9,16,128]{3,2,1,0:T(8,128)(2,1)S(1)}, u32[]{:S(2)}, u32[]{:S(2)}) async-start(bf16[32,9,16,128]{3,2,1,0:T(8,128)(2,1)} %cut_cot.1), calls=%async_computation | async-start | bytes 2359296 | tf_op jit(solution)/shard_map/all_to_all | solution.py:592
  30.5 2.2 %collective-permute-done.4.refs_6_ = bf16[192,1024]{1,0:T(8,128)(2,1)S(1)} collective-permute-done((bf16[192,1024]{1,0:T(8,128)(2,1)}, bf16[192,1024]{1,0:T(8,128)(2,1)S(1)}, u32[]{:S(2)}, u32[]{:S(2)}) %collective-permute-start.4) | collective-permute-done | bytes 393248 | tf_op jit(solution)/shard_map/ppermute | solution.py:572
  32.8 1.7 %collective-permute-done.6.refs_7_ = bf16[192,1024]{1,0:T(8,128)(2,1)S(1)} collective-permute-done((bf16[192,1024]{1,0:T(8,128)(2,1)S(1)}, bf16[192,1024]{1,0:T(8,128)(2,1)S(1)}, u32[]{:S(2)}, u32[]{:S(2)}) %collective-permute-start.6) | collective-permute-done | bytes 393248 | tf_op jit(solution)/shard_map/ppermute | solution.py:552
  34.5 0.7 copy-done.9
  35.2 5.6 %scores.1 = (f32[9,1024,512]{2,1,0:T(8,128)}, bf16[12,768,1024]{2,1,0:T(8,128)(2,1)}) custom-call(bf16[784,128]{1,0:T(8,128)(2,1)} %get-tuple-element.39.refs_0_, bf16[784,128]{1,0:T(8,128)(2,1)} %copy-done.10, bf16[784,128]{1,0:T(8,128)(2,1)} %copy-done.11, bf16[784,128]{1,0:T(8,128)(2,1)} %copy-done.12, bf16[192,1024]{1,0:T(8,128)(2,1)} %refs_4_, ...), custom_call_target="tpu_custom_call" | custom-call | flops 6499999744 | bytes 8388608 | tf_op jit(solution)/shard_map/scores/pallas_call | solution.py:204
  40.8 7.1 %all-to-all-done = bf16[32,9,16,128]{3,2,1,0:T(8,128)(2,1)S(1)} async-done(((bf16[32,9,16,128]{3,2,1,0:T(8,128)(2,1)}), bf16[32,9,16,128]{3,2,1,0:T(8,128)(2,1)S(1)}, u32[]{:S(2)}, u32[]{:S(2)}) %all-to-all-start) | async-done | bytes 1179680 | tf_op jit(solution)/shard_map/all_to_all | solution.py:592
  47.9 5.0 %head.1 = (bf16[1536,128]{1,0:T(8,128)(2,1)S(1)}, bf16[1536,128]{1,0:T(8,128)(2,1)S(1)}, bf16[96,128]{1,0:T(8,128)(2,1)S(1)}) custom-call(s32[4]{0:T(128)S(1)} %copy-done.1, s32[4]{0:T(128)S(1)} %copy-done.2, f32[9,1024,512]{2,1,0:T(8,128)} %get-tuple-element.53.wide_hbm, bf16[12,768,1024]{2,1,0:T(8,128)(2,1)} %get-tuple-element.54.narrow_hbm, ...), custom_call_target="tpu_custom_call" | custom-call | tf_op jit(solution)/shard_map/head/pallas_call | solution.py:292
  53.0 2.0 %collective-permute-start.10 = (bf16[1536,128]{1,0:T(8,128)(2,1)S(1)}, bf16[1536,128]{1,0:T(8,128)(2,1)S(1)}, u32[]{:S(2)}, u32[]{:S(2)}) collective-permute-start(bf16[1536,128]{1,0:T(8,128)(2,1)S(1)} %get-tuple-element.57), channel_id=1, source_target_pairs={{0,34},{1,35},{2,32},{3,33},{4,38},{5,39},{6,36},{7,37},{8,42},{9,... | collective-permute-start | bytes 1179656 | tf_op jit(solution)/shard_map/ppermute | solution.py:561
  55.0 2.0 %collective-permute-start.9 = (bf16[1536,128]{1,0:T(8,128)(2,1)S(1)}, bf16[1536,128]{1,0:T(8,128)(2,1)S(1)}, u32[]{:S(2)}, u32[]{:S(2)}) collective-permute-start(bf16[1536,128]{1,0:T(8,128)(2,1)S(1)} %get-tuple-element.57), channel_id=1, source_target_pairs={{0,32},{4,36},{8,40},{12,44},{16,48},{20,52},{24,56},{28,60},{32,0... | collective-permute-start | bytes 1179656 | tf_op jit(solution)/shard_map/ppermute | solution.py:556
  57.1 2.5 %collective-permute-start.8 = (bf16[1536,128]{1,0:T(8,128)(2,1)S(1)}, bf16[1536,128]{1,0:T(8,128)(2,1)S(1)}, u32[]{:S(2)}, u32[]{:S(2)}) collective-permute-start(bf16[1536,128]{1,0:T(8,128)(2,1)S(1)} %get-tuple-element.56.refs_0_), channel_id=1, source_target_pairs={{0,2},{1,3},{2,0},{3,1},{4,6},{5,7},{6,4},{7,5},{8,10},{9,11},{10,... | collective-permute-start | bytes 1179656 | tf_op jit(solution)/shard_map/ppermute | solution.py:552
  59.6 0.7 collective-permute-start.11
  60.3 1.6 %trunk_rows.1 = (bf16[2,1024,1152]{2,1,0:T(8,128)(2,1)S(1)}, bf16[128,1920]{1,0:T(8,128)(2,1)S(1)}) custom-call(s32[4]{0:T(128)S(1)} %copy-done.1, bf16[4,256,384]{2,1,0:T(8,128)(2,1)S(1)} %copy-done, bf16[4,256,384]{2,1,0:T(8,128)(2,1)S(1)} %collective-permute-done.3.far_ref, bf16[32,144,128]{2,1,0:T(8,128)(2,1)S(1)} %bitcast.10), custom_call_target="tpu_custom_call" | custom-call | flops 10000000 | bytes 8388608 | tf_op jit(solution)/shard_map/trunk_rows/pallas_call | solution.py:355
  62.0 7.1 %collective-permute-done.10.refs_6_ = bf16[1536,128]{1,0:T(8,128)(2,1)S(1)} collective-permute-done((bf16[1536,128]{1,0:T(8,128)(2,1)S(1)}, bf16[1536,128]{1,0:T(8,128)(2,1)S(1)}, u32[]{:S(2)}, u32[]{:S(2)}) %collective-permute-start.10) | collective-permute-done | bytes 393248 | tf_op jit(solution)/shard_map/ppermute | solution.py:561
  69.1 2.8 %collective-permute-done.9.refs_4_ = bf16[1536,128]{1,0:T(8,128)(2,1)S(1)} collective-permute-done((bf16[1536,128]{1,0:T(8,128)(2,1)S(1)}, bf16[1536,128]{1,0:T(8,128)(2,1)S(1)}, u32[]{:S(2)}, u32[]{:S(2)}) %collective-permute-start.9) | collective-permute-done | bytes 393248 | tf_op jit(solution)/shard_map/ppermute | solution.py:556
  71.8 2.0 %collective-permute-done.8.refs_2_ = bf16[1536,128]{1,0:T(8,128)(2,1)S(1)} collective-permute-done((bf16[1536,128]{1,0:T(8,128)(2,1)S(1)}, bf16[1536,128]{1,0:T(8,128)(2,1)S(1)}, u32[]{:S(2)}, u32[]{:S(2)}) %collective-permute-start.8) | collective-permute-done | bytes 393248 | tf_op jit(solution)/shard_map/ppermute | solution.py:552
  74.4 1.2 %collective-permute-start.16 = (bf16[1632,128]{1,0:T(8,128)(2,1)S(1)}, bf16[1632,128]{1,0:T(8,128)(2,1)S(1)}, u32[]{:S(2)}, u32[]{:S(2)}) collective-permute-start(bf16[1632,128]{1,0:T(8,128)(2,1)S(1)} %pad_maximum_fusion.refs_1_), channel_id=1, source_target_pairs={{0,2},{1,3},{2,0},{3,1},{4,6},{5,7},{6,4},{7,5},{8,10},{9,11},{10,... | collective-permute-start | bytes 1253384 | tf_op jit(solution)/shard_map/ppermute | solution.py:552
  76.1 0.6 collective-permute-done.12.refs_3_
  76.7 7.9 %weight_grad.1 = (bf16[16,368,128]{2,1,0:T(8,128)(2,1)}, bf16[18,1536,512]{2,1,0:T(8,128)(2,1)}) custom-call(s32[4]{0:T(128)S(1)} %copy-done.1, bf16[1536,128]{1,0:T(8,128)(2,1)S(1)} %get-tuple-element.56.refs_0_, bf16[1536,128]{1,0:T(8,128)(2,1)S(1)} %collective-permute-done.7.refs_1_, bf16[1536,128]{1,0:T(8,128)(2,1)S(1)} %collective-permute-done.8.refs_2_, ...), custom_call_target="tpu_custom_call" | custom-call | flops 4000000000 | bytes 10485760 | tf_op jit(solution)/shard_map/weight_grad/pallas_call | solution.py:438
  84.6 4.8 %all-to-all-start.1 = ((bf16[16,368,128]{2,1,0:T(8,128)(2,1)}), bf16[16,368,128]{2,1,0:T(8,128)(2,1)S(1)}, u32[]{:S(2)}, u32[]{:S(2)}) async-start(bf16[16,368,128]{2,1,0:T(8,128)(2,1)} %get-tuple-element.74), calls=%async_computation.1 | async-start | bytes 3014656 | tf_op jit(solution)/shard_map/all_to_all | solution.py:613
  90.0 1.2 %collective-permute-done.15.refs_2_ = bf16[1632,128]{1,0:T(8,128)(2,1)S(1)} collective-permute-done((bf16[1632,128]{1,0:T(8,128)(2,1)S(1)}, bf16[1632,128]{1,0:T(8,128)(2,1)S(1)}, u32[]{:S(2)}, u32[]{:S(2)}) %collective-permute-start.15) | collective-permute-done | bytes 417824 | tf_op jit(solution)/shard_map/ppermute | solution.py:552
  91.3 0.6 collective-permute-done.17.refs_4_
  92.0 0.7 copy-done.6
  92.8 12.3 %trunk_grad.1 = (bf16[4,256,384]{2,1,0:T(8,128)(2,1)}, bf16[4,192,512]{2,1,0:T(8,128)(2,1)}) custom-call(s32[4]{0:T(128)} %pad_add_fusion.ids_ref, bf16[18,1536,512]{2,1,0:T(8,128)(2,1)} %get-tuple-element.69.refs_0_, bf16[1632,128]{1,0:T(8,128)(2,1)} %copy-done.3, bf16[1632,128]{1,0:T(8,128)(2,1)} %copy-done.5, bf16[1632,128]{1,0:T(8,128)(2,1)} %copy-done.4, ...), custom_call_target="tpu_custom_call" | custom-call | flops 8000000000 | bytes 16777216 | tf_op jit(solution)/shard_map/trunk_grad/pallas_call | solution.py:513
  105.1 8.6 %all-to-all-done.1.in_ref = bf16[16,368,128]{2,1,0:T(8,128)(2,1)S(1)} async-done(((bf16[16,368,128]{2,1,0:T(8,128)(2,1)}), bf16[16,368,128]{2,1,0:T(8,128)(2,1)S(1)}, u32[]{:S(2)}, u32[]{:S(2)}) %all-to-all-start.1) | async-done | bytes 1507360 | tf_op jit(solution)/shard_map/all_to_all | solution.py:613
  113.7 0.9 sum_weights.1
  (48 shorter events, 2.8 us)
Async XLA Ops:
  0.6 32.0 %collective-permute-start.3 = (bf16[4,256,384]{2,1,0:T(8,128)(2,1)}, bf16[4,256,384]{2,1,0:T(8,128)(2,1)S(1)}, u32[]{:S(2)}, u32[]{:S(2)}) collective-permute-start(bf16[4,256,384]{2,1,0:T(8,128)(2,1)} %own_ref), channel_id=1, source_target_pairs={{0,32},{4,36},{8,40},{12,44},{16,48},{20,52},{24,56},{28,60},{32,0... | collective-permute-start | bytes 2359304 | tf_op jit(solution)/shard_map/ppermute | solution.py:556
  7.4 7.6 %copy-start.14 = (bf16[784,128]{1,0:T(8,128)(2,1)S(1)}, bf16[784,128]{1,0:T(8,128)(2,1)}, u32[]{:S(2)}) copy-start(bf16[784,128]{1,0:T(8,128)(2,1)} %get-tuple-element.45) | copy-start | bytes 602116
  7.4 7.6 %copy-start.13 = (bf16[784,128]{1,0:T(8,128)(2,1)S(1)}, bf16[784,128]{1,0:T(8,128)(2,1)}, u32[]{:S(2)}) copy-start(bf16[784,128]{1,0:T(8,128)(2,1)} %get-tuple-element.46) | copy-start | bytes 602116
  10.9 21.8 %collective-permute-start.4 = (bf16[192,1024]{1,0:T(8,128)(2,1)}, bf16[192,1024]{1,0:T(8,128)(2,1)S(1)}, u32[]{:S(2)}, u32[]{:S(2)}) collective-permute-start(bf16[192,1024]{1,0:T(8,128)(2,1)} %refs_4_), channel_id=1, source_target_pairs={{0,66},{1,67},{2,64},{3,65},{4,70},{5,71},{6,68},{7,69},{8,74},{9,... | collective-permute-start | bytes 1179656 | tf_op jit(solution)/shard_map/ppermute | solution.py:572
  15.0 3.4 %collective-permute-start = (bf16[784,128]{1,0:T(8,128)(2,1)S(1)}, bf16[784,128]{1,0:T(8,128)(2,1)S(1)}, u32[]{:S(2)}, u32[]{:S(2)}) collective-permute-start(bf16[784,128]{1,0:T(8,128)(2,1)S(1)} %copy-done.14), channel_id=1, source_target_pairs={{0,1},{1,0},{2,3},{3,2},{4,5},{5,4},{6,7},{7,6},{8,9},{9,8},{10,11... | collective-permute-start | bytes 602120 | tf_op jit(solution)/shard_map/ppermute | solution.py:552
  15.0 9.5 %collective-permute-start.1 = (bf16[784,128]{1,0:T(8,128)(2,1)S(1)}, bf16[784,128]{1,0:T(8,128)(2,1)S(1)}, u32[]{:S(2)}, u32[]{:S(2)}) collective-permute-start(bf16[784,128]{1,0:T(8,128)(2,1)S(1)} %copy-done.13), channel_id=1, source_target_pairs={{0,2},{1,3},{2,0},{3,1},{4,6},{5,7},{6,4},{7,5},{8,10},{9,11},{10,... | collective-permute-start | bytes 602120 | tf_op jit(solution)/shard_map/ppermute | solution.py:552
  15.1 15.4 %collective-permute-start.2 = (bf16[784,128]{1,0:T(8,128)(2,1)}, bf16[784,128]{1,0:T(8,128)(2,1)S(1)}, u32[]{:S(2)}, u32[]{:S(2)}) collective-permute-start(bf16[784,128]{1,0:T(8,128)(2,1)} %get-tuple-element.49), channel_id=1, source_target_pairs={{0,3},{1,2},{2,1},{3,0},{4,7},{5,6},{6,5},{7,4},{8,11},{9,10},{10,... | collective-permute-start | bytes 602120 | tf_op jit(solution)/shard_map/ppermute | solution.py:552
  18.4 6.1 %copy-start.10 = (bf16[784,128]{1,0:T(8,128)(2,1)}, bf16[784,128]{1,0:T(8,128)(2,1)S(1)}, u32[]{:S(2)}) copy-start(bf16[784,128]{1,0:T(8,128)(2,1)S(1)} %collective-permute-done.refs_1_) | copy-start | bytes 602116
  25.2 22.8 %all-to-all-start = ((bf16[32,9,16,128]{3,2,1,0:T(8,128)(2,1)}), bf16[32,9,16,128]{3,2,1,0:T(8,128)(2,1)S(1)}, u32[]{:S(2)}, u32[]{:S(2)}) async-start(bf16[32,9,16,128]{3,2,1,0:T(8,128)(2,1)} %cut_cot.1), calls=%async_computation | async-start | bytes 2359296 | tf_op jit(solution)/shard_map/all_to_all | solution.py:592
  30.4 2.4 %collective-permute-start.5 = (bf16[192,1024]{1,0:T(8,128)(2,1)}, bf16[192,1024]{1,0:T(8,128)(2,1)S(1)}, u32[]{:S(2)}, u32[]{:S(2)}) collective-permute-start(bf16[192,1024]{1,0:T(8,128)(2,1)} %refs_4_), channel_id=1, source_target_pairs={{0,1},{1,0},{2,3},{3,2},{4,5},{5,4},{6,7},{7,6},{8,9},{9,8},{10,11... | collective-permute-start | bytes 1179656 | tf_op jit(solution)/shard_map/ppermute | solution.py:552
  30.5 2.2 %copy-start.12 = (bf16[784,128]{1,0:T(8,128)(2,1)}, bf16[784,128]{1,0:T(8,128)(2,1)S(1)}, u32[]{:S(2)}) copy-start(bf16[784,128]{1,0:T(8,128)(2,1)S(1)} %collective-permute-done.2.refs_3_) | copy-start | bytes 602116
  32.7 1.8 %copy-start.7 = (bf16[192,1024]{1,0:T(8,128)(2,1)}, bf16[192,1024]{1,0:T(8,128)(2,1)S(1)}, u32[]{:S(2)}) copy-start(bf16[192,1024]{1,0:T(8,128)(2,1)S(1)} %collective-permute-done.4.refs_6_) | copy-start | bytes 1179652
  32.7 1.8 %collective-permute-start.6 = (bf16[192,1024]{1,0:T(8,128)(2,1)S(1)}, bf16[192,1024]{1,0:T(8,128)(2,1)S(1)}, u32[]{:S(2)}, u32[]{:S(2)}) collective-permute-start(bf16[192,1024]{1,0:T(8,128)(2,1)S(1)} %collective-permute-done.4.refs_6_), channel_id=1, source_target_pairs={{0,1},{1,0},{2,3},{3,2},{4,5},{5,4},{6,7},{7,6},{8,9},{9,8},{10,11... | collective-permute-start | bytes 1179656 | tf_op jit(solution)/shard_map/ppermute | solution.py:552
  32.8 1.7 %copy-start.8 = (bf16[192,1024]{1,0:T(8,128)(2,1)}, bf16[192,1024]{1,0:T(8,128)(2,1)S(1)}, u32[]{:S(2)}) copy-start(bf16[192,1024]{1,0:T(8,128)(2,1)S(1)} %collective-permute-done.5.refs_5_) | copy-start | bytes 1179652
  35.2 12.7 %copy-start.1 = (s32[4]{0:T(128)S(1)}, s32[4]{0:T(128)}, u32[]{:S(2)}) copy-start(s32[4]{0:T(128)} %pad_add_fusion.ids_ref) | copy-start | bytes 52
  35.2 12.7 %copy-start.2 = (s32[4]{0:T(128)S(1)}, s32[4]{0:T(128)}, u32[]{:S(2)}) copy-start(s32[4]{0:T(128)} %valid_ref.1) | copy-start | bytes 52
  47.9 12.4 %copy-start = (bf16[4,256,384]{2,1,0:T(8,128)(2,1)S(1)}, bf16[4,256,384]{2,1,0:T(8,128)(2,1)}, u32[]{:S(2)}) copy-start(bf16[4,256,384]{2,1,0:T(8,128)(2,1)} %own_ref) | copy-start | bytes 2359300
  53.0 16.1 %collective-permute-start.10 = (bf16[1536,128]{1,0:T(8,128)(2,1)S(1)}, bf16[1536,128]{1,0:T(8,128)(2,1)S(1)}, u32[]{:S(2)}, u32[]{:S(2)}) collective-permute-start(bf16[1536,128]{1,0:T(8,128)(2,1)S(1)} %get-tuple-element.57), channel_id=1, source_target_pairs={{0,34},{1,35},{2,32},{3,33},{4,38},{5,39},{6,36},{7,37},{8,42},{9,... | collective-permute-start | bytes 1179656 | tf_op jit(solution)/shard_map/ppermute | solution.py:561
  55.0 16.8 %collective-permute-start.9 = (bf16[1536,128]{1,0:T(8,128)(2,1)S(1)}, bf16[1536,128]{1,0:T(8,128)(2,1)S(1)}, u32[]{:S(2)}, u32[]{:S(2)}) collective-permute-start(bf16[1536,128]{1,0:T(8,128)(2,1)S(1)} %get-tuple-element.57), channel_id=1, source_target_pairs={{0,32},{4,36},{8,40},{12,44},{16,48},{20,52},{24,56},{28,60},{32,0... | collective-permute-start | bytes 1179656 | tf_op jit(solution)/shard_map/ppermute | solution.py:556
  57.1 16.8 %collective-permute-start.8 = (bf16[1536,128]{1,0:T(8,128)(2,1)S(1)}, bf16[1536,128]{1,0:T(8,128)(2,1)S(1)}, u32[]{:S(2)}, u32[]{:S(2)}) collective-permute-start(bf16[1536,128]{1,0:T(8,128)(2,1)S(1)} %get-tuple-element.56.refs_0_), channel_id=1, source_target_pairs={{0,2},{1,3},{2,0},{3,1},{4,6},{5,7},{6,4},{7,5},{8,10},{9,11},{10,... | collective-permute-start | bytes 1179656 | tf_op jit(solution)/shard_map/ppermute | solution.py:552
  59.6 2.4 %collective-permute-start.11 = (bf16[96,128]{1,0:T(8,128)(2,1)S(1)}, bf16[96,128]{1,0:T(8,128)(2,1)S(1)}, u32[]{:S(2)}, u32[]{:S(2)}) collective-permute-start(bf16[96,128]{1,0:T(8,128)(2,1)S(1)} %get-tuple-element.58), channel_id=1, source_target_pairs={{3,4},{7,8},{11,12},{15,16},{19,20},{23,24},{27,28},{31,32},{35,36... | collective-permute-start | bytes 73736 | tf_op jit(solution)/shard_map/ppermute | solution.py:567
  60.2 15.4 %collective-permute-start.7 = (bf16[1536,128]{1,0:T(8,128)(2,1)S(1)}, bf16[1536,128]{1,0:T(8,128)(2,1)S(1)}, u32[]{:S(2)}, u32[]{:S(2)}) collective-permute-start(bf16[1536,128]{1,0:T(8,128)(2,1)S(1)} %get-tuple-element.56.refs_0_), channel_id=1, source_target_pairs={{0,1},{1,0},{2,3},{3,2},{4,5},{5,4},{6,7},{7,6},{8,9},{9,8},{10,11... | collective-permute-start | bytes 1179656 | tf_op jit(solution)/shard_map/ppermute | solution.py:552
  62.0 27.4 %copy-start.3 = (bf16[1632,128]{1,0:T(8,128)(2,1)}, bf16[1632,128]{1,0:T(8,128)(2,1)S(1)}, u32[]{:S(2)}) copy-start(bf16[1632,128]{1,0:T(8,128)(2,1)S(1)} %pad_maximum_fusion.refs_1_) | copy-start | bytes 1253380
  73.8 1.8 %collective-permute-start.13 = (bf16[1536,128]{1,0:T(8,128)(2,1)S(1)}, bf16[1536,128]{1,0:T(8,128)(2,1)S(1)}, u32[]{:S(2)}, u32[]{:S(2)}) collective-permute-start(bf16[1536,128]{1,0:T(8,128)(2,1)S(1)} %collective-permute-done.9.refs_4_), channel_id=1, source_target_pairs={{0,1},{1,0},{2,3},{3,2},{4,5},{5,4},{6,7},{7,6},{8,9},{9,8},{10,11... | collective-permute-start | bytes 1179656 | tf_op jit(solution)/shard_map/ppermute | solution.py:552
  73.8 2.3 %collective-permute-start.14 = (bf16[1536,128]{1,0:T(8,128)(2,1)S(1)}, bf16[1536,128]{1,0:T(8,128)(2,1)S(1)}, u32[]{:S(2)}, u32[]{:S(2)}) collective-permute-start(bf16[1536,128]{1,0:T(8,128)(2,1)S(1)} %collective-permute-done.10.refs_6_), channel_id=1, source_target_pairs={{0,1},{1,0},{2,3},{3,2},{4,5},{5,4},{6,7},{7,6},{8,9},{9,8},{10,11... | collective-permute-start | bytes 1179656 | tf_op jit(solution)/shard_map/ppermute | solution.py:552
  74.3 2.3 %collective-permute-start.12 = (bf16[1536,128]{1,0:T(8,128)(2,1)S(1)}, bf16[1536,128]{1,0:T(8,128)(2,1)S(1)}, u32[]{:S(2)}, u32[]{:S(2)}) collective-permute-start(bf16[1536,128]{1,0:T(8,128)(2,1)S(1)} %collective-permute-done.8.refs_2_), channel_id=1, source_target_pairs={{0,1},{1,0},{2,3},{3,2},{4,5},{5,4},{6,7},{7,6},{8,9},{9,8},{10,11... | collective-permute-start | bytes 1179656 | tf_op jit(solution)/shard_map/ppermute | solution.py:552
  74.4 15.2 %collective-permute-start.16 = (bf16[1632,128]{1,0:T(8,128)(2,1)S(1)}, bf16[1632,128]{1,0:T(8,128)(2,1)S(1)}, u32[]{:S(2)}, u32[]{:S(2)}) collective-permute-start(bf16[1632,128]{1,0:T(8,128)(2,1)S(1)} %pad_maximum_fusion.refs_1_), channel_id=1, source_target_pairs={{0,2},{1,3},{2,0},{3,1},{4,6},{5,7},{6,4},{7,5},{8,10},{9,11},{10,... | collective-permute-start | bytes 1253384 | tf_op jit(solution)/shard_map/ppermute | solution.py:552
  84.6 29.1 %all-to-all-start.1 = ((bf16[16,368,128]{2,1,0:T(8,128)(2,1)}), bf16[16,368,128]{2,1,0:T(8,128)(2,1)S(1)}, u32[]{:S(2)}, u32[]{:S(2)}) async-start(bf16[16,368,128]{2,1,0:T(8,128)(2,1)} %get-tuple-element.74), calls=%async_computation.1 | async-start | bytes 3014656 | tf_op jit(solution)/shard_map/all_to_all | solution.py:613
  89.4 1.8 %collective-permute-start.15 = (bf16[1632,128]{1,0:T(8,128)(2,1)S(1)}, bf16[1632,128]{1,0:T(8,128)(2,1)S(1)}, u32[]{:S(2)}, u32[]{:S(2)}) collective-permute-start(bf16[1632,128]{1,0:T(8,128)(2,1)S(1)} %pad_maximum_fusion.refs_1_), channel_id=1, source_target_pairs={{0,1},{1,0},{2,3},{3,2},{4,5},{5,4},{6,7},{7,6},{8,9},{9,8},{10,11... | collective-permute-start | bytes 1253384 | tf_op jit(solution)/shard_map/ppermute | solution.py:552
  89.6 1.7 %copy-start.4 = (bf16[1632,128]{1,0:T(8,128)(2,1)}, bf16[1632,128]{1,0:T(8,128)(2,1)S(1)}, u32[]{:S(2)}) copy-start(bf16[1632,128]{1,0:T(8,128)(2,1)S(1)} %collective-permute-done.16.refs_3_) | copy-start | bytes 1253380
  89.6 2.3 %collective-permute-start.17 = (bf16[1632,128]{1,0:T(8,128)(2,1)S(1)}, bf16[1632,128]{1,0:T(8,128)(2,1)S(1)}, u32[]{:S(2)}, u32[]{:S(2)}) collective-permute-start(bf16[1632,128]{1,0:T(8,128)(2,1)S(1)} %collective-permute-done.16.refs_3_), channel_id=1, source_target_pairs={{0,1},{1,0},{2,3},{3,2},{4,5},{5,4},{6,7},{7,6},{8,9},{9,8},{10,11... | collective-permute-start | bytes 1253384 | tf_op jit(solution)/shard_map/ppermute | solution.py:552
  92.0 0.8 copy-start.6
  (3 other events, 2.2 us)

commit v7 on v6

--- a/solution.py
+++ b/solution.py
@@ -131,10 +131,8 @@
 
 def score_kernel(*refs):
     pieces, heads, (bias_ref, of_track_ref, scale_ref) = refs[:4], refs[4:8], refs[8:11]
-    wide_hbm, narrow_hbm, raw_ref, small_ref, weights_ref, merged_ref = refs[11:17]
-    parts, sems, head_sems, part_sems, out_sems = refs[17:]
-    cols_ref = small_ref.at[:, 0:LANES]
-    gain_ref = small_ref.at[0:C_OUT, LANES : 2 * LANES]
+    wide_hbm, narrow_hbm, raw_ref, cols_ref, inv_ref, gain_ref, weights_ref, merged_ref = refs[11:19]
+    parts, sems, head_sems, part_sems, out_sems = refs[19:]
     copies = []
     for r in range(CHAN):
         rows = pl.ds(r * 192, 192)
@@ -180,14 +178,15 @@
     total = jnp.sum(m32 * m32, axis=0, keepdims=True)
     inv = lax.rsqrt(total / C_OUT + epsilon)
     for b in range(BATCH):
-        small_ref[8 * b : 8 * b + 8, 2 * LANES : 3 * LANES] = jnp.broadcast_to(
-            inv[:, b * LANES : (b + 1) * LANES], (8, LANES)
-        )
+        inv_ref[8 * b : 8 * b + 8, :] = jnp.broadcast_to(inv[:, b * LANES : (b + 1) * LANES], (8, LANES))
+    lane = lax.broadcasted_iota(jnp.int32, (C_OUT, LANES), 1)
+    cols_ref[0:C_OUT, :] = jnp.where(lane == 2, gain_ref[...], cols_ref[0:C_OUT, :])
     normed = (m32 * gain_ref[:, 0:1]).astype(BF)
     for load in loads:
         load.wait()
     stores = [
-        pltpu.make_async_copy(small_ref, wide_hbm.at[1, :, pl.ds(0, 3 * LANES)], out_sems.at[0]),
+        pltpu.make_async_copy(cols_ref, wide_hbm.at[1, :, pl.ds(0, LANES)], out_sems.at[0]),
+        pltpu.make_async_copy(inv_ref, wide_hbm.at[1, pl.ds(0, 32), pl.ds(LANES, LANES)], out_sems.at[4]),
         pltpu.make_async_copy(weights_ref, narrow_hbm.at[0], out_sems.at[1]),
         pltpu.make_async_copy(merged_ref, narrow_hbm.at[1, :, pl.ds(0, BATCH * LANES)], out_sems.at[2]),
     ]
@@ -209,14 +208,16 @@
         out_specs=(HBM, HBM),
         scratch_shapes=[
             pltpu.VMEM((TRACKS, BATCH * LANES), F32),
-            pltpu.VMEM((TRACKS, 3 * LANES), F32),
+            pltpu.VMEM((TRACKS, LANES), F32),
+            pltpu.VMEM((32, LANES), F32),
+            pltpu.VMEM((C_OUT, LANES), F32),
             pltpu.VMEM((C_OUT, TRACKS), BF),
             pltpu.VMEM((C_OUT, BATCH * LANES), BF),
             pltpu.VMEM((CHAN, 16, LANES), BF),
             pltpu.SemaphoreType.DMA((CHAN, BATCH)),
             pltpu.SemaphoreType.DMA((CHAN,)),
             pltpu.SemaphoreType.DMA((CHAN,)),
-            pltpu.SemaphoreType.DMA((4,)),
+            pltpu.SemaphoreType.DMA((5,)),
         ],
         compiler_params=params(),
         cost_estimate=pl.CostEstimate(flops=6500000000, bytes_accessed=8 * 2**20, transcendentals=0),
@@ -229,10 +230,12 @@
 
 def head_kernel(
     ids_ref, valid_ref, wide_hbm, narrow_hbm, cot_ref,
-    mine_ref, other_ref, edge_ref, full, raw_ref, small_ref, weights_ref, merged_ref, sems
+    mine_ref, other_ref, edge_ref, full, raw_ref, cols_ref, inv_ref, weights_ref, merged_ref, sems
 ):
-    load_small = pltpu.make_async_copy(wide_hbm.at[1, :, pl.ds(0, 3 * LANES)], small_ref, sems.at[1, 2])
-    load_small.start()
+    load_cols = pltpu.make_async_copy(wide_hbm.at[1, :, pl.ds(0, LANES)], cols_ref, sems.at[1, 2])
+    load_inv = pltpu.make_async_copy(wide_hbm.at[1, pl.ds(0, 32), pl.ds(LANES, LANES)], inv_ref, sems.at[1, 3])
+    load_cols.start()
+    load_inv.start()
     loads = []
     for b in range(BATCH):
         loads.append(
@@ -244,19 +247,20 @@
         copy.start()
     load_weights.start()
     load_merged.start()
-    load_small.wait()
+    load_cols.wait()
+    load_inv.wait()
     me = ids_ref[0]
     first = ids_ref[1]
     half = ids_ref[2]
-    scale = small_ref[:, 1:2]
-    bias = small_ref[:, 0:1]
+    scale = cols_ref[:, 1:2]
+    bias = cols_ref[:, 0:1]
     lane = lax.broadcasted_iota(jnp.int32, (1, LANES), 1)
     scaled, coefs = [], []
     for b in range(BATCH):
         cols = slice(b * LANES, (b + 1) * LANES)
         loads[b].wait()
         raw = raw_ref[b]
-        inv = small_ref[8 * b : 8 * b + 1, 2 * LANES : 3 * LANES]
+        inv = inv_ref[8 * b : 8 * b + 1, :]
         live = (first + lane < valid_ref[b]).astype(F32)
         gate = 0.5 * jnp.tanh(0.5 * (inv * raw + bias)) + 0.5
         cot = cot_ref[:, b * 32 : (b + 1) * 32, :].reshape(TRACKS, LANES).astype(F32)
@@ -266,7 +270,7 @@
         coefs.append(inv * inv * inv * d_rms * (1.0 / C_OUT))
     load_weights.wait()
     load_merged.wait()
-    d = dot(weights_ref[...], jnp.concatenate(scaled, axis=1), (1, 0)) * small_ref[0:C_OUT, LANES : LANES + 1]
+    d = dot(weights_ref[...], jnp.concatenate(scaled, axis=1), (1, 0)) * cols_ref[0:C_OUT, 2:3]
     for r in range(CHAN):
         rows = slice(r * 192, (r + 1) * 192)
         for b in range(BATCH):
@@ -297,7 +301,8 @@
         scratch_shapes=[
             pltpu.VMEM((BATCH, CHAN, 192, LANES), F32),
             pltpu.VMEM((BATCH, TRACKS, LANES), F32),
-            pltpu.VMEM((TRACKS, 3 * LANES), F32),
+            pltpu.VMEM((TRACKS, LANES), F32),
+            pltpu.VMEM((32, LANES), F32),
             pltpu.VMEM((C_OUT, TRACKS), BF),
             pltpu.VMEM((C_OUT, BATCH * LANES), BF),
             pltpu.SemaphoreType.DMA((2, BATCH)),

time: 115 us -> 115 us (level)
  no operation moved by 1% of the time
where the time goes in v7:
time: 115 us; the launch traced here: 114 us
  waiting for transfers between devices  40.7 us (35%)
  Pallas kernels  39.1 us (34%)
  starting transfers between devices  30.7 us (27%)
  local copies, waits for them, and re-layouts  2.37 us (2%)
    ppermute x13, waiting for transfers between devices, flip(): return lax.ppermute(x, 'chan', [(i, i ^ r) for i in range(CHAN)])  12.7 us
    pallas_call x1, Pallas kernels, trunk_grad(): pl.pallas_call(trunk_kernel, out_shape=(jax.ShapeDtypeStruct((BATCH, 256,...  12.3 us
    all_to_all x1, waiting for transfers between devices, local(): lax.all_to_all(terms, 'seq', 0, 0, tiled=True, axis_index_groups=groups)  8.61 us
    ppermute x13, starting transfers between devices, flip(): return lax.ppermute(x, 'chan', [(i, i ^ r) for i in range(CHAN)])  8.47 us
    pallas_call x1, Pallas kernels, weight_grad(): pl.pallas_call(weight_kernel, out_shape=(jax.ShapeDtypeStruct((16, ROWS,...  7.9 us
    all_to_all x1, waiting for transfers between devices, local(): lax.all_to_all(send, 'seq', 0, 0, tiled=True).reshape(SEQ, COT_ROWS, LANES)  7.36 us
    ppermute x1, waiting for transfers between devices, partner_far(): return lax.ppermute(x, ('seq', 'chan'), pairs)  7.07 us
    ppermute x2, starting transfers between devices, partner(): return lax.ppermute(x, 'seq', [(i, i ^ 8) for i in range(SEQ)])  5.38 us
  transfers between devices with their start and end apart: 20, of which 12 were waited for; matrix products, arithmetic and copies ran while one was open for 1% of the time, Pallas kernels for 29%

profile of v7, /device:TPU:0, one launch (start us, length us, event | category | flops | bytes accessed | tf_op | source)
XLA Modules:
  0.0 114.3 jit_solution(17510379163965561002)
XLA Ops:
  0.6 3.4 %collective-permute-start.3 = (bf16[4,256,384]{2,1,0:T(8,128)(2,1)}, bf16[4,256,384]{2,1,0:T(8,128)(2,1)S(1)}, u32[]{:S(2)}, u32[]{:S(2)}) collective-permute-start(bf16[4,256,384]{2,1,0:T(8,128)(2,1)} %own_ref), channel_id=1, source_target_pairs={{0,32},{4,36},{8,40},{12,44},{16,48},{20,52},{24,56},{28,60},{32,0... | collective-permute-start | bytes 2359304 | tf_op jit(solution)/shard_map/ppermute | solution.py:561
  4.5 2.8 %cut_pieces.1 = (bf16[784,128]{1,0:T(8,128)(2,1)}, bf16[784,128]{1,0:T(8,128)(2,1)}, bf16[784,128]{1,0:T(8,128)(2,1)}, bf16[784,128]{1,0:T(8,128)(2,1)}) custom-call(s32[4]{0:T(128)} %pad_add_fusion.ids_ref, bf16[4,192,512]{2,1,0:T(8,128)(2,1)} %merged_ref.1, f32[1,192]{1,0:T(1,128)} %bitcast.12), custom_call_target="tpu_custom_call" | custom-call | tf_op jit(solution)/shard_map/cut_pieces/pallas_call | solution.py:70
  7.4 3.5 %cut_cot.1 = bf16[32,9,16,128]{3,2,1,0:T(8,128)(2,1)} custom-call(s32[4]{0:T(128)} %pad_add_fusion.ids_ref, bf16[8,16,16384]{2,1,0:T(8,128)(2,1)} %bitcast.11, bf16[4,256,384]{2,1,0:T(8,128)(2,1)} %own_ref), custom_call_target="tpu_custom_call" | custom-call | bytes 5242880 | tf_op jit(solution)/shard_map/cut_cot/pallas_call | solution.py:116
  10.9 4.1 %collective-permute-start.4 = (bf16[192,1024]{1,0:T(8,128)(2,1)}, bf16[192,1024]{1,0:T(8,128)(2,1)S(1)}, u32[]{:S(2)}, u32[]{:S(2)}) collective-permute-start(bf16[192,1024]{1,0:T(8,128)(2,1)} %refs_4_), channel_id=1, source_target_pairs={{0,66},{1,67},{2,64},{3,65},{4,70},{5,71},{6,68},{7,69},{8,74},{9,... | collective-permute-start | bytes 1179656 | tf_op jit(solution)/shard_map/ppermute | solution.py:577
  15.1 3.3 %collective-permute-start.2 = (bf16[784,128]{1,0:T(8,128)(2,1)}, bf16[784,128]{1,0:T(8,128)(2,1)S(1)}, u32[]{:S(2)}, u32[]{:S(2)}) collective-permute-start(bf16[784,128]{1,0:T(8,128)(2,1)} %get-tuple-element.49), channel_id=1, source_target_pairs={{0,3},{1,2},{2,1},{3,0},{4,7},{5,6},{6,5},{7,4},{8,11},{9,10},{10,... | collective-permute-start | bytes 602120 | tf_op jit(solution)/shard_map/ppermute | solution.py:557
  18.4 6.1 %collective-permute-done.1.refs_2_ = bf16[784,128]{1,0:T(8,128)(2,1)S(1)} collective-permute-done((bf16[784,128]{1,0:T(8,128)(2,1)S(1)}, bf16[784,128]{1,0:T(8,128)(2,1)S(1)}, u32[]{:S(2)}, u32[]{:S(2)}) %collective-permute-start.1) | collective-permute-done | bytes 200736 | tf_op jit(solution)/shard_map/ppermute | solution.py:557
  24.5 0.7 copy-done.11
  25.2 5.2 %all-to-all-start = ((bf16[32,9,16,128]{3,2,1,0:T(8,128)(2,1)}), bf16[32,9,16,128]{3,2,1,0:T(8,128)(2,1)S(1)}, u32[]{:S(2)}, u32[]{:S(2)}) async-start(bf16[32,9,16,128]{3,2,1,0:T(8,128)(2,1)} %cut_cot.1), calls=%async_computation | async-start | bytes 2359296 | tf_op jit(solution)/shard_map/all_to_all | solution.py:597
  30.5 2.2 %collective-permute-done.4.refs_6_ = bf16[192,1024]{1,0:T(8,128)(2,1)S(1)} collective-permute-done((bf16[192,1024]{1,0:T(8,128)(2,1)}, bf16[192,1024]{1,0:T(8,128)(2,1)S(1)}, u32[]{:S(2)}, u32[]{:S(2)}) %collective-permute-start.4) | collective-permute-done | bytes 393248 | tf_op jit(solution)/shard_map/ppermute | solution.py:577
  32.8 1.7 %collective-permute-done.6.refs_7_ = bf16[192,1024]{1,0:T(8,128)(2,1)S(1)} collective-permute-done((bf16[192,1024]{1,0:T(8,128)(2,1)S(1)}, bf16[192,1024]{1,0:T(8,128)(2,1)S(1)}, u32[]{:S(2)}, u32[]{:S(2)}) %collective-permute-start.6) | collective-permute-done | bytes 393248 | tf_op jit(solution)/shard_map/ppermute | solution.py:557
  34.5 0.7 copy-done.9
  35.2 5.4 %scores.1 = (f32[9,1024,512]{2,1,0:T(8,128)}, bf16[12,768,1024]{2,1,0:T(8,128)(2,1)}) custom-call(bf16[784,128]{1,0:T(8,128)(2,1)} %get-tuple-element.39.refs_0_, bf16[784,128]{1,0:T(8,128)(2,1)} %copy-done.10, bf16[784,128]{1,0:T(8,128)(2,1)} %copy-done.11, bf16[784,128]{1,0:T(8,128)(2,1)} %copy-done.12, bf16[192,1024]{1,0:T(8,128)(2,1)} %refs_4_, ...), custom_call_target="tpu_custom_call" | custom-call | flops 6499999744 | bytes 8388608 | tf_op jit(solution)/shard_map/scores/pallas_call | solution.py:203
  40.6 7.4 %all-to-all-done = bf16[32,9,16,128]{3,2,1,0:T(8,128)(2,1)S(1)} async-done(((bf16[32,9,16,128]{3,2,1,0:T(8,128)(2,1)}), bf16[32,9,16,128]{3,2,1,0:T(8,128)(2,1)S(1)}, u32[]{:S(2)}, u32[]{:S(2)}) %all-to-all-start) | async-done | bytes 1179680 | tf_op jit(solution)/shard_map/all_to_all | solution.py:597
  47.9 4.7 %head.1 = (bf16[1536,128]{1,0:T(8,128)(2,1)S(1)}, bf16[1536,128]{1,0:T(8,128)(2,1)S(1)}, bf16[96,128]{1,0:T(8,128)(2,1)S(1)}) custom-call(s32[4]{0:T(128)S(1)} %copy-done.1, s32[4]{0:T(128)S(1)} %copy-done.2, f32[9,1024,512]{2,1,0:T(8,128)} %get-tuple-element.53.wide_hbm, bf16[12,768,1024]{2,1,0:T(8,128)(2,1)} %get-tuple-element.54.narrow_hbm, ...), custom_call_target="tpu_custom_call" | custom-call | tf_op jit(solution)/shard_map/head/pallas_call | solution.py:296
  52.7 2.0 %collective-permute-start.10 = (bf16[1536,128]{1,0:T(8,128)(2,1)S(1)}, bf16[1536,128]{1,0:T(8,128)(2,1)S(1)}, u32[]{:S(2)}, u32[]{:S(2)}) collective-permute-start(bf16[1536,128]{1,0:T(8,128)(2,1)S(1)} %get-tuple-element.57), channel_id=1, source_target_pairs={{0,34},{1,35},{2,32},{3,33},{4,38},{5,39},{6,36},{7,37},{8,42},{9,... | collective-permute-start | bytes 1179656 | tf_op jit(solution)/shard_map/ppermute | solution.py:566
  54.7 2.0 %collective-permute-start.9 = (bf16[1536,128]{1,0:T(8,128)(2,1)S(1)}, bf16[1536,128]{1,0:T(8,128)(2,1)S(1)}, u32[]{:S(2)}, u32[]{:S(2)}) collective-permute-start(bf16[1536,128]{1,0:T(8,128)(2,1)S(1)} %get-tuple-element.57), channel_id=1, source_target_pairs={{0,32},{4,36},{8,40},{12,44},{16,48},{20,52},{24,56},{28,60},{32,0... | collective-permute-start | bytes 1179656 | tf_op jit(solution)/shard_map/ppermute | solution.py:561
  56.7 2.5 %collective-permute-start.8 = (bf16[1536,128]{1,0:T(8,128)(2,1)S(1)}, bf16[1536,128]{1,0:T(8,128)(2,1)S(1)}, u32[]{:S(2)}, u32[]{:S(2)}) collective-permute-start(bf16[1536,128]{1,0:T(8,128)(2,1)S(1)} %get-tuple-element.56.refs_0_), channel_id=1, source_target_pairs={{0,2},{1,3},{2,0},{3,1},{4,6},{5,7},{6,4},{7,5},{8,10},{9,11},{10,... | collective-permute-start | bytes 1179656 | tf_op jit(solution)/shard_map/ppermute | solution.py:557
  59.3 0.7 collective-permute-start.11
  60.0 1.6 %trunk_rows.1 = (bf16[2,1024,1152]{2,1,0:T(8,128)(2,1)S(1)}, bf16[128,1920]{1,0:T(8,128)(2,1)S(1)}) custom-call(s32[4]{0:T(128)S(1)} %copy-done.1, bf16[4,256,384]{2,1,0:T(8,128)(2,1)S(1)} %copy-done, bf16[4,256,384]{2,1,0:T(8,128)(2,1)S(1)} %collective-permute-done.3.far_ref, bf16[32,144,128]{2,1,0:T(8,128)(2,1)S(1)} %bitcast.10), custom_call_target="tpu_custom_call" | custom-call | flops 10000000 | bytes 8388608 | tf_op jit(solution)/shard_map/trunk_rows/pallas_call | solution.py:360
  61.7 7.1 %collective-permute-done.10.refs_6_ = bf16[1536,128]{1,0:T(8,128)(2,1)S(1)} collective-permute-done((bf16[1536,128]{1,0:T(8,128)(2,1)S(1)}, bf16[1536,128]{1,0:T(8,128)(2,1)S(1)}, u32[]{:S(2)}, u32[]{:S(2)}) %collective-permute-start.10) | collective-permute-done | bytes 393248 | tf_op jit(solution)/shard_map/ppermute | solution.py:566
  68.8 2.8 %collective-permute-done.9.refs_4_ = bf16[1536,128]{1,0:T(8,128)(2,1)S(1)} collective-permute-done((bf16[1536,128]{1,0:T(8,128)(2,1)S(1)}, bf16[1536,128]{1,0:T(8,128)(2,1)S(1)}, u32[]{:S(2)}, u32[]{:S(2)}) %collective-permute-start.9) | collective-permute-done | bytes 393248 | tf_op jit(solution)/shard_map/ppermute | solution.py:561
  71.5 2.0 %collective-permute-done.8.refs_2_ = bf16[1536,128]{1,0:T(8,128)(2,1)S(1)} collective-permute-done((bf16[1536,128]{1,0:T(8,128)(2,1)S(1)}, bf16[1536,128]{1,0:T(8,128)(2,1)S(1)}, u32[]{:S(2)}, u32[]{:S(2)}) %collective-permute-start.8) | collective-permute-done | bytes 393248 | tf_op jit(solution)/shard_map/ppermute | solution.py:557
  74.0 1.2 %collective-permute-start.16 = (bf16[1632,128]{1,0:T(8,128)(2,1)S(1)}, bf16[1632,128]{1,0:T(8,128)(2,1)S(1)}, u32[]{:S(2)}, u32[]{:S(2)}) collective-permute-start(bf16[1632,128]{1,0:T(8,128)(2,1)S(1)} %pad_maximum_fusion.refs_1_), channel_id=1, source_target_pairs={{0,2},{1,3},{2,0},{3,1},{4,6},{5,7},{6,4},{7,5},{8,10},{9,11},{10,... | collective-permute-start | bytes 1253384 | tf_op jit(solution)/shard_map/ppermute | solution.py:557
  75.8 0.6 collective-permute-done.12.refs_3_
  76.4 7.9 %weight_grad.1 = (bf16[16,368,128]{2,1,0:T(8,128)(2,1)}, bf16[18,1536,512]{2,1,0:T(8,128)(2,1)}) custom-call(s32[4]{0:T(128)S(1)} %copy-done.1, bf16[1536,128]{1,0:T(8,128)(2,1)S(1)} %get-tuple-element.56.refs_0_, bf16[1536,128]{1,0:T(8,128)(2,1)S(1)} %collective-permute-done.7.refs_1_, bf16[1536,128]{1,0:T(8,128)(2,1)S(1)} %collective-permute-done.8.refs_2_, ...), custom_call_target="tpu_custom_call" | custom-call | flops 4000000000 | bytes 10485760 | tf_op jit(solution)/shard_map/weight_grad/pallas_call | solution.py:443
  84.3 4.8 %all-to-all-start.1 = ((bf16[16,368,128]{2,1,0:T(8,128)(2,1)}), bf16[16,368,128]{2,1,0:T(8,128)(2,1)S(1)}, u32[]{:S(2)}, u32[]{:S(2)}) async-start(bf16[16,368,128]{2,1,0:T(8,128)(2,1)} %get-tuple-element.74), calls=%async_computation.1 | async-start | bytes 3014656 | tf_op jit(solution)/shard_map/all_to_all | solution.py:618
  89.7 1.2 %collective-permute-done.15.refs_2_ = bf16[1632,128]{1,0:T(8,128)(2,1)S(1)} collective-permute-done((bf16[1632,128]{1,0:T(8,128)(2,1)S(1)}, bf16[1632,128]{1,0:T(8,128)(2,1)S(1)}, u32[]{:S(2)}, u32[]{:S(2)}) %collective-permute-start.15) | collective-permute-done | bytes 417824 | tf_op jit(solution)/shard_map/ppermute | solution.py:557
  91.0 0.6 collective-permute-done.17.refs_4_
  91.7 0.7 copy-done.6
  92.5 12.3 %trunk_grad.1 = (bf16[4,256,384]{2,1,0:T(8,128)(2,1)}, bf16[4,192,512]{2,1,0:T(8,128)(2,1)}) custom-call(s32[4]{0:T(128)} %pad_add_fusion.ids_ref, bf16[18,1536,512]{2,1,0:T(8,128)(2,1)} %get-tuple-element.69.refs_0_, bf16[1632,128]{1,0:T(8,128)(2,1)} %copy-done.3, bf16[1632,128]{1,0:T(8,128)(2,1)} %copy-done.5, bf16[1632,128]{1,0:T(8,128)(2,1)} %copy-done.4, ...), custom_call_target="tpu_custom_call" | custom-call | flops 8000000000 | bytes 16777216 | tf_op jit(solution)/shard_map/trunk_grad/pallas_call | solution.py:518
  104.8 8.6 %all-to-all-done.1.in_ref = bf16[16,368,128]{2,1,0:T(8,128)(2,1)S(1)} async-done(((bf16[16,368,128]{2,1,0:T(8,128)(2,1)}), bf16[16,368,128]{2,1,0:T(8,128)(2,1)S(1)}, u32[]{:S(2)}, u32[]{:S(2)}) %all-to-all-start.1) | async-done | bytes 1507360 | tf_op jit(solution)/shard_map/all_to_all | solution.py:618
  113.4 0.9 sum_weights.1
  (48 shorter events, 2.8 us)
Async XLA Ops:
  0.6 32.0 %collective-permute-start.3 = (bf16[4,256,384]{2,1,0:T(8,128)(2,1)}, bf16[4,256,384]{2,1,0:T(8,128)(2,1)S(1)}, u32[]{:S(2)}, u32[]{:S(2)}) collective-permute-start(bf16[4,256,384]{2,1,0:T(8,128)(2,1)} %own_ref), channel_id=1, source_target_pairs={{0,32},{4,36},{8,40},{12,44},{16,48},{20,52},{24,56},{28,60},{32,0... | collective-permute-start | bytes 2359304 | tf_op jit(solution)/shard_map/ppermute | solution.py:561
  7.4 7.6 %copy-start.14 = (bf16[784,128]{1,0:T(8,128)(2,1)S(1)}, bf16[784,128]{1,0:T(8,128)(2,1)}, u32[]{:S(2)}) copy-start(bf16[784,128]{1,0:T(8,128)(2,1)} %get-tuple-element.45) | copy-start | bytes 602116
  7.4 7.6 %copy-start.13 = (bf16[784,128]{1,0:T(8,128)(2,1)S(1)}, bf16[784,128]{1,0:T(8,128)(2,1)}, u32[]{:S(2)}) copy-start(bf16[784,128]{1,0:T(8,128)(2,1)} %get-tuple-element.46) | copy-start | bytes 602116
  10.9 21.8 %collective-permute-start.4 = (bf16[192,1024]{1,0:T(8,128)(2,1)}, bf16[192,1024]{1,0:T(8,128)(2,1)S(1)}, u32[]{:S(2)}, u32[]{:S(2)}) collective-permute-start(bf16[192,1024]{1,0:T(8,128)(2,1)} %refs_4_), channel_id=1, source_target_pairs={{0,66},{1,67},{2,64},{3,65},{4,70},{5,71},{6,68},{7,69},{8,74},{9,... | collective-permute-start | bytes 1179656 | tf_op jit(solution)/shard_map/ppermute | solution.py:577
  15.0 3.4 %collective-permute-start = (bf16[784,128]{1,0:T(8,128)(2,1)S(1)}, bf16[784,128]{1,0:T(8,128)(2,1)S(1)}, u32[]{:S(2)}, u32[]{:S(2)}) collective-permute-start(bf16[784,128]{1,0:T(8,128)(2,1)S(1)} %copy-done.14), channel_id=1, source_target_pairs={{0,1},{1,0},{2,3},{3,2},{4,5},{5,4},{6,7},{7,6},{8,9},{9,8},{10,11... | collective-permute-start | bytes 602120 | tf_op jit(solution)/shard_map/ppermute | solution.py:557
  15.0 9.5 %collective-permute-start.1 = (bf16[784,128]{1,0:T(8,128)(2,1)S(1)}, bf16[784,128]{1,0:T(8,128)(2,1)S(1)}, u32[]{:S(2)}, u32[]{:S(2)}) collective-permute-start(bf16[784,128]{1,0:T(8,128)(2,1)S(1)} %copy-done.13), channel_id=1, source_target_pairs={{0,2},{1,3},{2,0},{3,1},{4,6},{5,7},{6,4},{7,5},{8,10},{9,11},{10,... | collective-permute-start | bytes 602120 | tf_op jit(solution)/shard_map/ppermute | solution.py:557
  15.1 15.4 %collective-permute-start.2 = (bf16[784,128]{1,0:T(8,128)(2,1)}, bf16[784,128]{1,0:T(8,128)(2,1)S(1)}, u32[]{:S(2)}, u32[]{:S(2)}) collective-permute-start(bf16[784,128]{1,0:T(8,128)(2,1)} %get-tuple-element.49), channel_id=1, source_target_pairs={{0,3},{1,2},{2,1},{3,0},{4,7},{5,6},{6,5},{7,4},{8,11},{9,10},{10,... | collective-permute-start | bytes 602120 | tf_op jit(solution)/shard_map/ppermute | solution.py:557
  18.4 6.1 %copy-start.10 = (bf16[784,128]{1,0:T(8,128)(2,1)}, bf16[784,128]{1,0:T(8,128)(2,1)S(1)}, u32[]{:S(2)}) copy-start(bf16[784,128]{1,0:T(8,128)(2,1)S(1)} %collective-permute-done.refs_1_) | copy-start | bytes 602116
  25.2 22.8 %all-to-all-start = ((bf16[32,9,16,128]{3,2,1,0:T(8,128)(2,1)}), bf16[32,9,16,128]{3,2,1,0:T(8,128)(2,1)S(1)}, u32[]{:S(2)}, u32[]{:S(2)}) async-start(bf16[32,9,16,128]{3,2,1,0:T(8,128)(2,1)} %cut_cot.1), calls=%async_computation | async-start | bytes 2359296 | tf_op jit(solution)/shard_map/all_to_all | solution.py:597
  30.4 2.4 %collective-permute-start.5 = (bf16[192,1024]{1,0:T(8,128)(2,1)}, bf16[192,1024]{1,0:T(8,128)(2,1)S(1)}, u32[]{:S(2)}, u32[]{:S(2)}) collective-permute-start(bf16[192,1024]{1,0:T(8,128)(2,1)} %refs_4_), channel_id=1, source_target_pairs={{0,1},{1,0},{2,3},{3,2},{4,5},{5,4},{6,7},{7,6},{8,9},{9,8},{10,11... | collective-permute-start | bytes 1179656 | tf_op jit(solution)/shard_map/ppermute | solution.py:557
  30.5 2.2 %copy-start.12 = (bf16[784,128]{1,0:T(8,128)(2,1)}, bf16[784,128]{1,0:T(8,128)(2,1)S(1)}, u32[]{:S(2)}) copy-start(bf16[784,128]{1,0:T(8,128)(2,1)S(1)} %collective-permute-done.2.refs_3_) | copy-start | bytes 602116
  32.7 1.8 %copy-start.7 = (bf16[192,1024]{1,0:T(8,128)(2,1)}, bf16[192,1024]{1,0:T(8,128)(2,1)S(1)}, u32[]{:S(2)}) copy-start(bf16[192,1024]{1,0:T(8,128)(2,1)S(1)} %collective-permute-done.4.refs_6_) | copy-start | bytes 1179652
  32.7 1.8 %collective-permute-start.6 = (bf16[192,1024]{1,0:T(8,128)(2,1)S(1)}, bf16[192,1024]{1,0:T(8,128)(2,1)S(1)}, u32[]{:S(2)}, u32[]{:S(2)}) collective-permute-start(bf16[192,1024]{1,0:T(8,128)(2,1)S(1)} %collective-permute-done.4.refs_6_), channel_id=1, source_target_pairs={{0,1},{1,0},{2,3},{3,2},{4,5},{5,4},{6,7},{7,6},{8,9},{9,8},{10,11... | collective-permute-start | bytes 1179656 | tf_op jit(solution)/shard_map/ppermute | solution.py:557
  32.8 1.7 %copy-start.8 = (bf16[192,1024]{1,0:T(8,128)(2,1)}, bf16[192,1024]{1,0:T(8,128)(2,1)S(1)}, u32[]{:S(2)}) copy-start(bf16[192,1024]{1,0:T(8,128)(2,1)S(1)} %collective-permute-done.5.refs_5_) | copy-start | bytes 1179652
  35.2 12.7 %copy-start.1 = (s32[4]{0:T(128)S(1)}, s32[4]{0:T(128)}, u32[]{:S(2)}) copy-start(s32[4]{0:T(128)} %pad_add_fusion.ids_ref) | copy-start | bytes 52
  35.2 12.7 %copy-start.2 = (s32[4]{0:T(128)S(1)}, s32[4]{0:T(128)}, u32[]{:S(2)}) copy-start(s32[4]{0:T(128)} %valid_ref.1) | copy-start | bytes 52
  47.9 12.1 %copy-start = (bf16[4,256,384]{2,1,0:T(8,128)(2,1)S(1)}, bf16[4,256,384]{2,1,0:T(8,128)(2,1)}, u32[]{:S(2)}) copy-start(bf16[4,256,384]{2,1,0:T(8,128)(2,1)} %own_ref) | copy-start | bytes 2359300
  52.7 16.1 %collective-permute-start.10 = (bf16[1536,128]{1,0:T(8,128)(2,1)S(1)}, bf16[1536,128]{1,0:T(8,128)(2,1)S(1)}, u32[]{:S(2)}, u32[]{:S(2)}) collective-permute-start(bf16[1536,128]{1,0:T(8,128)(2,1)S(1)} %get-tuple-element.57), channel_id=1, source_target_pairs={{0,34},{1,35},{2,32},{3,33},{4,38},{5,39},{6,36},{7,37},{8,42},{9,... | collective-permute-start | bytes 1179656 | tf_op jit(solution)/shard_map/ppermute | solution.py:566
  54.7 16.8 %collective-permute-start.9 = (bf16[1536,128]{1,0:T(8,128)(2,1)S(1)}, bf16[1536,128]{1,0:T(8,128)(2,1)S(1)}, u32[]{:S(2)}, u32[]{:S(2)}) collective-permute-start(bf16[1536,128]{1,0:T(8,128)(2,1)S(1)} %get-tuple-element.57), channel_id=1, source_target_pairs={{0,32},{4,36},{8,40},{12,44},{16,48},{20,52},{24,56},{28,60},{32,0... | collective-permute-start | bytes 1179656 | tf_op jit(solution)/shard_map/ppermute | solution.py:561
  56.7 16.8 %collective-permute-start.8 = (bf16[1536,128]{1,0:T(8,128)(2,1)S(1)}, bf16[1536,128]{1,0:T(8,128)(2,1)S(1)}, u32[]{:S(2)}, u32[]{:S(2)}) collective-permute-start(bf16[1536,128]{1,0:T(8,128)(2,1)S(1)} %get-tuple-element.56.refs_0_), channel_id=1, source_target_pairs={{0,2},{1,3},{2,0},{3,1},{4,6},{5,7},{6,4},{7,5},{8,10},{9,11},{10,... | collective-permute-start | bytes 1179656 | tf_op jit(solution)/shard_map/ppermute | solution.py:557
  59.3 2.4 %collective-permute-start.11 = (bf16[96,128]{1,0:T(8,128)(2,1)S(1)}, bf16[96,128]{1,0:T(8,128)(2,1)S(1)}, u32[]{:S(2)}, u32[]{:S(2)}) collective-permute-start(bf16[96,128]{1,0:T(8,128)(2,1)S(1)} %get-tuple-element.58), channel_id=1, source_target_pairs={{3,4},{7,8},{11,12},{15,16},{19,20},{23,24},{27,28},{31,32},{35,36... | collective-permute-start | bytes 73736 | tf_op jit(solution)/shard_map/ppermute | solution.py:572
  59.9 15.4 %collective-permute-start.7 = (bf16[1536,128]{1,0:T(8,128)(2,1)S(1)}, bf16[1536,128]{1,0:T(8,128)(2,1)S(1)}, u32[]{:S(2)}, u32[]{:S(2)}) collective-permute-start(bf16[1536,128]{1,0:T(8,128)(2,1)S(1)} %get-tuple-element.56.refs_0_), channel_id=1, source_target_pairs={{0,1},{1,0},{2,3},{3,2},{4,5},{5,4},{6,7},{7,6},{8,9},{9,8},{10,11... | collective-permute-start | bytes 1179656 | tf_op jit(solution)/shard_map/ppermute | solution.py:557
  61.7 27.4 %copy-start.3 = (bf16[1632,128]{1,0:T(8,128)(2,1)}, bf16[1632,128]{1,0:T(8,128)(2,1)S(1)}, u32[]{:S(2)}) copy-start(bf16[1632,128]{1,0:T(8,128)(2,1)S(1)} %pad_maximum_fusion.refs_1_) | copy-start | bytes 1253380
  73.5 1.8 %collective-permute-start.13 = (bf16[1536,128]{1,0:T(8,128)(2,1)S(1)}, bf16[1536,128]{1,0:T(8,128)(2,1)S(1)}, u32[]{:S(2)}, u32[]{:S(2)}) collective-permute-start(bf16[1536,128]{1,0:T(8,128)(2,1)S(1)} %collective-permute-done.9.refs_4_), channel_id=1, source_target_pairs={{0,1},{1,0},{2,3},{3,2},{4,5},{5,4},{6,7},{7,6},{8,9},{9,8},{10,11... | collective-permute-start | bytes 1179656 | tf_op jit(solution)/shard_map/ppermute | solution.py:557
  73.5 2.3 %collective-permute-start.14 = (bf16[1536,128]{1,0:T(8,128)(2,1)S(1)}, bf16[1536,128]{1,0:T(8,128)(2,1)S(1)}, u32[]{:S(2)}, u32[]{:S(2)}) collective-permute-start(bf16[1536,128]{1,0:T(8,128)(2,1)S(1)} %collective-permute-done.10.refs_6_), channel_id=1, source_target_pairs={{0,1},{1,0},{2,3},{3,2},{4,5},{5,4},{6,7},{7,6},{8,9},{9,8},{10,11... | collective-permute-start | bytes 1179656 | tf_op jit(solution)/shard_map/ppermute | solution.py:557
  74.0 2.3 %collective-permute-start.12 = (bf16[1536,128]{1,0:T(8,128)(2,1)S(1)}, bf16[1536,128]{1,0:T(8,128)(2,1)S(1)}, u32[]{:S(2)}, u32[]{:S(2)}) collective-permute-start(bf16[1536,128]{1,0:T(8,128)(2,1)S(1)} %collective-permute-done.8.refs_2_), channel_id=1, source_target_pairs={{0,1},{1,0},{2,3},{3,2},{4,5},{5,4},{6,7},{7,6},{8,9},{9,8},{10,11... | collective-permute-start | bytes 1179656 | tf_op jit(solution)/shard_map/ppermute | solution.py:557
  74.0 15.2 %collective-permute-start.16 = (bf16[1632,128]{1,0:T(8,128)(2,1)S(1)}, bf16[1632,128]{1,0:T(8,128)(2,1)S(1)}, u32[]{:S(2)}, u32[]{:S(2)}) collective-permute-start(bf16[1632,128]{1,0:T(8,128)(2,1)S(1)} %pad_maximum_fusion.refs_1_), channel_id=1, source_target_pairs={{0,2},{1,3},{2,0},{3,1},{4,6},{5,7},{6,4},{7,5},{8,10},{9,11},{10,... | collective-permute-start | bytes 1253384 | tf_op jit(solution)/shard_map/ppermute | solution.py:557
  84.3 29.1 %all-to-all-start.1 = ((bf16[16,368,128]{2,1,0:T(8,128)(2,1)}), bf16[16,368,128]{2,1,0:T(8,128)(2,1)S(1)}, u32[]{:S(2)}, u32[]{:S(2)}) async-start(bf16[16,368,128]{2,1,0:T(8,128)(2,1)} %get-tuple-element.74), calls=%async_computation.1 | async-start | bytes 3014656 | tf_op jit(solution)/shard_map/all_to_all | solution.py:618
  89.1 1.8 %collective-permute-start.15 = (bf16[1632,128]{1,0:T(8,128)(2,1)S(1)}, bf16[1632,128]{1,0:T(8,128)(2,1)S(1)}, u32[]{:S(2)}, u32[]{:S(2)}) collective-permute-start(bf16[1632,128]{1,0:T(8,128)(2,1)S(1)} %pad_maximum_fusion.refs_1_), channel_id=1, source_target_pairs={{0,1},{1,0},{2,3},{3,2},{4,5},{5,4},{6,7},{7,6},{8,9},{9,8},{10,11... | collective-permute-start | bytes 1253384 | tf_op jit(solution)/shard_map/ppermute | solution.py:557
  89.2 1.7 %copy-start.4 = (bf16[1632,128]{1,0:T(8,128)(2,1)}, bf16[1632,128]{1,0:T(8,128)(2,1)S(1)}, u32[]{:S(2)}) copy-start(bf16[1632,128]{1,0:T(8,128)(2,1)S(1)} %collective-permute-done.16.refs_3_) | copy-start | bytes 1253380
  89.2 2.3 %collective-permute-start.17 = (bf16[1632,128]{1,0:T(8,128)(2,1)S(1)}, bf16[1632,128]{1,0:T(8,128)(2,1)S(1)}, u32[]{:S(2)}, u32[]{:S(2)}) collective-permute-start(bf16[1632,128]{1,0:T(8,128)(2,1)S(1)} %collective-permute-done.16.refs_3_), channel_id=1, source_target_pairs={{0,1},{1,0},{2,3},{3,2},{4,5},{5,4},{6,7},{7,6},{8,9},{9,8},{10,11... | collective-permute-start | bytes 1253384 | tf_op jit(solution)/shard_map/ppermute | solution.py:557
  91.7 0.8 copy-start.6
  (3 other events, 2.2 us)

commit v8 on v7

--- a/solution.py
+++ b/solution.py
@@ -392,8 +392,8 @@
     odd = (q_ >= 128) & ((p + 1) // 2 == q_ - 128)
     pick = (even | odd).astype(BF)
     last = jnp.zeros((384, LANES), F32)
-    p1 = lax.broadcasted_iota(jnp.int32, (LANES, LANES), 0)
-    q1 = lax.broadcasted_iota(jnp.int32, (LANES, LANES), 1)
+    p1 = lax.broadcasted_iota(jnp.int32, (256, LANES), 0)
+    q1 = lax.broadcasted_iota(jnp.int32, (256, LANES), 1)
     g_even = jnp.zeros((384, 1152), F32)
     g_odd = jnp.zeros((384, 768), F32)
     for q in range(PAIR):
@@ -405,17 +405,15 @@
         for b in range(BATCH):
             for h in range(2):
                 block = full[q, b * 384 : (b + 1) * 384, h * 256 : (h + 1) * 256]
-                e = dot(block, pick, (1, 0)).astype(BF)
-                evens.append(e[:, :128])
-                odds.append(e[:, 128:])
                 place = q1 - (q * BATCH + b) * 5
                 if h == 0:
-                    sel = (((p1 < 2) & (place == 3)) | ((p1 == 0) & (place == 4))).astype(BF)
-                    last = last + dot(block[:, :128], sel, (1, 0))
-                    sel = (p1 == 127) & (place == 0)
+                    sel = ((p1 == 255) & (place == 0)) | ((p1 < 2) & (place == 3)) | ((p1 == 0) & (place == 4))
                 else:
-                    sel = ((p1 == 127) & (place == 1)) | ((p1 >= 126) & (place == 2))
-                last = last + dot(block[:, 128:], sel.astype(BF), (1, 0))
+                    sel = ((p1 == 255) & (place == 1)) | ((p1 >= 254) & (place == 2))
+                e = dot(block, jnp.concatenate([pick, sel.astype(BF)], axis=1), (1, 0))
+                evens.append(e[:, :128].astype(BF))
+                odds.append(e[:, 128:256].astype(BF))
+                last = last + e[:, 256:]
         g_even = g_even + dot(jnp.concatenate(evens, axis=1), tr_ref[q], (1, 0))
         g_odd = g_odd + dot(jnp.concatenate(odds, axis=1), tr_ref[q, :, :768], (1, 0))
     last = last.astype(BF)

time: 115 us -> 115 us (level)
  no operation moved by 1% of the time
where the time goes in v8:
time: 115 us; the launch traced here: 114 us
  waiting for transfers between devices  40.6 us (35%)
  Pallas kernels  39.3 us (34%)
  starting transfers between devices  30.7 us (27%)
  local copies, waits for them, and re-layouts  2.37 us (2%)
    ppermute x13, waiting for transfers between devices, flip(): return lax.ppermute(x, 'chan', [(i, i ^ r) for i in range(CHAN)])  12.7 us
    pallas_call x1, Pallas kernels, trunk_grad(): pl.pallas_call(trunk_kernel, out_shape=(jax.ShapeDtypeStruct((BATCH, 256,...  12.3 us
    all_to_all x1, waiting for transfers between devices, local(): lax.all_to_all(terms, 'seq', 0, 0, tiled=True, axis_index_groups=groups)  8.57 us
    ppermute x13, starting transfers between devices, flip(): return lax.ppermute(x, 'chan', [(i, i ^ r) for i in range(CHAN)])  8.47 us
    pallas_call x1, Pallas kernels, weight_grad(): pl.pallas_call(weight_kernel, out_shape=(jax.ShapeDtypeStruct((16, ROWS,...  8.14 us
    all_to_all x1, waiting for transfers between devices, local(): lax.all_to_all(send, 'seq', 0, 0, tiled=True).reshape(SEQ, COT_ROWS, LANES)  7.36 us
    ppermute x1, waiting for transfers between devices, partner_far(): return lax.ppermute(x, ('seq', 'chan'), pairs)  7.07 us
    ppermute x2, starting transfers between devices, partner(): return lax.ppermute(x, 'seq', [(i, i ^ 8) for i in range(SEQ)])  5.38 us
  transfers between devices with their start and end apart: 20, of which 12 were waited for; matrix products, arithmetic and copies ran while one was open for 1% of the time, Pallas kernels for 29%

profile of v8, /device:TPU:0, one launch (start us, length us, event | category | flops | bytes accessed | tf_op | source)
XLA Modules:
  0.0 114.5 jit_solution(7150732402817463205)
XLA Ops:
  0.6 3.4 %collective-permute-start.3 = (bf16[4,256,384]{2,1,0:T(8,128)(2,1)}, bf16[4,256,384]{2,1,0:T(8,128)(2,1)S(1)}, u32[]{:S(2)}, u32[]{:S(2)}) collective-permute-start(bf16[4,256,384]{2,1,0:T(8,128)(2,1)} %own_ref), channel_id=1, source_target_pairs={{0,32},{4,36},{8,40},{12,44},{16,48},{20,52},{24,56},{28,60},{32,0... | collective-permute-start | bytes 2359304 | tf_op jit(solution)/shard_map/ppermute | solution.py:559
  4.5 2.8 %cut_pieces.1 = (bf16[784,128]{1,0:T(8,128)(2,1)}, bf16[784,128]{1,0:T(8,128)(2,1)}, bf16[784,128]{1,0:T(8,128)(2,1)}, bf16[784,128]{1,0:T(8,128)(2,1)}) custom-call(s32[4]{0:T(128)} %pad_add_fusion.ids_ref, bf16[4,192,512]{2,1,0:T(8,128)(2,1)} %merged_ref.1, f32[1,192]{1,0:T(1,128)} %bitcast.12), custom_call_target="tpu_custom_call" | custom-call | tf_op jit(solution)/shard_map/cut_pieces/pallas_call | solution.py:70
  7.4 3.5 %cut_cot.1 = bf16[32,9,16,128]{3,2,1,0:T(8,128)(2,1)} custom-call(s32[4]{0:T(128)} %pad_add_fusion.ids_ref, bf16[8,16,16384]{2,1,0:T(8,128)(2,1)} %bitcast.11, bf16[4,256,384]{2,1,0:T(8,128)(2,1)} %own_ref), custom_call_target="tpu_custom_call" | custom-call | bytes 5242880 | tf_op jit(solution)/shard_map/cut_cot/pallas_call | solution.py:116
  10.9 4.1 %collective-permute-start.4 = (bf16[192,1024]{1,0:T(8,128)(2,1)}, bf16[192,1024]{1,0:T(8,128)(2,1)S(1)}, u32[]{:S(2)}, u32[]{:S(2)}) collective-permute-start(bf16[192,1024]{1,0:T(8,128)(2,1)} %refs_4_), channel_id=1, source_target_pairs={{0,66},{1,67},{2,64},{3,65},{4,70},{5,71},{6,68},{7,69},{8,74},{9,... | collective-permute-start | bytes 1179656 | tf_op jit(solution)/shard_map/ppermute | solution.py:575
  15.1 3.3 %collective-permute-start.2 = (bf16[784,128]{1,0:T(8,128)(2,1)}, bf16[784,128]{1,0:T(8,128)(2,1)S(1)}, u32[]{:S(2)}, u32[]{:S(2)}) collective-permute-start(bf16[784,128]{1,0:T(8,128)(2,1)} %get-tuple-element.49), channel_id=1, source_target_pairs={{0,3},{1,2},{2,1},{3,0},{4,7},{5,6},{6,5},{7,4},{8,11},{9,10},{10,... | collective-permute-start | bytes 602120 | tf_op jit(solution)/shard_map/ppermute | solution.py:555
  18.4 6.1 %collective-permute-done.1.refs_2_ = bf16[784,128]{1,0:T(8,128)(2,1)S(1)} collective-permute-done((bf16[784,128]{1,0:T(8,128)(2,1)S(1)}, bf16[784,128]{1,0:T(8,128)(2,1)S(1)}, u32[]{:S(2)}, u32[]{:S(2)}) %collective-permute-start.1) | collective-permute-done | bytes 200736 | tf_op jit(solution)/shard_map/ppermute | solution.py:555
  24.5 0.7 copy-done.11
  25.2 5.2 %all-to-all-start = ((bf16[32,9,16,128]{3,2,1,0:T(8,128)(2,1)}), bf16[32,9,16,128]{3,2,1,0:T(8,128)(2,1)S(1)}, u32[]{:S(2)}, u32[]{:S(2)}) async-start(bf16[32,9,16,128]{3,2,1,0:T(8,128)(2,1)} %cut_cot.1), calls=%async_computation | async-start | bytes 2359296 | tf_op jit(solution)/shard_map/all_to_all | solution.py:595
  30.5 2.2 %collective-permute-done.4.refs_6_ = bf16[192,1024]{1,0:T(8,128)(2,1)S(1)} collective-permute-done((bf16[192,1024]{1,0:T(8,128)(2,1)}, bf16[192,1024]{1,0:T(8,128)(2,1)S(1)}, u32[]{:S(2)}, u32[]{:S(2)}) %collective-permute-start.4) | collective-permute-done | bytes 393248 | tf_op jit(solution)/shard_map/ppermute | solution.py:575
  32.8 1.7 %collective-permute-done.6.refs_7_ = bf16[192,1024]{1,0:T(8,128)(2,1)S(1)} collective-permute-done((bf16[192,1024]{1,0:T(8,128)(2,1)S(1)}, bf16[192,1024]{1,0:T(8,128)(2,1)S(1)}, u32[]{:S(2)}, u32[]{:S(2)}) %collective-permute-start.6) | collective-permute-done | bytes 393248 | tf_op jit(solution)/shard_map/ppermute | solution.py:555
  34.5 0.7 copy-done.9
  35.2 5.4 %scores.1 = (f32[9,1024,512]{2,1,0:T(8,128)}, bf16[12,768,1024]{2,1,0:T(8,128)(2,1)}) custom-call(bf16[784,128]{1,0:T(8,128)(2,1)} %get-tuple-element.39.refs_0_, bf16[784,128]{1,0:T(8,128)(2,1)} %copy-done.10, bf16[784,128]{1,0:T(8,128)(2,1)} %copy-done.11, bf16[784,128]{1,0:T(8,128)(2,1)} %copy-done.12, bf16[192,1024]{1,0:T(8,128)(2,1)} %refs_4_, ...), custom_call_target="tpu_custom_call" | custom-call | flops 6499999744 | bytes 8388608 | tf_op jit(solution)/shard_map/scores/pallas_call | solution.py:203
  40.6 7.4 %all-to-all-done = bf16[32,9,16,128]{3,2,1,0:T(8,128)(2,1)S(1)} async-done(((bf16[32,9,16,128]{3,2,1,0:T(8,128)(2,1)}), bf16[32,9,16,128]{3,2,1,0:T(8,128)(2,1)S(1)}, u32[]{:S(2)}, u32[]{:S(2)}) %all-to-all-start) | async-done | bytes 1179680 | tf_op jit(solution)/shard_map/all_to_all | solution.py:595
  47.9 4.7 %head.1 = (bf16[1536,128]{1,0:T(8,128)(2,1)S(1)}, bf16[1536,128]{1,0:T(8,128)(2,1)S(1)}, bf16[96,128]{1,0:T(8,128)(2,1)S(1)}) custom-call(s32[4]{0:T(128)S(1)} %copy-done.1, s32[4]{0:T(128)S(1)} %copy-done.2, f32[9,1024,512]{2,1,0:T(8,128)} %get-tuple-element.53.wide_hbm, bf16[12,768,1024]{2,1,0:T(8,128)(2,1)} %get-tuple-element.54.narrow_hbm, ...), custom_call_target="tpu_custom_call" | custom-call | tf_op jit(solution)/shard_map/head/pallas_call | solution.py:296
  52.7 2.0 %collective-permute-start.10 = (bf16[1536,128]{1,0:T(8,128)(2,1)S(1)}, bf16[1536,128]{1,0:T(8,128)(2,1)S(1)}, u32[]{:S(2)}, u32[]{:S(2)}) collective-permute-start(bf16[1536,128]{1,0:T(8,128)(2,1)S(1)} %get-tuple-element.57), channel_id=1, source_target_pairs={{0,34},{1,35},{2,32},{3,33},{4,38},{5,39},{6,36},{7,37},{8,42},{9,... | collective-permute-start | bytes 1179656 | tf_op jit(solution)/shard_map/ppermute | solution.py:564
  54.7 2.0 %collective-permute-start.9 = (bf16[1536,128]{1,0:T(8,128)(2,1)S(1)}, bf16[1536,128]{1,0:T(8,128)(2,1)S(1)}, u32[]{:S(2)}, u32[]{:S(2)}) collective-permute-start(bf16[1536,128]{1,0:T(8,128)(2,1)S(1)} %get-tuple-element.57), channel_id=1, source_target_pairs={{0,32},{4,36},{8,40},{12,44},{16,48},{20,52},{24,56},{28,60},{32,0... | collective-permute-start | bytes 1179656 | tf_op jit(solution)/shard_map/ppermute | solution.py:559
  56.7 2.5 %collective-permute-start.8 = (bf16[1536,128]{1,0:T(8,128)(2,1)S(1)}, bf16[1536,128]{1,0:T(8,128)(2,1)S(1)}, u32[]{:S(2)}, u32[]{:S(2)}) collective-permute-start(bf16[1536,128]{1,0:T(8,128)(2,1)S(1)} %get-tuple-element.56.refs_0_), channel_id=1, source_target_pairs={{0,2},{1,3},{2,0},{3,1},{4,6},{5,7},{6,4},{7,5},{8,10},{9,11},{10,... | collective-permute-start | bytes 1179656 | tf_op jit(solution)/shard_map/ppermute | solution.py:555
  59.3 0.7 collective-permute-start.11
  60.0 1.6 %trunk_rows.1 = (bf16[2,1024,1152]{2,1,0:T(8,128)(2,1)S(1)}, bf16[128,1920]{1,0:T(8,128)(2,1)S(1)}) custom-call(s32[4]{0:T(128)S(1)} %copy-done.1, bf16[4,256,384]{2,1,0:T(8,128)(2,1)S(1)} %copy-done, bf16[4,256,384]{2,1,0:T(8,128)(2,1)S(1)} %collective-permute-done.3.far_ref, bf16[32,144,128]{2,1,0:T(8,128)(2,1)S(1)} %bitcast.10), custom_call_target="tpu_custom_call" | custom-call | flops 10000000 | bytes 8388608 | tf_op jit(solution)/shard_map/trunk_rows/pallas_call | solution.py:360
  61.7 7.1 %collective-permute-done.10.refs_6_ = bf16[1536,128]{1,0:T(8,128)(2,1)S(1)} collective-permute-done((bf16[1536,128]{1,0:T(8,128)(2,1)S(1)}, bf16[1536,128]{1,0:T(8,128)(2,1)S(1)}, u32[]{:S(2)}, u32[]{:S(2)}) %collective-permute-start.10) | collective-permute-done | bytes 393248 | tf_op jit(solution)/shard_map/ppermute | solution.py:564
  68.8 2.8 %collective-permute-done.9.refs_4_ = bf16[1536,128]{1,0:T(8,128)(2,1)S(1)} collective-permute-done((bf16[1536,128]{1,0:T(8,128)(2,1)S(1)}, bf16[1536,128]{1,0:T(8,128)(2,1)S(1)}, u32[]{:S(2)}, u32[]{:S(2)}) %collective-permute-start.9) | collective-permute-done | bytes 393248 | tf_op jit(solution)/shard_map/ppermute | solution.py:559
  71.5 2.0 %collective-permute-done.8.refs_2_ = bf16[1536,128]{1,0:T(8,128)(2,1)S(1)} collective-permute-done((bf16[1536,128]{1,0:T(8,128)(2,1)S(1)}, bf16[1536,128]{1,0:T(8,128)(2,1)S(1)}, u32[]{:S(2)}, u32[]{:S(2)}) %collective-permute-start.8) | collective-permute-done | bytes 393248 | tf_op jit(solution)/shard_map/ppermute | solution.py:555
  74.0 1.2 %collective-permute-start.16 = (bf16[1632,128]{1,0:T(8,128)(2,1)S(1)}, bf16[1632,128]{1,0:T(8,128)(2,1)S(1)}, u32[]{:S(2)}, u32[]{:S(2)}) collective-permute-start(bf16[1632,128]{1,0:T(8,128)(2,1)S(1)} %pad_maximum_fusion.refs_1_), channel_id=1, source_target_pairs={{0,2},{1,3},{2,0},{3,1},{4,6},{5,7},{6,4},{7,5},{8,10},{9,11},{10,... | collective-permute-start | bytes 1253384 | tf_op jit(solution)/shard_map/ppermute | solution.py:555
  75.8 0.6 collective-permute-done.12.refs_3_
  76.4 8.1 %weight_grad.1 = (bf16[16,368,128]{2,1,0:T(8,128)(2,1)}, bf16[18,1536,512]{2,1,0:T(8,128)(2,1)}) custom-call(s32[4]{0:T(128)S(1)} %copy-done.1, bf16[1536,128]{1,0:T(8,128)(2,1)S(1)} %get-tuple-element.56.refs_0_, bf16[1536,128]{1,0:T(8,128)(2,1)S(1)} %collective-permute-done.7.refs_1_, bf16[1536,128]{1,0:T(8,128)(2,1)S(1)} %collective-permute-done.8.refs_2_, ...), custom_call_target="tpu_custom_call" | custom-call | flops 4000000000 | bytes 10485760 | tf_op jit(solution)/shard_map/weight_grad/pallas_call | solution.py:441
  84.5 4.8 %all-to-all-start.1 = ((bf16[16,368,128]{2,1,0:T(8,128)(2,1)}), bf16[16,368,128]{2,1,0:T(8,128)(2,1)S(1)}, u32[]{:S(2)}, u32[]{:S(2)}) async-start(bf16[16,368,128]{2,1,0:T(8,128)(2,1)} %get-tuple-element.74), calls=%async_computation.1 | async-start | bytes 3014656 | tf_op jit(solution)/shard_map/all_to_all | solution.py:616
  90.0 1.2 %collective-permute-done.15.refs_2_ = bf16[1632,128]{1,0:T(8,128)(2,1)S(1)} collective-permute-done((bf16[1632,128]{1,0:T(8,128)(2,1)S(1)}, bf16[1632,128]{1,0:T(8,128)(2,1)S(1)}, u32[]{:S(2)}, u32[]{:S(2)}) %collective-permute-start.15) | collective-permute-done | bytes 417824 | tf_op jit(solution)/shard_map/ppermute | solution.py:555
  91.2 0.6 collective-permute-done.17.refs_4_
  92.0 0.7 copy-done.6
  92.7 12.3 %trunk_grad.1 = (bf16[4,256,384]{2,1,0:T(8,128)(2,1)}, bf16[4,192,512]{2,1,0:T(8,128)(2,1)}) custom-call(s32[4]{0:T(128)} %pad_add_fusion.ids_ref, bf16[18,1536,512]{2,1,0:T(8,128)(2,1)} %get-tuple-element.69.refs_0_, bf16[1632,128]{1,0:T(8,128)(2,1)} %copy-done.3, bf16[1632,128]{1,0:T(8,128)(2,1)} %copy-done.5, bf16[1632,128]{1,0:T(8,128)(2,1)} %copy-done.4, ...), custom_call_target="tpu_custom_call" | custom-call | flops 8000000000 | bytes 16777216 | tf_op jit(solution)/shard_map/trunk_grad/pallas_call | solution.py:516
  105.0 8.6 %all-to-all-done.1.in_ref = bf16[16,368,128]{2,1,0:T(8,128)(2,1)S(1)} async-done(((bf16[16,368,128]{2,1,0:T(8,128)(2,1)}), bf16[16,368,128]{2,1,0:T(8,128)(2,1)S(1)}, u32[]{:S(2)}, u32[]{:S(2)}) %all-to-all-start.1) | async-done | bytes 1507360 | tf_op jit(solution)/shard_map/all_to_all | solution.py:616
  113.6 0.9 sum_weights.1
  (48 shorter events, 2.8 us)
Async XLA Ops:
  0.6 32.0 %collective-permute-start.3 = (bf16[4,256,384]{2,1,0:T(8,128)(2,1)}, bf16[4,256,384]{2,1,0:T(8,128)(2,1)S(1)}, u32[]{:S(2)}, u32[]{:S(2)}) collective-permute-start(bf16[4,256,384]{2,1,0:T(8,128)(2,1)} %own_ref), channel_id=1, source_target_pairs={{0,32},{4,36},{8,40},{12,44},{16,48},{20,52},{24,56},{28,60},{32,0... | collective-permute-start | bytes 2359304 | tf_op jit(solution)/shard_map/ppermute | solution.py:559
  7.4 7.6 %copy-start.14 = (bf16[784,128]{1,0:T(8,128)(2,1)S(1)}, bf16[784,128]{1,0:T(8,128)(2,1)}, u32[]{:S(2)}) copy-start(bf16[784,128]{1,0:T(8,128)(2,1)} %get-tuple-element.45) | copy-start | bytes 602116
  7.4 7.6 %copy-start.13 = (bf16[784,128]{1,0:T(8,128)(2,1)S(1)}, bf16[784,128]{1,0:T(8,128)(2,1)}, u32[]{:S(2)}) copy-start(bf16[784,128]{1,0:T(8,128)(2,1)} %get-tuple-element.46) | copy-start | bytes 602116
  10.9 21.8 %collective-permute-start.4 = (bf16[192,1024]{1,0:T(8,128)(2,1)}, bf16[192,1024]{1,0:T(8,128)(2,1)S(1)}, u32[]{:S(2)}, u32[]{:S(2)}) collective-permute-start(bf16[192,1024]{1,0:T(8,128)(2,1)} %refs_4_), channel_id=1, source_target_pairs={{0,66},{1,67},{2,64},{3,65},{4,70},{5,71},{6,68},{7,69},{8,74},{9,... | collective-permute-start | bytes 1179656 | tf_op jit(solution)/shard_map/ppermute | solution.py:575
  15.0 3.4 %collective-permute-start = (bf16[784,128]{1,0:T(8,128)(2,1)S(1)}, bf16[784,128]{1,0:T(8,128)(2,1)S(1)}, u32[]{:S(2)}, u32[]{:S(2)}) collective-permute-start(bf16[784,128]{1,0:T(8,128)(2,1)S(1)} %copy-done.14), channel_id=1, source_target_pairs={{0,1},{1,0},{2,3},{3,2},{4,5},{5,4},{6,7},{7,6},{8,9},{9,8},{10,11... | collective-permute-start | bytes 602120 | tf_op jit(solution)/shard_map/ppermute | solution.py:555
  15.0 9.5 %collective-permute-start.1 = (bf16[784,128]{1,0:T(8,128)(2,1)S(1)}, bf16[784,128]{1,0:T(8,128)(2,1)S(1)}, u32[]{:S(2)}, u32[]{:S(2)}) collective-permute-start(bf16[784,128]{1,0:T(8,128)(2,1)S(1)} %copy-done.13), channel_id=1, source_target_pairs={{0,2},{1,3},{2,0},{3,1},{4,6},{5,7},{6,4},{7,5},{8,10},{9,11},{10,... | collective-permute-start | bytes 602120 | tf_op jit(solution)/shard_map/ppermute | solution.py:555
  15.1 15.4 %collective-permute-start.2 = (bf16[784,128]{1,0:T(8,128)(2,1)}, bf16[784,128]{1,0:T(8,128)(2,1)S(1)}, u32[]{:S(2)}, u32[]{:S(2)}) collective-permute-start(bf16[784,128]{1,0:T(8,128)(2,1)} %get-tuple-element.49), channel_id=1, source_target_pairs={{0,3},{1,2},{2,1},{3,0},{4,7},{5,6},{6,5},{7,4},{8,11},{9,10},{10,... | collective-permute-start | bytes 602120 | tf_op jit(solution)/shard_map/ppermute | solution.py:555
  18.4 6.1 %copy-start.10 = (bf16[784,128]{1,0:T(8,128)(2,1)}, bf16[784,128]{1,0:T(8,128)(2,1)S(1)}, u32[]{:S(2)}) copy-start(bf16[784,128]{1,0:T(8,128)(2,1)S(1)} %collective-permute-done.refs_1_) | copy-start | bytes 602116
  25.2 22.8 %all-to-all-start = ((bf16[32,9,16,128]{3,2,1,0:T(8,128)(2,1)}), bf16[32,9,16,128]{3,2,1,0:T(8,128)(2,1)S(1)}, u32[]{:S(2)}, u32[]{:S(2)}) async-start(bf16[32,9,16,128]{3,2,1,0:T(8,128)(2,1)} %cut_cot.1), calls=%async_computation | async-start | bytes 2359296 | tf_op jit(solution)/shard_map/all_to_all | solution.py:595
  30.4 2.4 %collective-permute-start.5 = (bf16[192,1024]{1,0:T(8,128)(2,1)}, bf16[192,1024]{1,0:T(8,128)(2,1)S(1)}, u32[]{:S(2)}, u32[]{:S(2)}) collective-permute-start(bf16[192,1024]{1,0:T(8,128)(2,1)} %refs_4_), channel_id=1, source_target_pairs={{0,1},{1,0},{2,3},{3,2},{4,5},{5,4},{6,7},{7,6},{8,9},{9,8},{10,11... | collective-permute-start | bytes 1179656 | tf_op jit(solution)/shard_map/ppermute | solution.py:555
  30.5 2.2 %copy-start.12 = (bf16[784,128]{1,0:T(8,128)(2,1)}, bf16[784,128]{1,0:T(8,128)(2,1)S(1)}, u32[]{:S(2)}) copy-start(bf16[784,128]{1,0:T(8,128)(2,1)S(1)} %collective-permute-done.2.refs_3_) | copy-start | bytes 602116
  32.7 1.8 %copy-start.7 = (bf16[192,1024]{1,0:T(8,128)(2,1)}, bf16[192,1024]{1,0:T(8,128)(2,1)S(1)}, u32[]{:S(2)}) copy-start(bf16[192,1024]{1,0:T(8,128)(2,1)S(1)} %collective-permute-done.4.refs_6_) | copy-start | bytes 1179652
  32.7 1.8 %collective-permute-start.6 = (bf16[192,1024]{1,0:T(8,128)(2,1)S(1)}, bf16[192,1024]{1,0:T(8,128)(2,1)S(1)}, u32[]{:S(2)}, u32[]{:S(2)}) collective-permute-start(bf16[192,1024]{1,0:T(8,128)(2,1)S(1)} %collective-permute-done.4.refs_6_), channel_id=1, source_target_pairs={{0,1},{1,0},{2,3},{3,2},{4,5},{5,4},{6,7},{7,6},{8,9},{9,8},{10,11... | collective-permute-start | bytes 1179656 | tf_op jit(solution)/shard_map/ppermute | solution.py:555
  32.8 1.7 %copy-start.8 = (bf16[192,1024]{1,0:T(8,128)(2,1)}, bf16[192,1024]{1,0:T(8,128)(2,1)S(1)}, u32[]{:S(2)}) copy-start(bf16[192,1024]{1,0:T(8,128)(2,1)S(1)} %collective-permute-done.5.refs_5_) | copy-start | bytes 1179652
  35.2 12.7 %copy-start.1 = (s32[4]{0:T(128)S(1)}, s32[4]{0:T(128)}, u32[]{:S(2)}) copy-start(s32[4]{0:T(128)} %pad_add_fusion.ids_ref) | copy-start | bytes 52
  35.2 12.7 %copy-start.2 = (s32[4]{0:T(128)S(1)}, s32[4]{0:T(128)}, u32[]{:S(2)}) copy-start(s32[4]{0:T(128)} %valid_ref.1) | copy-start | bytes 52
  47.9 12.1 %copy-start = (bf16[4,256,384]{2,1,0:T(8,128)(2,1)S(1)}, bf16[4,256,384]{2,1,0:T(8,128)(2,1)}, u32[]{:S(2)}) copy-start(bf16[4,256,384]{2,1,0:T(8,128)(2,1)} %own_ref) | copy-start | bytes 2359300
  52.7 16.1 %collective-permute-start.10 = (bf16[1536,128]{1,0:T(8,128)(2,1)S(1)}, bf16[1536,128]{1,0:T(8,128)(2,1)S(1)}, u32[]{:S(2)}, u32[]{:S(2)}) collective-permute-start(bf16[1536,128]{1,0:T(8,128)(2,1)S(1)} %get-tuple-element.57), channel_id=1, source_target_pairs={{0,34},{1,35},{2,32},{3,33},{4,38},{5,39},{6,36},{7,37},{8,42},{9,... | collective-permute-start | bytes 1179656 | tf_op jit(solution)/shard_map/ppermute | solution.py:564
  54.7 16.8 %collective-permute-start.9 = (bf16[1536,128]{1,0:T(8,128)(2,1)S(1)}, bf16[1536,128]{1,0:T(8,128)(2,1)S(1)}, u32[]{:S(2)}, u32[]{:S(2)}) collective-permute-start(bf16[1536,128]{1,0:T(8,128)(2,1)S(1)} %get-tuple-element.57), channel_id=1, source_target_pairs={{0,32},{4,36},{8,40},{12,44},{16,48},{20,52},{24,56},{28,60},{32,0... | collective-permute-start | bytes 1179656 | tf_op jit(solution)/shard_map/ppermute | solution.py:559
  56.7 16.8 %collective-permute-start.8 = (bf16[1536,128]{1,0:T(8,128)(2,1)S(1)}, bf16[1536,128]{1,0:T(8,128)(2,1)S(1)}, u32[]{:S(2)}, u32[]{:S(2)}) collective-permute-start(bf16[1536,128]{1,0:T(8,128)(2,1)S(1)} %get-tuple-element.56.refs_0_), channel_id=1, source_target_pairs={{0,2},{1,3},{2,0},{3,1},{4,6},{5,7},{6,4},{7,5},{8,10},{9,11},{10,... | collective-permute-start | bytes 1179656 | tf_op jit(solution)/shard_map/ppermute | solution.py:555
  59.3 2.4 %collective-permute-start.11 = (bf16[96,128]{1,0:T(8,128)(2,1)S(1)}, bf16[96,128]{1,0:T(8,128)(2,1)S(1)}, u32[]{:S(2)}, u32[]{:S(2)}) collective-permute-start(bf16[96,128]{1,0:T(8,128)(2,1)S(1)} %get-tuple-element.58), channel_id=1, source_target_pairs={{3,4},{7,8},{11,12},{15,16},{19,20},{23,24},{27,28},{31,32},{35,36... | collective-permute-start | bytes 73736 | tf_op jit(solution)/shard_map/ppermute | solution.py:570
  59.9 15.4 %collective-permute-start.7 = (bf16[1536,128]{1,0:T(8,128)(2,1)S(1)}, bf16[1536,128]{1,0:T(8,128)(2,1)S(1)}, u32[]{:S(2)}, u32[]{:S(2)}) collective-permute-start(bf16[1536,128]{1,0:T(8,128)(2,1)S(1)} %get-tuple-element.56.refs_0_), channel_id=1, source_target_pairs={{0,1},{1,0},{2,3},{3,2},{4,5},{5,4},{6,7},{7,6},{8,9},{9,8},{10,11... | collective-permute-start | bytes 1179656 | tf_op jit(solution)/shard_map/ppermute | solution.py:555
  61.7 27.7 %copy-start.3 = (bf16[1632,128]{1,0:T(8,128)(2,1)}, bf16[1632,128]{1,0:T(8,128)(2,1)S(1)}, u32[]{:S(2)}) copy-start(bf16[1632,128]{1,0:T(8,128)(2,1)S(1)} %pad_maximum_fusion.refs_1_) | copy-start | bytes 1253380
  73.5 1.8 %collective-permute-start.13 = (bf16[1536,128]{1,0:T(8,128)(2,1)S(1)}, bf16[1536,128]{1,0:T(8,128)(2,1)S(1)}, u32[]{:S(2)}, u32[]{:S(2)}) collective-permute-start(bf16[1536,128]{1,0:T(8,128)(2,1)S(1)} %collective-permute-done.9.refs_4_), channel_id=1, source_target_pairs={{0,1},{1,0},{2,3},{3,2},{4,5},{5,4},{6,7},{7,6},{8,9},{9,8},{10,11... | collective-permute-start | bytes 1179656 | tf_op jit(solution)/shard_map/ppermute | solution.py:555
  73.5 2.3 %collective-permute-start.14 = (bf16[1536,128]{1,0:T(8,128)(2,1)S(1)}, bf16[1536,128]{1,0:T(8,128)(2,1)S(1)}, u32[]{:S(2)}, u32[]{:S(2)}) collective-permute-start(bf16[1536,128]{1,0:T(8,128)(2,1)S(1)} %collective-permute-done.10.refs_6_), channel_id=1, source_target_pairs={{0,1},{1,0},{2,3},{3,2},{4,5},{5,4},{6,7},{7,6},{8,9},{9,8},{10,11... | collective-permute-start | bytes 1179656 | tf_op jit(solution)/shard_map/ppermute | solution.py:555
  74.0 2.3 %collective-permute-start.12 = (bf16[1536,128]{1,0:T(8,128)(2,1)S(1)}, bf16[1536,128]{1,0:T(8,128)(2,1)S(1)}, u32[]{:S(2)}, u32[]{:S(2)}) collective-permute-start(bf16[1536,128]{1,0:T(8,128)(2,1)S(1)} %collective-permute-done.8.refs_2_), channel_id=1, source_target_pairs={{0,1},{1,0},{2,3},{3,2},{4,5},{5,4},{6,7},{7,6},{8,9},{9,8},{10,11... | collective-permute-start | bytes 1179656 | tf_op jit(solution)/shard_map/ppermute | solution.py:555
  74.0 15.4 %collective-permute-start.16 = (bf16[1632,128]{1,0:T(8,128)(2,1)S(1)}, bf16[1632,128]{1,0:T(8,128)(2,1)S(1)}, u32[]{:S(2)}, u32[]{:S(2)}) collective-permute-start(bf16[1632,128]{1,0:T(8,128)(2,1)S(1)} %pad_maximum_fusion.refs_1_), channel_id=1, source_target_pairs={{0,2},{1,3},{2,0},{3,1},{4,6},{5,7},{6,4},{7,5},{8,10},{9,11},{10,... | collective-permute-start | bytes 1253384 | tf_op jit(solution)/shard_map/ppermute | solution.py:555
  84.5 29.1 %all-to-all-start.1 = ((bf16[16,368,128]{2,1,0:T(8,128)(2,1)}), bf16[16,368,128]{2,1,0:T(8,128)(2,1)S(1)}, u32[]{:S(2)}, u32[]{:S(2)}) async-start(bf16[16,368,128]{2,1,0:T(8,128)(2,1)} %get-tuple-element.74), calls=%async_computation.1 | async-start | bytes 3014656 | tf_op jit(solution)/shard_map/all_to_all | solution.py:616
  89.4 1.8 %collective-permute-start.15 = (bf16[1632,128]{1,0:T(8,128)(2,1)S(1)}, bf16[1632,128]{1,0:T(8,128)(2,1)S(1)}, u32[]{:S(2)}, u32[]{:S(2)}) collective-permute-start(bf16[1632,128]{1,0:T(8,128)(2,1)S(1)} %pad_maximum_fusion.refs_1_), channel_id=1, source_target_pairs={{0,1},{1,0},{2,3},{3,2},{4,5},{5,4},{6,7},{7,6},{8,9},{9,8},{10,11... | collective-permute-start | bytes 1253384 | tf_op jit(solution)/shard_map/ppermute | solution.py:555
  89.5 1.7 %copy-start.4 = (bf16[1632,128]{1,0:T(8,128)(2,1)}, bf16[1632,128]{1,0:T(8,128)(2,1)S(1)}, u32[]{:S(2)}) copy-start(bf16[1632,128]{1,0:T(8,128)(2,1)S(1)} %collective-permute-done.16.refs_3_) | copy-start | bytes 1253380
  89.5 2.3 %collective-permute-start.17 = (bf16[1632,128]{1,0:T(8,128)(2,1)S(1)}, bf16[1632,128]{1,0:T(8,128)(2,1)S(1)}, u32[]{:S(2)}, u32[]{:S(2)}) collective-permute-start(bf16[1632,128]{1,0:T(8,128)(2,1)S(1)} %collective-permute-done.16.refs_3_), channel_id=1, source_target_pairs={{0,1},{1,0},{2,3},{3,2},{4,5},{5,4},{6,7},{7,6},{8,9},{9,8},{10,11... | collective-permute-start | bytes 1253384 | tf_op jit(solution)/shard_map/ppermute | solution.py:555
  92.0 0.8 copy-start.6
  (3 other events, 2.2 us)
